TPU v7x, 32 devices: a whole 2x2x4 slice. The times are simulated.
32 devices in a mesh: ctx: 8 (over y, x, core), ch: 4 (over z).
Axes of the slice: x: 2, y: 2, z: 4, core: 2. Of those that a mesh axis runs over, the one named last changes fastest.
Arguments:
- queries: bfloat16 [1024, 8192], P('ctx', 'ch'), may hold values from -6 to 6
- key_input: bfloat16 [1024, 8192], P('ctx', 'ch'), may hold values from -6 to 6
- value_input: bfloat16 [1024, 8192], P('ctx', 'ch'), may hold values from -6 to 6
- cotangent: bfloat16 [1024, 8192], P('ctx', 'ch'), may hold values from -60 to 60, as said below
- residues: float32 [512, 16], replicated, may hold values from -1 to 1
- log_rates: float32 [512, 16], replicated, may hold values from -14 to -3
- skip_gain: float32 [8192], replicated, may hold values from -1 to 1
Outputs:
- grad_query: bfloat16 [1024, 8192], P('ctx', 'ch')
- grad_key: bfloat16 [1024, 8192], P('ctx', 'ch')
- grad_value: bfloat16 [1024, 8192], P('ctx', 'ch')
- grad_residue: float32 [512, 16], replicated
- grad_lograte: float32 [512, 16], replicated
- grad_skip: float32 [8192], replicated
Inputs may be any that keep to these rules, and one draw needn't show every extreme that they name: Every row of the cotangent has its own scale.
All inputs are finite; a program needn't handle non-finite values.
Results may differ from a plain program's by a relative error of at most 0.017.
Values may be sent and summed in bfloat16 or wider, within the bound.
No kernel may reach another device: no remote copies, remote signals or barrier semaphores. Data moves between devices by JAX's collectives and lax.ppermute only.
A program may use at most 64 MiB of HBM per device.

v0:
```python
import math

import jax
import jax.numpy as jnp
from jax import lax
from jax.experimental import pallas as pl
from jax.experimental.pallas import tpu as pltpu
from jax.sharding import PartitionSpec as P

LANES = 128
F32 = jnp.float32
BF16 = jnp.bfloat16
EXACT = lax.Precision.HIGHEST
VMEM_LIMIT = 48 * 1024 * 1024


def iota(shape, axis):
    return lax.broadcasted_iota(jnp.int32, shape, axis)


def mxu(left, right):
    return jnp.dot(left, right, preferred_element_type=F32)


def exact_dot(left, right):
    return jnp.dot(left, right, precision=EXACT, preferred_element_type=F32)


def gate(left, right):
    return (left.astype(F32) * right.astype(F32)).astype(BF16)


def reversal(size):
    return jnp.where(iota((size, size), 0) + iota((size, size), 1) == size - 1, 1.0, 0.0).astype(BF16)


def split_pair(value):
    high = value.astype(BF16).astype(F32)
    return high, value - high


def flat_rows(table, poles):
    groups = table.shape[0]
    per_row = LANES // poles
    spread = jnp.where(iota((poles, LANES), 0) == iota((poles, LANES), 1) % poles, 1.0, 0.0)
    wide = exact_dot(table, spread)
    keep = iota((groups, LANES), 0) % per_row == iota((groups, LANES), 1) // poles
    wide = jnp.where(keep, wide, 0.0)
    return jnp.sum(wide.reshape(groups // per_row, per_row, LANES), axis=1)


def states_kernel(logs_ref, res_ref, q_ref, k_ref, v_ref, c_ref, send_ref, pair_ref, rows_ref, *, group, poles):
    tokens, width = q_ref.shape
    per_block = LANES // group
    shard_groups = rows_ref.shape[1] * per_block
    owners, _, own_width = send_ref.shape
    step = pl.program_id(0)
    blocks = width // LANES

    @pl.when(step == 0)
    def _():
        first = lax.axis_index("ch") * shard_groups
        rows_ref[0] = jnp.exp(flat_rows(logs_ref[pl.ds(first, shard_groups), :], poles))
        rows_ref[1] = flat_rows(res_ref[pl.ds(first, shard_groups), :], poles)

    flip = reversal(tokens)
    back_pos = (tokens - 1 - iota((tokens, LANES), 0)).astype(F32)
    back_lane = (tokens - 1 - iota((per_block, tokens), 1)).astype(F32)
    lane_group = iota((tokens, LANES), 1) // group
    causal = iota((tokens, tokens), 0) + iota((tokens, tokens), 1) <= tokens - 1
    wide_group = (iota((poles, 2 * LANES), 1) % LANES) // group
    half = per_block // 2
    own_rows = iota((per_block, LANES), 0) == iota((per_block, LANES), 1) // poles
    zero = jnp.zeros((tokens, LANES), BF16)

    for j in range(blocks):
        cut = slice(j * LANES, (j + 1) * LANES)
        gated = gate(k_ref[:, cut], v_ref[:, cut])
        dgate = gate(c_ref[:, cut], q_ref[:, cut])
        skip = jnp.sum(gated.astype(F32) * dgate.astype(F32), axis=0, keepdims=True)
        turned = mxu(flip, dgate).astype(BF16)
        pair = jnp.concatenate([gated, turned], axis=1)
        pair_ref[:, 2 * j * LANES : 2 * (j + 1) * LANES] = pair
        rate = rows_ref[0, pl.ds(step * blocks + j, 1), :]
        table = jnp.exp(-rate * back_pos)
        table_low = table.astype(BF16)
        both = jnp.concatenate([table.T.astype(BF16), (table * back_pos).T.astype(BF16)], axis=0)
        summed = mxu(both, pair)
        folded = []
        for part in range(2):
            total = jnp.zeros((poles, 2 * LANES), F32)
            for g in range(per_block):
                start = part * LANES + g * poles
                total = jnp.where(wide_group == g, summed[start : start + poles], total)
            folded.append(total)
        left = [
            jnp.where((lane_group == i) | (lane_group == i + half), turned, zero) for i in range(half)
        ]
        right = [
            jnp.where(lane_group < half, gated, zero),
            jnp.where(lane_group >= half, gated, zero),
        ]
        outer = lax.dot_general(
            jnp.concatenate(left, axis=0),
            jnp.concatenate(right, axis=0),
            (((1,), (1,)), ((), ())),
            preferred_element_type=F32,
        )
        lags = []
        for h in range(2):
            for i in range(half):
                tile = outer[i * tokens : (i + 1) * tokens, h * tokens : (h + 1) * tokens]
                tile = jnp.where(causal, tile, 0.0)
                total = tile[:8]
                for a in range(1, tokens // 8):
                    total = total + pltpu.roll(tile[8 * a : 8 * a + 8], 8 * a, 1)
                total = pltpu.roll(total, 0, 1, stride=1, stride_axis=0)
                lags.append(jnp.sum(total, axis=0, keepdims=True))
        lag = jnp.concatenate(lags, axis=0)
        lag_high, lag_low = split_pair(lag)
        mom_high, mom_low = split_pair(lag * back_lane)
        stack = jnp.concatenate([lag_high, lag_low, mom_high, mom_low], axis=0).astype(BF16)
        local = mxu(stack, table_low)
        res_part = local[:per_block] + local[per_block : 2 * per_block]
        mom_part = local[2 * per_block : 3 * per_block] + local[3 * per_block :]
        res_row = jnp.sum(jnp.where(own_rows, res_part, 0.0), axis=0, keepdims=True)
        mom_row = jnp.sum(jnp.where(own_rows, mom_part, 0.0), axis=0, keepdims=True)
        extra = jnp.concatenate(
            [*split_pair(res_row), *split_pair(mom_row), *split_pair(skip), jnp.zeros((10, LANES), F32)],
            axis=0,
        )
        out = jnp.concatenate(
            [
                folded[0][:, :LANES],
                folded[0][:, LANES:],
                folded[1][:, :LANES],
                folded[1][:, LANES:],
                extra,
            ],
            axis=0,
        ).astype(BF16)
        if own_width >= LANES:
            place = j * LANES // own_width
            offset = j * LANES % own_width
            send_ref[place, :, offset : offset + LANES] = out
        else:
            for n in range(LANES // own_width):
                send_ref[j * (LANES // own_width) + n] = out[:, n * own_width : (n + 1) * own_width]


def conv_kernel(rows_ref, skip_ref, pair_ref, conv_ref, *, group, poles):
    tokens, width = pair_ref.shape
    per_block = LANES // group
    step = pl.program_id(0)
    blocks = width // (2 * LANES)
    all_blocks = rows_ref.shape[1]
    first = lax.axis_index("ch") * all_blocks
    back_pos = (tokens - 1 - iota((tokens, LANES), 0)).astype(F32)
    wide_group = (iota((tokens, 2 * LANES), 1) % LANES) // group
    causal = iota((tokens, tokens), 0) >= iota((tokens, tokens), 1)
    for j in range(blocks):
        cut = slice(2 * j * LANES, 2 * (j + 1) * LANES)
        pair = pair_ref[:, cut]
        here = step * blocks + j
        rate = rows_ref[0, pl.ds(here, 1), :]
        res = rows_ref[1, pl.ds(here, 1), :]
        table = (res * jnp.exp(-rate * back_pos)).T
        left, right = [], []
        for g in range(per_block):
            taps = jnp.sum(table[g * poles : (g + 1) * poles], axis=0, keepdims=True)
            base = pltpu.roll(jnp.broadcast_to(taps, (8, tokens)), 1, 1, stride=1, stride_axis=0)
            rolled = [base] + [pltpu.roll(base, 8 * a, 1) for a in range(1, tokens // 8)]
            left.append(jnp.where(causal, jnp.concatenate(rolled, axis=0), 0.0).astype(BF16))
            right.append(jnp.where(wide_group == g, pair, jnp.zeros_like(pair)))
        total = mxu(jnp.concatenate(left, axis=1), jnp.concatenate(right, axis=0))
        gain = skip_ref[pl.ds(first + here, 1), :]
        conv_ref[:, cut] = total + jnp.concatenate([gain, gain], axis=1) * pair.astype(F32)


def scan_kernel(logs_ref, res_ref, got_ref, back_ref, grad_ref, *, group, poles, tokens, first_of):
    parts, _, width = got_ref.shape
    groups = width // group
    first = first_of(groups)
    scale = tokens * parts
    spread = jnp.where(iota((poles, width), 0) == iota((poles, width), 1) % poles, 1.0, 0.0)
    keep = iota((groups, width), 0) == iota((groups, width), 1) // poles
    pick = iota((poles, width), 0) == iota((poles, width), 1) % poles
    same = jnp.where(iota((width, width), 0) // group == iota((width, width), 1) // group, 1.0, 0.0)

    def flat(ref):
        wide = exact_dot(ref[pl.ds(first, groups), :], spread)
        return jnp.sum(jnp.where(keep, wide, 0.0), axis=0, keepdims=True)

    rate = jnp.exp(flat(logs_ref))
    res = flat(res_ref)
    rates = exact_dot(jnp.where(pick, rate, 0.0), same)
    decay = jnp.exp(-rates * tokens)
    one = jnp.exp(-rates)

    def rows(i, n):
        return got_ref[i, n * poles : (n + 1) * poles, :].astype(F32)

    zeros = jnp.zeros((poles, width), F32)
    state, moment, sum_res, sum_mom = zeros, zeros, zeros, zeros
    extra = jnp.zeros((16, width), F32)
    for i in range(parts):
        back_ref[i, :poles, :] = state.astype(BF16)
        begin = rows(i, 1)
        sum_res += begin * state
        sum_mom += rows(i, 3) * state + begin * moment
        ahead = rows(i, 0)
        moment = decay * (moment + tokens * state) + rows(i, 2) + ahead
        state = decay * state + ahead
        extra += got_ref[i, 4 * poles :, :].astype(F32)
    state = zeros
    for i in reversed(range(parts)):
        back_ref[i, poles:, :] = state.astype(BF16)
        state = decay * state + rows(i, 1)

    def gather(total, high, low):
        wide = exact_dot(total * one, same)
        return jnp.sum(jnp.where(pick, wide, 0.0), axis=0, keepdims=True) + high + low

    grad_res = gather(sum_res, extra[0:1], extra[1:2]) / scale
    grad_log = -rate * res * gather(sum_mom, extra[2:3], extra[3:4]) / math.sqrt(scale)
    grad_skip = (extra[4:5] + extra[5:6]) / math.sqrt(scale)
    grad_ref[...] = jnp.concatenate(
        [grad_res, grad_log, grad_skip, jnp.zeros((5, width), F32)], axis=0
    )


def output_kernel(rows_ref, conv_ref, back_ref, k_ref, v_ref, c_ref, gq_ref, gk_ref, gv_ref, *, group, poles):
    tokens, width = k_ref.shape
    per_block = LANES // group
    own_width = back_ref.shape[2]
    step = pl.program_id(0)
    blocks = width // LANES
    flip = reversal(tokens)
    ahead = (1 + iota((tokens, LANES), 0)).astype(F32)
    wide_group = (iota((poles, 2 * LANES), 1) % LANES) // group
    for j in range(blocks):
        cut = slice(j * LANES, (j + 1) * LANES)
        here = step * blocks + j
        rate = rows_ref[0, pl.ds(here, 1), :]
        res = rows_ref[1, pl.ds(here, 1), :]
        table = (res * jnp.exp(-rate * ahead)).astype(BF16)
        if own_width >= LANES:
            place, offset = j * LANES // own_width, j * LANES % own_width
            states = back_ref[place, :, offset : offset + LANES]
        else:
            count = LANES // own_width
            states = jnp.concatenate([back_ref[j * count + n] for n in range(count)], axis=1)
        states = jnp.concatenate([states[:poles], states[poles:]], axis=1)
        stack = jnp.concatenate(
            [jnp.where(wide_group == g, states, jnp.zeros_like(states)) for g in range(per_block)], axis=0
        )
        total = (conv_ref[:, 2 * j * LANES : 2 * (j + 1) * LANES] + mxu(table, stack)).astype(BF16)
        flow = mxu(flip, total[:, LANES:])
        gq_ref[:, cut] = (c_ref[:, cut].astype(F32) * total[:, :LANES].astype(F32)).astype(BF16)
        gk_ref[:, cut] = (flow * v_ref[:, cut].astype(F32)).astype(BF16)
        gv_ref[:, cut] = (flow * k_ref[:, cut].astype(F32)).astype(BF16)


def local(queries, key_input, value_input, cotangent, residues, log_rates, skip_gain):
    tokens, width = queries.shape
    parts = lax.axis_size("ctx")
    shards = lax.axis_size("ch")
    all_groups, poles = residues.shape
    group = width * shards // all_groups
    own_width = width // parts
    step_width = min(width, max(4 * LANES, own_width))
    steps = width // step_width
    blocks = width // LANES
    payload = 4 * poles + 16
    owners = step_width // own_width
    sizes = dict(group=group, poles=poles)
    params = pltpu.CompilerParams(vmem_limit_bytes=VMEM_LIMIT)

    whole = pl.BlockSpec((all_groups, poles), lambda i: (0, 0))
    main = pl.BlockSpec((tokens, step_width), lambda i: (0, i))
    twice = pl.BlockSpec((tokens, 2 * step_width), lambda i: (0, i))
    row_table = pl.BlockSpec((2, blocks, LANES), lambda i: (0, 0, 0))

    send, pair, rows = pl.pallas_call(
        lambda *refs: states_kernel(*refs, **sizes),
        grid=(steps,),
        in_specs=[whole, whole, main, main, main, main],
        out_specs=[
            pl.BlockSpec((owners, payload, own_width), lambda i: (i, 0, 0)),
            twice,
            row_table,
        ],
        out_shape=[
            jax.ShapeDtypeStruct((parts, payload, own_width), BF16),
            jax.ShapeDtypeStruct((tokens, 2 * width), BF16),
            jax.ShapeDtypeStruct((2, blocks, LANES), F32),
        ],
        compiler_params=params,
        name="states",
    )(log_rates, residues, queries, key_input, value_input, cotangent)

    got = lax.all_to_all(send, "ctx", split_axis=0, concat_axis=0, tiled=True)

    skip_rows = skip_gain.reshape(-1, LANES)
    conv = pl.pallas_call(
        lambda *refs: conv_kernel(*refs, **sizes),
        grid=(steps,),
        in_specs=[row_table, pl.BlockSpec(skip_rows.shape, lambda i: (0, 0)), twice],
        out_specs=twice,
        out_shape=jax.ShapeDtypeStruct((tokens, 2 * width), F32),
        compiler_params=params,
        cost_estimate=pl.CostEstimate(
            flops=16 * tokens * tokens * width, bytes_accessed=12 * tokens * width, transcendentals=tokens * width
        ),
        name="conv",
    )(rows, skip_rows, pair)

    def first_of(groups):
        return (lax.axis_index("ch") * parts + lax.axis_index("ctx")) * groups

    vmem = pl.BlockSpec(memory_space=pltpu.VMEM)
    back, grads = pl.pallas_call(
        lambda *refs: scan_kernel(*refs, tokens=tokens, first_of=first_of, **sizes),
        in_specs=[vmem, vmem, vmem],
        out_specs=[vmem, vmem],
        out_shape=[
            jax.ShapeDtypeStruct((parts, 2 * poles, own_width), BF16),
            jax.ShapeDtypeStruct((8, own_width), F32),
        ],
        compiler_params=params,
        name="scan",
    )(log_rates, residues, got)

    states = lax.all_to_all(back, "ctx", split_axis=0, concat_axis=0, tiled=True)
    spread = jnp.broadcast_to(grads[None], (parts * shards, 8, own_width))
    final = lax.all_to_all(spread, ("ctx", "ch"), split_axis=0, concat_axis=0, tiled=True)

    grad_query, grad_key, grad_value = pl.pallas_call(
        lambda *refs: output_kernel(*refs, **sizes),
        grid=(steps,),
        in_specs=[
            row_table,
            twice,
            pl.BlockSpec((owners, 2 * poles, own_width), lambda i: (i, 0, 0)),
            main,
            main,
            main,
        ],
        out_specs=[main, main, main],
        out_shape=[jax.ShapeDtypeStruct((tokens, width), BF16)] * 3,
        compiler_params=params,
        name="outputs",
    )(rows, conv, states, key_input, value_input, cotangent)

    final = final.reshape(parts, shards, 8, own_width).transpose(2, 1, 0, 3)
    grad_residue = final[0].reshape(all_groups, poles)
    grad_lograte = final[1].reshape(all_groups, poles)
    grad_skip = final[2].reshape(-1)
    return (grad_query, grad_key, grad_value, grad_residue, grad_lograte, grad_skip)


def solution(mesh):
    placed = (P("ctx", "ch"), P("ctx", "ch"), P("ctx", "ch"), P("ctx", "ch"), P(), P(), P())
    return jax.shard_map(
        local,
        mesh=mesh,
        in_specs=placed,
        out_specs=(P("ctx", "ch"), P("ctx", "ch"), P("ctx", "ch"), P(), P(), P()),
        check_vma=False,
    )
```

profile of v0, /device:TPU:0, one launch (start us, length us, event | category | flops | bytes accessed | tf_op | source)
XLA Modules:
  0.0 56.4 jit_solution(3933025814356562028)
XLA Ops:
  0.6 0.9 %copy.24.refs_1_ = f32[512,16]{1,0:T(8,128)S(1)} copy(f32[512,16]{0,1:T(8,128)} %param.11) | data formatting | bytes 65536 | tf_op args[4]
  1.5 0.9 %copy.23.refs_0_ = f32[512,16]{1,0:T(8,128)S(1)} copy(f32[512,16]{0,1:T(8,128)} %param.12) | data formatting | bytes 65536 | tf_op args[5]
  2.4 0.0 copy-start
  2.4 1.0 %copy-done = bf16[128,2048]{1,0:T(8,128)(2,1)S(1)} copy-done((bf16[128,2048]{1,0:T(8,128)(2,1)S(1)}, bf16[128,2048]{1,0:T(8,128)(2,1)}, u32[]{:S(2)}) %copy-start) | copy-done | bytes 524312
  3.5 0.0 copy-start.2
  3.5 1.0 %copy-done.2 = bf16[128,2048]{1,0:T(8,128)(2,1)S(1)} copy-done((bf16[128,2048]{1,0:T(8,128)(2,1)S(1)}, bf16[128,2048]{1,0:T(8,128)(2,1)}, u32[]{:S(2)}) %copy-start.2) | copy-done | bytes 524312
  4.5 0.0 copy-start.4
  4.5 1.0 %copy-done.4 = bf16[128,2048]{1,0:T(8,128)(2,1)S(1)} copy-done((bf16[128,2048]{1,0:T(8,128)(2,1)S(1)}, bf16[128,2048]{1,0:T(8,128)(2,1)}, u32[]{:S(2)}) %copy-start.4) | copy-done | bytes 524312
  5.5 0.0 copy-start.6
  5.5 1.0 %copy-done.6 = bf16[128,2048]{1,0:T(8,128)(2,1)S(1)} copy-done((bf16[128,2048]{1,0:T(8,128)(2,1)S(1)}, bf16[128,2048]{1,0:T(8,128)(2,1)}, u32[]{:S(2)}) %copy-start.6) | copy-done | bytes 524312
  6.6 0.0 copy-start.7
  6.6 11.0 %states.1 = (bf16[8,80,256]{2,1,0:T(8,128)(2,1)S(1)}, bf16[128,4096]{1,0:T(8,128)(2,1)S(1)}, f32[2,16,128]{2,1,0:T(8,128)S(1)}) custom-call(f32[512,16]{1,0:T(8,128)S(1)} %copy.23.refs_0_, f32[512,16]{1,0:T(8,128)S(1)} %copy.24.refs_1_, bf16[128,2048]{1,0:T(8,128)(2,1)S(1)} %copy-done.6, bf16[128,2048]{1,0:T(8,128)(2,1)S(1)} %copy-done, ...), custom_call_target="tpu_custom_call" | custom-call | tf_op jit(solution)/shard_map/states/pallas_call | solution.py:284
  17.6 12.6 %all_to_all.15.refs_2_ = bf16[8,80,256]{2,1,0:T(8,128)(2,1)S(1)} all-to-all(bf16[8,80,256]{2,1,0:T(8,128)(2,1)S(1)} %get-tuple-element.16), channel_id=1, replica_groups=mesh['ctx'=8,'ch'=4] {'ctx'}, dimensions={0} | all-to-all | bytes 655360 | tf_op jit(solution)/shard_map/all_to_all | solution.py:302
  30.2 0.8 %scan.1 = (bf16[8,32,256]{2,1,0:T(8,128)(2,1)S(1)}, f32[8,256]{1,0:T(8,128)S(1)}) custom-call(f32[512,16]{1,0:T(8,128)S(1)} %copy.23.refs_0_, f32[512,16]{1,0:T(8,128)S(1)} %copy.24.refs_1_, bf16[8,80,256]{2,1,0:T(8,128)(2,1)S(1)} %all_to_all.15.refs_2_), custom_call_target="tpu_custom_call" | custom-call | tf_op jit(solution)/shard_map/scan/pallas_call | solution.py:322
  31.0 0.0 copy-start.1
  31.0 0.0 copy-start.3
  31.0 0.0 copy-start.5
  31.0 8.1 %all_to_all.16.refs_2_ = bf16[8,32,256]{2,1,0:T(8,128)(2,1)S(1)} all-to-all(bf16[8,32,256]{2,1,0:T(8,128)(2,1)S(1)} %get-tuple-element.17), channel_id=1, replica_groups=mesh['ctx'=8,'ch'=4] {'ctx'}, dimensions={0} | all-to-all | bytes 262144 | tf_op jit(solution)/shard_map/all_to_all | solution.py:334
  39.1 0.7 %broadcast_in_dim.2 = f32[32,8,256]{2,1,0:T(8,128)} broadcast(f32[8,256]{1,0:T(8,128)S(1)} %get-tuple-element.21), dimensions={1,2} | broadcast | bytes 270336 | tf_op jit(solution)/shard_map/broadcast_in_dim | solution.py:335
  39.8 4.0 %all-to-all-start.2 = ((f32[32,8,256]{2,1,0:T(8,128)}), f32[32,8,256]{2,1,0:T(8,128)S(1)}, u32[]{:S(2)}, u32[]{:S(2)}) async-start(f32[32,8,256]{2,1,0:T(8,128)} %broadcast_in_dim.2), calls=%async_computation.2 | async-start | bytes 524288 | tf_op jit(solution)/shard_map/all_to_all | solution.py:336
  43.8 0.0 copy-done.7
  43.8 4.0 %conv.1.refs_1_ = f32[128,4096]{1,0:T(8,128)S(1)} custom-call(f32[2,16,128]{2,1,0:T(8,128)S(1)} %get-tuple-element.14.refs_0_, f32[64,128]{1,0:T(8,128)S(1)} %bitcast.12, bf16[128,4096]{1,0:T(8,128)(2,1)S(1)} %get-tuple-element.15.refs_2_), custom_call_target="tpu_custom_call" | custom-call | flops 536870912 | bytes 3145728 | tf_op jit(solution)/shard_map/conv/pallas_call | solution.py:305
  47.8 0.0 copy-done.1
  47.8 0.0 copy-done.3
  47.9 0.0 copy-done.5
  47.9 4.3 %outputs.1 = (bf16[128,2048]{1,0:T(8,128)(2,1)}, bf16[128,2048]{1,0:T(8,128)(2,1)}, bf16[128,2048]{1,0:T(8,128)(2,1)}) custom-call(f32[2,16,128]{2,1,0:T(8,128)S(1)} %get-tuple-element.14.refs_0_, f32[128,4096]{1,0:T(8,128)S(1)} %conv.1.refs_1_, bf16[8,32,256]{2,1,0:T(8,128)(2,1)S(1)} %all_to_all.16.refs_2_, bf16[128,2048]{1,0:T(8,128)(2,1)S(1)} %copy-done.1, ...), custom_call_target="tpu_custom_call" | custom-call | tf_op jit(solution)/shard_map/outputs/pallas_call | solution.py:338
  52.2 1.8 %all-to-all-done.2 = f32[32,8,256]{2,1,0:T(8,128)S(1)} async-done(((f32[32,8,256]{2,1,0:T(8,128)}), f32[32,8,256]{2,1,0:T(8,128)S(1)}, u32[]{:S(2)}, u32[]{:S(2)}) %all-to-all-start.2) | async-done | bytes 262176 | tf_op jit(solution)/shard_map/all_to_all | solution.py:336
  54.0 0.1 fusion
  54.1 0.6 %copy.32 = f32[4,2,8,128]{3,1,2,0:T(2,128)} copy(f32[4,2,8,128]{3,2,1,0:T(8,128)S(1)} %bitcast.14) | data formatting | bytes 65536
  54.7 0.1 reshape_squeeze.9
  54.8 0.7 %copy.30 = f32[512,16]{0,1:T(8,128)} copy(f32[512,16]{1,0:T(8,128)S(1)} %reshape_squeeze.9) | data formatting | bytes 65536
  55.6 0.1 reshape_squeeze.10
  55.7 0.7 %copy.31 = f32[512,16]{0,1:T(8,128)} copy(f32[512,16]{1,0:T(8,128)S(1)} %reshape_squeeze.10) | data formatting | bytes 65536
  (3 shorter events, 0.0 us)
Async XLA Ops:
  2.4 1.0 %copy-start = (bf16[128,2048]{1,0:T(8,128)(2,1)S(1)}, bf16[128,2048]{1,0:T(8,128)(2,1)}, u32[]{:S(2)}) copy-start(bf16[128,2048]{1,0:T(8,128)(2,1)} %refs_3_.3) | copy-start | bytes 1572868
  3.5 1.0 %copy-start.2 = (bf16[128,2048]{1,0:T(8,128)(2,1)S(1)}, bf16[128,2048]{1,0:T(8,128)(2,1)}, u32[]{:S(2)}) copy-start(bf16[128,2048]{1,0:T(8,128)(2,1)} %refs_4_.3) | copy-start | bytes 1572868
  4.5 1.0 %copy-start.4 = (bf16[128,2048]{1,0:T(8,128)(2,1)S(1)}, bf16[128,2048]{1,0:T(8,128)(2,1)}, u32[]{:S(2)}) copy-start(bf16[128,2048]{1,0:T(8,128)(2,1)} %refs_5_.3) | copy-start | bytes 1572868
  5.5 1.0 %copy-start.6 = (bf16[128,2048]{1,0:T(8,128)(2,1)S(1)}, bf16[128,2048]{1,0:T(8,128)(2,1)}, u32[]{:S(2)}) copy-start(bf16[128,2048]{1,0:T(8,128)(2,1)} %refs_2_.1) | copy-start | bytes 1572868
  6.6 37.2 %copy-start.7 = (f32[8192]{0:T(1024)S(1)}, f32[8192]{0:T(1024)}, u32[]{:S(2)}) copy-start(f32[8192]{0:T(1024)} %param.13) | copy-start | bytes 98308
  31.0 16.8 %copy-start.1 = (bf16[128,2048]{1,0:T(8,128)(2,1)S(1)}, bf16[128,2048]{1,0:T(8,128)(2,1)}, u32[]{:S(2)}) copy-start(bf16[128,2048]{1,0:T(8,128)(2,1)} %refs_3_.3) | copy-start | bytes 1572868
  31.0 16.8 %copy-start.3 = (bf16[128,2048]{1,0:T(8,128)(2,1)S(1)}, bf16[128,2048]{1,0:T(8,128)(2,1)}, u32[]{:S(2)}) copy-start(bf16[128,2048]{1,0:T(8,128)(2,1)} %refs_4_.3) | copy-start | bytes 1572868
  31.0 16.8 %copy-start.5 = (bf16[128,2048]{1,0:T(8,128)(2,1)S(1)}, bf16[128,2048]{1,0:T(8,128)(2,1)}, u32[]{:S(2)}) copy-start(bf16[128,2048]{1,0:T(8,128)(2,1)} %refs_5_.3) | copy-start | bytes 1572868
  39.8 14.2 %all-to-all-start.2 = ((f32[32,8,256]{2,1,0:T(8,128)}), f32[32,8,256]{2,1,0:T(8,128)S(1)}, u32[]{:S(2)}, u32[]{:S(2)}) async-start(f32[32,8,256]{2,1,0:T(8,128)} %broadcast_in_dim.2), calls=%async_computation.2 | async-start | bytes 524288 | tf_op jit(solution)/shard_map/all_to_all | solution.py:336
where the time goes:
time: 57 us; the launch traced here: 56.4 us
  blocking collectives  20.7 us (36%)
  Pallas kernels  20.2 us (35%)
  local copies, waits for them, and re-layouts  9.06 us (16%)
  starting transfers between devices  3.96 us (7%)
  waiting for transfers between devices  1.79 us (3%)
  between operations  0.78 us (1%)
    all_to_all x1, blocking collectives, local(): got = lax.all_to_all(send, 'ctx', split_axis=0, concat_axis=0, tiled=True)  12.6 us
    pallas_call x1, Pallas kernels, local(): pl.pallas_call(lambda *refs: states_kernel(*refs, **sizes), grid=(steps,)...  11 us
    all_to_all x1, blocking collectives, local(): lax.all_to_all(back, 'ctx', split_axis=0, concat_axis=0, tiled=True)  8.05 us
    unnamed x21, local copies, waits for them, and re-layouts  8.02 us
    pallas_call x1, Pallas kernels, local(): pl.pallas_call(lambda *refs: output_kernel(*refs, **sizes), grid=(steps,)...  4.32 us
    pallas_call x1, Pallas kernels, local(): pl.pallas_call(lambda *refs: conv_kernel(*refs, **sizes), grid=(steps,),...  4.04 us
    all_to_all x1, starting transfers between devices, local(): lax.all_to_all(spread, ('ctx', 'ch'), split_axis=0, concat_axis=0, tiled=...  3.96 us
    all_to_all x1, waiting for transfers between devices, local(): lax.all_to_all(spread, ('ctx', 'ch'), split_axis=0, concat_axis=0, tiled=...  1.79 us
  transfers between devices with their start and end apart: 1, of which 1 were waited for; matrix products, arithmetic and copies ran while one was open for 0% of the time, Pallas kernels for 15%

commit v1 on v0

--- a/solution.py
+++ b/solution.py
@@ -40,6 +40,7 @@
 
 
 def flat_rows(table, poles):
+    table = table.T
     groups = table.shape[0]
     per_row = LANES // poles
     spread = jnp.where(iota((poles, LANES), 0) == iota((poles, LANES), 1) % poles, 1.0, 0.0)
@@ -49,19 +50,21 @@
     return jnp.sum(wide.reshape(groups // per_row, per_row, LANES), axis=1)
 
 
-def states_kernel(logs_ref, res_ref, q_ref, k_ref, v_ref, c_ref, send_ref, pair_ref, rows_ref, *, group, poles):
+def states_kernel(logs_ref, res_ref, q_ref, k_ref, v_ref, c_ref, *rest, group, poles, parts):
+    *slots, pair_ref, rows_ref, all_ref = rest
     tokens, width = q_ref.shape
     per_block = LANES // group
     shard_groups = rows_ref.shape[1] * per_block
-    owners, _, own_width = send_ref.shape
+    _, own_width = slots[0].shape
+    owners = width // own_width
     step = pl.program_id(0)
     blocks = width // LANES
 
     @pl.when(step == 0)
     def _():
-        first = lax.axis_index("ch") * shard_groups
-        rows_ref[0] = jnp.exp(flat_rows(logs_ref[pl.ds(first, shard_groups), :], poles))
-        rows_ref[1] = flat_rows(res_ref[pl.ds(first, shard_groups), :], poles)
+        first = pl.multiple_of(lax.axis_index("ch") * shard_groups, LANES)
+        rows_ref[0] = jnp.exp(flat_rows(logs_ref[:, pl.ds(first, shard_groups)], poles))
+        rows_ref[1] = flat_rows(res_ref[:, pl.ds(first, shard_groups)], poles)
 
     flip = reversal(tokens)
     back_pos = (tokens - 1 - iota((tokens, LANES), 0)).astype(F32)
@@ -142,10 +145,16 @@
         if own_width >= LANES:
             place = j * LANES // own_width
             offset = j * LANES % own_width
-            send_ref[place, :, offset : offset + LANES] = out
+            all_ref[step * owners + place, :, offset : offset + LANES] = out
         else:
             for n in range(LANES // own_width):
-                send_ref[j * (LANES // own_width) + n] = out[:, n * own_width : (n + 1) * own_width]
+                place = j * (LANES // own_width) + n
+                all_ref[step * owners + place] = out[:, n * own_width : (n + 1) * own_width]
+
+    @pl.when(step == pl.num_programs(0) - 1)
+    def _():
+        for shift, slot in enumerate(slots):
+            slot[...] = all_ref[lax.rem(lax.axis_index("ctx") + shift, parts)]
 
 
 def conv_kernel(rows_ref, skip_ref, pair_ref, conv_ref, *, group, poles):
@@ -177,10 +186,19 @@
         conv_ref[:, cut] = total + jnp.concatenate([gain, gain], axis=1) * pair.astype(F32)
 
 
-def scan_kernel(logs_ref, res_ref, got_ref, back_ref, grad_ref, *, group, poles, tokens, first_of):
-    parts, _, width = got_ref.shape
+def scan_kernel(logs_ref, res_ref, *rest, group, poles, tokens, parts):
+    slots, backs = rest[:parts], rest[parts : 2 * parts]
+    grad_ref, got_ref, back_ref = rest[2 * parts :]
+    _, width = slots[0].shape
     groups = width // group
-    first = first_of(groups)
+    me = lax.axis_index("ctx")
+    for shift in range(parts):
+        got_ref[lax.rem(me - shift + parts, parts)] = slots[shift][...]
+    shard_groups = groups * parts
+    start = pl.multiple_of(lax.axis_index("ch") * shard_groups, LANES)
+    mine = jnp.where(
+        iota((shard_groups, groups), 0) == me * groups + iota((shard_groups, groups), 1), 1.0, 0.0
+    )
     scale = tokens * parts
     spread = jnp.where(iota((poles, width), 0) == iota((poles, width), 1) % poles, 1.0, 0.0)
     keep = iota((groups, width), 0) == iota((groups, width), 1) // poles
@@ -188,7 +206,8 @@
     same = jnp.where(iota((width, width), 0) // group == iota((width, width), 1) // group, 1.0, 0.0)
 
     def flat(ref):
-        wide = exact_dot(ref[pl.ds(first, groups), :], spread)
+        table = exact_dot(ref[:, pl.ds(start, shard_groups)], mine).T
+        wide = exact_dot(table, spread)
         return jnp.sum(jnp.where(keep, wide, 0.0), axis=0, keepdims=True)
 
     rate = jnp.exp(flat(logs_ref))
@@ -224,12 +243,16 @@
     grad_res = gather(sum_res, extra[0:1], extra[1:2]) / scale
     grad_log = -rate * res * gather(sum_mom, extra[2:3], extra[3:4]) / math.sqrt(scale)
     grad_skip = (extra[4:5] + extra[5:6]) / math.sqrt(scale)
+    for shift in range(parts):
+        backs[shift][...] = back_ref[lax.rem(me + shift, parts)]
     grad_ref[...] = jnp.concatenate(
         [grad_res, grad_log, grad_skip, jnp.zeros((5, width), F32)], axis=0
     )
 
 
-def output_kernel(rows_ref, conv_ref, back_ref, k_ref, v_ref, c_ref, gq_ref, gk_ref, gv_ref, *, group, poles):
+def output_kernel(rows_ref, conv_ref, k_ref, v_ref, c_ref, *rest, group, poles, parts):
+    slots = rest[:parts]
+    gq_ref, gk_ref, gv_ref, back_ref = rest[parts:]
     tokens, width = k_ref.shape
     per_block = LANES // group
     own_width = back_ref.shape[2]
@@ -238,6 +261,13 @@
     flip = reversal(tokens)
     ahead = (1 + iota((tokens, LANES), 0)).astype(F32)
     wide_group = (iota((poles, 2 * LANES), 1) % LANES) // group
+    owners = max(1, width // own_width)
+
+    @pl.when(step == 0)
+    def _():
+        for shift, slot in enumerate(slots):
+            back_ref[lax.rem(lax.axis_index("ctx") - shift + parts, parts)] = slot[...]
+
     for j in range(blocks):
         cut = slice(j * LANES, (j + 1) * LANES)
         here = step * blocks + j
@@ -246,10 +276,10 @@
         table = (res * jnp.exp(-rate * ahead)).astype(BF16)
         if own_width >= LANES:
             place, offset = j * LANES // own_width, j * LANES % own_width
-            states = back_ref[place, :, offset : offset + LANES]
+            states = back_ref[step * owners + place, :, offset : offset + LANES]
         else:
             count = LANES // own_width
-            states = jnp.concatenate([back_ref[j * count + n] for n in range(count)], axis=1)
+            states = jnp.concatenate([back_ref[step * owners + j * count + n] for n in range(count)], axis=1)
         states = jnp.concatenate([states[:poles], states[poles:]], axis=1)
         stack = jnp.concatenate(
             [jnp.where(wide_group == g, states, jnp.zeros_like(states)) for g in range(per_block)], axis=0
@@ -272,40 +302,47 @@
     steps = width // step_width
     blocks = width // LANES
     payload = 4 * poles + 16
-    owners = step_width // own_width
     sizes = dict(group=group, poles=poles)
     params = pltpu.CompilerParams(vmem_limit_bytes=VMEM_LIMIT)
 
-    whole = pl.BlockSpec((all_groups, poles), lambda i: (0, 0))
+    def fixed(*shape):
+        return pl.BlockSpec(shape, lambda i: (0,) * len(shape))
+
+    def shifted(arrays):
+        moved = [arrays[0]]
+        for shift in range(1, parts):
+            pairs = [(source, (source + shift) % parts) for source in range(parts)]
+            moved.append(lax.ppermute(arrays[shift], "ctx", pairs))
+        return moved
+
+    log_rates, residues = log_rates.T, residues.T
+    whole = fixed(poles, all_groups)
     main = pl.BlockSpec((tokens, step_width), lambda i: (0, i))
     twice = pl.BlockSpec((tokens, 2 * step_width), lambda i: (0, i))
-    row_table = pl.BlockSpec((2, blocks, LANES), lambda i: (0, 0, 0))
-
-    send, pair, rows = pl.pallas_call(
-        lambda *refs: states_kernel(*refs, **sizes),
+    row_table = fixed(2, blocks, LANES)
+
+    *send, pair, rows = pl.pallas_call(
+        lambda *refs: states_kernel(*refs, parts=parts, **sizes),
         grid=(steps,),
         in_specs=[whole, whole, main, main, main, main],
-        out_specs=[
-            pl.BlockSpec((owners, payload, own_width), lambda i: (i, 0, 0)),
-            twice,
-            row_table,
-        ],
-        out_shape=[
-            jax.ShapeDtypeStruct((parts, payload, own_width), BF16),
+        out_specs=[fixed(payload, own_width)] * parts + [twice, row_table],
+        out_shape=[jax.ShapeDtypeStruct((payload, own_width), BF16)] * parts
+        + [
             jax.ShapeDtypeStruct((tokens, 2 * width), BF16),
             jax.ShapeDtypeStruct((2, blocks, LANES), F32),
         ],
+        scratch_shapes=[pltpu.VMEM((parts, payload, own_width), BF16)],
         compiler_params=params,
         name="states",
     )(log_rates, residues, queries, key_input, value_input, cotangent)
 
-    got = lax.all_to_all(send, "ctx", split_axis=0, concat_axis=0, tiled=True)
+    got = shifted(send)
 
     skip_rows = skip_gain.reshape(-1, LANES)
     conv = pl.pallas_call(
         lambda *refs: conv_kernel(*refs, **sizes),
         grid=(steps,),
-        in_specs=[row_table, pl.BlockSpec(skip_rows.shape, lambda i: (0, 0)), twice],
+        in_specs=[row_table, fixed(*skip_rows.shape), twice],
         out_specs=twice,
         out_shape=jax.ShapeDtypeStruct((tokens, 2 * width), F32),
         compiler_params=params,
@@ -315,42 +352,35 @@
         name="conv",
     )(rows, skip_rows, pair)
 
-    def first_of(groups):
-        return (lax.axis_index("ch") * parts + lax.axis_index("ctx")) * groups
-
     vmem = pl.BlockSpec(memory_space=pltpu.VMEM)
-    back, grads = pl.pallas_call(
-        lambda *refs: scan_kernel(*refs, tokens=tokens, first_of=first_of, **sizes),
-        in_specs=[vmem, vmem, vmem],
-        out_specs=[vmem, vmem],
-        out_shape=[
-            jax.ShapeDtypeStruct((parts, 2 * poles, own_width), BF16),
-            jax.ShapeDtypeStruct((8, own_width), F32),
+    *back, grads = pl.pallas_call(
+        lambda *refs: scan_kernel(*refs, tokens=tokens, parts=parts, **sizes),
+        in_specs=[vmem] * (2 + parts),
+        out_specs=[vmem] * (parts + 1),
+        out_shape=[jax.ShapeDtypeStruct((2 * poles, own_width), BF16)] * parts
+        + [jax.ShapeDtypeStruct((8, own_width), F32)],
+        scratch_shapes=[
+            pltpu.VMEM((parts, payload, own_width), BF16),
+            pltpu.VMEM((parts, 2 * poles, own_width), BF16),
         ],
         compiler_params=params,
         name="scan",
-    )(log_rates, residues, got)
-
-    states = lax.all_to_all(back, "ctx", split_axis=0, concat_axis=0, tiled=True)
+    )(log_rates, residues, *got)
+
+    states = shifted(back)
     spread = jnp.broadcast_to(grads[None], (parts * shards, 8, own_width))
     final = lax.all_to_all(spread, ("ctx", "ch"), split_axis=0, concat_axis=0, tiled=True)
 
     grad_query, grad_key, grad_value = pl.pallas_call(
-        lambda *refs: output_kernel(*refs, **sizes),
+        lambda *refs: output_kernel(*refs, parts=parts, **sizes),
         grid=(steps,),
-        in_specs=[
-            row_table,
-            twice,
-            pl.BlockSpec((owners, 2 * poles, own_width), lambda i: (i, 0, 0)),
-            main,
-            main,
-            main,
-        ],
+        in_specs=[row_table, twice, main, main, main] + [fixed(2 * poles, own_width)] * parts,
         out_specs=[main, main, main],
         out_shape=[jax.ShapeDtypeStruct((tokens, width), BF16)] * 3,
+        scratch_shapes=[pltpu.VMEM((parts, 2 * poles, own_width), BF16)],
         compiler_params=params,
         name="outputs",
-    )(rows, conv, states, key_input, value_input, cotangent)
+    )(rows, conv, key_input, value_input, cotangent, *states)
 
     final = final.reshape(parts, shards, 8, own_width).transpose(2, 1, 0, 3)
     grad_residue = final[0].reshape(all_groups, poles)

time: 57 us -> 56.3 us (0.988)
  blocking collectives: 20.7 us -> 0 us
  starting transfers between devices: 3.96 us -> 23.5 us
  Pallas kernels: 20.2 us -> 21 us
    all_to_all x2 -> x0, blocking collectives: 20.7 us -> none  [the longest x1 12.6 us: local(): got = lax.all_to_all(send, 'ctx', split_axis=0, concat_axis=0, tiled=True)]
    ppermute x0 -> x14, starting transfers between devices: none -> 17.5 us  [shifted(): moved.append(lax.ppermute(arrays[shift], 'ctx', pairs))]
    all_to_all x1, starting transfers between devices: 3.96 us -> 6.05 us  [local(): lax.all_to_all(spread, ('ctx', 'ch'), split_axis=0, concat_axis=0, tiled=...]
    all_to_all x1, waiting for transfers between devices: 1.79 us -> 0.01 us  [local(): lax.all_to_all(spread, ('ctx', 'ch'), split_axis=0, concat_axis=0, tiled=...]
    ppermute x0 -> x14, waiting for transfers between devices: none -> 1.69 us  [shifted(): moved.append(lax.ppermute(arrays[shift], 'ctx', pairs))]
    pallas_call x3, Pallas kernels: 16.1 us -> 17 us  [the longest x1 11.2 us: local(): pl.pallas_call(lambda *refs: states_kernel(*refs, parts=parts, **sizes),...]
    unnamed x21 -> x23, local copies, waits for them, and re-layouts: 8.02 us -> 7.77 us
  transfers between devices with their start and end apart: 1 -> 15, of which waited for: 1 -> 2; matrix products, arithmetic and copies ran while one was open for 0% -> 0% of each run, Pallas kernels for 15% -> 15%
where the time goes in v1:
time: 56.3 us; the launch traced here: 55.8 us
  starting transfers between devices  23.5 us (42%)
  Pallas kernels  21 us (37%)
  local copies, waits for them, and re-layouts  8.82 us (16%)
  waiting for transfers between devices  1.7 us (3%)
  between operations  0.83 us (1%)
    ppermute x14, starting transfers between devices, shifted(): moved.append(lax.ppermute(arrays[shift], 'ctx', pairs))  17.5 us
    pallas_call x1, Pallas kernels, local(): pl.pallas_call(lambda *refs: states_kernel(*refs, parts=parts, **sizes),...  11.2 us
    unnamed x23, local copies, waits for them, and re-layouts  7.77 us
    all_to_all x1, starting transfers between devices, local(): lax.all_to_all(spread, ('ctx', 'ch'), split_axis=0, concat_axis=0, tiled=...  6.05 us
    pallas_call x1, Pallas kernels, local(): pl.pallas_call(lambda *refs: output_kernel(*refs, parts=parts, **sizes),...  4.46 us
    pallas_call x1, Pallas kernels, local(): pl.pallas_call(lambda *refs: conv_kernel(*refs, **sizes), grid=(steps,),...  4.02 us
    ppermute x14, waiting for transfers between devices, shifted(): moved.append(lax.ppermute(arrays[shift], 'ctx', pairs))  1.69 us
    pallas_call x1, Pallas kernels, local(): pl.pallas_call(lambda *refs: scan_kernel(*refs, tokens=tokens, parts=part...  1.26 us
  transfers between devices with their start and end apart: 15, of which 2 were waited for; matrix products, arithmetic and copies ran while one was open for 0% of the time, Pallas kernels for 15%

profile of v1, /device:TPU:0, one launch (start us, length us, event | category | flops | bytes accessed | tf_op | source)
XLA Modules:
  0.0 55.8 jit_solution(14682121899735490989)
XLA Ops:
  0.6 0.0 copy-start
  0.6 1.0 %copy-done = bf16[128,2048]{1,0:T(8,128)(2,1)S(1)} copy-done((bf16[128,2048]{1,0:T(8,128)(2,1)S(1)}, bf16[128,2048]{1,0:T(8,128)(2,1)}, u32[]{:S(2)}) %copy-start) | copy-done | bytes 524312
  1.7 1.0 %copy-done.2 = bf16[128,2048]{1,0:T(8,128)(2,1)S(1)} copy-done((bf16[128,2048]{1,0:T(8,128)(2,1)S(1)}, bf16[128,2048]{1,0:T(8,128)(2,1)}, u32[]{:S(2)}) %copy-start.2) | copy-done | bytes 524312
  2.7 1.0 %copy-done.4 = bf16[128,2048]{1,0:T(8,128)(2,1)S(1)} copy-done((bf16[128,2048]{1,0:T(8,128)(2,1)S(1)}, bf16[128,2048]{1,0:T(8,128)(2,1)}, u32[]{:S(2)}) %copy-start.4) | copy-done | bytes 524312
  3.8 1.0 %copy-done.6 = bf16[128,2048]{1,0:T(8,128)(2,1)S(1)} copy-done((bf16[128,2048]{1,0:T(8,128)(2,1)S(1)}, bf16[128,2048]{1,0:T(8,128)(2,1)}, u32[]{:S(2)}) %copy-start.6) | copy-done | bytes 524312
  4.8 0.8 %copy-done.7 = f32[512,16]{0,1:T(8,128)S(1)} copy-done((f32[512,16]{0,1:T(8,128)S(1)}, f32[512,16]{0,1:T(8,128)}, u32[]{:S(2)}) %copy-start.7) | copy-done | bytes 32792
  5.6 0.8 %copy-done.8 = f32[512,16]{0,1:T(8,128)S(1)} copy-done((f32[512,16]{0,1:T(8,128)S(1)}, f32[512,16]{0,1:T(8,128)}, u32[]{:S(2)}) %copy-start.8) | copy-done | bytes 32792
  6.3 11.2 %states.1 = (bf16[80,256]{1,0:T(8,128)(2,1)S(1)}, bf16[80,256]{1,0:T(8,128)(2,1)S(1)}, bf16[80,256]{1,0:T(8,128)(2,1)S(1)}, bf16[80,256]{1,0:T(8,128)(2,1)S(1)},...) custom-call(f32[16,512]{1,0:T(8,128)S(1)} %bitcast.14, ...), custom_call_target="tpu_custom_call" | custom-call | tf_op jit(solution)/shard_map/states/pallas_call | solution.py:324
  17.6 0.5 collective-permute-start
  18.1 2.5 %collective-permute-start.1 = (bf16[80,256]{1,0:T(8,128)(2,1)S(1)}, bf16[80,256]{1,0:T(8,128)(2,1)S(1)}, u32[]{:S(2)}, u32[]{:S(2)}) collective-permute-start(bf16[80,256]{1,0:T(8,128)(2,1)S(1)} %get-tuple-element.32), channel_id=1, source_target_pairs={{0,8},{4,12},{8,16},{12,20},{16,24},{20,28},{24,0},{28,4},{1,9},{5... | collective-permute-start | bytes 122888 | tf_op jit(solution)/shard_map/ppermute | solution.py:315
  20.6 2.4 %collective-permute-start.2 = (bf16[80,256]{1,0:T(8,128)(2,1)S(1)}, bf16[80,256]{1,0:T(8,128)(2,1)S(1)}, u32[]{:S(2)}, u32[]{:S(2)}) collective-permute-start(bf16[80,256]{1,0:T(8,128)(2,1)S(1)} %get-tuple-element.33), channel_id=1, source_target_pairs={{0,12},{4,16},{8,20},{12,24},{16,28},{20,0},{24,4},{28,8},{1,13},{... | collective-permute-start | bytes 122888 | tf_op jit(solution)/shard_map/ppermute | solution.py:315
  23.0 0.5 collective-permute-start.3
  23.5 0.1 collective-permute-start.4
  23.6 0.0 collective-permute-done.refs_3_
  23.6 1.4 %collective-permute-start.5 = (bf16[80,256]{1,0:T(8,128)(2,1)S(1)}, bf16[80,256]{1,0:T(8,128)(2,1)S(1)}, u32[]{:S(2)}, u32[]{:S(2)}) collective-permute-start(bf16[80,256]{1,0:T(8,128)(2,1)S(1)} %get-tuple-element.36), channel_id=1, source_target_pairs={{0,24},{4,28},{8,0},{12,4},{16,8},{20,12},{24,16},{28,20},{1,25},{... | collective-permute-start | bytes 122888 | tf_op jit(solution)/shard_map/ppermute | solution.py:315
  25.0 0.0 collective-permute-done.1.refs_4_
  25.0 2.3 %collective-permute-start.6 = (bf16[80,256]{1,0:T(8,128)(2,1)S(1)}, bf16[80,256]{1,0:T(8,128)(2,1)S(1)}, u32[]{:S(2)}, u32[]{:S(2)}) collective-permute-start(bf16[80,256]{1,0:T(8,128)(2,1)S(1)} %get-tuple-element.37), channel_id=1, source_target_pairs={{0,28},{4,0},{8,4},{12,8},{16,12},{20,16},{24,20},{28,24},{1,29},{... | collective-permute-start | bytes 122888 | tf_op jit(solution)/shard_map/ppermute | solution.py:315
  27.3 0.0 collective-permute-done.2.refs_5_
  27.4 0.0 collective-permute-done.3.refs_6_
  27.4 0.0 collective-permute-done.4.refs_7_
  27.4 0.4 collective-permute-done.5.refs_8_
  27.8 1.3 %collective-permute-done.6.refs_9_ = bf16[80,256]{1,0:T(8,128)(2,1)S(1)} collective-permute-done((bf16[80,256]{1,0:T(8,128)(2,1)S(1)}, bf16[80,256]{1,0:T(8,128)(2,1)S(1)}, u32[]{:S(2)}, u32[]{:S(2)}) %collective-permute-start.6) | collective-permute-done | bytes 40992 | tf_op jit(solution)/shard_map/ppermute | solution.py:315
  29.0 1.3 %scan.1 = (bf16[32,256]{1,0:T(8,128)(2,1)S(1)}, bf16[32,256]{1,0:T(8,128)(2,1)S(1)}, bf16[32,256]{1,0:T(8,128)(2,1)S(1)}, bf16[32,256]{1,0:T(8,128)(2,1)S(1)}, b...) custom-call(f32[16,512]{1,0:T(8,128)S(1)} %bitcast.15, ...), custom_call_target="tpu_custom_call" | custom-call | tf_op jit(solution)/shard_map/scan/pallas_call | solution.py:356
  30.3 0.0 copy-start.1
  30.3 0.0 copy-start.3
  30.3 0.0 copy-start.5
  30.3 0.7 %broadcast_in_dim.2 = f32[32,8,256]{2,1,0:T(8,128)} broadcast(f32[8,256]{1,0:T(8,128)S(1)} %get-tuple-element.49), dimensions={1,2} | broadcast | bytes 270336 | tf_op jit(solution)/shard_map/broadcast_in_dim | solution.py:371
  31.0 6.1 %all-to-all-start = ((f32[32,8,256]{2,1,0:T(8,128)}), f32[32,8,256]{2,1,0:T(8,128)S(1)}, u32[]{:S(2)}, u32[]{:S(2)}) async-start(f32[32,8,256]{2,1,0:T(8,128)} %broadcast_in_dim.2), calls=%async_computation | async-start | bytes 524288 | tf_op jit(solution)/shard_map/all_to_all | solution.py:372
  37.1 1.8 %collective-permute-start.10 = (bf16[32,256]{1,0:T(8,128)(2,1)S(1)}, bf16[32,256]{1,0:T(8,128)(2,1)S(1)}, u32[]{:S(2)}, u32[]{:S(2)}) collective-permute-start(bf16[32,256]{1,0:T(8,128)(2,1)S(1)} %get-tuple-element.42), channel_id=1, source_target_pairs={{0,16},{4,20},{8,24},{12,28},{16,0},{20,4},{24,8},{28,12},{1,17},{... | collective-permute-start | bytes 49160 | tf_op jit(solution)/shard_map/ppermute | solution.py:315
  38.9 0.0 collective-permute-start.11
  38.9 2.4 %collective-permute-start.12 = (bf16[32,256]{1,0:T(8,128)(2,1)S(1)}, bf16[32,256]{1,0:T(8,128)(2,1)S(1)}, u32[]{:S(2)}, u32[]{:S(2)}) collective-permute-start(bf16[32,256]{1,0:T(8,128)(2,1)S(1)} %get-tuple-element.44), channel_id=1, source_target_pairs={{0,24},{4,28},{8,0},{12,4},{16,8},{20,12},{24,16},{28,20},{1,25},{... | collective-permute-start | bytes 49160 | tf_op jit(solution)/shard_map/ppermute | solution.py:315
  41.3 1.4 %collective-permute-start.13 = (bf16[32,256]{1,0:T(8,128)(2,1)S(1)}, bf16[32,256]{1,0:T(8,128)(2,1)S(1)}, u32[]{:S(2)}, u32[]{:S(2)}) collective-permute-start(bf16[32,256]{1,0:T(8,128)(2,1)S(1)} %get-tuple-element.45), channel_id=1, source_target_pairs={{0,28},{4,0},{8,4},{12,8},{16,12},{20,16},{24,20},{28,24},{1,29},{... | collective-permute-start | bytes 49160 | tf_op jit(solution)/shard_map/ppermute | solution.py:315
  42.8 0.0 collective-permute-start.7
  42.8 0.0 collective-permute-done.10.refs_9_
  42.8 0.0 collective-permute-start.8
  42.8 2.0 %collective-permute-start.9 = (bf16[32,256]{1,0:T(8,128)(2,1)S(1)}, bf16[32,256]{1,0:T(8,128)(2,1)S(1)}, u32[]{:S(2)}, u32[]{:S(2)}) collective-permute-start(bf16[32,256]{1,0:T(8,128)(2,1)S(1)} %get-tuple-element.41), channel_id=1, source_target_pairs={{0,12},{4,16},{8,20},{12,24},{16,28},{20,0},{24,4},{28,8},{1,13},{... | collective-permute-start | bytes 49160 | tf_op jit(solution)/shard_map/ppermute | solution.py:315
  44.8 4.0 %conv.1.refs_1_ = f32[128,4096]{1,0:T(8,128)S(1)} custom-call(f32[2,16,128]{2,1,0:T(8,128)S(1)} %get-tuple-element.28.refs_0_, f32[64,128]{1,0:T(8,128)S(1)} %bitcast.18, bf16[128,4096]{1,0:T(8,128)(2,1)S(1)} %get-tuple-element.29.refs_2_), custom_call_target="tpu_custom_call" | custom-call | flops 536870912 | bytes 3145728 | tf_op jit(solution)/shard_map/conv/pallas_call | solution.py:342
  48.8 0.0 collective-permute-done.12.refs_11_
  48.9 0.0 collective-permute-done.13.refs_12_
  48.9 0.0 collective-permute-done.8.refs_7_
  48.9 0.0 collective-permute-done.9.refs_8_
  48.9 4.5 %outputs.1 = (bf16[128,2048]{1,0:T(8,128)(2,1)}, bf16[128,2048]{1,0:T(8,128)(2,1)}, bf16[128,2048]{1,0:T(8,128)(2,1)}) custom-call(f32[2,16,128]{2,1,0:T(8,128)S(1)} %get-tuple-element.28.refs_0_, f32[128,4096]{1,0:T(8,128)S(1)} %conv.1.refs_1_, bf16[128,2048]{1,0:T(8,128)(2,1)S(1)} %copy-done.1, bf16[128,2048]{1,0:T(8,128)(2,1)S(1)} %copy-done.3, ...), custom_call_target="tpu_custom_call" | custom-call | tf_op jit(solution)/shard_map/outputs/pallas_call | solution.py:374
  53.4 0.1 fusion
  53.5 0.1 reshape_squeeze.9
  53.6 0.7 %copy.18 = f32[512,16]{0,1:T(8,128)} copy(f32[512,16]{1,0:T(8,128)S(1)} %reshape_squeeze.9) | data formatting | bytes 65536
  54.3 0.1 reshape_squeeze.10
  54.5 0.7 %copy.19 = f32[512,16]{0,1:T(8,128)} copy(f32[512,16]{1,0:T(8,128)S(1)} %reshape_squeeze.10) | data formatting | bytes 65536
  55.2 0.6 %copy.20 = f32[4,2,8,128]{3,1,2,0:T(2,128)} copy(f32[4,2,8,128]{3,2,1,0:T(8,128)S(1)} %bitcast.20) | data formatting | bytes 65536
  (16 shorter events, 0.0 us)
Async XLA Ops:
  0.6 1.0 %copy-start = (bf16[128,2048]{1,0:T(8,128)(2,1)S(1)}, bf16[128,2048]{1,0:T(8,128)(2,1)}, u32[]{:S(2)}) copy-start(bf16[128,2048]{1,0:T(8,128)(2,1)} %refs_2_.3) | copy-start | bytes 1572868
  1.7 1.0 %copy-start.2 = (bf16[128,2048]{1,0:T(8,128)(2,1)S(1)}, bf16[128,2048]{1,0:T(8,128)(2,1)}, u32[]{:S(2)}) copy-start(bf16[128,2048]{1,0:T(8,128)(2,1)} %refs_3_.3) | copy-start | bytes 1572868
  2.7 1.0 %copy-start.4 = (bf16[128,2048]{1,0:T(8,128)(2,1)S(1)}, bf16[128,2048]{1,0:T(8,128)(2,1)}, u32[]{:S(2)}) copy-start(bf16[128,2048]{1,0:T(8,128)(2,1)} %refs_4_.3) | copy-start | bytes 1572868
  3.8 1.0 %copy-start.6 = (bf16[128,2048]{1,0:T(8,128)(2,1)S(1)}, bf16[128,2048]{1,0:T(8,128)(2,1)}, u32[]{:S(2)}) copy-start(bf16[128,2048]{1,0:T(8,128)(2,1)} %refs_2_.2) | copy-start | bytes 1572868
  4.8 0.8 %copy-start.7 = (f32[512,16]{0,1:T(8,128)S(1)}, f32[512,16]{0,1:T(8,128)}, u32[]{:S(2)}) copy-start(f32[512,16]{0,1:T(8,128)} %param.12) | copy-start | bytes 98308
  5.6 0.8 %copy-start.8 = (f32[512,16]{0,1:T(8,128)S(1)}, f32[512,16]{0,1:T(8,128)}, u32[]{:S(2)}) copy-start(f32[512,16]{0,1:T(8,128)} %param.11) | copy-start | bytes 98308
  6.3 38.5 %copy-start.9 = (f32[8192]{0:T(1024)S(1)}, f32[8192]{0:T(1024)}, u32[]{:S(2)}) copy-start(f32[8192]{0:T(1024)} %param.13) | copy-start | bytes 98308
  17.6 6.0 %collective-permute-start = (bf16[80,256]{1,0:T(8,128)(2,1)S(1)}, bf16[80,256]{1,0:T(8,128)(2,1)S(1)}, u32[]{:S(2)}, u32[]{:S(2)}) collective-permute-start(bf16[80,256]{1,0:T(8,128)(2,1)S(1)} %get-tuple-element.31), channel_id=1, source_target_pairs={{0,4},{4,8},{8,12},{12,16},{16,20},{20,24},{24,28},{28,0},{1,5},{5... | collective-permute-start | bytes 122888 | tf_op jit(solution)/shard_map/ppermute | solution.py:315
  18.1 7.0 %collective-permute-start.1 = (bf16[80,256]{1,0:T(8,128)(2,1)S(1)}, bf16[80,256]{1,0:T(8,128)(2,1)S(1)}, u32[]{:S(2)}, u32[]{:S(2)}) collective-permute-start(bf16[80,256]{1,0:T(8,128)(2,1)S(1)} %get-tuple-element.32), channel_id=1, source_target_pairs={{0,8},{4,12},{8,16},{12,20},{16,24},{20,28},{24,0},{28,4},{1,9},{5... | collective-permute-start | bytes 122888 | tf_op jit(solution)/shard_map/ppermute | solution.py:315
  20.6 6.7 %collective-permute-start.2 = (bf16[80,256]{1,0:T(8,128)(2,1)S(1)}, bf16[80,256]{1,0:T(8,128)(2,1)S(1)}, u32[]{:S(2)}, u32[]{:S(2)}) collective-permute-start(bf16[80,256]{1,0:T(8,128)(2,1)S(1)} %get-tuple-element.33), channel_id=1, source_target_pairs={{0,12},{4,16},{8,20},{12,24},{16,28},{20,0},{24,4},{28,8},{1,13},{... | collective-permute-start | bytes 122888 | tf_op jit(solution)/shard_map/ppermute | solution.py:315
  23.0 4.4 %collective-permute-start.3 = (bf16[80,256]{1,0:T(8,128)(2,1)S(1)}, bf16[80,256]{1,0:T(8,128)(2,1)S(1)}, u32[]{:S(2)}, u32[]{:S(2)}) collective-permute-start(bf16[80,256]{1,0:T(8,128)(2,1)S(1)} %get-tuple-element.34), channel_id=1, source_target_pairs={{0,16},{4,20},{8,24},{12,28},{16,0},{20,4},{24,8},{28,12},{1,17},{... | collective-permute-start | bytes 122888 | tf_op jit(solution)/shard_map/ppermute | solution.py:315
  23.5 3.9 %collective-permute-start.4 = (bf16[80,256]{1,0:T(8,128)(2,1)S(1)}, bf16[80,256]{1,0:T(8,128)(2,1)S(1)}, u32[]{:S(2)}, u32[]{:S(2)}) collective-permute-start(bf16[80,256]{1,0:T(8,128)(2,1)S(1)} %get-tuple-element.35), channel_id=1, source_target_pairs={{0,20},{4,24},{8,28},{12,0},{16,4},{20,8},{24,12},{28,16},{1,21},{... | collective-permute-start | bytes 122888 | tf_op jit(solution)/shard_map/ppermute | solution.py:315
  23.6 4.1 %collective-permute-start.5 = (bf16[80,256]{1,0:T(8,128)(2,1)S(1)}, bf16[80,256]{1,0:T(8,128)(2,1)S(1)}, u32[]{:S(2)}, u32[]{:S(2)}) collective-permute-start(bf16[80,256]{1,0:T(8,128)(2,1)S(1)} %get-tuple-element.36), channel_id=1, source_target_pairs={{0,24},{4,28},{8,0},{12,4},{16,8},{20,12},{24,16},{28,20},{1,25},{... | collective-permute-start | bytes 122888 | tf_op jit(solution)/shard_map/ppermute | solution.py:315
  25.0 4.0 %collective-permute-start.6 = (bf16[80,256]{1,0:T(8,128)(2,1)S(1)}, bf16[80,256]{1,0:T(8,128)(2,1)S(1)}, u32[]{:S(2)}, u32[]{:S(2)}) collective-permute-start(bf16[80,256]{1,0:T(8,128)(2,1)S(1)} %get-tuple-element.37), channel_id=1, source_target_pairs={{0,28},{4,0},{8,4},{12,8},{16,12},{20,16},{24,20},{28,24},{1,29},{... | collective-permute-start | bytes 122888 | tf_op jit(solution)/shard_map/ppermute | solution.py:315
  30.3 18.6 %copy-start.1 = (bf16[128,2048]{1,0:T(8,128)(2,1)S(1)}, bf16[128,2048]{1,0:T(8,128)(2,1)}, u32[]{:S(2)}) copy-start(bf16[128,2048]{1,0:T(8,128)(2,1)} %refs_2_.3) | copy-start | bytes 1572868
  30.3 18.6 %copy-start.3 = (bf16[128,2048]{1,0:T(8,128)(2,1)S(1)}, bf16[128,2048]{1,0:T(8,128)(2,1)}, u32[]{:S(2)}) copy-start(bf16[128,2048]{1,0:T(8,128)(2,1)} %refs_3_.3) | copy-start | bytes 1572868
  30.3 18.6 %copy-start.5 = (bf16[128,2048]{1,0:T(8,128)(2,1)S(1)}, bf16[128,2048]{1,0:T(8,128)(2,1)}, u32[]{:S(2)}) copy-start(bf16[128,2048]{1,0:T(8,128)(2,1)} %refs_4_.3) | copy-start | bytes 1572868
  31.0 22.3 %all-to-all-start = ((f32[32,8,256]{2,1,0:T(8,128)}), f32[32,8,256]{2,1,0:T(8,128)S(1)}, u32[]{:S(2)}, u32[]{:S(2)}) async-start(f32[32,8,256]{2,1,0:T(8,128)} %broadcast_in_dim.2), calls=%async_computation | async-start | bytes 524288 | tf_op jit(solution)/shard_map/all_to_all | solution.py:372
  37.1 5.7 %collective-permute-start.10 = (bf16[32,256]{1,0:T(8,128)(2,1)S(1)}, bf16[32,256]{1,0:T(8,128)(2,1)S(1)}, u32[]{:S(2)}, u32[]{:S(2)}) collective-permute-start(bf16[32,256]{1,0:T(8,128)(2,1)S(1)} %get-tuple-element.42), channel_id=1, source_target_pairs={{0,16},{4,20},{8,24},{12,28},{16,0},{20,4},{24,8},{28,12},{1,17},{... | collective-permute-start | bytes 49160 | tf_op jit(solution)/shard_map/ppermute | solution.py:315
  38.9 3.8 %collective-permute-start.11 = (bf16[32,256]{1,0:T(8,128)(2,1)S(1)}, bf16[32,256]{1,0:T(8,128)(2,1)S(1)}, u32[]{:S(2)}, u32[]{:S(2)}) collective-permute-start(bf16[32,256]{1,0:T(8,128)(2,1)S(1)} %get-tuple-element.43), channel_id=1, source_target_pairs={{0,20},{4,24},{8,28},{12,0},{16,4},{20,8},{24,12},{28,16},{1,21},{... | collective-permute-start | bytes 49160 | tf_op jit(solution)/shard_map/ppermute | solution.py:315
  38.9 9.9 %collective-permute-start.12 = (bf16[32,256]{1,0:T(8,128)(2,1)S(1)}, bf16[32,256]{1,0:T(8,128)(2,1)S(1)}, u32[]{:S(2)}, u32[]{:S(2)}) collective-permute-start(bf16[32,256]{1,0:T(8,128)(2,1)S(1)} %get-tuple-element.44), channel_id=1, source_target_pairs={{0,24},{4,28},{8,0},{12,4},{16,8},{20,12},{24,16},{28,20},{1,25},{... | collective-permute-start | bytes 49160 | tf_op jit(solution)/shard_map/ppermute | solution.py:315
  41.3 7.5 %collective-permute-start.13 = (bf16[32,256]{1,0:T(8,128)(2,1)S(1)}, bf16[32,256]{1,0:T(8,128)(2,1)S(1)}, u32[]{:S(2)}, u32[]{:S(2)}) collective-permute-start(bf16[32,256]{1,0:T(8,128)(2,1)S(1)} %get-tuple-element.45), channel_id=1, source_target_pairs={{0,28},{4,0},{8,4},{12,8},{16,12},{20,16},{24,20},{28,24},{1,29},{... | collective-permute-start | bytes 49160 | tf_op jit(solution)/shard_map/ppermute | solution.py:315
  42.8 6.1 %collective-permute-start.7 = (bf16[32,256]{1,0:T(8,128)(2,1)S(1)}, bf16[32,256]{1,0:T(8,128)(2,1)S(1)}, u32[]{:S(2)}, u32[]{:S(2)}) collective-permute-start(bf16[32,256]{1,0:T(8,128)(2,1)S(1)} %get-tuple-element.39), channel_id=1, source_target_pairs={{0,4},{4,8},{8,12},{12,16},{16,20},{20,24},{24,28},{28,0},{1,5},{5... | collective-permute-start | bytes 49160 | tf_op jit(solution)/shard_map/ppermute | solution.py:315
  42.8 6.1 %collective-permute-start.8 = (bf16[32,256]{1,0:T(8,128)(2,1)S(1)}, bf16[32,256]{1,0:T(8,128)(2,1)S(1)}, u32[]{:S(2)}, u32[]{:S(2)}) collective-permute-start(bf16[32,256]{1,0:T(8,128)(2,1)S(1)} %get-tuple-element.40), channel_id=1, source_target_pairs={{0,8},{4,12},{8,16},{12,20},{16,24},{20,28},{24,0},{28,4},{1,9},{5... | collective-permute-start | bytes 49160 | tf_op jit(solution)/shard_map/ppermute | solution.py:315
  42.8 6.1 %collective-permute-start.9 = (bf16[32,256]{1,0:T(8,128)(2,1)S(1)}, bf16[32,256]{1,0:T(8,128)(2,1)S(1)}, u32[]{:S(2)}, u32[]{:S(2)}) collective-permute-start(bf16[32,256]{1,0:T(8,128)(2,1)S(1)} %get-tuple-element.41), channel_id=1, source_target_pairs={{0,12},{4,16},{8,20},{12,24},{16,28},{20,0},{24,4},{28,8},{1,13},{... | collective-permute-start | bytes 49160 | tf_op jit(solution)/shard_map/ppermute | solution.py:315

commit v2 on v0

v2 whole, which is shorter than its diff:
```python
import math

import jax
import jax.numpy as jnp
from jax import lax
from jax.experimental import pallas as pl
from jax.experimental.pallas import tpu as pltpu
from jax.sharding import PartitionSpec as P

LANES = 128
SUB = 32
F32 = jnp.float32
BF16 = jnp.bfloat16
EXACT = lax.Precision.HIGHEST
VMEM_LIMIT = 40 * 1024 * 1024
PARAMS = pltpu.CompilerParams(vmem_limit_bytes=VMEM_LIMIT)


def iota(shape, axis):
    return lax.broadcasted_iota(jnp.int32, shape, axis)


def mxu(left, right):
    return jnp.dot(left, right, preferred_element_type=F32)


def mxu_t(left, right):
    return lax.dot_general(left, right, (((1,), (1,)), ((), ())), preferred_element_type=F32)


def exact_dot(left, right):
    return jnp.dot(left, right, precision=EXACT, preferred_element_type=F32)


def gate(left, right):
    return (left.astype(F32) * right.astype(F32)).astype(BF16)


def reversal(size):
    return jnp.where(iota((size, size), 0) + iota((size, size), 1) == size - 1, 1.0, 0.0).astype(BF16)


def split(value, pieces):
    parts = []
    for _ in range(pieces):
        parts.append(value.astype(BF16))
        value = value - parts[-1].astype(F32)
    return jnp.concatenate(parts, axis=0)


def join(stacked, rows):
    total = stacked[:rows].astype(F32)
    for start in range(rows, stacked.shape[0], rows):
        total = total + stacked[start : start + rows].astype(F32)
    return total


def flat_rows(table, poles):
    table = table.T
    groups = table.shape[0]
    per_row = LANES // poles
    spread = jnp.where(iota((poles, LANES), 0) == iota((poles, LANES), 1) % poles, 1.0, 0.0)
    wide = exact_dot(table, spread)
    keep = iota((groups, LANES), 0) % per_row == iota((groups, LANES), 1) // poles
    wide = jnp.where(keep, wide, 0.0)
    return jnp.sum(wide.reshape(groups // per_row, per_row, LANES), axis=1)


def members(groups, first, span, width):
    return jnp.where(iota((groups, width), 0) == first + iota((groups, width), 1) // span, 1.0, 0.0).astype(BF16)


def shard_start(groups):
    return pl.multiple_of(lax.axis_index("ch") * groups, LANES)


def states_kernel(logs_ref, res_ref, q_any, k_any, v_any, c_any, msg_ref, pair_ref, rows_ref, rates_ref,
                  q_ref, k_ref, v_ref, c_ref, skip_ref, sems, *, group, poles, steps):
    tokens, width = q_ref.shape
    per_block = LANES // group
    blocks, _, _ = rates_ref.shape
    groups = blocks * per_block
    inner = blocks // steps
    chunk = width // steps
    subs = tokens // SUB
    lag_width = per_block * SUB

    def copies(step):
        cut = pl.ds(pl.multiple_of(step * chunk, LANES), chunk)
        pairs = ((k_any, k_ref), (v_any, v_ref), (c_any, c_ref), (q_any, q_ref))
        return [
            pltpu.make_async_copy(far.at[:, cut], near.at[:, cut], sems.at[n, step])
            for n, (far, near) in enumerate(pairs)
        ]

    for step in range(steps):
        for copy in copies(step):
            copy.start()

    first = shard_start(groups)
    logs = logs_ref[:, pl.ds(first, groups)]
    rows_ref[0] = jnp.exp(flat_rows(logs, poles))
    rows_ref[1] = flat_rows(res_ref[:, pl.ds(first, groups)], poles)
    logs = split(logs, 3)

    flip = reversal(tokens)
    lag = (SUB - 1 - iota((poles, lag_width), 1) % SUB).astype(F32)
    wide_group = (iota((SUB, 2 * LANES), 1) % LANES) // group
    causal = iota((SUB, lag_width), 0) + iota((SUB, lag_width), 1) % SUB <= SUB - 1

    def body(step, sums):
        for copy in copies(step):
            copy.wait()
        for j in range(inner):
            block = step * inner + j
            cut = pl.ds(pl.multiple_of(block * LANES, LANES), LANES)
            gated = gate(k_ref[:, cut], v_ref[:, cut])
            dgate = gate(c_ref[:, cut], q_ref[:, cut])
            skip = jnp.sum(gated.astype(F32) * dgate.astype(F32), axis=0, keepdims=True)
            skip_ref[pl.ds(block, 1), :] = skip
            turned = mxu(flip, dgate).astype(BF16)
            pair = jnp.concatenate([gated, turned], axis=1)
            pair_ref[:, pl.ds(pl.multiple_of(2 * block * LANES, LANES), 2 * LANES)] = pair

            lag_of = members(groups, block * per_block, SUB, lag_width)
            lane_of = members(groups, block * per_block, group, LANES)
            spread = jnp.concatenate([lag_of, lane_of], axis=1)
            rates = jnp.exp(join(mxu(logs, spread), poles))
            lag_rate, rate = rates[:, :lag_width], rates[:, lag_width:]
            rates_ref[block] = rate
            table = jnp.exp(-lag_rate * lag)
            moment_table = table * lag
            tables = jnp.concatenate([table, moment_table], axis=0).astype(BF16)

            found, outer = [], jnp.zeros((SUB, lag_width), F32)
            for k in range(subs):
                part = pair[k * SUB : (k + 1) * SUB]
                stack = jnp.concatenate(
                    [jnp.where(wide_group == g, part, jnp.zeros_like(part)) for g in range(per_block)], axis=0
                )
                found.append(mxu(tables, stack))
                mate = turned[(subs - 1 - k) * SUB : (subs - k) * SUB]
                outer = outer + mxu_t(mate, stack[:, :LANES])
            outer = jnp.where(causal, outer, 0.0)
            outer = pltpu.roll(outer, 0, 1, stride=1, stride_axis=0)
            lags = jnp.sum(outer, axis=0, keepdims=True)

            once = jnp.exp(-rate)
            decay = jnp.exp(-rate * SUB)
            decay = jnp.concatenate([decay, decay], axis=1)
            state = jnp.zeros((poles, 2 * LANES), F32)
            moment = state
            cross_res = jnp.zeros((poles, LANES), F32)
            cross_mom = cross_res
            for k in range(subs):
                back = found[subs - 1 - k][:, LANES:]
                held, held_moment = state[:, :LANES], moment[:, :LANES]
                cross_res = cross_res + back[:poles] * held
                cross_mom = cross_mom + back[poles:] * held + back[:poles] * (held_moment + held)
                moment = decay * (moment + SUB * state) + found[k][poles:]
                state = decay * state + found[k][:poles]
            out = jnp.concatenate(
                [state[:, :LANES], state[:, LANES:], moment[:, :LANES], moment[:, LANES:]], axis=0
            )
            msg_ref[pl.ds(pl.multiple_of(block * 4 * poles, 16), 4 * poles), :] = out.astype(BF16)
            near = jnp.concatenate([lags * table, lags * moment_table], axis=0)
            far = jnp.concatenate([once * cross_res, once * cross_mom], axis=0)
            terms = split(jnp.concatenate([near, far], axis=1), 2)
            sums = sums + join(mxu_t(terms, spread), 2 * poles)
        return sums

    sums = lax.fori_loop(0, steps, body, jnp.zeros((2 * poles, groups), F32))
    tail = blocks * 4 * poles
    msg_ref[tail : tail + 4 * poles, :] = split(sums, 2)
    msg_ref[tail + 4 * poles :, :] = split(skip_ref[...], 2)


def conv_kernel(rows_ref, skip_ref, pair_ref, conv_ref, *, group, poles):
    tokens, width = pair_ref.shape
    per_block = LANES // group
    step = pl.program_id(0)
    blocks = width // (2 * LANES)
    all_blocks = rows_ref.shape[1]
    first = lax.axis_index("ch") * all_blocks
    back_pos = (tokens - 1 - iota((tokens, LANES), 0)).astype(F32)
    wide_group = (iota((tokens, 2 * LANES), 1) % LANES) // group
    causal = iota((tokens, tokens), 0) >= iota((tokens, tokens), 1)
    for j in range(blocks):
        cut = slice(2 * j * LANES, 2 * (j + 1) * LANES)
        pair = pair_ref[:, cut]
        here = step * blocks + j
        rate = rows_ref[0, pl.ds(here, 1), :]
        res = rows_ref[1, pl.ds(here, 1), :]
        table = (res * jnp.exp(-rate * back_pos)).T
        left, right = [], []
        for g in range(per_block):
            taps = jnp.sum(table[g * poles : (g + 1) * poles], axis=0, keepdims=True)
            base = pltpu.roll(jnp.broadcast_to(taps, (8, tokens)), 1, 1, stride=1, stride_axis=0)
            rolled = [base] + [pltpu.roll(base, 8 * a, 1) for a in range(1, tokens // 8)]
            left.append(jnp.where(causal, jnp.concatenate(rolled, axis=0), 0.0).astype(BF16))
            right.append(jnp.where(wide_group == g, pair, jnp.zeros_like(pair)))
        total = mxu(jnp.concatenate(left, axis=1), jnp.concatenate(right, axis=0))
        gain = skip_ref[pl.ds(first + here, 1), :]
        conv_ref[:, cut] = total + jnp.concatenate([gain, gain], axis=1) * pair.astype(F32)


def combine_kernel(*refs, level, levels, group, poles, tokens):
    last = level == levels - 1
    refs = list(refs)
    rates_ref, own_ref, got_ref = refs[:3]
    rest = refs[3:]
    held_ref = rest.pop(0) if level else None
    if last:
        logs_ref, res_ref = rest.pop(0), rest.pop(0)
    slim_ref = rest.pop() if level == levels - 2 else None
    out_ref, new_held_ref = rest
    blocks = rates_ref.shape[0]
    groups = blocks * (LANES // group)
    me = lax.axis_index("ctx")
    is_right = lax.rem(lax.shift_right_logical(me, level), 2) == 1
    before = lax.rem(me, 2**level)
    gap_left = (tokens * before).astype(F32)
    gap_right = (tokens * (2**level - 1 - before)).astype(F32)
    span = float(tokens * 2**level)
    next_right = lax.rem(lax.shift_right_logical(me, level + 1), 2) == 1
    own_rows = 4 * poles
    got_rows = 2 * poles if last else 4 * poles
    slim_rows = 2 * poles
    sums = jnp.zeros((4 * poles, groups), F32)
    for b in range(blocks):
        rate = rates_ref[b]
        own = own_ref[b * own_rows : (b + 1) * own_rows].astype(F32)
        got = got_ref[b * got_rows : (b + 1) * got_rows].astype(F32)
        own_f, own_b, own_fm, own_bm = (own[n * poles : (n + 1) * poles] for n in range(4))
        if last:
            got_f = got_b = got[:poles]
            got_fm = got_bm = got[poles:]
        else:
            got_f, got_b, got_fm, got_bm = (got[n * poles : (n + 1) * poles] for n in range(4))
        left_f = jnp.where(is_right, got_f, own_f)
        left_fm = jnp.where(is_right, got_fm, own_fm)
        right_b = jnp.where(is_right, own_b, got_b)
        right_bm = jnp.where(is_right, own_bm, got_bm)
        once = jnp.exp(-rate)
        cross_res = once * (right_b * left_f)
        cross_mom = once * (right_bm * left_f + right_b * (left_fm + left_f))
        terms = split(jnp.concatenate([cross_res, cross_mom], axis=0), 2)
        sums = sums + mxu_t(terms, members(groups, b * (LANES // group), group, LANES))
        if level:
            hold = held_ref[b]
        else:
            hold = jnp.zeros((2 * poles, LANES), F32)
        carry = jnp.exp(-rate * jnp.where(is_right, gap_left, gap_right)) * jnp.where(is_right, left_f, right_b)
        zero = jnp.zeros_like(carry)
        hold = hold + jnp.concatenate(
            [jnp.where(is_right, carry, zero), jnp.where(is_right, zero, carry)], axis=0
        )
        new_held_ref[b] = hold.astype(new_held_ref.dtype)
        if not last:
            right_f = jnp.where(is_right, own_f, got_f)
            right_fm = jnp.where(is_right, own_fm, got_fm)
            left_b = jnp.where(is_right, got_b, own_b)
            left_bm = jnp.where(is_right, got_bm, own_bm)
            decay = jnp.exp(-rate * span)
            new = [
                decay * left_f + right_f,
                left_b + decay * right_b,
                decay * (left_fm + span * left_f) + right_fm,
                left_bm + decay * (right_bm + span * right_b),
            ]
            out_ref[b * own_rows : (b + 1) * own_rows, :] = jnp.concatenate(new, axis=0).astype(BF16)
            if slim_ref is not None:
                chosen = jnp.concatenate(
                    [jnp.where(next_right, new[1], new[0]), jnp.where(next_right, new[3], new[2])], axis=0
                )
                slim_ref[b * slim_rows : (b + 1) * slim_rows, :] = chosen.astype(BF16)
    own_tail, got_tail = blocks * own_rows, blocks * got_rows
    total = (
        join(sums, 2 * poles)
        + join(own_ref[own_tail : own_tail + 4 * poles], 2 * poles)
        + join(got_ref[got_tail : got_tail + 4 * poles], 2 * poles)
    )
    skip = join(own_ref[own_tail + 4 * poles :], blocks) + join(got_ref[got_tail + 4 * poles :], blocks)
    if last:
        start = shard_start(groups)
        rate = jnp.exp(logs_ref[:, pl.ds(start, groups)])
        res = res_ref[:, pl.ds(start, groups)]
        length = 2 * span
        out_ref[:poles, :] = total[:poles] / length
        out_ref[poles : 2 * poles, :] = -rate * res * total[poles:] / math.sqrt(length)
        out_ref[2 * poles :, :] = skip / math.sqrt(length)
    else:
        rests = jnp.concatenate([split(total, 2), split(skip, 2)], axis=0)
        out_ref[own_tail:, :] = rests
        if slim_ref is not None:
            slim_ref[blocks * slim_rows :, :] = rests


def output_kernel(rows_ref, conv_ref, held_ref, k_ref, v_ref, c_ref, gq_ref, gk_ref, gv_ref, *, group, poles):
    tokens, width = k_ref.shape
    per_block = LANES // group
    step = pl.program_id(0)
    blocks = width // LANES
    flip = reversal(tokens)
    ahead = (1 + iota((tokens, LANES), 0)).astype(F32)
    wide_group = (iota((poles, 2 * LANES), 1) % LANES) // group
    for j in range(blocks):
        cut = slice(j * LANES, (j + 1) * LANES)
        here = step * blocks + j
        rate = rows_ref[0, pl.ds(here, 1), :]
        res = rows_ref[1, pl.ds(here, 1), :]
        table = (res * jnp.exp(-rate * ahead)).astype(BF16)
        held = held_ref[j]
        states = jnp.concatenate([held[:poles], held[poles:]], axis=1)
        stack = jnp.concatenate(
            [jnp.where(wide_group == g, states, jnp.zeros_like(states)) for g in range(per_block)], axis=0
        )
        total = (conv_ref[:, 2 * j * LANES : 2 * (j + 1) * LANES] + mxu(table, stack)).astype(BF16)
        flow = mxu(flip, total[:, LANES:])
        gq_ref[:, cut] = (c_ref[:, cut].astype(F32) * total[:, :LANES].astype(F32)).astype(BF16)
        gk_ref[:, cut] = (flow * v_ref[:, cut].astype(F32)).astype(BF16)
        gv_ref[:, cut] = (flow * k_ref[:, cut].astype(F32)).astype(BF16)


def assemble_kernel(*refs, shards, poles):
    slots = refs[:shards]
    res_ref, log_ref, skip_ref = refs[shards:]
    me = lax.axis_index("ch")
    groups = slots[0].shape[1]
    rows = slots[0].shape[0] - 2 * poles
    for shift, slot in enumerate(slots):
        source = lax.rem(me - shift + shards, shards)
        cut = pl.ds(pl.multiple_of(source * groups, LANES), groups)
        res_ref[:, cut] = slot[:poles, :]
        log_ref[:, cut] = slot[poles : 2 * poles, :]
        skip_ref[pl.ds(pl.multiple_of(source * rows, 8), rows), :] = slot[2 * poles :, :]


def local(queries, key_input, value_input, cotangent, residues, log_rates, skip_gain):
    tokens, width = queries.shape
    parts = lax.axis_size("ctx")
    shards = lax.axis_size("ch")
    levels = parts.bit_length() - 1
    all_groups, poles = residues.shape
    groups = all_groups // shards
    group = width // groups
    blocks = width // LANES
    steps = 4
    step_width = width // steps
    sizes = dict(group=group, poles=poles)
    tail = 4 * poles + 2 * blocks

    def fixed(*shape):
        return pl.BlockSpec(shape, lambda i: (0,) * len(shape))

    vmem = pl.BlockSpec(memory_space=pltpu.VMEM)
    far = pl.BlockSpec(memory_space=pltpu.HBM)
    log_rates, residues = log_rates.T, residues.T
    main = pl.BlockSpec((tokens, step_width), lambda i: (0, i))
    twice = pl.BlockSpec((tokens, 2 * step_width), lambda i: (0, i))
    row_table = fixed(2, blocks, LANES)

    message, pair, rows, rates = pl.pallas_call(
        lambda *refs: states_kernel(*refs, steps=steps, **sizes),
        in_specs=[vmem, vmem, far, far, far, far],
        out_specs=[vmem] * 4,
        out_shape=[
            jax.ShapeDtypeStruct((blocks * 4 * poles + tail, LANES), BF16),
            jax.ShapeDtypeStruct((tokens, 2 * width), BF16),
            jax.ShapeDtypeStruct((2, blocks, LANES), F32),
            jax.ShapeDtypeStruct((blocks, poles, LANES), F32),
        ],
        scratch_shapes=[pltpu.VMEM((tokens, width), BF16)] * 4
        + [pltpu.VMEM((blocks, LANES), F32), pltpu.SemaphoreType.DMA((4, steps))],
        compiler_params=PARAMS,
        name="states",
    )(log_rates, residues, queries, key_input, value_input, cotangent)

    skip_rows = skip_gain.reshape(-1, LANES)
    conv = pl.pallas_call(
        lambda *refs: conv_kernel(*refs, **sizes),
        grid=(steps,),
        in_specs=[row_table, fixed(*skip_rows.shape), twice],
        out_specs=twice,
        out_shape=jax.ShapeDtypeStruct((tokens, 2 * width), F32),
        compiler_params=PARAMS,
        cost_estimate=pl.CostEstimate(
            flops=16 * tokens * tokens * width, bytes_accessed=12 * tokens * width, transcendentals=tokens * width
        ),
        name="conv",
    )(rows, skip_rows, pair)

    held, outgoing = None, message
    for level in range(levels):
        last = level == levels - 1
        got = lax.ppermute(outgoing, "ctx", [(i, i ^ (1 << level)) for i in range(parts)])
        operands = [rates, message, got]
        if level:
            operands.append(held)
        if last:
            operands += [log_rates, residues]
            out = jax.ShapeDtypeStruct((2 * poles + blocks, LANES), F32)
        else:
            out = jax.ShapeDtypeStruct(message.shape, BF16)
        outs = [out, jax.ShapeDtypeStruct((blocks, 2 * poles, LANES), BF16 if last else F32)]
        if level == levels - 2:
            outs.append(jax.ShapeDtypeStruct((blocks * 2 * poles + tail, LANES), BF16))
        message, held, *slim = pl.pallas_call(
            lambda *refs, level=level: combine_kernel(*refs, level=level, levels=levels, tokens=tokens, **sizes),
            in_specs=[vmem] * len(operands),
            out_specs=[vmem] * len(outs),
            out_shape=outs,
            compiler_params=PARAMS,
            name="combine",
        )(*operands)
        outgoing = slim[0] if slim else message

    gathered = [message]
    for shift in range(1, shards):
        gathered.append(lax.ppermute(message, "ch", [(i, (i + shift) % shards) for i in range(shards)]))

    grad_query, grad_key, grad_value = pl.pallas_call(
        lambda *refs: output_kernel(*refs, **sizes),
        grid=(steps,),
        in_specs=[
            row_table,
            twice,
            pl.BlockSpec((blocks // steps, 2 * poles, LANES), lambda i: (i, 0, 0)),
            main,
            main,
            main,
        ],
        out_specs=[main, main, main],
        out_shape=[jax.ShapeDtypeStruct((tokens, width), BF16)] * 3,
        compiler_params=PARAMS,
        name="outputs",
    )(rows, conv, held, key_input, value_input, cotangent)

    grad_residue, grad_lograte, grad_skip = pl.pallas_call(
        lambda *refs: assemble_kernel(*refs, shards=shards, poles=poles),
        in_specs=[vmem] * shards,
        out_specs=[vmem] * 3,
        out_shape=[
            jax.ShapeDtypeStruct((poles, all_groups), F32),
            jax.ShapeDtypeStruct((poles, all_groups), F32),
            jax.ShapeDtypeStruct((shards * blocks, LANES), F32),
        ],
        compiler_params=PARAMS,
        name="assemble",
    )(*gathered)
    return (grad_query, grad_key, grad_value, grad_residue.T, grad_lograte.T, grad_skip.reshape(-1))


def solution(mesh):
    placed = (P("ctx", "ch"), P("ctx", "ch"), P("ctx", "ch"), P("ctx", "ch"), P(), P(), P())
    return jax.shard_map(
        local,
        mesh=mesh,
        in_specs=placed,
        out_specs=(P("ctx", "ch"), P("ctx", "ch"), P("ctx", "ch"), P(), P(), P()),
        check_vma=False,
    )
```

time: 57 us -> 50.8 us (0.89)
  blocking collectives: 20.7 us -> 0 us
  waiting for transfers between devices: 1.79 us -> 12.1 us
  starting transfers between devices: 3.96 us -> 10.7 us
  local copies, waits for them, and re-layouts: 9.06 us -> 5.7 us
  Pallas kernels: 20.2 us -> 21.1 us
    all_to_all x2 -> x0, blocking collectives: 20.7 us -> none  [the longest x1 12.6 us: local(): got = lax.all_to_all(send, 'ctx', split_axis=0, concat_axis=0, tiled=True)]
    ppermute x0 -> x6, waiting for transfers between devices: none -> 12.1 us  [the longest x3 12.1 us: local(): lax.ppermute(outgoing, 'ctx', [(i, i ^ 1 << level) for i in range(parts)])]
    ppermute x0 -> x6, starting transfers between devices: none -> 10.7 us  [the longest x3 5.46 us: local(): lax.ppermute(message, 'ch', [(i, (i + shift) % shards) for i in range(sha...]
    all_to_all x1 -> x0, starting transfers between devices: 3.96 us -> none  [local(): lax.all_to_all(spread, ('ctx', 'ch'), split_axis=0, concat_axis=0, tiled=...]
    unnamed x21 -> x24, local copies, waits for them, and re-layouts: 8.02 us -> 5.7 us
    all_to_all x1 -> x0, waiting for transfers between devices: 1.79 us -> none  [local(): lax.all_to_all(spread, ('ctx', 'ch'), split_axis=0, concat_axis=0, tiled=...]
    pallas_call x2 -> x5, Pallas kernels: 11.8 us -> 12.7 us  [the longest x1 10.6 us: local(): pl.pallas_call(lambda *refs: states_kernel(*refs, steps=steps, **sizes),...]
    broadcast_in_dim x1 -> x0, local copies, waits for them, and re-layouts: 0.71 us -> none  [local(): spread = jnp.broadcast_to(grads[None], (parts * shards, 8, own_width))]
  transfers between devices with their start and end apart: 1 -> 6, of which waited for: 1 -> 3; matrix products, arithmetic and copies ran while one was open for 0% -> 0% of each run, Pallas kernels for 15% -> 17%
where the time goes in v2:
time: 50.8 us; the launch traced here: 50.4 us
  Pallas kernels  21.1 us (42%)
  waiting for transfers between devices  12.1 us (24%)
  starting transfers between devices  10.7 us (21%)
  local copies, waits for them, and re-layouts  5.7 us (11%)
  between operations  0.74 us (1%)
    ppermute x3, waiting for transfers between devices, local(): lax.ppermute(outgoing, 'ctx', [(i, i ^ 1 << level) for i in range(parts)])  12.1 us
    pallas_call x1, Pallas kernels, local(): pl.pallas_call(lambda *refs: states_kernel(*refs, steps=steps, **sizes),...  10.6 us
    unnamed x24, local copies, waits for them, and re-layouts  5.7 us
    ppermute x3, starting transfers between devices, local(): lax.ppermute(message, 'ch', [(i, (i + shift) % shards) for i in range(sha...  5.46 us
    ppermute x3, starting transfers between devices, local(): lax.ppermute(outgoing, 'ctx', [(i, i ^ 1 << level) for i in range(parts)])  5.28 us
    pallas_call x1, Pallas kernels, local(): pl.pallas_call(lambda *refs: output_kernel(*refs, **sizes), grid=(steps,)...  4.33 us
    pallas_call x1, Pallas kernels, local(): pl.pallas_call(lambda *refs: conv_kernel(*refs, **sizes), grid=(steps,),...  4.03 us
    pallas_call x3, Pallas kernels, local(): pl.pallas_call(lambda *refs, level=level: combine_kernel(*refs, level=lev...  1.49 us
  transfers between devices with their start and end apart: 6, of which 3 were waited for; matrix products, arithmetic and copies ran while one was open for 0% of the time, Pallas kernels for 17%

profile of v2, /device:TPU:0, one launch (start us, length us, event | category | flops | bytes accessed | tf_op | source)
XLA Modules:
  0.0 50.4 jit_solution(6316135184396777879)
XLA Ops:
  0.6 0.0 copy-start
  0.6 1.0 %copy-done = bf16[128,2048]{1,0:T(8,128)(2,1)S(1)} copy-done((bf16[128,2048]{1,0:T(8,128)(2,1)S(1)}, bf16[128,2048]{1,0:T(8,128)(2,1)}, u32[]{:S(2)}) %copy-start) | copy-done | bytes 524312
  1.7 0.0 copy-start.2
  1.7 1.0 %copy-done.2 = bf16[128,2048]{1,0:T(8,128)(2,1)S(1)} copy-done((bf16[128,2048]{1,0:T(8,128)(2,1)S(1)}, bf16[128,2048]{1,0:T(8,128)(2,1)}, u32[]{:S(2)}) %copy-start.2) | copy-done | bytes 524312
  2.7 0.0 copy-start.4
  2.7 1.0 %copy-done.4 = bf16[128,2048]{1,0:T(8,128)(2,1)S(1)} copy-done((bf16[128,2048]{1,0:T(8,128)(2,1)S(1)}, bf16[128,2048]{1,0:T(8,128)(2,1)}, u32[]{:S(2)}) %copy-start.4) | copy-done | bytes 524312
  3.8 0.0 copy-start.6
  3.8 1.0 %copy-done.6 = bf16[128,2048]{1,0:T(8,128)(2,1)S(1)} copy-done((bf16[128,2048]{1,0:T(8,128)(2,1)S(1)}, bf16[128,2048]{1,0:T(8,128)(2,1)}, u32[]{:S(2)}) %copy-start.6) | copy-done | bytes 524312
  4.8 0.0 copy-start.7
  4.8 0.8 %copy-done.7 = f32[512,16]{0,1:T(8,128)S(1)} copy-done((f32[512,16]{0,1:T(8,128)S(1)}, f32[512,16]{0,1:T(8,128)}, u32[]{:S(2)}) %copy-start.7) | copy-done | bytes 32792
  5.6 0.0 copy-start.9
  5.6 0.8 %copy-done.9 = f32[512,16]{0,1:T(8,128)S(1)} copy-done((f32[512,16]{0,1:T(8,128)S(1)}, f32[512,16]{0,1:T(8,128)}, u32[]{:S(2)}) %copy-start.9) | copy-done | bytes 32792
  6.3 0.0 copy-start.8
  6.3 0.0 copy-start.10
  6.3 0.0 copy-start.11
  6.3 10.6 %states.1 = (bf16[1120,128]{1,0:T(8,128)(2,1)S(1)}, bf16[128,4096]{1,0:T(8,128)(2,1)S(1)}, f32[2,16,128]{2,1,0:T(8,128)S(1)}, f32[16,16,128]{2,1,0:T(8,128)S(1)}) custom-call(f32[16,512]{1,0:T(8,128)S(1)} %bitcast.6, f32[16,512]{1,0:T(8,128)S(1)} %bitcast.8, bf16[128,2048]{1,0:T(8,128)(2,1)S(1)} %copy-done.6, bf16[128,2048]{1,0:T(8,128)(2,1)S(1)} %copy-done, ...), custom_call_target="tpu_custom_call" | custom-call | tf_op jit(solution)/shard_map/states/pallas_call | solution.py:363
  16.9 0.5 %collective-permute-start = (bf16[1120,128]{1,0:T(8,128)(2,1)S(1)}, bf16[1120,128]{1,0:T(8,128)(2,1)S(1)}, u32[]{:S(2)}, u32[]{:S(2)}) collective-permute-start(bf16[1120,128]{1,0:T(8,128)(2,1)S(1)} %get-tuple-element.26.refs_1_), channel_id=1, source_target_pairs={{0,4},{4,0},{8,12},{12,8},{16,20},{20,16},{24,28},{28,24},{1,5},{5... | collective-permute-start | bytes 860168 | tf_op jit(solution)/shard_map/ppermute | solution.py:396
  17.4 1.2 %collective-permute-done.refs_2_ = bf16[1120,128]{1,0:T(8,128)(2,1)S(1)} collective-permute-done((bf16[1120,128]{1,0:T(8,128)(2,1)S(1)}, bf16[1120,128]{1,0:T(8,128)(2,1)S(1)}, u32[]{:S(2)}, u32[]{:S(2)}) %collective-permute-start) | collective-permute-done | bytes 286752 | tf_op jit(solution)/shard_map/ppermute | solution.py:396
  18.6 0.5 %combine.3 = (bf16[1120,128]{1,0:T(8,128)(2,1)S(1)}, f32[16,32,128]{2,1,0:T(8,128)S(1)}) custom-call(f32[16,16,128]{2,1,0:T(8,128)S(1)} %get-tuple-element.25.refs_0_, bf16[1120,128]{1,0:T(8,128)(2,1)S(1)} %get-tuple-element.26.refs_1_, bf16[1120,128]{1,0:T(8,128)(2,1)S(1)} %collective-permute-done.refs_2_), custom_call_target="tpu_custom_call" | custom-call | tf_op jit(solution)/shard_map/combine/pallas_call | solution.py:408
  19.1 2.9 %collective-permute-start.1 = (bf16[1120,128]{1,0:T(8,128)(2,1)S(1)}, bf16[1120,128]{1,0:T(8,128)(2,1)S(1)}, u32[]{:S(2)}, u32[]{:S(2)}) collective-permute-start(bf16[1120,128]{1,0:T(8,128)(2,1)S(1)} %get-tuple-element.27.refs_1_), channel_id=1, source_target_pairs={{0,8},{4,12},{8,0},{12,4},{16,24},{20,28},{24,16},{28,20},{1,9},{5... | collective-permute-start | bytes 860168 | tf_op jit(solution)/shard_map/ppermute | solution.py:396
  22.0 7.1 %collective-permute-done.1.refs_2_ = bf16[1120,128]{1,0:T(8,128)(2,1)S(1)} collective-permute-done((bf16[1120,128]{1,0:T(8,128)(2,1)S(1)}, bf16[1120,128]{1,0:T(8,128)(2,1)S(1)}, u32[]{:S(2)}, u32[]{:S(2)}) %collective-permute-start.1) | collective-permute-done | bytes 286752 | tf_op jit(solution)/shard_map/ppermute | solution.py:396
  29.2 0.5 %combine.4 = (bf16[1120,128]{1,0:T(8,128)(2,1)S(1)}, f32[16,32,128]{2,1,0:T(8,128)S(1)}, bf16[608,128]{1,0:T(8,128)(2,1)S(1)}) custom-call(f32[16,16,128]{2,1,0:T(8,128)S(1)} %get-tuple-element.25.refs_0_, bf16[1120,128]{1,0:T(8,128)(2,1)S(1)} %get-tuple-element.27.refs_1_, bf16[1120,128]{1,0:T(8,128)(2,1)S(1)} %collective-permute-done.1.refs_2_, ...), custom_call_target="tpu_custom_call" | custom-call | tf_op jit(solution)/shard_map/combine/pallas_call | solution.py:408
  29.7 0.0 copy-start.1
  29.7 0.0 copy-start.3
  29.7 0.0 copy-start.5
  29.7 1.8 %collective-permute-start.2 = (bf16[608,128]{1,0:T(8,128)(2,1)S(1)}, bf16[608,128]{1,0:T(8,128)(2,1)S(1)}, u32[]{:S(2)}, u32[]{:S(2)}) collective-permute-start(bf16[608,128]{1,0:T(8,128)(2,1)S(1)} %get-tuple-element.30), channel_id=1, source_target_pairs={{0,16},{4,20},{8,24},{12,28},{16,0},{20,4},{24,8},{28,12},{1,17},{... | collective-permute-start | bytes 466952 | tf_op jit(solution)/shard_map/ppermute | solution.py:396
  31.6 3.8 %collective-permute-done.2.refs_2_ = bf16[608,128]{1,0:T(8,128)(2,1)S(1)} collective-permute-done((bf16[608,128]{1,0:T(8,128)(2,1)S(1)}, bf16[608,128]{1,0:T(8,128)(2,1)S(1)}, u32[]{:S(2)}, u32[]{:S(2)}) %collective-permute-start.2) | collective-permute-done | bytes 155680 | tf_op jit(solution)/shard_map/ppermute | solution.py:396
  35.4 0.0 copy-done.8
  35.4 0.0 copy-done.10
  35.4 0.5 combine.5
  35.8 1.5 %collective-permute-start.3 = (f32[48,128]{1,0:T(8,128)S(1)}, f32[48,128]{1,0:T(8,128)S(1)}, u32[]{:S(2)}, u32[]{:S(2)}) collective-permute-start(f32[48,128]{1,0:T(8,128)S(1)} %get-tuple-element.36.refs_0_), channel_id=1, source_target_pairs={{0,1},{1,2},{2,3},{3,0},{4,5},{5,6},{6,7},{7,4},{8,9},{9,10},{10,1... | collective-permute-start | bytes 73736 | tf_op jit(solution)/shard_map/ppermute | solution.py:420
  37.3 2.6 %collective-permute-start.4 = (f32[48,128]{1,0:T(8,128)S(1)}, f32[48,128]{1,0:T(8,128)S(1)}, u32[]{:S(2)}, u32[]{:S(2)}) collective-permute-start(f32[48,128]{1,0:T(8,128)S(1)} %get-tuple-element.36.refs_0_), channel_id=1, source_target_pairs={{0,2},{1,3},{2,0},{3,1},{4,6},{5,7},{6,4},{7,5},{8,10},{9,11},{10,... | collective-permute-start | bytes 73736 | tf_op jit(solution)/shard_map/ppermute | solution.py:420
  39.9 1.3 %collective-permute-start.5 = (f32[48,128]{1,0:T(8,128)S(1)}, f32[48,128]{1,0:T(8,128)S(1)}, u32[]{:S(2)}, u32[]{:S(2)}) collective-permute-start(f32[48,128]{1,0:T(8,128)S(1)} %get-tuple-element.36.refs_0_), channel_id=1, source_target_pairs={{0,3},{1,0},{2,1},{3,2},{4,7},{5,4},{6,5},{7,6},{8,11},{9,8},{10,9... | collective-permute-start | bytes 73736 | tf_op jit(solution)/shard_map/ppermute | solution.py:420
  41.3 0.0 copy-done.11
  41.3 4.0 %conv.1.refs_1_ = f32[128,4096]{1,0:T(8,128)S(1)} custom-call(f32[2,16,128]{2,1,0:T(8,128)S(1)} %get-tuple-element.23.refs_0_, f32[64,128]{1,0:T(8,128)S(1)} %bitcast.10, bf16[128,4096]{1,0:T(8,128)(2,1)S(1)} %get-tuple-element.24.refs_2_), custom_call_target="tpu_custom_call" | custom-call | flops 536870912 | bytes 3145728 | tf_op jit(solution)/shard_map/conv/pallas_call | solution.py:380
  45.3 0.0 copy-done.1
  45.3 0.0 copy-done.3
  45.3 0.0 copy-done.5
  45.4 4.3 %outputs.1 = (bf16[128,2048]{1,0:T(8,128)(2,1)}, bf16[128,2048]{1,0:T(8,128)(2,1)}, bf16[128,2048]{1,0:T(8,128)(2,1)}) custom-call(f32[2,16,128]{2,1,0:T(8,128)S(1)} %get-tuple-element.23.refs_0_, f32[128,4096]{1,0:T(8,128)S(1)} %conv.1.refs_1_, bf16[16,32,128]{2,1,0:T(8,128)(2,1)S(1)} %get-tuple-element.32.refs_2_, bf16[128,2048]{1,0:T(8,128)(2,1)S(1)} %copy-done.1, ...), custom_call_target="tpu_custom_call" | custom-call | tf_op jit(solution)/shard_map/outputs/pallas_call | solution.py:422
  49.7 0.0 collective-permute-done.3.refs_1_
  49.7 0.0 collective-permute-done.4.refs_2_
  49.7 0.0 collective-permute-done.5.refs_3_
  49.7 0.7 %assemble.1 = (f32[16,512]{1,0:T(8,128)}, f32[16,512]{1,0:T(8,128)}, f32[64,128]{1,0:T(8,128)}) custom-call(f32[48,128]{1,0:T(8,128)S(1)} %get-tuple-element.36.refs_0_, f32[48,128]{1,0:T(8,128)S(1)} %collective-permute-done.3.refs_1_, f32[48,128]{1,0:T(8,128)S(1)} %collective-permute-done.4.refs_2_, f32[48,128]{1,0:T(8,128)S(1)} %collective-permute-done.5.refs_3_), custom_call_target="tpu_custom_call" | custom-call | tf_op jit(solution)/shard_map/assemble/pallas_call | solution.py:439
Async XLA Ops:
  0.6 1.0 %copy-start = (bf16[128,2048]{1,0:T(8,128)(2,1)S(1)}, bf16[128,2048]{1,0:T(8,128)(2,1)}, u32[]{:S(2)}) copy-start(bf16[128,2048]{1,0:T(8,128)(2,1)} %refs_3_.3) | copy-start | bytes 1572868
  1.7 1.0 %copy-start.2 = (bf16[128,2048]{1,0:T(8,128)(2,1)S(1)}, bf16[128,2048]{1,0:T(8,128)(2,1)}, u32[]{:S(2)}) copy-start(bf16[128,2048]{1,0:T(8,128)(2,1)} %refs_4_.3) | copy-start | bytes 1572868
  2.7 1.0 %copy-start.4 = (bf16[128,2048]{1,0:T(8,128)(2,1)S(1)}, bf16[128,2048]{1,0:T(8,128)(2,1)}, u32[]{:S(2)}) copy-start(bf16[128,2048]{1,0:T(8,128)(2,1)} %refs_5_.3) | copy-start | bytes 1572868
  3.8 1.0 %copy-start.6 = (bf16[128,2048]{1,0:T(8,128)(2,1)S(1)}, bf16[128,2048]{1,0:T(8,128)(2,1)}, u32[]{:S(2)}) copy-start(bf16[128,2048]{1,0:T(8,128)(2,1)} %refs_2_.1) | copy-start | bytes 1572868
  4.8 0.8 %copy-start.7 = (f32[512,16]{0,1:T(8,128)S(1)}, f32[512,16]{0,1:T(8,128)}, u32[]{:S(2)}) copy-start(f32[512,16]{0,1:T(8,128)} %param.12) | copy-start | bytes 98308
  5.6 0.8 %copy-start.9 = (f32[512,16]{0,1:T(8,128)S(1)}, f32[512,16]{0,1:T(8,128)}, u32[]{:S(2)}) copy-start(f32[512,16]{0,1:T(8,128)} %param.11) | copy-start | bytes 98308
  6.3 29.0 %copy-start.8 = (f32[512,16]{0,1:T(8,128)S(1)}, f32[512,16]{0,1:T(8,128)}, u32[]{:S(2)}) copy-start(f32[512,16]{0,1:T(8,128)} %param.12) | copy-start | bytes 98308
  6.3 29.0 %copy-start.10 = (f32[512,16]{0,1:T(8,128)S(1)}, f32[512,16]{0,1:T(8,128)}, u32[]{:S(2)}) copy-start(f32[512,16]{0,1:T(8,128)} %param.11) | copy-start | bytes 98308
  6.3 35.0 %copy-start.11 = (f32[8192]{0:T(1024)S(1)}, f32[8192]{0:T(1024)}, u32[]{:S(2)}) copy-start(f32[8192]{0:T(1024)} %param.13) | copy-start | bytes 98308
  16.9 1.7 %collective-permute-start = (bf16[1120,128]{1,0:T(8,128)(2,1)S(1)}, bf16[1120,128]{1,0:T(8,128)(2,1)S(1)}, u32[]{:S(2)}, u32[]{:S(2)}) collective-permute-start(bf16[1120,128]{1,0:T(8,128)(2,1)S(1)} %get-tuple-element.26.refs_1_), channel_id=1, source_target_pairs={{0,4},{4,0},{8,12},{12,8},{16,20},{20,16},{24,28},{28,24},{1,5},{5... | collective-permute-start | bytes 860168 | tf_op jit(solution)/shard_map/ppermute | solution.py:396
  19.1 10.1 %collective-permute-start.1 = (bf16[1120,128]{1,0:T(8,128)(2,1)S(1)}, bf16[1120,128]{1,0:T(8,128)(2,1)S(1)}, u32[]{:S(2)}, u32[]{:S(2)}) collective-permute-start(bf16[1120,128]{1,0:T(8,128)(2,1)S(1)} %get-tuple-element.27.refs_1_), channel_id=1, source_target_pairs={{0,8},{4,12},{8,0},{12,4},{16,24},{20,28},{24,16},{28,20},{1,9},{5... | collective-permute-start | bytes 860168 | tf_op jit(solution)/shard_map/ppermute | solution.py:396
  29.7 15.6 %copy-start.1 = (bf16[128,2048]{1,0:T(8,128)(2,1)S(1)}, bf16[128,2048]{1,0:T(8,128)(2,1)}, u32[]{:S(2)}) copy-start(bf16[128,2048]{1,0:T(8,128)(2,1)} %refs_3_.3) | copy-start | bytes 1572868
  29.7 15.6 %copy-start.3 = (bf16[128,2048]{1,0:T(8,128)(2,1)S(1)}, bf16[128,2048]{1,0:T(8,128)(2,1)}, u32[]{:S(2)}) copy-start(bf16[128,2048]{1,0:T(8,128)(2,1)} %refs_4_.3) | copy-start | bytes 1572868
  29.7 15.6 %copy-start.5 = (bf16[128,2048]{1,0:T(8,128)(2,1)S(1)}, bf16[128,2048]{1,0:T(8,128)(2,1)}, u32[]{:S(2)}) copy-start(bf16[128,2048]{1,0:T(8,128)(2,1)} %refs_5_.3) | copy-start | bytes 1572868
  29.7 5.6 %collective-permute-start.2 = (bf16[608,128]{1,0:T(8,128)(2,1)S(1)}, bf16[608,128]{1,0:T(8,128)(2,1)S(1)}, u32[]{:S(2)}, u32[]{:S(2)}) collective-permute-start(bf16[608,128]{1,0:T(8,128)(2,1)S(1)} %get-tuple-element.30), channel_id=1, source_target_pairs={{0,16},{4,20},{8,24},{12,28},{16,0},{20,4},{24,8},{28,12},{1,17},{... | collective-permute-start | bytes 466952 | tf_op jit(solution)/shard_map/ppermute | solution.py:396
  35.8 13.9 %collective-permute-start.3 = (f32[48,128]{1,0:T(8,128)S(1)}, f32[48,128]{1,0:T(8,128)S(1)}, u32[]{:S(2)}, u32[]{:S(2)}) collective-permute-start(f32[48,128]{1,0:T(8,128)S(1)} %get-tuple-element.36.refs_0_), channel_id=1, source_target_pairs={{0,1},{1,2},{2,3},{3,0},{4,5},{5,6},{6,7},{7,4},{8,9},{9,10},{10,1... | collective-permute-start | bytes 73736 | tf_op jit(solution)/shard_map/ppermute | solution.py:420
  37.3 12.3 %collective-permute-start.4 = (f32[48,128]{1,0:T(8,128)S(1)}, f32[48,128]{1,0:T(8,128)S(1)}, u32[]{:S(2)}, u32[]{:S(2)}) collective-permute-start(f32[48,128]{1,0:T(8,128)S(1)} %get-tuple-element.36.refs_0_), channel_id=1, source_target_pairs={{0,2},{1,3},{2,0},{3,1},{4,6},{5,7},{6,4},{7,5},{8,10},{9,11},{10,... | collective-permute-start | bytes 73736 | tf_op jit(solution)/shard_map/ppermute | solution.py:420
  39.9 9.8 %collective-permute-start.5 = (f32[48,128]{1,0:T(8,128)S(1)}, f32[48,128]{1,0:T(8,128)S(1)}, u32[]{:S(2)}, u32[]{:S(2)}) collective-permute-start(f32[48,128]{1,0:T(8,128)S(1)} %get-tuple-element.36.refs_0_), channel_id=1, source_target_pairs={{0,3},{1,0},{2,1},{3,2},{4,7},{5,4},{6,5},{7,6},{8,11},{9,8},{10,9... | collective-permute-start | bytes 73736 | tf_op jit(solution)/shard_map/ppermute | solution.py:420

commit v3 on v2

--- a/solution.py
+++ b/solution.py
@@ -20,6 +20,14 @@
     return lax.broadcasted_iota(jnp.int32, shape, axis)
 
 
+def over(value, size):
+    return lax.shift_right_logical(value, size.bit_length() - 1)
+
+
+def within(value, size):
+    return lax.bitwise_and(value, size - 1)
+
+
 def mxu(left, right):
     return jnp.dot(left, right, preferred_element_type=F32)
 
@@ -59,73 +67,58 @@
     table = table.T
     groups = table.shape[0]
     per_row = LANES // poles
-    spread = jnp.where(iota((poles, LANES), 0) == iota((poles, LANES), 1) % poles, 1.0, 0.0)
+    spread = jnp.where(iota((poles, LANES), 0) == within(iota((poles, LANES), 1), poles), 1.0, 0.0)
     wide = exact_dot(table, spread)
-    keep = iota((groups, LANES), 0) % per_row == iota((groups, LANES), 1) // poles
+    keep = within(iota((groups, LANES), 0), per_row) == over(iota((groups, LANES), 1), poles)
     wide = jnp.where(keep, wide, 0.0)
     return jnp.sum(wide.reshape(groups // per_row, per_row, LANES), axis=1)
 
 
 def members(groups, first, span, width):
-    return jnp.where(iota((groups, width), 0) == first + iota((groups, width), 1) // span, 1.0, 0.0).astype(BF16)
+    return jnp.where(iota((groups, width), 0) == first + over(iota((groups, width), 1), span), 1.0, 0.0).astype(BF16)
 
 
 def shard_start(groups):
     return pl.multiple_of(lax.axis_index("ch") * groups, LANES)
 
 
-def states_kernel(logs_ref, res_ref, q_any, k_any, v_any, c_any, msg_ref, pair_ref, rows_ref, rates_ref,
-                  q_ref, k_ref, v_ref, c_ref, skip_ref, sems, *, group, poles, steps):
-    tokens, width = q_ref.shape
+def states_kernel(logs_ref, res_ref, gated_ref, dgate_ref, msg_ref, pair_ref, rows_ref, rates_ref, skip_ref,
+                  *, group, poles, steps):
+    tokens, _ = gated_ref.shape
     per_block = LANES // group
     blocks, _, _ = rates_ref.shape
     groups = blocks * per_block
     inner = blocks // steps
-    chunk = width // steps
     subs = tokens // SUB
     lag_width = per_block * SUB
-
-    def copies(step):
-        cut = pl.ds(pl.multiple_of(step * chunk, LANES), chunk)
-        pairs = ((k_any, k_ref), (v_any, v_ref), (c_any, c_ref), (q_any, q_ref))
-        return [
-            pltpu.make_async_copy(far.at[:, cut], near.at[:, cut], sems.at[n, step])
-            for n, (far, near) in enumerate(pairs)
-        ]
-
-    for step in range(steps):
-        for copy in copies(step):
-            copy.start()
 
     first = shard_start(groups)
     logs = logs_ref[:, pl.ds(first, groups)]
     rows_ref[0] = jnp.exp(flat_rows(logs, poles))
     rows_ref[1] = flat_rows(res_ref[:, pl.ds(first, groups)], poles)
-    logs = split(logs, 3)
+    pieces = split(logs, 3).astype(F32)
+    spread = jnp.concatenate(
+        [members(groups, 0, SUB, lag_width), members(groups, 0, group, LANES)], axis=1
+    )
 
     flip = reversal(tokens)
-    lag = (SUB - 1 - iota((poles, lag_width), 1) % SUB).astype(F32)
-    wide_group = (iota((SUB, 2 * LANES), 1) % LANES) // group
-    causal = iota((SUB, lag_width), 0) + iota((SUB, lag_width), 1) % SUB <= SUB - 1
+    lag = (SUB - 1 - within(iota((poles, lag_width), 1), SUB)).astype(F32)
+    wide_group = over(within(iota((SUB, 2 * LANES), 1), LANES), group)
+    causal = iota((SUB, lag_width), 0) + within(iota((SUB, lag_width), 1), SUB) <= SUB - 1
 
     def body(step, sums):
-        for copy in copies(step):
-            copy.wait()
         for j in range(inner):
             block = step * inner + j
             cut = pl.ds(pl.multiple_of(block * LANES, LANES), LANES)
-            gated = gate(k_ref[:, cut], v_ref[:, cut])
-            dgate = gate(c_ref[:, cut], q_ref[:, cut])
+            gated, dgate = gated_ref[:, cut], dgate_ref[:, cut]
             skip = jnp.sum(gated.astype(F32) * dgate.astype(F32), axis=0, keepdims=True)
             skip_ref[pl.ds(block, 1), :] = skip
             turned = mxu(flip, dgate).astype(BF16)
             pair = jnp.concatenate([gated, turned], axis=1)
             pair_ref[:, pl.ds(pl.multiple_of(2 * block * LANES, LANES), 2 * LANES)] = pair
 
-            lag_of = members(groups, block * per_block, SUB, lag_width)
-            lane_of = members(groups, block * per_block, group, LANES)
-            spread = jnp.concatenate([lag_of, lane_of], axis=1)
-            rates = jnp.exp(join(mxu(logs, spread), poles))
+            turned_pieces = pltpu.roll(pieces, groups - block * per_block, 1).astype(BF16)
+            rates = jnp.exp(join(mxu(turned_pieces, spread), poles))
             lag_rate, rate = rates[:, :lag_width], rates[:, lag_width:]
             rates_ref[block] = rate
             table = jnp.exp(-lag_rate * lag)
@@ -166,7 +159,7 @@
             near = jnp.concatenate([lags * table, lags * moment_table], axis=0)
             far = jnp.concatenate([once * cross_res, once * cross_mom], axis=0)
             terms = split(jnp.concatenate([near, far], axis=1), 2)
-            sums = sums + join(mxu_t(terms, spread), 2 * poles)
+            sums = sums + pltpu.roll(join(mxu_t(terms, spread), 2 * poles), block * per_block, 1)
         return sums
 
     sums = lax.fori_loop(0, steps, body, jnp.zeros((2 * poles, groups), F32))
@@ -175,33 +168,34 @@
     msg_ref[tail + 4 * poles :, :] = split(skip_ref[...], 2)
 
 
-def conv_kernel(rows_ref, skip_ref, pair_ref, conv_ref, *, group, poles):
+def conv_kernel(rows_ref, skip_ref, pair_ref, conv_ref, *, group, poles, steps):
     tokens, width = pair_ref.shape
     per_block = LANES // group
-    step = pl.program_id(0)
-    blocks = width // (2 * LANES)
     all_blocks = rows_ref.shape[1]
+    blocks = all_blocks // steps
     first = lax.axis_index("ch") * all_blocks
     back_pos = (tokens - 1 - iota((tokens, LANES), 0)).astype(F32)
-    wide_group = (iota((tokens, 2 * LANES), 1) % LANES) // group
+    wide_group = over(within(iota((tokens, 2 * LANES), 1), LANES), group)
     causal = iota((tokens, tokens), 0) >= iota((tokens, tokens), 1)
-    for j in range(blocks):
-        cut = slice(2 * j * LANES, 2 * (j + 1) * LANES)
-        pair = pair_ref[:, cut]
-        here = step * blocks + j
-        rate = rows_ref[0, pl.ds(here, 1), :]
-        res = rows_ref[1, pl.ds(here, 1), :]
-        table = (res * jnp.exp(-rate * back_pos)).T
-        left, right = [], []
-        for g in range(per_block):
-            taps = jnp.sum(table[g * poles : (g + 1) * poles], axis=0, keepdims=True)
-            base = pltpu.roll(jnp.broadcast_to(taps, (8, tokens)), 1, 1, stride=1, stride_axis=0)
-            rolled = [base] + [pltpu.roll(base, 8 * a, 1) for a in range(1, tokens // 8)]
-            left.append(jnp.where(causal, jnp.concatenate(rolled, axis=0), 0.0).astype(BF16))
-            right.append(jnp.where(wide_group == g, pair, jnp.zeros_like(pair)))
-        total = mxu(jnp.concatenate(left, axis=1), jnp.concatenate(right, axis=0))
-        gain = skip_ref[pl.ds(first + here, 1), :]
-        conv_ref[:, cut] = total + jnp.concatenate([gain, gain], axis=1) * pair.astype(F32)
+    @pl.loop(0, steps)
+    def _(step):
+        for j in range(blocks):
+            here = step * blocks + j
+            cut = pl.ds(pl.multiple_of(2 * here * LANES, LANES), 2 * LANES)
+            pair = pair_ref[:, cut]
+            rate = rows_ref[0, pl.ds(here, 1), :]
+            res = rows_ref[1, pl.ds(here, 1), :]
+            table = (res * jnp.exp(-rate * back_pos)).T
+            left, right = [], []
+            for g in range(per_block):
+                taps = jnp.sum(table[g * poles : (g + 1) * poles], axis=0, keepdims=True)
+                base = pltpu.roll(jnp.broadcast_to(taps, (8, tokens)), 1, 1, stride=1, stride_axis=0)
+                rolled = [base] + [pltpu.roll(base, 8 * a, 1) for a in range(1, tokens // 8)]
+                left.append(jnp.where(causal, jnp.concatenate(rolled, axis=0), 0.0).astype(BF16))
+                right.append(jnp.where(wide_group == g, pair, jnp.zeros_like(pair)))
+            total = mxu(jnp.concatenate(left, axis=1), jnp.concatenate(right, axis=0))
+            gain = skip_ref[pl.ds(first + here, 1), :]
+            conv_ref[:, cut] = total + jnp.concatenate([gain, gain], axis=1) * pair.astype(F32)
 
 
 def combine_kernel(*refs, level, levels, group, poles, tokens):
@@ -210,6 +204,8 @@
     rates_ref, own_ref, got_ref = refs[:3]
     rest = refs[3:]
     held_ref = rest.pop(0) if level else None
+    if level == 1:
+        rest.pop(0)
     if last:
         logs_ref, res_ref = rest.pop(0), rest.pop(0)
     slim_ref = rest.pop() if level == levels - 2 else None
@@ -297,29 +293,31 @@
 
 
 def output_kernel(rows_ref, conv_ref, held_ref, k_ref, v_ref, c_ref, gq_ref, gk_ref, gv_ref, *, group, poles):
-    tokens, width = k_ref.shape
+    tokens, width = gq_ref.shape
     per_block = LANES // group
     step = pl.program_id(0)
     blocks = width // LANES
     flip = reversal(tokens)
     ahead = (1 + iota((tokens, LANES), 0)).astype(F32)
-    wide_group = (iota((poles, 2 * LANES), 1) % LANES) // group
+    wide_group = over(within(iota((poles, 2 * LANES), 1), LANES), group)
     for j in range(blocks):
         cut = slice(j * LANES, (j + 1) * LANES)
         here = step * blocks + j
+        wide = pl.ds(pl.multiple_of(here * LANES, LANES), LANES)
+        both = pl.ds(pl.multiple_of(2 * here * LANES, LANES), 2 * LANES)
         rate = rows_ref[0, pl.ds(here, 1), :]
         res = rows_ref[1, pl.ds(here, 1), :]
         table = (res * jnp.exp(-rate * ahead)).astype(BF16)
-        held = held_ref[j]
+        held = held_ref[here]
         states = jnp.concatenate([held[:poles], held[poles:]], axis=1)
         stack = jnp.concatenate(
             [jnp.where(wide_group == g, states, jnp.zeros_like(states)) for g in range(per_block)], axis=0
         )
-        total = (conv_ref[:, 2 * j * LANES : 2 * (j + 1) * LANES] + mxu(table, stack)).astype(BF16)
+        total = (conv_ref[:, both] + mxu(table, stack)).astype(BF16)
         flow = mxu(flip, total[:, LANES:])
-        gq_ref[:, cut] = (c_ref[:, cut].astype(F32) * total[:, :LANES].astype(F32)).astype(BF16)
-        gk_ref[:, cut] = (flow * v_ref[:, cut].astype(F32)).astype(BF16)
-        gv_ref[:, cut] = (flow * k_ref[:, cut].astype(F32)).astype(BF16)
+        gq_ref[:, cut] = (c_ref[:, wide].astype(F32) * total[:, :LANES].astype(F32)).astype(BF16)
+        gk_ref[:, cut] = (flow * v_ref[:, wide].astype(F32)).astype(BF16)
+        gv_ref[:, cut] = (flow * k_ref[:, wide].astype(F32)).astype(BF16)
 
 
 def assemble_kernel(*refs, shards, poles):
@@ -350,19 +348,14 @@
     sizes = dict(group=group, poles=poles)
     tail = 4 * poles + 2 * blocks
 
-    def fixed(*shape):
-        return pl.BlockSpec(shape, lambda i: (0,) * len(shape))
-
     vmem = pl.BlockSpec(memory_space=pltpu.VMEM)
-    far = pl.BlockSpec(memory_space=pltpu.HBM)
     log_rates, residues = log_rates.T, residues.T
     main = pl.BlockSpec((tokens, step_width), lambda i: (0, i))
-    twice = pl.BlockSpec((tokens, 2 * step_width), lambda i: (0, i))
-    row_table = fixed(2, blocks, LANES)
-
+
+    gated, dgate = gate(key_input, value_input), gate(cotangent, queries)
     message, pair, rows, rates = pl.pallas_call(
         lambda *refs: states_kernel(*refs, steps=steps, **sizes),
-        in_specs=[vmem, vmem, far, far, far, far],
+        in_specs=[vmem] * 4,
         out_specs=[vmem] * 4,
         out_shape=[
             jax.ShapeDtypeStruct((blocks * 4 * poles + tail, LANES), BF16),
@@ -370,18 +363,16 @@
             jax.ShapeDtypeStruct((2, blocks, LANES), F32),
             jax.ShapeDtypeStruct((blocks, poles, LANES), F32),
         ],
-        scratch_shapes=[pltpu.VMEM((tokens, width), BF16)] * 4
-        + [pltpu.VMEM((blocks, LANES), F32), pltpu.SemaphoreType.DMA((4, steps))],
+        scratch_shapes=[pltpu.VMEM((blocks, LANES), F32)],
         compiler_params=PARAMS,
         name="states",
-    )(log_rates, residues, queries, key_input, value_input, cotangent)
+    )(log_rates, residues, gated, dgate)
 
     skip_rows = skip_gain.reshape(-1, LANES)
     conv = pl.pallas_call(
-        lambda *refs: conv_kernel(*refs, **sizes),
-        grid=(steps,),
-        in_specs=[row_table, fixed(*skip_rows.shape), twice],
-        out_specs=twice,
+        lambda *refs: conv_kernel(*refs, steps=steps, **sizes),
+        in_specs=[vmem] * 3,
+        out_specs=vmem,
         out_shape=jax.ShapeDtypeStruct((tokens, 2 * width), F32),
         compiler_params=PARAMS,
         cost_estimate=pl.CostEstimate(
@@ -397,6 +388,8 @@
         operands = [rates, message, got]
         if level:
             operands.append(held)
+        if level == 1:
+            operands.append(conv)
         if last:
             operands += [log_rates, residues]
             out = jax.ShapeDtypeStruct((2 * poles + blocks, LANES), F32)
@@ -407,7 +400,7 @@
             outs.append(jax.ShapeDtypeStruct((blocks * 2 * poles + tail, LANES), BF16))
         message, held, *slim = pl.pallas_call(
             lambda *refs, level=level: combine_kernel(*refs, level=level, levels=levels, tokens=tokens, **sizes),
-            in_specs=[vmem] * len(operands),
+            in_specs=[pl.BlockSpec(memory_space=pl.ANY) if x is conv else vmem for x in operands],
             out_specs=[vmem] * len(outs),
             out_shape=outs,
             compiler_params=PARAMS,
@@ -422,14 +415,7 @@
     grad_query, grad_key, grad_value = pl.pallas_call(
         lambda *refs: output_kernel(*refs, **sizes),
         grid=(steps,),
-        in_specs=[
-            row_table,
-            twice,
-            pl.BlockSpec((blocks // steps, 2 * poles, LANES), lambda i: (i, 0, 0)),
-            main,
-            main,
-            main,
-        ],
+        in_specs=[vmem] * 6,
         out_specs=[main, main, main],
         out_shape=[jax.ShapeDtypeStruct((tokens, width), BF16)] * 3,
         compiler_params=PARAMS,

time: 50.8 us -> 41.1 us (0.81)
  local copies, waits for them, and re-layouts: 5.7 us -> 0.03 us
  waiting for transfers between devices: 12.1 us -> 8.22 us
  other arithmetic: 0 us -> 1.92 us
  Pallas kernels: 21.1 us -> 19.3 us
    unnamed x24 -> x12, local copies, waits for them, and re-layouts: 5.7 us -> 0.03 us
    ppermute x3, waiting for transfers between devices: 12.1 us -> 8.22 us  [local(): lax.ppermute(outgoing, 'ctx', [(i, i ^ 1 << level) for i in range(parts)])]
    convert_element_type x0 -> x1, other arithmetic: none -> 1.92 us  [gate(): return (left.astype(F32) * right.astype(F32)).astype(BF16)]
    pallas_call x1, Pallas kernels: 10.6 us -> 9.58 us  [local(): pl.pallas_call(lambda *refs: states_kernel(*refs, steps=steps, **sizes),...]
  transfers between devices with their start and end apart: 6 -> 6, of which waited for: 3 -> 3; matrix products, arithmetic and copies ran while one was open for 0% -> 0% of each run, Pallas kernels for 17% -> 19%
where the time goes in v3:
time: 41.1 us; the launch traced here: 40.9 us
  Pallas kernels  19.3 us (47%)
  starting transfers between devices  10.7 us (26%)
  waiting for transfers between devices  8.22 us (20%)
  other arithmetic  1.92 us (5%)
  between operations  0.75 us (2%)
    pallas_call x1, Pallas kernels, local(): pl.pallas_call(lambda *refs: states_kernel(*refs, steps=steps, **sizes),...  9.58 us
    ppermute x3, waiting for transfers between devices, local(): lax.ppermute(outgoing, 'ctx', [(i, i ^ 1 << level) for i in range(parts)])  8.22 us
    ppermute x3, starting transfers between devices, local(): lax.ppermute(message, 'ch', [(i, (i + shift) % shards) for i in range(sha...  5.5 us
    ppermute x3, starting transfers between devices, local(): lax.ppermute(outgoing, 'ctx', [(i, i ^ 1 << level) for i in range(parts)])  5.24 us
    pallas_call x1, Pallas kernels, local(): pl.pallas_call(lambda *refs: output_kernel(*refs, **sizes), grid=(steps,)...  4.02 us
    pallas_call x1, Pallas kernels, local(): pl.pallas_call(lambda *refs: conv_kernel(*refs, steps=steps, **sizes), in...  3.85 us
    convert_element_type x1, other arithmetic, gate(): return (left.astype(F32) * right.astype(F32)).astype(BF16)  1.92 us
    pallas_call x3, Pallas kernels, local(): pl.pallas_call(lambda *refs, level=level: combine_kernel(*refs, level=lev...  1.14 us
  transfers between devices with their start and end apart: 6, of which 3 were waited for; matrix products, arithmetic and copies ran while one was open for 0% of the time, Pallas kernels for 19%

profile of v3, /device:TPU:0, one launch (start us, length us, event | category | flops | bytes accessed | tf_op | source)
XLA Modules:
  0.0 40.9 jit_solution(9857608767943118427)
XLA Ops:
  0.6 0.0 copy-start.3
  0.6 0.0 copy-start.4
  0.7 0.0 copy-start.5
  0.7 1.9 %multiply_convert_fusion = (bf16[128,2048]{1,0:T(8,128)(2,1)S(1)}, bf16[128,2048]{1,0:T(8,128)(2,1)S(1)}) fusion(bf16[128,2048]{1,0:T(8,128)(2,1)} %param.7, bf16[128,2048]{1,0:T(8,128)(2,1)} %refs_5_.1, bf16[128,2048]{1,0:T(8,128)(2,1)} %refs_4_.1, bf16[128,2048]{1,0:T(8,128)(2,1)} %refs_3_.1), kind=kLoop, calls=%fused_computation | loop fusion | flops 2097152 | bytes 3145728 | tf_op jit(solution)/shard_map/convert_element_type | solution.py:44
  2.6 0.0 copy-done.3
  2.6 0.0 copy-done.4
  2.6 9.6 %states.1 = (bf16[1120,128]{1,0:T(8,128)(2,1)S(1)}, bf16[128,4096]{1,0:T(8,128)(2,1)S(1)}, f32[2,16,128]{2,1,0:T(8,128)S(1)}, f32[16,16,128]{2,1,0:T(8,128)S(1)}) custom-call(f32[16,512]{1,0:T(8,128)S(1)} %bitcast.6, f32[16,512]{1,0:T(8,128)S(1)} %bitcast.8, bf16[128,2048]{1,0:T(8,128)(2,1)S(1)} %get-tuple-element.41.refs_2_, ...), custom_call_target="tpu_custom_call" | custom-call | tf_op jit(solution)/shard_map/states/pallas_call | solution.py:356
  12.2 0.5 %collective-permute-start = (bf16[1120,128]{1,0:T(8,128)(2,1)S(1)}, bf16[1120,128]{1,0:T(8,128)(2,1)S(1)}, u32[]{:S(2)}, u32[]{:S(2)}) collective-permute-start(bf16[1120,128]{1,0:T(8,128)(2,1)S(1)} %get-tuple-element.26.refs_1_), channel_id=1, source_target_pairs={{0,4},{4,0},{8,12},{12,8},{16,20},{20,16},{24,28},{28,24},{1,5},{5... | collective-permute-start | bytes 860168 | tf_op jit(solution)/shard_map/ppermute | solution.py:387
  12.7 1.2 %collective-permute-done.refs_2_ = bf16[1120,128]{1,0:T(8,128)(2,1)S(1)} collective-permute-done((bf16[1120,128]{1,0:T(8,128)(2,1)S(1)}, bf16[1120,128]{1,0:T(8,128)(2,1)S(1)}, u32[]{:S(2)}, u32[]{:S(2)}) %collective-permute-start) | collective-permute-done | bytes 286752 | tf_op jit(solution)/shard_map/ppermute | solution.py:387
  13.9 0.4 combine.3
  14.3 2.9 %collective-permute-start.1 = (bf16[1120,128]{1,0:T(8,128)(2,1)S(1)}, bf16[1120,128]{1,0:T(8,128)(2,1)S(1)}, u32[]{:S(2)}, u32[]{:S(2)}) collective-permute-start(bf16[1120,128]{1,0:T(8,128)(2,1)S(1)} %get-tuple-element.27.refs_1_), channel_id=1, source_target_pairs={{0,8},{4,12},{8,0},{12,4},{16,24},{20,28},{24,16},{28,20},{1,9},{5... | collective-permute-start | bytes 860168 | tf_op jit(solution)/shard_map/ppermute | solution.py:387
  17.2 0.0 copy-done.5
  17.2 3.9 %conv.1.refs_4_.refs_1_ = f32[128,4096]{1,0:T(8,128)S(1)} custom-call(f32[2,16,128]{2,1,0:T(8,128)S(1)} %get-tuple-element.23.refs_0_, f32[64,128]{1,0:T(8,128)S(1)} %bitcast.10, bf16[128,4096]{1,0:T(8,128)(2,1)S(1)} %get-tuple-element.24.refs_2_), custom_call_target="tpu_custom_call" | custom-call | flops 536870912 | bytes 3145728 | tf_op jit(solution)/shard_map/conv/pallas_call | solution.py:372
  21.1 0.0 copy-start
  21.1 0.0 copy-start.1
  21.1 0.0 copy-start.2
  21.1 3.2 %collective-permute-done.1.refs_2_ = bf16[1120,128]{1,0:T(8,128)(2,1)S(1)} collective-permute-done((bf16[1120,128]{1,0:T(8,128)(2,1)S(1)}, bf16[1120,128]{1,0:T(8,128)(2,1)S(1)}, u32[]{:S(2)}, u32[]{:S(2)}) %collective-permute-start.1) | collective-permute-done | bytes 286752 | tf_op jit(solution)/shard_map/ppermute | solution.py:387
  24.3 0.4 %combine.4 = (bf16[1120,128]{1,0:T(8,128)(2,1)S(1)}, f32[16,32,128]{2,1,0:T(8,128)S(1)}, bf16[608,128]{1,0:T(8,128)(2,1)S(1)}) custom-call(f32[16,16,128]{2,1,0:T(8,128)S(1)} %get-tuple-element.25.refs_0_, bf16[1120,128]{1,0:T(8,128)(2,1)S(1)} %get-tuple-element.27.refs_1_, bf16[1120,128]{1,0:T(8,128)(2,1)S(1)} %collective-permute-done.1.refs_2_, ...), custom_call_target="tpu_custom_call" | custom-call | tf_op jit(solution)/shard_map/combine/pallas_call | solution.py:401
  24.8 1.8 %collective-permute-start.2 = (bf16[608,128]{1,0:T(8,128)(2,1)S(1)}, bf16[608,128]{1,0:T(8,128)(2,1)S(1)}, u32[]{:S(2)}, u32[]{:S(2)}) collective-permute-start(bf16[608,128]{1,0:T(8,128)(2,1)S(1)} %get-tuple-element.30), channel_id=1, source_target_pairs={{0,16},{4,20},{8,24},{12,28},{16,0},{20,4},{24,8},{28,12},{1,17},{... | collective-permute-start | bytes 466952 | tf_op jit(solution)/shard_map/ppermute | solution.py:387
  26.6 3.8 %collective-permute-done.2.refs_2_ = bf16[608,128]{1,0:T(8,128)(2,1)S(1)} collective-permute-done((bf16[608,128]{1,0:T(8,128)(2,1)S(1)}, bf16[608,128]{1,0:T(8,128)(2,1)S(1)}, u32[]{:S(2)}, u32[]{:S(2)}) %collective-permute-start.2) | collective-permute-done | bytes 155680 | tf_op jit(solution)/shard_map/ppermute | solution.py:387
  30.4 0.3 combine.5
  30.7 1.6 %collective-permute-start.3 = (f32[48,128]{1,0:T(8,128)S(1)}, f32[48,128]{1,0:T(8,128)S(1)}, u32[]{:S(2)}, u32[]{:S(2)}) collective-permute-start(f32[48,128]{1,0:T(8,128)S(1)} %get-tuple-element.36.refs_0_), channel_id=1, source_target_pairs={{0,1},{1,2},{2,3},{3,0},{4,5},{5,6},{6,7},{7,4},{8,9},{9,10},{10,1... | collective-permute-start | bytes 73736 | tf_op jit(solution)/shard_map/ppermute | solution.py:413
  32.3 2.6 %collective-permute-start.4 = (f32[48,128]{1,0:T(8,128)S(1)}, f32[48,128]{1,0:T(8,128)S(1)}, u32[]{:S(2)}, u32[]{:S(2)}) collective-permute-start(f32[48,128]{1,0:T(8,128)S(1)} %get-tuple-element.36.refs_0_), channel_id=1, source_target_pairs={{0,2},{1,3},{2,0},{3,1},{4,6},{5,7},{6,4},{7,5},{8,10},{9,11},{10,... | collective-permute-start | bytes 73736 | tf_op jit(solution)/shard_map/ppermute | solution.py:413
  34.9 1.4 %collective-permute-start.5 = (f32[48,128]{1,0:T(8,128)S(1)}, f32[48,128]{1,0:T(8,128)S(1)}, u32[]{:S(2)}, u32[]{:S(2)}) collective-permute-start(f32[48,128]{1,0:T(8,128)S(1)} %get-tuple-element.36.refs_0_), channel_id=1, source_target_pairs={{0,3},{1,0},{2,1},{3,2},{4,7},{5,4},{6,5},{7,6},{8,11},{9,8},{10,9... | collective-permute-start | bytes 73736 | tf_op jit(solution)/shard_map/ppermute | solution.py:413
  36.2 0.0 copy-done
  36.2 0.0 copy-done.1
  36.2 0.0 copy-done.2
  36.2 4.0 %outputs.1 = (bf16[128,2048]{1,0:T(8,128)(2,1)}, bf16[128,2048]{1,0:T(8,128)(2,1)}, bf16[128,2048]{1,0:T(8,128)(2,1)}) custom-call(f32[2,16,128]{2,1,0:T(8,128)S(1)} %get-tuple-element.23.refs_0_, f32[128,4096]{1,0:T(8,128)S(1)} %conv.1.refs_4_.refs_1_, bf16[16,32,128]{2,1,0:T(8,128)(2,1)S(1)} %get-tuple-element.32.refs_2_, bf16[128,2048]{1,0:T(8,128)(2,1)S(1)} %copy-done.2, ...), custom_call_target="tpu_custom_call" | custom-call | tf_op jit(solution)/shard_map/outputs/pallas_call | solution.py:415
  40.2 0.0 collective-permute-done.3.refs_1_
  40.2 0.0 collective-permute-done.4.refs_2_
  40.3 0.0 collective-permute-done.5.refs_3_
  40.3 0.7 %assemble.1 = (f32[16,512]{1,0:T(8,128)}, f32[16,512]{1,0:T(8,128)}, f32[64,128]{1,0:T(8,128)}) custom-call(f32[48,128]{1,0:T(8,128)S(1)} %get-tuple-element.36.refs_0_, f32[48,128]{1,0:T(8,128)S(1)} %collective-permute-done.3.refs_1_, f32[48,128]{1,0:T(8,128)S(1)} %collective-permute-done.4.refs_2_, f32[48,128]{1,0:T(8,128)S(1)} %collective-permute-done.5.refs_3_), custom_call_target="tpu_custom_call" | custom-call | tf_op jit(solution)/shard_map/assemble/pallas_call | solution.py:425
Async XLA Ops:
  0.6 2.0 %copy-start.3 = (f32[512,16]{0,1:T(8,128)S(1)}, f32[512,16]{0,1:T(8,128)}, u32[]{:S(2)}) copy-start(f32[512,16]{0,1:T(8,128)} %param.12) | copy-start | bytes 98308
  0.6 2.0 %copy-start.4 = (f32[512,16]{0,1:T(8,128)S(1)}, f32[512,16]{0,1:T(8,128)}, u32[]{:S(2)}) copy-start(f32[512,16]{0,1:T(8,128)} %param.11) | copy-start | bytes 98308
  0.7 16.5 %copy-start.5 = (f32[8192]{0:T(1024)S(1)}, f32[8192]{0:T(1024)}, u32[]{:S(2)}) copy-start(f32[8192]{0:T(1024)} %param.13) | copy-start | bytes 98308
  12.2 1.7 %collective-permute-start = (bf16[1120,128]{1,0:T(8,128)(2,1)S(1)}, bf16[1120,128]{1,0:T(8,128)(2,1)S(1)}, u32[]{:S(2)}, u32[]{:S(2)}) collective-permute-start(bf16[1120,128]{1,0:T(8,128)(2,1)S(1)} %get-tuple-element.26.refs_1_), channel_id=1, source_target_pairs={{0,4},{4,0},{8,12},{12,8},{16,20},{20,16},{24,28},{28,24},{1,5},{5... | collective-permute-start | bytes 860168 | tf_op jit(solution)/shard_map/ppermute | solution.py:387
  14.3 10.1 %collective-permute-start.1 = (bf16[1120,128]{1,0:T(8,128)(2,1)S(1)}, bf16[1120,128]{1,0:T(8,128)(2,1)S(1)}, u32[]{:S(2)}, u32[]{:S(2)}) collective-permute-start(bf16[1120,128]{1,0:T(8,128)(2,1)S(1)} %get-tuple-element.27.refs_1_), channel_id=1, source_target_pairs={{0,8},{4,12},{8,0},{12,4},{16,24},{20,28},{24,16},{28,20},{1,9},{5... | collective-permute-start | bytes 860168 | tf_op jit(solution)/shard_map/ppermute | solution.py:387
  21.1 15.2 %copy-start = (bf16[128,2048]{1,0:T(8,128)(2,1)S(1)}, bf16[128,2048]{1,0:T(8,128)(2,1)}, u32[]{:S(2)}) copy-start(bf16[128,2048]{1,0:T(8,128)(2,1)} %refs_5_.1) | copy-start | bytes 1572868
  21.1 15.1 %copy-start.1 = (bf16[128,2048]{1,0:T(8,128)(2,1)S(1)}, bf16[128,2048]{1,0:T(8,128)(2,1)}, u32[]{:S(2)}) copy-start(bf16[128,2048]{1,0:T(8,128)(2,1)} %refs_4_.1) | copy-start | bytes 1572868
  21.1 15.1 %copy-start.2 = (bf16[128,2048]{1,0:T(8,128)(2,1)S(1)}, bf16[128,2048]{1,0:T(8,128)(2,1)}, u32[]{:S(2)}) copy-start(bf16[128,2048]{1,0:T(8,128)(2,1)} %refs_3_.1) | copy-start | bytes 1572868
  24.8 5.6 %collective-permute-start.2 = (bf16[608,128]{1,0:T(8,128)(2,1)S(1)}, bf16[608,128]{1,0:T(8,128)(2,1)S(1)}, u32[]{:S(2)}, u32[]{:S(2)}) collective-permute-start(bf16[608,128]{1,0:T(8,128)(2,1)S(1)} %get-tuple-element.30), channel_id=1, source_target_pairs={{0,16},{4,20},{8,24},{12,28},{16,0},{20,4},{24,8},{28,12},{1,17},{... | collective-permute-start | bytes 466952 | tf_op jit(solution)/shard_map/ppermute | solution.py:387
  30.7 9.5 %collective-permute-start.3 = (f32[48,128]{1,0:T(8,128)S(1)}, f32[48,128]{1,0:T(8,128)S(1)}, u32[]{:S(2)}, u32[]{:S(2)}) collective-permute-start(f32[48,128]{1,0:T(8,128)S(1)} %get-tuple-element.36.refs_0_), channel_id=1, source_target_pairs={{0,1},{1,2},{2,3},{3,0},{4,5},{5,6},{6,7},{7,4},{8,9},{9,10},{10,1... | collective-permute-start | bytes 73736 | tf_op jit(solution)/shard_map/ppermute | solution.py:413
  32.3 8.0 %collective-permute-start.4 = (f32[48,128]{1,0:T(8,128)S(1)}, f32[48,128]{1,0:T(8,128)S(1)}, u32[]{:S(2)}, u32[]{:S(2)}) collective-permute-start(f32[48,128]{1,0:T(8,128)S(1)} %get-tuple-element.36.refs_0_), channel_id=1, source_target_pairs={{0,2},{1,3},{2,0},{3,1},{4,6},{5,7},{6,4},{7,5},{8,10},{9,11},{10,... | collective-permute-start | bytes 73736 | tf_op jit(solution)/shard_map/ppermute | solution.py:413
  34.9 5.4 %collective-permute-start.5 = (f32[48,128]{1,0:T(8,128)S(1)}, f32[48,128]{1,0:T(8,128)S(1)}, u32[]{:S(2)}, u32[]{:S(2)}) collective-permute-start(f32[48,128]{1,0:T(8,128)S(1)} %get-tuple-element.36.refs_0_), channel_id=1, source_target_pairs={{0,3},{1,0},{2,1},{3,2},{4,7},{5,4},{6,5},{7,6},{8,11},{9,8},{10,9... | collective-permute-start | bytes 73736 | tf_op jit(solution)/shard_map/ppermute | solution.py:413

commit v4 on v3

v4 whole, which is shorter than its diff:
```python
import math

import jax
import jax.numpy as jnp
from jax import lax
from jax.experimental import pallas as pl
from jax.experimental.pallas import tpu as pltpu
from jax.sharding import PartitionSpec as P

LANES = 128
SUB = 32
F32 = jnp.float32
BF16 = jnp.bfloat16
EXACT = lax.Precision.HIGHEST
VMEM_LIMIT = 40 * 1024 * 1024
PARAMS = pltpu.CompilerParams(vmem_limit_bytes=VMEM_LIMIT)


def iota(shape, axis):
    return lax.broadcasted_iota(jnp.int32, shape, axis)


def over(value, size):
    return lax.shift_right_logical(value, size.bit_length() - 1)


def within(value, size):
    return lax.bitwise_and(value, size - 1)


def mxu(left, right):
    return jnp.dot(left, right, preferred_element_type=F32)


def mxu_t(left, right):
    return lax.dot_general(left, right, (((1,), (1,)), ((), ())), preferred_element_type=F32)


def exact_dot(left, right):
    return jnp.dot(left, right, precision=EXACT, preferred_element_type=F32)


def gate(left, right):
    return (left.astype(F32) * right.astype(F32)).astype(BF16)


def reversal(size):
    return jnp.where(iota((size, size), 0) + iota((size, size), 1) == size - 1, 1.0, 0.0).astype(BF16)


def split(value, pieces):
    parts = []
    for _ in range(pieces):
        parts.append(value.astype(BF16))
        value = value - parts[-1].astype(F32)
    return jnp.concatenate(parts, axis=0)


def join(stacked, rows):
    total = stacked[:rows].astype(F32)
    for start in range(rows, stacked.shape[0], rows):
        total = total + stacked[start : start + rows].astype(F32)
    return total


def flat_rows(table, poles):
    table = table.T
    groups = table.shape[0]
    per_row = LANES // poles
    spread = jnp.where(iota((poles, LANES), 0) == within(iota((poles, LANES), 1), poles), 1.0, 0.0)
    wide = exact_dot(table, spread)
    keep = within(iota((groups, LANES), 0), per_row) == over(iota((groups, LANES), 1), poles)
    wide = jnp.where(keep, wide, 0.0)
    return jnp.sum(wide.reshape(groups // per_row, per_row, LANES), axis=1)


def members(groups, first, span, width):
    return jnp.where(iota((groups, width), 0) == first + over(iota((groups, width), 1), span), 1.0, 0.0).astype(BF16)


def shard_start(groups):
    return pl.multiple_of(lax.axis_index("ch") * groups, LANES)


def pack_half(value, half):
    chosen = jnp.where(half > 0, pltpu.roll(value, LANES // 2, 1), value)
    high = chosen.astype(BF16).astype(F32)
    low = pltpu.roll(chosen - high, LANES // 2, 1)
    return jnp.where(iota(value.shape, 1) < LANES // 2, high, low).astype(BF16)


def open_half(packed):
    value = packed.astype(F32)
    return value + pltpu.roll(value, LANES // 2, 1)


def states_kernel(logs_ref, res_ref, gated_ref, dgate_ref, send_ref, keep_ref, turned_ref, rows_ref, rates_ref,
                  taps_ref, tables_ref, skip_ref, *, group, poles, inner):
    tokens, _ = gated_ref.shape
    per_block = LANES // group
    blocks, _, _ = rates_ref.shape
    half_blocks = blocks // 2
    groups = blocks * per_block
    subs = tokens // SUB
    lag_width = per_block * SUB
    step_groups = inner * per_block
    wide, lag_wide = inner * LANES, inner * lag_width
    core = lax.rem(lax.axis_index("ctx"), 2)

    first = shard_start(groups)
    logs = logs_ref[:, pl.ds(first, groups)]
    res = res_ref[:, pl.ds(first, groups)]
    rows_ref[0] = jnp.exp(flat_rows(logs, poles))
    rows_ref[1] = flat_rows(res, poles)
    pieces = jnp.concatenate([split(logs, 3), split(res, 3)], axis=0).astype(F32)
    spread = jnp.concatenate([members(groups, 0, SUB, lag_wide), members(groups, 0, group, wide)], axis=1)

    flip = reversal(tokens)
    lag = (SUB - 1 - within(iota((poles, lag_wide), 1), SUB)).astype(F32)
    wide_group = over(within(iota((SUB, 2 * LANES), 1), LANES), group)
    causal = iota((SUB, lag_wide), 0) + within(iota((SUB, lag_wide), 1), SUB) <= SUB - 1

    sums = jnp.zeros((2 * poles, groups), F32)
    for turn, msg_ref in enumerate((send_ref, keep_ref)):
        base = lax.rem(core + 1 + turn, 2) * half_blocks

        def body(step, sums, base=base, msg_ref=msg_ref):
            start = base + step * inner
            cut = pl.ds(pl.multiple_of(start * LANES, LANES), wide)
            gated, dgate = gated_ref[:, cut], dgate_ref[:, cut]
            turned = mxu(flip, dgate).astype(BF16)
            turned_ref[:, cut] = turned
            skip = jnp.sum(gated.astype(F32) * dgate.astype(F32), axis=0, keepdims=True)
            for j in range(inner):
                skip_ref[pl.ds(start + j, 1), :] = skip[:, j * LANES : (j + 1) * LANES]

            moved = pltpu.roll(pieces, groups - start * per_block, 1).astype(BF16)
            spreads = mxu(moved, spread)
            rates = jnp.exp(join(spreads[: 3 * poles], poles))
            res_lag = join(spreads[3 * poles :, :lag_wide], poles)
            lag_rate, rate = rates[:, :lag_wide], rates[:, lag_wide:]
            table = jnp.exp(-lag_rate * lag)
            moment_table = table * lag
            tables = jnp.concatenate([table, moment_table], axis=0).astype(BF16)
            taps = jnp.sum(res_lag * table, axis=0, keepdims=True)
            for j in range(inner):
                lanes = slice(j * lag_width, (j + 1) * lag_width)
                rates_ref[start + j] = rate[:, j * LANES : (j + 1) * LANES]
                taps_ref[pl.ds(start + j, 1), :] = taps[:, lanes]
                tables_ref[start + j] = tables[:poles, lanes]

            found = [[] for _ in range(subs)]
            outers = []
            for j in range(inner):
                lanes = slice(j * LANES, (j + 1) * LANES)
                mine = tables[:, j * lag_width : (j + 1) * lag_width]
                outer = None
                for k in range(subs):
                    part = jnp.concatenate(
                        [gated[k * SUB : (k + 1) * SUB, lanes], turned[k * SUB : (k + 1) * SUB, lanes]], axis=1
                    )
                    stack = jnp.concatenate(
                        [jnp.where(wide_group == g, part, jnp.zeros_like(part)) for g in range(per_block)], axis=0
                    )
                    found[k].append(mxu(mine, stack))
                    mate = turned[(subs - 1 - k) * SUB : (subs - k) * SUB, lanes]
                    term = mxu_t(mate, stack[:, :LANES])
                    outer = term if outer is None else outer + term
                outers.append(outer)
            outer = jnp.where(causal, jnp.concatenate(outers, axis=1), 0.0)
            outer = pltpu.roll(outer, 0, 1, stride=1, stride_axis=0)
            lags = jnp.sum(outer, axis=0, keepdims=True)

            ahead = [jnp.concatenate([f[:, :LANES] for f in found[k]], axis=1) for k in range(subs)]
            behind = [jnp.concatenate([f[:, LANES:] for f in found[k]], axis=1) for k in range(subs)]
            once = jnp.exp(-rate)
            decay = jnp.exp(-rate * SUB)
            state = jnp.zeros((poles, wide), F32)
            moment, back, back_moment, cross_res, cross_mom = state, state, state, state, state
            for k in range(subs):
                other = behind[subs - 1 - k]
                cross_res = cross_res + other[:poles] * state
                cross_mom = cross_mom + other[poles:] * state + other[:poles] * (moment + state)
                moment = decay * (moment + SUB * state) + ahead[k][poles:]
                state = decay * state + ahead[k][:poles]
                back_moment = decay * (back_moment + SUB * back) + behind[k][poles:]
                back = decay * back + behind[k][:poles]
            out = jnp.concatenate([state, back, moment, back_moment], axis=0).astype(BF16)
            for j in range(inner):
                row = pl.multiple_of((step * inner + j) * 4 * poles, 4 * poles)
                msg_ref[pl.ds(row, 4 * poles), :] = out[:, j * LANES : (j + 1) * LANES]
            near = jnp.concatenate([lags * table, lags * moment_table], axis=0)
            far = jnp.concatenate([once * cross_res, once * cross_mom], axis=0)
            terms = split(jnp.concatenate([near, far], axis=1), 2)
            return sums + pltpu.roll(join(mxu_t(terms, spread), 2 * poles), start * per_block, 1)

        sums = lax.fori_loop(0, half_blocks // inner, body, sums)
    tail = half_blocks * 4 * poles
    for turn, msg_ref in enumerate((send_ref, keep_ref)):
        half = lax.rem(core + 1 + turn, 2)
        msg_ref[tail : tail + 2 * poles, :] = pack_half(sums, half)
        skip = skip_ref[pl.ds(pl.multiple_of(half * half_blocks, 8), half_blocks), :]
        msg_ref[tail + 2 * poles :, :] = split(skip, 2)


def conv_kernel(rows_ref, skip_ref, rates_ref, taps_ref, tables_ref, gated_ref, turned_ref, conv_ref,
                *, group, poles, inner):
    tokens, _ = gated_ref.shape
    per_block = LANES // group
    blocks, _, _ = rates_ref.shape
    subs = tokens // SUB
    lag_width = per_block * SUB
    first = lax.axis_index("ch") * blocks
    lead = (1 + iota((SUB, LANES), 0)).astype(F32)
    wide_group = over(within(iota((SUB, 2 * LANES), 1), LANES), group)
    state_group = over(within(iota((poles, 2 * LANES), 1), LANES), group)
    causal = iota((SUB, lag_width), 0) >= within(iota((SUB, lag_width), 1), SUB)

    def body(step, carry):
        start = step * inner
        lefts, lead_tables, decays, pairs, gains = [], [], [], [], []
        for j in range(inner):
            here = start + j
            taps = jnp.broadcast_to(taps_ref[pl.ds(here, 1), :], (SUB, lag_width))
            taps = pltpu.roll(taps, lag_width - SUB + 1, 1, stride=1, stride_axis=0)
            taps = jnp.where(causal, taps, 0.0).astype(BF16)
            lefts.append(jnp.concatenate([taps, tables_ref[here]], axis=0))
            rate = rows_ref[0, pl.ds(here, 1), :]
            res = rows_ref[1, pl.ds(here, 1), :]
            lead_tables.append((res * jnp.exp(-rate * lead)).astype(BF16))
            decay = jnp.exp(-rates_ref[here] * SUB)
            decays.append(jnp.concatenate([decay, decay], axis=1))
            cut = pl.ds(pl.multiple_of(here * LANES, LANES), LANES)
            pairs.append(jnp.concatenate([gated_ref[:, cut], turned_ref[:, cut]], axis=1))
            gain = skip_ref[pl.ds(first + here, 1), :]
            gains.append(jnp.concatenate([gain, gain], axis=1))
        states = [jnp.zeros((poles, 2 * LANES), F32)] * inner
        totals = [[] for _ in range(inner)]
        for k in range(subs):
            rows = slice(k * SUB, (k + 1) * SUB)
            found = []
            for j in range(inner):
                part = pairs[j][rows]
                stack = [jnp.where(wide_group == g, part, jnp.zeros_like(part)) for g in range(per_block)]
                found.append(mxu(lefts[j], jnp.concatenate(stack, axis=0)))
            for j in range(inner):
                total = found[j][:SUB] + gains[j] * pairs[j][rows].astype(F32)
                if k:
                    held = states[j].astype(BF16)
                    stack = [jnp.where(state_group == g, held, jnp.zeros_like(held)) for g in range(per_block)]
                    total = total + mxu(lead_tables[j], jnp.concatenate(stack, axis=0))
                totals[j].append(total)
            states = [decays[j] * states[j] + found[j][SUB:] for j in range(inner)]
        for j in range(inner):
            cut = pl.ds(pl.multiple_of(2 * (start + j) * LANES, LANES), 2 * LANES)
            conv_ref[:, cut] = jnp.concatenate(totals[j], axis=0)
        return carry

    lax.fori_loop(0, blocks // inner, body, 0)


def combine_kernel(*refs, level, levels, group, poles, tokens):
    last = level == levels - 1
    refs = list(refs)
    rates_ref, own_ref, got_ref = refs[:3]
    rest = refs[3:]
    near_ref = held_ref = slim_ref = None
    if level == 0:
        out_ref, near_ref = rest[:2]
        rest = rest[2:]
    else:
        if level > 1:
            held_ref = rest.pop(0)
        else:
            rest.pop(0)
        if last:
            near_ref, logs_ref, res_ref = rest[:3]
            mine_ref, out_ref = rest[3:]
        else:
            out_ref, new_held_ref = rest[:2]
            rest = rest[2:]
    if level == levels - 2:
        slim_ref = rest[0]
    all_blocks = rates_ref.shape[0]
    blocks = all_blocks // 2
    per_block = LANES // group
    groups = all_blocks * per_block
    me = lax.axis_index("ctx")
    core = lax.rem(me, 2)
    is_right = lax.rem(lax.shift_right_logical(me, level), 2) == 1
    before = lax.rem(me, 2**level) - (core if level else 0)
    gap_left = (tokens * before).astype(F32)
    gap_right = (tokens * (2**level - 2 - before)).astype(F32)
    gap = jnp.where(is_right, gap_left, gap_right)
    span = float(tokens * 2**level)
    next_right = lax.rem(lax.shift_right_logical(me, level + 1), 2) == 1
    own_rows = 4 * poles
    got_rows = 2 * poles if last else 4 * poles
    slim_rows = 2 * poles

    def thirds(value):
        return [value[n * poles : (n + 1) * poles] for n in range(4)]

    wide_terms = []
    for b in range(blocks):
        rate = rates_ref[core * blocks + b]
        own_f, own_b, own_fm, own_bm = thirds(own_ref[b * own_rows : (b + 1) * own_rows].astype(F32))
        got = got_ref[b * got_rows : (b + 1) * got_rows].astype(F32)
        if last:
            got_f = got_b = got[:poles]
            got_fm = got_bm = got[poles:]
        else:
            got_f, got_b, got_fm, got_bm = thirds(got)
        left_f = jnp.where(is_right, got_f, own_f)
        left_fm = jnp.where(is_right, got_fm, own_fm)
        right_b = jnp.where(is_right, own_b, got_b)
        right_bm = jnp.where(is_right, own_bm, got_bm)
        once = jnp.exp(-rate)
        cross_res = once * (right_b * left_f)
        cross_mom = once * (right_bm * left_f + right_b * (left_fm + left_f))
        wide_terms.append(split(jnp.concatenate([cross_res, cross_mom], axis=0), 2))
        if level == 0:
            near_ref[b] = jnp.concatenate([left_f, right_b], axis=0)
        else:
            carry = jnp.exp(-rate * gap) * jnp.where(is_right, left_f, right_b)
            zero = jnp.zeros_like(carry)
            hold = jnp.concatenate([jnp.where(is_right, carry, zero), jnp.where(is_right, zero, carry)], axis=0)
            if level > 1:
                hold = hold + held_ref[b]
            if last:
                step = jnp.exp(-rate * tokens)
                near = near_ref[b]
                first_core = jnp.concatenate([hold[:poles], near[poles:] + step * hold[poles:]], axis=0)
                second_core = jnp.concatenate([near[:poles] + step * hold[:poles], hold[poles:]], axis=0)
                mine_ref[b] = jnp.where(core > 0, second_core, first_core).astype(BF16)
                out_ref[b * 2 * poles : (b + 1) * 2 * poles, :] = jnp.where(
                    core > 0, first_core, second_core
                ).astype(BF16)
            else:
                new_held_ref[b] = hold
        if not last:
            right_f = jnp.where(is_right, own_f, got_f)
            right_fm = jnp.where(is_right, own_fm, got_fm)
            left_b = jnp.where(is_right, got_b, own_b)
            left_bm = jnp.where(is_right, got_bm, own_bm)
            decay = jnp.exp(-rate * span)
            new = [
                decay * left_f + right_f,
                left_b + decay * right_b,
                decay * (left_fm + span * left_f) + right_fm,
                left_bm + decay * (right_bm + span * right_b),
            ]
            out_ref[b * own_rows : (b + 1) * own_rows, :] = jnp.concatenate(new, axis=0).astype(BF16)
            if slim_ref is not None:
                chosen = jnp.concatenate(
                    [jnp.where(next_right, new[1], new[0]), jnp.where(next_right, new[3], new[2])], axis=0
                )
                slim_ref[b * slim_rows : (b + 1) * slim_rows, :] = chosen.astype(BF16)
    own_tail, got_tail = blocks * own_rows, blocks * got_rows
    cross = mxu_t(jnp.concatenate(wide_terms, axis=1), members(groups, 0, group, blocks * LANES))
    total = (
        join(cross, 2 * poles)
        + open_half(own_ref[own_tail : own_tail + 2 * poles, :])
        + open_half(got_ref[got_tail : got_tail + 2 * poles, :])
    )
    skip = join(own_ref[own_tail + 2 * poles :, :], blocks) + join(got_ref[got_tail + 2 * poles :, :], blocks)
    if last:
        start = shard_start(groups)
        rate = jnp.exp(logs_ref[:, pl.ds(start, groups)])
        factor = -rate * res_ref[:, pl.ds(start, groups)]
        factor = jnp.where(core > 0, pltpu.roll(factor, LANES // 2, 1), factor)
        length = 2 * span
        total = jnp.concatenate(
            [total[:poles] / length, factor * total[poles:] / math.sqrt(length)], axis=0
        )
        skip = skip / math.sqrt(length)
    rests = jnp.concatenate([pack_half(total, 0), split(skip, 2)], axis=0)
    if last:
        out_ref[blocks * 2 * poles :, :] = rests
    else:
        out_ref[own_tail:, :] = rests
        if slim_ref is not None:
            slim_ref[blocks * slim_rows :, :] = rests


def merge_kernel(own_ref, got_ref, out_ref, *, poles):
    core = lax.rem(lax.axis_index("ctx"), 2)
    blocks = (out_ref.shape[0] - 2 * poles) // 2
    rows = own_ref.shape[0] - 2 * poles - 2 * blocks
    own, got = open_half(own_ref[rows : rows + 2 * poles, :]), open_half(got_ref[rows : rows + 2 * poles, :])
    left, right = jnp.where(core > 0, got, own), jnp.where(core > 0, own, got)
    out_ref[: 2 * poles, :] = jnp.where(iota(own.shape, 1) < LANES // 2, left, pltpu.roll(right, LANES // 2, 1))
    own, got = join(own_ref[rows + 2 * poles :, :], blocks), join(got_ref[rows + 2 * poles :, :], blocks)
    out_ref[2 * poles : 2 * poles + blocks, :] = jnp.where(core > 0, got, own)
    out_ref[2 * poles + blocks :, :] = jnp.where(core > 0, own, got)


def output_kernel(rows_ref, conv_ref, mine_ref, got_ref, k_ref, v_ref, c_ref, gq_ref, gk_ref, gv_ref,
                  *, group, poles):
    tokens, width = gq_ref.shape
    per_block = LANES // group
    step = pl.program_id(0)
    inner = width // LANES
    half_blocks = mine_ref.shape[0]
    core = lax.rem(lax.axis_index("ctx"), 2)
    flip = reversal(tokens)
    ahead = (1 + iota((tokens, LANES), 0)).astype(F32)
    state_group = over(within(iota((poles, 2 * LANES), 1), LANES), group)
    start = step * inner
    is_mine = over(start, half_blocks) == core
    totals = []
    for j in range(inner):
        here = start + j
        rate = rows_ref[0, pl.ds(here, 1), :]
        res = rows_ref[1, pl.ds(here, 1), :]
        table = (res * jnp.exp(-rate * ahead)).astype(BF16)
        place = within(here, half_blocks)
        held = jnp.where(
            is_mine, mine_ref[place], got_ref[pl.ds(pl.multiple_of(place * 2 * poles, 2 * poles), 2 * poles), :]
        )
        states = jnp.concatenate([held[:poles], held[poles:]], axis=1)
        stack = jnp.concatenate(
            [jnp.where(state_group == g, states, jnp.zeros_like(states)) for g in range(per_block)], axis=0
        )
        both = pl.ds(pl.multiple_of(2 * here * LANES, LANES), 2 * LANES)
        totals.append((conv_ref[:, both] + mxu(table, stack)).astype(BF16))
    hidden = jnp.concatenate([t[:, :LANES] for t in totals], axis=1)
    flow = mxu(flip, jnp.concatenate([t[:, LANES:] for t in totals], axis=1))
    cut = pl.ds(pl.multiple_of(start * LANES, LANES), width)
    gq_ref[...] = (c_ref[:, cut].astype(F32) * hidden.astype(F32)).astype(BF16)
    gk_ref[...] = (flow * v_ref[:, cut].astype(F32)).astype(BF16)
    gv_ref[...] = (flow * k_ref[:, cut].astype(F32)).astype(BF16)


def assemble_kernel(*refs, shards, poles):
    slots = refs[:shards]
    res_ref, log_ref, skip_ref = refs[shards:]
    me = lax.axis_index("ch")
    groups = slots[0].shape[1]
    rows = slots[0].shape[0] - 2 * poles
    for shift, slot in enumerate(slots):
        source = lax.rem(me - shift + shards, shards)
        cut = pl.ds(pl.multiple_of(source * groups, LANES), groups)
        res_ref[:, cut] = slot[:poles, :]
        log_ref[:, cut] = slot[poles : 2 * poles, :]
        skip_ref[pl.ds(pl.multiple_of(source * rows, 8), rows), :] = slot[2 * poles :, :]


def local(queries, key_input, value_input, cotangent, residues, log_rates, skip_gain):
    tokens, width = queries.shape
    parts = lax.axis_size("ctx")
    shards = lax.axis_size("ch")
    levels = parts.bit_length() - 1
    all_groups, poles = residues.shape
    groups = all_groups // shards
    group = width // groups
    blocks = width // LANES
    inner = 4
    steps = blocks // inner
    half_blocks = blocks // 2
    lag_width = LANES // group * SUB
    sizes = dict(group=group, poles=poles)
    tail = 2 * poles + blocks
    full_rows, slim_rows = half_blocks * 4 * poles + tail, half_blocks * 2 * poles + tail

    vmem = pl.BlockSpec(memory_space=pltpu.VMEM)
    anywhere = pl.BlockSpec(memory_space=pl.ANY)
    log_rates, residues = log_rates.T, residues.T
    main = pl.BlockSpec((tokens, inner * LANES), lambda i: (0, i))

    def shape(*dims, dtype=F32):
        return jax.ShapeDtypeStruct(dims, dtype)

    def swap(value, level):
        return lax.ppermute(value, "ctx", [(i, i ^ (1 << level)) for i in range(parts)])

    gated, dgate = gate(key_input, value_input), gate(cotangent, queries)
    outgoing, message, turned, rows, rates, taps, tables = pl.pallas_call(
        lambda *refs: states_kernel(*refs, inner=inner, **sizes),
        in_specs=[vmem] * 4,
        out_specs=[vmem] * 7,
        out_shape=[
            shape(full_rows, LANES, dtype=BF16),
            shape(full_rows, LANES, dtype=BF16),
            shape(tokens, width, dtype=BF16),
            shape(2, blocks, LANES),
            shape(blocks, poles, LANES),
            shape(blocks, lag_width),
            shape(blocks, poles, lag_width, dtype=BF16),
        ],
        scratch_shapes=[pltpu.VMEM((blocks, LANES), F32)],
        compiler_params=PARAMS,
        name="states",
    )(log_rates, residues, gated, dgate)

    skip_rows = skip_gain.reshape(-1, LANES)
    conv = pl.pallas_call(
        lambda *refs: conv_kernel(*refs, inner=inner, **sizes),
        in_specs=[vmem] * 7,
        out_specs=vmem,
        out_shape=shape(tokens, 2 * width),
        compiler_params=PARAMS,
        cost_estimate=pl.CostEstimate(
            flops=16 * tokens * tokens * width, bytes_accessed=12 * tokens * width, transcendentals=tokens * width
        ),
        name="conv",
    )(rows, skip_rows, rates, taps, tables, gated, turned)

    held = near = None
    for level in range(levels):
        last = level == levels - 1
        got = swap(outgoing, level)
        operands, specs = [rates, message, got], [vmem] * 3
        if level == 1:
            operands.append(conv)
            specs.append(anywhere)
        elif level > 1:
            operands.append(held)
            specs.append(vmem)
        if last:
            operands += [near, log_rates, residues]
            specs += [vmem] * 3
            outs = [shape(half_blocks, 2 * poles, LANES, dtype=BF16), shape(slim_rows, LANES, dtype=BF16)]
        else:
            outs = [shape(full_rows, LANES, dtype=BF16), shape(half_blocks, 2 * poles, LANES)]
        if level == levels - 2:
            outs.append(shape(slim_rows, LANES, dtype=BF16))
        results = pl.pallas_call(
            lambda *refs, level=level: combine_kernel(*refs, level=level, levels=levels, tokens=tokens, **sizes),
            in_specs=specs,
            out_specs=[vmem] * len(outs),
            out_shape=outs,
            compiler_params=PARAMS,
            name="combine",
        )(*operands)
        if last:
            mine, outgoing = results
        else:
            message = results[0]
            outgoing = results[-1] if level == levels - 2 else message
            if level == 0:
                near = results[1]
            else:
                held = results[1]
    got = swap(outgoing, 0)
    merged = pl.pallas_call(
        lambda *refs: merge_kernel(*refs, poles=poles),
        in_specs=[vmem] * 2,
        out_specs=vmem,
        out_shape=shape(2 * poles + blocks, LANES),
        compiler_params=PARAMS,
        name="merge",
    )(outgoing, got)

    gathered = [merged]
    for shift in range(1, shards):
        gathered.append(lax.ppermute(merged, "ch", [(i, (i + shift) % shards) for i in range(shards)]))

    grad_query, grad_key, grad_value = pl.pallas_call(
        lambda *refs: output_kernel(*refs, **sizes),
        grid=(steps,),
        in_specs=[vmem] * 7,
        out_specs=[main, main, main],
        out_shape=[jax.ShapeDtypeStruct((tokens, width), BF16)] * 3,
        compiler_params=PARAMS,
        name="outputs",
    )(rows, conv, mine, got, key_input, value_input, cotangent)

    grad_residue, grad_lograte, grad_skip = pl.pallas_call(
        lambda *refs: assemble_kernel(*refs, shards=shards, poles=poles),
        in_specs=[vmem] * shards,
        out_specs=[vmem] * 3,
        out_shape=[
            jax.ShapeDtypeStruct((poles, all_groups), F32),
            jax.ShapeDtypeStruct((poles, all_groups), F32),
            jax.ShapeDtypeStruct((shards * blocks, LANES), F32),
        ],
        compiler_params=PARAMS,
        name="assemble",
    )(*gathered)
    return (grad_query, grad_key, grad_value, grad_residue.T, grad_lograte.T, grad_skip.reshape(-1))


def solution(mesh):
    placed = (P("ctx", "ch"), P("ctx", "ch"), P("ctx", "ch"), P("ctx", "ch"), P(), P(), P())
    return jax.shard_map(
        local,
        mesh=mesh,
        in_specs=placed,
        out_specs=(P("ctx", "ch"), P("ctx", "ch"), P("ctx", "ch"), P(), P(), P()),
        check_vma=False,
    )
```

time: 41.1 us -> 34.4 us (0.84)
  Pallas kernels: 19.3 us -> 13.5 us
  starting transfers between devices: 10.7 us -> 10 us
    pallas_call x2 -> x3, Pallas kernels: 13.4 us -> 9.22 us  [the longest x1 6.27 us: local(): pl.pallas_call(lambda *refs: states_kernel(*refs, inner=inner, **sizes),...]
    pallas_call x1, Pallas kernels: 4.02 us -> 2.6 us  [local(): pl.pallas_call(lambda *refs: output_kernel(*refs, **sizes), grid=(steps,)...]
    ppermute x6 -> x7, starting transfers between devices: 10.7 us -> 10 us  [the longest x4 5.14 us: swap(): lax.ppermute(value, 'ctx', [(i, i ^ 1 << level) for i in range(parts)])]
    ppermute x6 -> x7, waiting for transfers between devices: 8.22 us -> 8.11 us  [the longest x4 6.11 us: swap(): lax.ppermute(value, 'ctx', [(i, i ^ 1 << level) for i in range(parts)])]
  transfers between devices with their start and end apart: 6 -> 7, of which waited for: 3 -> 6; matrix products, arithmetic and copies ran while one was open for 0% -> 0% of each run, Pallas kernels for 19% -> 16%
where the time goes in v4:
time: 34.4 us; the launch traced here: 34.2 us
  Pallas kernels  13.5 us (39%)
  starting transfers between devices  10 us (29%)
  waiting for transfers between devices  8.11 us (24%)
  other arithmetic  1.88 us (5%)
  between operations  0.73 us (2%)
    pallas_call x1, Pallas kernels, local(): pl.pallas_call(lambda *refs: states_kernel(*refs, inner=inner, **sizes),...  6.27 us
    ppermute x4, waiting for transfers between devices, swap(): lax.ppermute(value, 'ctx', [(i, i ^ 1 << level) for i in range(parts)])  6.11 us
    ppermute x4, starting transfers between devices, swap(): lax.ppermute(value, 'ctx', [(i, i ^ 1 << level) for i in range(parts)])  5.14 us
    ppermute x3, starting transfers between devices, local(): lax.ppermute(merged, 'ch', [(i, (i + shift) % shards) for i in range(shar...  4.86 us
    pallas_call x1, Pallas kernels, local(): pl.pallas_call(lambda *refs: conv_kernel(*refs, inner=inner, **sizes), in...  2.8 us
    pallas_call x1, Pallas kernels, local(): pl.pallas_call(lambda *refs: output_kernel(*refs, **sizes), grid=(steps,)...  2.6 us
    ppermute x3, waiting for transfers between devices, local(): lax.ppermute(merged, 'ch', [(i, (i + shift) % shards) for i in range(shar...  2 us
    convert_element_type x1, other arithmetic, gate(): return (left.astype(F32) * right.astype(F32)).astype(BF16)  1.88 us
  transfers between devices with their start and end apart: 7, of which 6 were waited for; matrix products, arithmetic and copies ran while one was open for 0% of the time, Pallas kernels for 16%

profile of v4, /device:TPU:0, one launch (start us, length us, event | category | flops | bytes accessed | tf_op | source)
XLA Modules:
  0.0 34.2 jit_solution(14428840864543737309)
XLA Ops:
  0.6 0.0 copy-start.3
  0.6 0.0 copy-start.4
  0.7 0.0 copy-start.5
  0.7 1.9 %multiply_convert_fusion = (bf16[128,2048]{1,0:T(8,128)(2,1)S(1)}, bf16[128,2048]{1,0:T(8,128)(2,1)S(1)}) fusion(bf16[128,2048]{1,0:T(8,128)(2,1)} %param.7, bf16[128,2048]{1,0:T(8,128)(2,1)} %refs_6_.1, bf16[128,2048]{1,0:T(8,128)(2,1)} %refs_5_.1, bf16[128,2048]{1,0:T(8,128)(2,1)} %refs_4_.1), kind=kLoop, calls=%fused_computation | loop fusion | flops 2097152 | bytes 3145728 | tf_op jit(solution)/shard_map/convert_element_type | solution.py:44
  2.6 0.0 copy-done.3
  2.6 0.0 copy-done.4
  2.6 6.3 %states.1 = (bf16[560,128]{1,0:T(8,128)(2,1)S(1)}, bf16[560,128]{1,0:T(8,128)(2,1)S(1)}, bf16[128,2048]{1,0:T(8,128)(2,1)S(1)}, f32[2,16,128]{2,1,0:T(8,128)S(1)...) custom-call(f32[16,512]{1,0:T(8,128)S(1)} %bitcast.6, ...), custom_call_target="tpu_custom_call" | custom-call | tf_op jit(solution)/shard_map/states/pallas_call | solution.py:478
  8.8 0.5 %collective-permute-start = (bf16[560,128]{1,0:T(8,128)(2,1)S(1)}, bf16[560,128]{1,0:T(8,128)(2,1)S(1)}, u32[]{:S(2)}, u32[]{:S(2)}) collective-permute-start(bf16[560,128]{1,0:T(8,128)(2,1)S(1)} %get-tuple-element.32), channel_id=1, source_target_pairs={{0,4},{4,0},{8,12},{12,8},{16,20},{20,16},{24,28},{28,24},{1,5},{5... | collective-permute-start | bytes 430088 | tf_op jit(solution)/shard_map/ppermute | solution.py:475
  9.3 1.0 %collective-permute-done.refs_2_ = bf16[560,128]{1,0:T(8,128)(2,1)S(1)} collective-permute-done((bf16[560,128]{1,0:T(8,128)(2,1)S(1)}, bf16[560,128]{1,0:T(8,128)(2,1)S(1)}, u32[]{:S(2)}, u32[]{:S(2)}) %collective-permute-start) | collective-permute-done | bytes 143392 | tf_op jit(solution)/shard_map/ppermute | solution.py:475
  10.3 0.3 combine.3
  10.7 2.9 %collective-permute-start.1 = (bf16[560,128]{1,0:T(8,128)(2,1)S(1)}, bf16[560,128]{1,0:T(8,128)(2,1)S(1)}, u32[]{:S(2)}, u32[]{:S(2)}) collective-permute-start(bf16[560,128]{1,0:T(8,128)(2,1)S(1)} %get-tuple-element.33.refs_1_), channel_id=1, source_target_pairs={{0,8},{4,12},{8,0},{12,4},{16,24},{20,28},{24,16},{28,20},{1,9},{5... | collective-permute-start | bytes 430088 | tf_op jit(solution)/shard_map/ppermute | solution.py:475
  13.5 0.0 copy-done.5
  13.5 2.8 %conv.1.refs_3_.refs_1_ = f32[128,4096]{1,0:T(8,128)S(1)} custom-call(f32[2,16,128]{2,1,0:T(8,128)S(1)} %get-tuple-element.26.refs_0_, f32[64,128]{1,0:T(8,128)S(1)} %bitcast.10, f32[16,16,128]{2,1,0:T(8,128)S(1)} %get-tuple-element.27.refs_2_.refs_0_, f32[16,256]{1,0:T(8,128)S(1)} %get-tuple-element.28.refs_3_, ...), custom_call_target="tpu_custom_call" | custom-call | flops 536870912 | bytes 3145728 | tf_op jit(solution)/shard_map/conv/pallas_call | solution.py:497
  16.3 0.0 copy-start
  16.4 0.0 copy-start.1
  16.4 0.0 copy-start.2
  16.4 1.2 %collective-permute-done.1.refs_2_ = bf16[560,128]{1,0:T(8,128)(2,1)S(1)} collective-permute-done((bf16[560,128]{1,0:T(8,128)(2,1)S(1)}, bf16[560,128]{1,0:T(8,128)(2,1)S(1)}, u32[]{:S(2)}, u32[]{:S(2)}) %collective-permute-start.1) | collective-permute-done | bytes 143392 | tf_op jit(solution)/shard_map/ppermute | solution.py:475
  17.6 0.3 combine.4
  17.9 1.8 %collective-permute-start.2 = (bf16[304,128]{1,0:T(8,128)(2,1)S(1)}, bf16[304,128]{1,0:T(8,128)(2,1)S(1)}, u32[]{:S(2)}, u32[]{:S(2)}) collective-permute-start(bf16[304,128]{1,0:T(8,128)(2,1)S(1)} %get-tuple-element.35), channel_id=1, source_target_pairs={{0,16},{4,20},{8,24},{12,28},{16,0},{20,4},{24,8},{28,12},{1,17},{... | collective-permute-start | bytes 233480 | tf_op jit(solution)/shard_map/ppermute | solution.py:475
  19.7 2.6 %collective-permute-done.2.refs_2_ = bf16[304,128]{1,0:T(8,128)(2,1)S(1)} collective-permute-done((bf16[304,128]{1,0:T(8,128)(2,1)S(1)}, bf16[304,128]{1,0:T(8,128)(2,1)S(1)}, u32[]{:S(2)}, u32[]{:S(2)}) %collective-permute-start.2) | collective-permute-done | bytes 77856 | tf_op jit(solution)/shard_map/ppermute | solution.py:475
  22.3 0.3 combine.5
  22.7 0.0 collective-permute-start.3
  22.7 1.3 %collective-permute-done.3.refs_3_.refs_1_ = bf16[304,128]{1,0:T(8,128)(2,1)S(1)} collective-permute-done((bf16[304,128]{1,0:T(8,128)(2,1)S(1)}, bf16[304,128]{1,0:T(8,128)(2,1)S(1)}, u32[]{:S(2)}, u32[]{:S(2)}) %collective-permute-start.3) | collective-permute-done | bytes 77856 | tf_op jit(solution)/shard_map/ppermute | solution.py:475
  23.9 0.1 merge.1.refs_0_
  24.1 3.8 %collective-permute-start.6 = (f32[48,128]{1,0:T(8,128)S(1)}, f32[48,128]{1,0:T(8,128)S(1)}, u32[]{:S(2)}, u32[]{:S(2)}) collective-permute-start(f32[48,128]{1,0:T(8,128)S(1)} %merge.1.refs_0_), channel_id=1, source_target_pairs={{0,3},{1,0},{2,1},{3,2},{4,7},{5,4},{6,5},{7,6},{8,11},{9,8},{10,9... | collective-permute-start | bytes 73736 | tf_op jit(solution)/shard_map/ppermute | solution.py:557
  27.9 0.0 collective-permute-start.5
  27.9 1.0 %collective-permute-start.4 = (f32[48,128]{1,0:T(8,128)S(1)}, f32[48,128]{1,0:T(8,128)S(1)}, u32[]{:S(2)}, u32[]{:S(2)}) collective-permute-start(f32[48,128]{1,0:T(8,128)S(1)} %merge.1.refs_0_), channel_id=1, source_target_pairs={{0,1},{1,2},{2,3},{3,0},{4,5},{5,6},{6,7},{7,4},{8,9},{9,10},{10,1... | collective-permute-start | bytes 73736 | tf_op jit(solution)/shard_map/ppermute | solution.py:557
  29.0 0.0 copy-done
  29.0 0.0 copy-done.1
  29.0 0.0 copy-done.2
  29.0 2.6 %outputs.1 = (bf16[128,2048]{1,0:T(8,128)(2,1)}, bf16[128,2048]{1,0:T(8,128)(2,1)}, bf16[128,2048]{1,0:T(8,128)(2,1)}) custom-call(f32[2,16,128]{2,1,0:T(8,128)S(1)} %get-tuple-element.26.refs_0_, f32[128,4096]{1,0:T(8,128)S(1)} %conv.1.refs_3_.refs_1_, bf16[8,32,128]{2,1,0:T(8,128)(2,1)S(1)} %get-tuple-element.38.refs_2_, ...), custom_call_target="tpu_custom_call" | custom-call | tf_op jit(solution)/shard_map/outputs/pallas_call | solution.py:559
  31.6 0.0 collective-permute-done.6.refs_3_
  31.6 1.2 %collective-permute-done.5.refs_2_ = f32[48,128]{1,0:T(8,128)S(1)} collective-permute-done((f32[48,128]{1,0:T(8,128)S(1)}, f32[48,128]{1,0:T(8,128)S(1)}, u32[]{:S(2)}, u32[]{:S(2)}) %collective-permute-start.5) | collective-permute-done | bytes 24608 | tf_op jit(solution)/shard_map/ppermute | solution.py:557
  32.7 0.8 %collective-permute-done.4.refs_1_ = f32[48,128]{1,0:T(8,128)S(1)} collective-permute-done((f32[48,128]{1,0:T(8,128)S(1)}, f32[48,128]{1,0:T(8,128)S(1)}, u32[]{:S(2)}, u32[]{:S(2)}) %collective-permute-start.4) | collective-permute-done | bytes 24608 | tf_op jit(solution)/shard_map/ppermute | solution.py:557
  33.6 0.6 %assemble.1 = (f32[16,512]{1,0:T(8,128)}, f32[16,512]{1,0:T(8,128)}, f32[64,128]{1,0:T(8,128)}) custom-call(f32[48,128]{1,0:T(8,128)S(1)} %merge.1.refs_0_, f32[48,128]{1,0:T(8,128)S(1)} %collective-permute-done.4.refs_1_, f32[48,128]{1,0:T(8,128)S(1)} %collective-permute-done.5.refs_2_, f32[48,128]{1,0:T(8,128)S(1)} %collective-permute-done.6.refs_3_), custom_call_target="tpu_custom_call" | custom-call | tf_op jit(solution)/shard_map/assemble/pallas_call | solution.py:569
Async XLA Ops:
  0.6 1.9 %copy-start.3 = (f32[512,16]{0,1:T(8,128)S(1)}, f32[512,16]{0,1:T(8,128)}, u32[]{:S(2)}) copy-start(f32[512,16]{0,1:T(8,128)} %param.12) | copy-start | bytes 98308
  0.6 1.9 %copy-start.4 = (f32[512,16]{0,1:T(8,128)S(1)}, f32[512,16]{0,1:T(8,128)}, u32[]{:S(2)}) copy-start(f32[512,16]{0,1:T(8,128)} %param.11) | copy-start | bytes 98308
  0.7 12.9 %copy-start.5 = (f32[8192]{0:T(1024)S(1)}, f32[8192]{0:T(1024)}, u32[]{:S(2)}) copy-start(f32[8192]{0:T(1024)} %param.13) | copy-start | bytes 98308
  8.8 1.5 %collective-permute-start = (bf16[560,128]{1,0:T(8,128)(2,1)S(1)}, bf16[560,128]{1,0:T(8,128)(2,1)S(1)}, u32[]{:S(2)}, u32[]{:S(2)}) collective-permute-start(bf16[560,128]{1,0:T(8,128)(2,1)S(1)} %get-tuple-element.32), channel_id=1, source_target_pairs={{0,4},{4,0},{8,12},{12,8},{16,20},{20,16},{24,28},{28,24},{1,5},{5... | collective-permute-start | bytes 430088 | tf_op jit(solution)/shard_map/ppermute | solution.py:475
  10.7 6.9 %collective-permute-start.1 = (bf16[560,128]{1,0:T(8,128)(2,1)S(1)}, bf16[560,128]{1,0:T(8,128)(2,1)S(1)}, u32[]{:S(2)}, u32[]{:S(2)}) collective-permute-start(bf16[560,128]{1,0:T(8,128)(2,1)S(1)} %get-tuple-element.33.refs_1_), channel_id=1, source_target_pairs={{0,8},{4,12},{8,0},{12,4},{16,24},{20,28},{24,16},{28,20},{1,9},{5... | collective-permute-start | bytes 430088 | tf_op jit(solution)/shard_map/ppermute | solution.py:475
  16.3 12.6 %copy-start = (bf16[128,2048]{1,0:T(8,128)(2,1)S(1)}, bf16[128,2048]{1,0:T(8,128)(2,1)}, u32[]{:S(2)}) copy-start(bf16[128,2048]{1,0:T(8,128)(2,1)} %refs_6_.1) | copy-start | bytes 1572868
  16.4 12.6 %copy-start.1 = (bf16[128,2048]{1,0:T(8,128)(2,1)S(1)}, bf16[128,2048]{1,0:T(8,128)(2,1)}, u32[]{:S(2)}) copy-start(bf16[128,2048]{1,0:T(8,128)(2,1)} %refs_5_.1) | copy-start | bytes 1572868
  16.4 12.6 %copy-start.2 = (bf16[128,2048]{1,0:T(8,128)(2,1)S(1)}, bf16[128,2048]{1,0:T(8,128)(2,1)}, u32[]{:S(2)}) copy-start(bf16[128,2048]{1,0:T(8,128)(2,1)} %refs_4_.1) | copy-start | bytes 1572868
  17.9 4.4 %collective-permute-start.2 = (bf16[304,128]{1,0:T(8,128)(2,1)S(1)}, bf16[304,128]{1,0:T(8,128)(2,1)S(1)}, u32[]{:S(2)}, u32[]{:S(2)}) collective-permute-start(bf16[304,128]{1,0:T(8,128)(2,1)S(1)} %get-tuple-element.35), channel_id=1, source_target_pairs={{0,16},{4,20},{8,24},{12,28},{16,0},{20,4},{24,8},{28,12},{1,17},{... | collective-permute-start | bytes 233480 | tf_op jit(solution)/shard_map/ppermute | solution.py:475
  22.7 1.3 %collective-permute-start.3 = (bf16[304,128]{1,0:T(8,128)(2,1)S(1)}, bf16[304,128]{1,0:T(8,128)(2,1)S(1)}, u32[]{:S(2)}, u32[]{:S(2)}) collective-permute-start(bf16[304,128]{1,0:T(8,128)(2,1)S(1)} %get-tuple-element.39.refs_0_), channel_id=1, source_target_pairs={{0,4},{4,0},{8,12},{12,8},{16,20},{20,16},{24,28},{28,24},{1,5},{5... | collective-permute-start | bytes 233480 | tf_op jit(solution)/shard_map/ppermute | solution.py:475
  24.1 7.5 %collective-permute-start.6 = (f32[48,128]{1,0:T(8,128)S(1)}, f32[48,128]{1,0:T(8,128)S(1)}, u32[]{:S(2)}, u32[]{:S(2)}) collective-permute-start(f32[48,128]{1,0:T(8,128)S(1)} %merge.1.refs_0_), channel_id=1, source_target_pairs={{0,3},{1,0},{2,1},{3,2},{4,7},{5,4},{6,5},{7,6},{8,11},{9,8},{10,9... | collective-permute-start | bytes 73736 | tf_op jit(solution)/shard_map/ppermute | solution.py:557
  27.9 4.8 %collective-permute-start.5 = (f32[48,128]{1,0:T(8,128)S(1)}, f32[48,128]{1,0:T(8,128)S(1)}, u32[]{:S(2)}, u32[]{:S(2)}) collective-permute-start(f32[48,128]{1,0:T(8,128)S(1)} %merge.1.refs_0_), channel_id=1, source_target_pairs={{0,2},{1,3},{2,0},{3,1},{4,6},{5,7},{6,4},{7,5},{8,10},{9,11},{10,... | collective-permute-start | bytes 73736 | tf_op jit(solution)/shard_map/ppermute | solution.py:557
  27.9 5.6 %collective-permute-start.4 = (f32[48,128]{1,0:T(8,128)S(1)}, f32[48,128]{1,0:T(8,128)S(1)}, u32[]{:S(2)}, u32[]{:S(2)}) collective-permute-start(f32[48,128]{1,0:T(8,128)S(1)} %merge.1.refs_0_), channel_id=1, source_target_pairs={{0,1},{1,2},{2,3},{3,0},{4,5},{5,6},{6,7},{7,4},{8,9},{9,10},{10,1... | collective-permute-start | bytes 73736 | tf_op jit(solution)/shard_map/ppermute | solution.py:557

commit v5 on v4

--- a/solution.py
+++ b/solution.py
@@ -94,37 +94,34 @@
     return value + pltpu.roll(value, LANES // 2, 1)
 
 
-def states_kernel(logs_ref, res_ref, gated_ref, dgate_ref, send_ref, keep_ref, turned_ref, rows_ref, rates_ref,
-                  taps_ref, tables_ref, skip_ref, *, group, poles, inner):
+def states_kernel(logs_ref, res_ref, gated_ref, dgate_ref, send_ref, keep_ref, turned_ref, rows_ref,
+                  skip_ref, near_ref, *, group, poles, inner):
     tokens, _ = gated_ref.shape
     per_block = LANES // group
-    blocks, _, _ = rates_ref.shape
+    _, blocks, _ = rows_ref.shape
     half_blocks = blocks // 2
     groups = blocks * per_block
-    subs = tokens // SUB
-    lag_width = per_block * SUB
-    step_groups = inner * per_block
-    wide, lag_wide = inner * LANES, inner * lag_width
+    wide = inner * LANES
     core = lax.rem(lax.axis_index("ctx"), 2)
 
     first = shard_start(groups)
-    logs = logs_ref[:, pl.ds(first, groups)]
-    res = res_ref[:, pl.ds(first, groups)]
-    rows_ref[0] = jnp.exp(flat_rows(logs, poles))
-    rows_ref[1] = flat_rows(res, poles)
-    pieces = jnp.concatenate([split(logs, 3), split(res, 3)], axis=0).astype(F32)
-    spread = jnp.concatenate([members(groups, 0, SUB, lag_wide), members(groups, 0, group, wide)], axis=1)
+    rows_ref[0] = jnp.exp(flat_rows(logs_ref[:, pl.ds(first, groups)], poles))
+    rows_ref[1] = flat_rows(res_ref[:, pl.ds(first, groups)], poles)
 
     flip = reversal(tokens)
-    lag = (SUB - 1 - within(iota((poles, lag_wide), 1), SUB)).astype(F32)
-    wide_group = over(within(iota((SUB, 2 * LANES), 1), LANES), group)
-    causal = iota((SUB, lag_wide), 0) + within(iota((SUB, lag_wide), 1), SUB) <= SUB - 1
-
-    sums = jnp.zeros((2 * poles, groups), F32)
+    back_pos = (tokens - 1 - iota((tokens, LANES), 0)).astype(F32)
+    back_lane = (tokens - 1 - iota((per_block, tokens), 1)).astype(F32)
+    lane_group = over(iota((tokens, LANES), 1), group)
+    causal = iota((tokens, tokens), 0) + iota((tokens, tokens), 1) <= tokens - 1
+    wide_group = over(within(iota((poles, 2 * LANES), 1), LANES), group)
+    own_rows = iota((per_block, LANES), 0) == over(iota((per_block, LANES), 1), poles)
+    half = per_block // 2
+    zero = jnp.zeros((tokens, LANES), BF16)
+
     for turn, msg_ref in enumerate((send_ref, keep_ref)):
         base = lax.rem(core + 1 + turn, 2) * half_blocks
 
-        def body(step, sums, base=base, msg_ref=msg_ref):
+        def body(step, carry, base=base, msg_ref=msg_ref):
             start = base + step * inner
             cut = pl.ds(pl.multiple_of(start * LANES, LANES), wide)
             gated, dgate = gated_ref[:, cut], dgate_ref[:, cut]
@@ -133,74 +130,100 @@
             skip = jnp.sum(gated.astype(F32) * dgate.astype(F32), axis=0, keepdims=True)
             for j in range(inner):
                 skip_ref[pl.ds(start + j, 1), :] = skip[:, j * LANES : (j + 1) * LANES]
-
-            moved = pltpu.roll(pieces, groups - start * per_block, 1).astype(BF16)
-            spreads = mxu(moved, spread)
-            rates = jnp.exp(join(spreads[: 3 * poles], poles))
-            res_lag = join(spreads[3 * poles :, :lag_wide], poles)
-            lag_rate, rate = rates[:, :lag_wide], rates[:, lag_wide:]
-            table = jnp.exp(-lag_rate * lag)
-            moment_table = table * lag
-            tables = jnp.concatenate([table, moment_table], axis=0).astype(BF16)
-            taps = jnp.sum(res_lag * table, axis=0, keepdims=True)
+            lanes = [slice(j * LANES, (j + 1) * LANES) for j in range(inner)]
+            tables = [jnp.exp(-rows_ref[0, pl.ds(start + j, 1), :] * back_pos) for j in range(inner)]
+            lows = [table.astype(BF16) for table in tables]
+            found = []
             for j in range(inner):
-                lanes = slice(j * lag_width, (j + 1) * lag_width)
-                rates_ref[start + j] = rate[:, j * LANES : (j + 1) * LANES]
-                taps_ref[pl.ds(start + j, 1), :] = taps[:, lanes]
-                tables_ref[start + j] = tables[:poles, lanes]
-
-            found = [[] for _ in range(subs)]
+                table = tables[j].T
+                moment_table = table * back_lane[:1]
+                both = jnp.concatenate([table.astype(BF16), moment_table.astype(BF16)], axis=0)
+                pair = jnp.concatenate([gated[:, lanes[j]], turned[:, lanes[j]]], axis=1)
+                found.append(mxu(both, pair))
             outers = []
             for j in range(inner):
-                lanes = slice(j * LANES, (j + 1) * LANES)
-                mine = tables[:, j * lag_width : (j + 1) * lag_width]
-                outer = None
-                for k in range(subs):
-                    part = jnp.concatenate(
-                        [gated[k * SUB : (k + 1) * SUB, lanes], turned[k * SUB : (k + 1) * SUB, lanes]], axis=1
-                    )
-                    stack = jnp.concatenate(
-                        [jnp.where(wide_group == g, part, jnp.zeros_like(part)) for g in range(per_block)], axis=0
-                    )
-                    found[k].append(mxu(mine, stack))
-                    mate = turned[(subs - 1 - k) * SUB : (subs - k) * SUB, lanes]
-                    term = mxu_t(mate, stack[:, :LANES])
-                    outer = term if outer is None else outer + term
-                outers.append(outer)
-            outer = jnp.where(causal, jnp.concatenate(outers, axis=1), 0.0)
-            outer = pltpu.roll(outer, 0, 1, stride=1, stride_axis=0)
-            lags = jnp.sum(outer, axis=0, keepdims=True)
-
-            ahead = [jnp.concatenate([f[:, :LANES] for f in found[k]], axis=1) for k in range(subs)]
-            behind = [jnp.concatenate([f[:, LANES:] for f in found[k]], axis=1) for k in range(subs)]
-            once = jnp.exp(-rate)
-            decay = jnp.exp(-rate * SUB)
-            state = jnp.zeros((poles, wide), F32)
-            moment, back, back_moment, cross_res, cross_mom = state, state, state, state, state
-            for k in range(subs):
-                other = behind[subs - 1 - k]
-                cross_res = cross_res + other[:poles] * state
-                cross_mom = cross_mom + other[poles:] * state + other[:poles] * (moment + state)
-                moment = decay * (moment + SUB * state) + ahead[k][poles:]
-                state = decay * state + ahead[k][:poles]
-                back_moment = decay * (back_moment + SUB * back) + behind[k][poles:]
-                back = decay * back + behind[k][:poles]
-            out = jnp.concatenate([state, back, moment, back_moment], axis=0).astype(BF16)
+                one, other = gated[:, lanes[j]], turned[:, lanes[j]]
+                left = [
+                    jnp.where((lane_group == i) | (lane_group == i + half), other, zero) for i in range(half)
+                ]
+                right = [jnp.where(lane_group < half, one, zero), jnp.where(lane_group >= half, one, zero)]
+                outers.append(mxu_t(jnp.concatenate(left, axis=0), jnp.concatenate(right, axis=0)))
             for j in range(inner):
+                folded = []
+                for part in range(2):
+                    total = found[j][part * LANES : part * LANES + poles]
+                    for g in range(1, per_block):
+                        row = part * LANES + g * poles
+                        total = jnp.where(wide_group == g, found[j][row : row + poles], total)
+                    folded.append(total)
+                out = [folded[0][:, :LANES], folded[0][:, LANES:], folded[1][:, :LANES], folded[1][:, LANES:]]
                 row = pl.multiple_of((step * inner + j) * 4 * poles, 4 * poles)
-                msg_ref[pl.ds(row, 4 * poles), :] = out[:, j * LANES : (j + 1) * LANES]
-            near = jnp.concatenate([lags * table, lags * moment_table], axis=0)
-            far = jnp.concatenate([once * cross_res, once * cross_mom], axis=0)
-            terms = split(jnp.concatenate([near, far], axis=1), 2)
-            return sums + pltpu.roll(join(mxu_t(terms, spread), 2 * poles), start * per_block, 1)
-
-        sums = lax.fori_loop(0, half_blocks // inner, body, sums)
+                msg_ref[pl.ds(row, 4 * poles), :] = jnp.concatenate(out, axis=0).astype(BF16)
+            for j in range(inner):
+                totals = []
+                for g in range(per_block):
+                    i, h = g % half, g // half
+                    tile = outers[j][i * tokens : (i + 1) * tokens, h * tokens : (h + 1) * tokens]
+                    tile = jnp.where(causal, tile, 0.0)
+                    total = None
+                    for a in range(tokens // 8):
+                        shift = (8 * (a - g)) % tokens
+                        piece = tile[8 * a : 8 * a + 8]
+                        piece = pltpu.roll(piece, shift, 1) if shift else piece
+                        total = piece if total is None else total + piece
+                    totals.append(total)
+                total = pltpu.roll(jnp.concatenate(totals, axis=0), 0, 1, stride=1, stride_axis=0)
+                lag = jnp.sum(total.reshape(per_block, 8, tokens), axis=1)
+                stack = jnp.concatenate([split(lag, 2), split(lag * back_lane, 2)], axis=0)
+                local = mxu(stack, lows[j])
+                for n in range(2):
+                    part = join(local[2 * n * per_block : 2 * (n + 1) * per_block], per_block)
+                    row = jnp.sum(jnp.where(own_rows, part, 0.0), axis=0, keepdims=True)
+                    near_ref[n, pl.ds(start + j, 1), :] = row
+            return carry
+
+        lax.fori_loop(0, half_blocks // inner, body, 0)
+    pick = iota((poles, LANES), 0) == within(iota((poles, LANES), 1), poles)
+    terms = []
+    for b in range(blocks):
+        near = [jnp.where(pick, near_ref[n, b : b + 1, :], 0.0) for n in range(2)]
+        terms.append(split(jnp.concatenate(near, axis=0), 2))
+    sums = mxu_t(jnp.concatenate(terms, axis=1), members(groups, 0, poles, blocks * LANES))
+    sums = join(sums, 2 * poles)
     tail = half_blocks * 4 * poles
     for turn, msg_ref in enumerate((send_ref, keep_ref)):
         half = lax.rem(core + 1 + turn, 2)
         msg_ref[tail : tail + 2 * poles, :] = pack_half(sums, half)
         skip = skip_ref[pl.ds(pl.multiple_of(half * half_blocks, 8), half_blocks), :]
         msg_ref[tail + 2 * poles :, :] = split(skip, 2)
+
+
+def tables_kernel(logs_ref, res_ref, _, rates_ref, taps_ref, tables_ref, *, group, poles, inner):
+    blocks, _, lag_width = tables_ref.shape
+    per_block = LANES // group
+    groups = blocks * per_block
+    step_groups = inner * per_block
+    wide, lag_wide = inner * LANES, inner * lag_width
+    first = shard_start(groups)
+    logs = logs_ref[:, pl.ds(first, groups)]
+    res = res_ref[:, pl.ds(first, groups)]
+    pieces = jnp.concatenate([split(logs, 3), split(res, 3)], axis=0)
+    spread = jnp.concatenate([members(step_groups, 0, SUB, lag_wide), members(step_groups, 0, group, wide)], axis=1)
+    lag = (SUB - 1 - within(iota((poles, lag_wide), 1), SUB)).astype(F32)
+    for step in range(blocks // inner):
+        spreads = mxu(pieces[:, step * step_groups : (step + 1) * step_groups], spread)
+        rates = jnp.exp(join(spreads[: 3 * poles], poles))
+        res_lag = join(spreads[3 * poles :, :lag_wide], poles)
+        rate = rates[:, lag_wide:]
+        table = jnp.exp(-rates[:, :lag_wide] * lag)
+        taps = jnp.sum(res_lag * table, axis=0, keepdims=True)
+        table = table.astype(BF16)
+        for j in range(inner):
+            here = step * inner + j
+            lanes = slice(j * lag_width, (j + 1) * lag_width)
+            rates_ref[here] = rate[:, j * LANES : (j + 1) * LANES]
+            taps_ref[here : here + 1, :] = taps[:, lanes]
+            tables_ref[here] = table[:, lanes]
 
 
 def conv_kernel(rows_ref, skip_ref, rates_ref, taps_ref, tables_ref, gated_ref, turned_ref, conv_ref,
@@ -475,23 +498,34 @@
         return lax.ppermute(value, "ctx", [(i, i ^ (1 << level)) for i in range(parts)])
 
     gated, dgate = gate(key_input, value_input), gate(cotangent, queries)
-    outgoing, message, turned, rows, rates, taps, tables = pl.pallas_call(
+    outgoing, message, turned, rows = pl.pallas_call(
         lambda *refs: states_kernel(*refs, inner=inner, **sizes),
         in_specs=[vmem] * 4,
-        out_specs=[vmem] * 7,
+        out_specs=[vmem] * 4,
         out_shape=[
             shape(full_rows, LANES, dtype=BF16),
             shape(full_rows, LANES, dtype=BF16),
             shape(tokens, width, dtype=BF16),
             shape(2, blocks, LANES),
+        ],
+        scratch_shapes=[pltpu.VMEM((blocks, LANES), F32), pltpu.VMEM((2, blocks, LANES), F32)],
+        compiler_params=PARAMS,
+        name="states",
+    )(log_rates, residues, gated, dgate)
+
+    rates, taps, tables = pl.pallas_call(
+        lambda *refs: tables_kernel(*refs, inner=inner, **sizes),
+        in_specs=[vmem, vmem, anywhere],
+        out_specs=[vmem] * 3,
+        out_shape=[
             shape(blocks, poles, LANES),
             shape(blocks, lag_width),
             shape(blocks, poles, lag_width, dtype=BF16),
         ],
-        scratch_shapes=[pltpu.VMEM((blocks, LANES), F32)],
         compiler_params=PARAMS,
-        name="states",
-    )(log_rates, residues, gated, dgate)
+        cost_estimate=pl.CostEstimate(flops=10**9, bytes_accessed=10**6, transcendentals=10**5),
+        name="tables",
+    )(log_rates, residues, rows)
 
     skip_rows = skip_gain.reshape(-1, LANES)
     conv = pl.pallas_call(

time: 34.4 us -> 33.9 us (0.985)
  waiting for transfers between devices: 8.11 us -> 7.56 us
    ppermute x4, waiting for transfers between devices: 6.11 us -> 5.56 us  [swap(): lax.ppermute(value, 'ctx', [(i, i ^ 1 << level) for i in range(parts)])]
    pallas_call x0 -> x1, Pallas kernels: none -> 0.54 us  [local(): pl.pallas_call(lambda *refs: tables_kernel(*refs, inner=inner, **sizes),...]
    pallas_call x1, Pallas kernels: 6.27 us -> 5.75 us  [local(): pl.pallas_call(lambda *refs: states_kernel(*refs, inner=inner, **sizes),...]
  transfers between devices with their start and end apart: 7 -> 7, of which waited for: 6 -> 6; matrix products, arithmetic and copies ran while one was open for 0% -> 0% of each run, Pallas kernels for 16% -> 18%
where the time goes in v5:
time: 33.9 us; the launch traced here: 33.7 us
  Pallas kernels  13.5 us (40%)
  starting transfers between devices  10 us (29%)
  waiting for transfers between devices  7.56 us (22%)
  other arithmetic  1.88 us (6%)
  between operations  0.74 us (2%)
    pallas_call x1, Pallas kernels, local(): pl.pallas_call(lambda *refs: states_kernel(*refs, inner=inner, **sizes),...  5.75 us
    ppermute x4, waiting for transfers between devices, swap(): lax.ppermute(value, 'ctx', [(i, i ^ 1 << level) for i in range(parts)])  5.56 us
    ppermute x4, starting transfers between devices, swap(): lax.ppermute(value, 'ctx', [(i, i ^ 1 << level) for i in range(parts)])  5.16 us
    ppermute x3, starting transfers between devices, local(): lax.ppermute(merged, 'ch', [(i, (i + shift) % shards) for i in range(shar...  4.86 us
    pallas_call x1, Pallas kernels, local(): pl.pallas_call(lambda *refs: conv_kernel(*refs, inner=inner, **sizes), in...  2.8 us
    pallas_call x1, Pallas kernels, local(): pl.pallas_call(lambda *refs: output_kernel(*refs, **sizes), grid=(steps,)...  2.6 us
    ppermute x3, waiting for transfers between devices, local(): lax.ppermute(merged, 'ch', [(i, (i + shift) % shards) for i in range(shar...  2 us
    convert_element_type x1, other arithmetic, gate(): return (left.astype(F32) * right.astype(F32)).astype(BF16)  1.88 us
  transfers between devices with their start and end apart: 7, of which 6 were waited for; matrix products, arithmetic and copies ran while one was open for 0% of the time, Pallas kernels for 18%

profile of v5, /device:TPU:0, one launch (start us, length us, event | category | flops | bytes accessed | tf_op | source)
XLA Modules:
  0.0 33.7 jit_solution(9798842689575793536)
XLA Ops:
  0.6 0.0 copy-start.3
  0.6 0.0 copy-start.4
  0.7 1.9 %multiply_convert_fusion = (bf16[128,2048]{1,0:T(8,128)(2,1)S(1)}, bf16[128,2048]{1,0:T(8,128)(2,1)S(1)}) fusion(bf16[128,2048]{1,0:T(8,128)(2,1)} %param.7, bf16[128,2048]{1,0:T(8,128)(2,1)} %refs_6_.1, bf16[128,2048]{1,0:T(8,128)(2,1)} %refs_5_.1, bf16[128,2048]{1,0:T(8,128)(2,1)} %refs_4_.1), kind=kLoop, calls=%fused_computation | loop fusion | flops 2097152 | bytes 3145728 | tf_op jit(solution)/shard_map/convert_element_type | solution.py:44
  2.5 0.0 copy-done.3
  2.5 0.0 copy-done.4
  2.6 5.7 %states.1 = (bf16[560,128]{1,0:T(8,128)(2,1)S(1)}, bf16[560,128]{1,0:T(8,128)(2,1)S(1)}, bf16[128,2048]{1,0:T(8,128)(2,1)S(1)}, f32[2,16,128]{2,1,0:T(8,128)S(1)}) custom-call(f32[16,512]{1,0:T(8,128)S(1)} %bitcast.6, f32[16,512]{1,0:T(8,128)S(1)} %bitcast.9, bf16[128,2048]{1,0:T(8,128)(2,1)S(1)} %get-tuple-element.47.refs_2_.refs_5_, ...), custom_call_target="tpu_custom_call" | custom-call | tf_op jit(solution)/shard_map/states/pallas_call | solution.py:501
  8.3 0.0 copy-start.5
  8.3 0.5 %collective-permute-start = (bf16[560,128]{1,0:T(8,128)(2,1)S(1)}, bf16[560,128]{1,0:T(8,128)(2,1)S(1)}, u32[]{:S(2)}, u32[]{:S(2)}) collective-permute-start(bf16[560,128]{1,0:T(8,128)(2,1)S(1)} %get-tuple-element.32), channel_id=1, source_target_pairs={{0,4},{4,0},{8,12},{12,8},{16,20},{20,16},{24,28},{28,24},{1,5},{5... | collective-permute-start | bytes 430088 | tf_op jit(solution)/shard_map/ppermute | solution.py:498
  8.8 0.5 %tables.1 = (f32[16,16,128]{2,1,0:T(8,128)S(1)}, f32[16,256]{1,0:T(8,128)S(1)}, bf16[16,16,256]{2,1,0:T(8,128)(2,1)S(1)}) custom-call(f32[16,512]{1,0:T(8,128)S(1)} %bitcast.7, f32[16,512]{1,0:T(8,128)S(1)} %bitcast.10, f32[2,16,128]{2,1,0:T(8,128)S(1)} %get-tuple-element.26.refs_2_.refs_0_), custom_call_target="tpu_custom_call" | custom-call | flops 1000000000 | bytes 1000000 | tf_op jit(solution)/shard_map/tables/pallas_call | solution.py:516
  9.4 0.5 %collective-permute-done.refs_2_ = bf16[560,128]{1,0:T(8,128)(2,1)S(1)} collective-permute-done((bf16[560,128]{1,0:T(8,128)(2,1)S(1)}, bf16[560,128]{1,0:T(8,128)(2,1)S(1)}, u32[]{:S(2)}, u32[]{:S(2)}) %collective-permute-start) | collective-permute-done | bytes 143392 | tf_op jit(solution)/shard_map/ppermute | solution.py:498
  9.8 0.3 combine.3
  10.2 2.9 %collective-permute-start.1 = (bf16[560,128]{1,0:T(8,128)(2,1)S(1)}, bf16[560,128]{1,0:T(8,128)(2,1)S(1)}, u32[]{:S(2)}, u32[]{:S(2)}) collective-permute-start(bf16[560,128]{1,0:T(8,128)(2,1)S(1)} %get-tuple-element.33.refs_1_), channel_id=1, source_target_pairs={{0,8},{4,12},{8,0},{12,4},{16,24},{20,28},{24,16},{28,20},{1,9},{5... | collective-permute-start | bytes 430088 | tf_op jit(solution)/shard_map/ppermute | solution.py:498
  13.0 0.0 copy-done.5
  13.0 2.8 %conv.1.refs_3_.refs_1_ = f32[128,4096]{1,0:T(8,128)S(1)} custom-call(f32[2,16,128]{2,1,0:T(8,128)S(1)} %get-tuple-element.26.refs_2_.refs_0_, f32[64,128]{1,0:T(8,128)S(1)} %bitcast.12, f32[16,16,128]{2,1,0:T(8,128)S(1)} %get-tuple-element.27.refs_2_.refs_0_, f32[16,256]{1,0:T(8,128)S(1)} %get-tuple-element.28.refs_3_, ...), custom_call_target="tpu_custom_call" | custom-call | flops 536870912 | bytes 3145728 | tf_op jit(solution)/shard_map/conv/pallas_call | solution.py:531
  15.8 0.0 copy-start
  15.9 0.0 copy-start.1
  15.9 0.0 copy-start.2
  15.9 1.2 %collective-permute-done.1.refs_2_ = bf16[560,128]{1,0:T(8,128)(2,1)S(1)} collective-permute-done((bf16[560,128]{1,0:T(8,128)(2,1)S(1)}, bf16[560,128]{1,0:T(8,128)(2,1)S(1)}, u32[]{:S(2)}, u32[]{:S(2)}) %collective-permute-start.1) | collective-permute-done | bytes 143392 | tf_op jit(solution)/shard_map/ppermute | solution.py:498
  17.1 0.3 %combine.4 = (bf16[560,128]{1,0:T(8,128)(2,1)S(1)}, f32[8,32,128]{2,1,0:T(8,128)S(1)}, bf16[304,128]{1,0:T(8,128)(2,1)S(1)}) custom-call(f32[16,16,128]{2,1,0:T(8,128)S(1)} %get-tuple-element.27.refs_2_.refs_0_, bf16[560,128]{1,0:T(8,128)(2,1)S(1)} %get-tuple-element.33.refs_1_, bf16[560,128]{1,0:T(8,128)(2,1)S(1)} %collective-permute-done.1.refs_2_, ...), custom_call_target="tpu_custom_call" | custom-call | tf_op jit(solution)/shard_map/combine/pallas_call | solution.py:562
  17.4 1.8 %collective-permute-start.2 = (bf16[304,128]{1,0:T(8,128)(2,1)S(1)}, bf16[304,128]{1,0:T(8,128)(2,1)S(1)}, u32[]{:S(2)}, u32[]{:S(2)}) collective-permute-start(bf16[304,128]{1,0:T(8,128)(2,1)S(1)} %get-tuple-element.35), channel_id=1, source_target_pairs={{0,16},{4,20},{8,24},{12,28},{16,0},{20,4},{24,8},{28,12},{1,17},{... | collective-permute-start | bytes 233480 | tf_op jit(solution)/shard_map/ppermute | solution.py:498
  19.2 2.6 %collective-permute-done.2.refs_2_ = bf16[304,128]{1,0:T(8,128)(2,1)S(1)} collective-permute-done((bf16[304,128]{1,0:T(8,128)(2,1)S(1)}, bf16[304,128]{1,0:T(8,128)(2,1)S(1)}, u32[]{:S(2)}, u32[]{:S(2)}) %collective-permute-start.2) | collective-permute-done | bytes 77856 | tf_op jit(solution)/shard_map/ppermute | solution.py:498
  21.9 0.3 combine.5
  22.2 0.0 collective-permute-start.3
  22.2 1.3 %collective-permute-done.3.refs_3_.refs_1_ = bf16[304,128]{1,0:T(8,128)(2,1)S(1)} collective-permute-done((bf16[304,128]{1,0:T(8,128)(2,1)S(1)}, bf16[304,128]{1,0:T(8,128)(2,1)S(1)}, u32[]{:S(2)}, u32[]{:S(2)}) %collective-permute-start.3) | collective-permute-done | bytes 77856 | tf_op jit(solution)/shard_map/ppermute | solution.py:498
  23.5 0.1 merge.1.refs_0_
  23.6 3.8 %collective-permute-start.6 = (f32[48,128]{1,0:T(8,128)S(1)}, f32[48,128]{1,0:T(8,128)S(1)}, u32[]{:S(2)}, u32[]{:S(2)}) collective-permute-start(f32[48,128]{1,0:T(8,128)S(1)} %merge.1.refs_0_), channel_id=1, source_target_pairs={{0,3},{1,0},{2,1},{3,2},{4,7},{5,4},{6,5},{7,6},{8,11},{9,8},{10,9... | collective-permute-start | bytes 73736 | tf_op jit(solution)/shard_map/ppermute | solution.py:591
  27.4 0.0 collective-permute-start.5
  27.4 1.0 %collective-permute-start.4 = (f32[48,128]{1,0:T(8,128)S(1)}, f32[48,128]{1,0:T(8,128)S(1)}, u32[]{:S(2)}, u32[]{:S(2)}) collective-permute-start(f32[48,128]{1,0:T(8,128)S(1)} %merge.1.refs_0_), channel_id=1, source_target_pairs={{0,1},{1,2},{2,3},{3,0},{4,5},{5,6},{6,7},{7,4},{8,9},{9,10},{10,1... | collective-permute-start | bytes 73736 | tf_op jit(solution)/shard_map/ppermute | solution.py:591
  28.5 0.0 copy-done
  28.5 0.0 copy-done.1
  28.5 0.0 copy-done.2
  28.5 2.6 %outputs.1 = (bf16[128,2048]{1,0:T(8,128)(2,1)}, bf16[128,2048]{1,0:T(8,128)(2,1)}, bf16[128,2048]{1,0:T(8,128)(2,1)}) custom-call(f32[2,16,128]{2,1,0:T(8,128)S(1)} %get-tuple-element.26.refs_2_.refs_0_, f32[128,4096]{1,0:T(8,128)S(1)} %conv.1.refs_3_.refs_1_, bf16[8,32,128]{2,1,0:T(8,128)(2,1)S(1)} %get-tuple-element.38.refs_2_, ...), custom_call_target="tpu_custom_call" | custom-call | tf_op jit(solution)/shard_map/outputs/pallas_call | solution.py:593
  31.1 0.0 collective-permute-done.6.refs_3_
  31.1 1.2 %collective-permute-done.5.refs_2_ = f32[48,128]{1,0:T(8,128)S(1)} collective-permute-done((f32[48,128]{1,0:T(8,128)S(1)}, f32[48,128]{1,0:T(8,128)S(1)}, u32[]{:S(2)}, u32[]{:S(2)}) %collective-permute-start.5) | collective-permute-done | bytes 24608 | tf_op jit(solution)/shard_map/ppermute | solution.py:591
  32.2 0.8 %collective-permute-done.4.refs_1_ = f32[48,128]{1,0:T(8,128)S(1)} collective-permute-done((f32[48,128]{1,0:T(8,128)S(1)}, f32[48,128]{1,0:T(8,128)S(1)}, u32[]{:S(2)}, u32[]{:S(2)}) %collective-permute-start.4) | collective-permute-done | bytes 24608 | tf_op jit(solution)/shard_map/ppermute | solution.py:591
  33.1 0.6 %assemble.1 = (f32[16,512]{1,0:T(8,128)}, f32[16,512]{1,0:T(8,128)}, f32[64,128]{1,0:T(8,128)}) custom-call(f32[48,128]{1,0:T(8,128)S(1)} %merge.1.refs_0_, f32[48,128]{1,0:T(8,128)S(1)} %collective-permute-done.4.refs_1_, f32[48,128]{1,0:T(8,128)S(1)} %collective-permute-done.5.refs_2_, f32[48,128]{1,0:T(8,128)S(1)} %collective-permute-done.6.refs_3_), custom_call_target="tpu_custom_call" | custom-call | tf_op jit(solution)/shard_map/assemble/pallas_call | solution.py:603
Async XLA Ops:
  0.6 1.9 %copy-start.3 = (f32[512,16]{0,1:T(8,128)S(1)}, f32[512,16]{0,1:T(8,128)}, u32[]{:S(2)}) copy-start(f32[512,16]{0,1:T(8,128)} %param.12) | copy-start | bytes 98308
  0.6 1.9 %copy-start.4 = (f32[512,16]{0,1:T(8,128)S(1)}, f32[512,16]{0,1:T(8,128)}, u32[]{:S(2)}) copy-start(f32[512,16]{0,1:T(8,128)} %param.11) | copy-start | bytes 98308
  8.3 4.7 %copy-start.5 = (f32[8192]{0:T(1024)S(1)}, f32[8192]{0:T(1024)}, u32[]{:S(2)}) copy-start(f32[8192]{0:T(1024)} %param.13) | copy-start | bytes 98308
  8.3 1.5 %collective-permute-start = (bf16[560,128]{1,0:T(8,128)(2,1)S(1)}, bf16[560,128]{1,0:T(8,128)(2,1)S(1)}, u32[]{:S(2)}, u32[]{:S(2)}) collective-permute-start(bf16[560,128]{1,0:T(8,128)(2,1)S(1)} %get-tuple-element.32), channel_id=1, source_target_pairs={{0,4},{4,0},{8,12},{12,8},{16,20},{20,16},{24,28},{28,24},{1,5},{5... | collective-permute-start | bytes 430088 | tf_op jit(solution)/shard_map/ppermute | solution.py:498
  10.2 6.9 %collective-permute-start.1 = (bf16[560,128]{1,0:T(8,128)(2,1)S(1)}, bf16[560,128]{1,0:T(8,128)(2,1)S(1)}, u32[]{:S(2)}, u32[]{:S(2)}) collective-permute-start(bf16[560,128]{1,0:T(8,128)(2,1)S(1)} %get-tuple-element.33.refs_1_), channel_id=1, source_target_pairs={{0,8},{4,12},{8,0},{12,4},{16,24},{20,28},{24,16},{28,20},{1,9},{5... | collective-permute-start | bytes 430088 | tf_op jit(solution)/shard_map/ppermute | solution.py:498
  15.8 12.6 %copy-start = (bf16[128,2048]{1,0:T(8,128)(2,1)S(1)}, bf16[128,2048]{1,0:T(8,128)(2,1)}, u32[]{:S(2)}) copy-start(bf16[128,2048]{1,0:T(8,128)(2,1)} %refs_6_.1) | copy-start | bytes 1572868
  15.9 12.6 %copy-start.1 = (bf16[128,2048]{1,0:T(8,128)(2,1)S(1)}, bf16[128,2048]{1,0:T(8,128)(2,1)}, u32[]{:S(2)}) copy-start(bf16[128,2048]{1,0:T(8,128)(2,1)} %refs_5_.1) | copy-start | bytes 1572868
  15.9 12.6 %copy-start.2 = (bf16[128,2048]{1,0:T(8,128)(2,1)S(1)}, bf16[128,2048]{1,0:T(8,128)(2,1)}, u32[]{:S(2)}) copy-start(bf16[128,2048]{1,0:T(8,128)(2,1)} %refs_4_.1) | copy-start | bytes 1572868
  17.4 4.4 %collective-permute-start.2 = (bf16[304,128]{1,0:T(8,128)(2,1)S(1)}, bf16[304,128]{1,0:T(8,128)(2,1)S(1)}, u32[]{:S(2)}, u32[]{:S(2)}) collective-permute-start(bf16[304,128]{1,0:T(8,128)(2,1)S(1)} %get-tuple-element.35), channel_id=1, source_target_pairs={{0,16},{4,20},{8,24},{12,28},{16,0},{20,4},{24,8},{28,12},{1,17},{... | collective-permute-start | bytes 233480 | tf_op jit(solution)/shard_map/ppermute | solution.py:498
  22.2 1.3 %collective-permute-start.3 = (bf16[304,128]{1,0:T(8,128)(2,1)S(1)}, bf16[304,128]{1,0:T(8,128)(2,1)S(1)}, u32[]{:S(2)}, u32[]{:S(2)}) collective-permute-start(bf16[304,128]{1,0:T(8,128)(2,1)S(1)} %get-tuple-element.39.refs_0_), channel_id=1, source_target_pairs={{0,4},{4,0},{8,12},{12,8},{16,20},{20,16},{24,28},{28,24},{1,5},{5... | collective-permute-start | bytes 233480 | tf_op jit(solution)/shard_map/ppermute | solution.py:498
  23.6 7.5 %collective-permute-start.6 = (f32[48,128]{1,0:T(8,128)S(1)}, f32[48,128]{1,0:T(8,128)S(1)}, u32[]{:S(2)}, u32[]{:S(2)}) collective-permute-start(f32[48,128]{1,0:T(8,128)S(1)} %merge.1.refs_0_), channel_id=1, source_target_pairs={{0,3},{1,0},{2,1},{3,2},{4,7},{5,4},{6,5},{7,6},{8,11},{9,8},{10,9... | collective-permute-start | bytes 73736 | tf_op jit(solution)/shard_map/ppermute | solution.py:591
  27.4 4.8 %collective-permute-start.5 = (f32[48,128]{1,0:T(8,128)S(1)}, f32[48,128]{1,0:T(8,128)S(1)}, u32[]{:S(2)}, u32[]{:S(2)}) collective-permute-start(f32[48,128]{1,0:T(8,128)S(1)} %merge.1.refs_0_), channel_id=1, source_target_pairs={{0,2},{1,3},{2,0},{3,1},{4,6},{5,7},{6,4},{7,5},{8,10},{9,11},{10,... | collective-permute-start | bytes 73736 | tf_op jit(solution)/shard_map/ppermute | solution.py:591
  27.4 5.6 %collective-permute-start.4 = (f32[48,128]{1,0:T(8,128)S(1)}, f32[48,128]{1,0:T(8,128)S(1)}, u32[]{:S(2)}, u32[]{:S(2)}) collective-permute-start(f32[48,128]{1,0:T(8,128)S(1)} %merge.1.refs_0_), channel_id=1, source_target_pairs={{0,1},{1,2},{2,3},{3,0},{4,5},{5,6},{6,7},{7,4},{8,9},{9,10},{10,1... | collective-permute-start | bytes 73736 | tf_op jit(solution)/shard_map/ppermute | solution.py:591

commit v6 on v5

--- a/solution.py
+++ b/solution.py
@@ -82,20 +82,8 @@
     return pl.multiple_of(lax.axis_index("ch") * groups, LANES)
 
 
-def pack_half(value, half):
-    chosen = jnp.where(half > 0, pltpu.roll(value, LANES // 2, 1), value)
-    high = chosen.astype(BF16).astype(F32)
-    low = pltpu.roll(chosen - high, LANES // 2, 1)
-    return jnp.where(iota(value.shape, 1) < LANES // 2, high, low).astype(BF16)
-
-
-def open_half(packed):
-    value = packed.astype(F32)
-    return value + pltpu.roll(value, LANES // 2, 1)
-
-
 def states_kernel(logs_ref, res_ref, gated_ref, dgate_ref, send_ref, keep_ref, turned_ref, rows_ref,
-                  skip_ref, near_ref, *, group, poles, inner):
+                  *, group, poles, inner):
     tokens, _ = gated_ref.shape
     per_block = LANES // group
     _, blocks, _ = rows_ref.shape
@@ -110,13 +98,9 @@
 
     flip = reversal(tokens)
     back_pos = (tokens - 1 - iota((tokens, LANES), 0)).astype(F32)
-    back_lane = (tokens - 1 - iota((per_block, tokens), 1)).astype(F32)
-    lane_group = over(iota((tokens, LANES), 1), group)
-    causal = iota((tokens, tokens), 0) + iota((tokens, tokens), 1) <= tokens - 1
+    back_lane = (tokens - 1 - iota((1, tokens), 1)).astype(F32)
     wide_group = over(within(iota((poles, 2 * LANES), 1), LANES), group)
-    own_rows = iota((per_block, LANES), 0) == over(iota((per_block, LANES), 1), poles)
-    half = per_block // 2
-    zero = jnp.zeros((tokens, LANES), BF16)
+    lanes = [slice(j * LANES, (j + 1) * LANES) for j in range(inner)]
 
     for turn, msg_ref in enumerate((send_ref, keep_ref)):
         base = lax.rem(core + 1 + turn, 2) * half_blocks
@@ -127,27 +111,12 @@
             gated, dgate = gated_ref[:, cut], dgate_ref[:, cut]
             turned = mxu(flip, dgate).astype(BF16)
             turned_ref[:, cut] = turned
-            skip = jnp.sum(gated.astype(F32) * dgate.astype(F32), axis=0, keepdims=True)
-            for j in range(inner):
-                skip_ref[pl.ds(start + j, 1), :] = skip[:, j * LANES : (j + 1) * LANES]
-            lanes = [slice(j * LANES, (j + 1) * LANES) for j in range(inner)]
-            tables = [jnp.exp(-rows_ref[0, pl.ds(start + j, 1), :] * back_pos) for j in range(inner)]
-            lows = [table.astype(BF16) for table in tables]
+            tables = [jnp.exp(-rows_ref[0, pl.ds(start + j, 1), :] * back_pos).T for j in range(inner)]
             found = []
             for j in range(inner):
-                table = tables[j].T
-                moment_table = table * back_lane[:1]
-                both = jnp.concatenate([table.astype(BF16), moment_table.astype(BF16)], axis=0)
+                both = jnp.concatenate([tables[j].astype(BF16), (tables[j] * back_lane).astype(BF16)], axis=0)
                 pair = jnp.concatenate([gated[:, lanes[j]], turned[:, lanes[j]]], axis=1)
                 found.append(mxu(both, pair))
-            outers = []
-            for j in range(inner):
-                one, other = gated[:, lanes[j]], turned[:, lanes[j]]
-                left = [
-                    jnp.where((lane_group == i) | (lane_group == i + half), other, zero) for i in range(half)
-                ]
-                right = [jnp.where(lane_group < half, one, zero), jnp.where(lane_group >= half, one, zero)]
-                outers.append(mxu_t(jnp.concatenate(left, axis=0), jnp.concatenate(right, axis=0)))
             for j in range(inner):
                 folded = []
                 for part in range(2):
@@ -159,43 +128,72 @@
                 out = [folded[0][:, :LANES], folded[0][:, LANES:], folded[1][:, :LANES], folded[1][:, LANES:]]
                 row = pl.multiple_of((step * inner + j) * 4 * poles, 4 * poles)
                 msg_ref[pl.ds(row, 4 * poles), :] = jnp.concatenate(out, axis=0).astype(BF16)
-            for j in range(inner):
-                totals = []
-                for g in range(per_block):
-                    i, h = g % half, g // half
-                    tile = outers[j][i * tokens : (i + 1) * tokens, h * tokens : (h + 1) * tokens]
-                    tile = jnp.where(causal, tile, 0.0)
-                    total = None
-                    for a in range(tokens // 8):
-                        shift = (8 * (a - g)) % tokens
-                        piece = tile[8 * a : 8 * a + 8]
-                        piece = pltpu.roll(piece, shift, 1) if shift else piece
-                        total = piece if total is None else total + piece
-                    totals.append(total)
-                total = pltpu.roll(jnp.concatenate(totals, axis=0), 0, 1, stride=1, stride_axis=0)
-                lag = jnp.sum(total.reshape(per_block, 8, tokens), axis=1)
-                stack = jnp.concatenate([split(lag, 2), split(lag * back_lane, 2)], axis=0)
-                local = mxu(stack, lows[j])
-                for n in range(2):
-                    part = join(local[2 * n * per_block : 2 * (n + 1) * per_block], per_block)
-                    row = jnp.sum(jnp.where(own_rows, part, 0.0), axis=0, keepdims=True)
-                    near_ref[n, pl.ds(start + j, 1), :] = row
             return carry
 
         lax.fori_loop(0, half_blocks // inner, body, 0)
+
+
+def lags_kernel(rows_ref, gated_ref, dgate_ref, turned_ref, _, sums_ref, skip_ref, near_ref, *, group, poles, inner):
+    tokens, _ = gated_ref.shape
+    per_block = LANES // group
+    _, blocks, _ = rows_ref.shape
+    groups = blocks * per_block
+    wide = inner * LANES
+    back_pos = (tokens - 1 - iota((tokens, LANES), 0)).astype(F32)
+    back_lane = (tokens - 1 - iota((per_block, tokens), 1)).astype(F32)
+    lane_group = over(iota((tokens, LANES), 1), group)
+    causal = iota((tokens, tokens), 0) + iota((tokens, tokens), 1) <= tokens - 1
+    own_rows = iota((per_block, LANES), 0) == over(iota((per_block, LANES), 1), poles)
+    half = per_block // 2
+    zero = jnp.zeros((tokens, LANES), BF16)
+    lanes = [slice(j * LANES, (j + 1) * LANES) for j in range(inner)]
+
+    def body(step, carry):
+        start = step * inner
+        cut = pl.ds(pl.multiple_of(start * LANES, LANES), wide)
+        gated, turned = gated_ref[:, cut], turned_ref[:, cut]
+        skip = jnp.sum(gated.astype(F32) * dgate_ref[:, cut].astype(F32), axis=0, keepdims=True)
+        for j in range(inner):
+            skip_ref[pl.ds(start + j, 1), :] = skip[:, lanes[j]]
+        lows = [jnp.exp(-rows_ref[0, pl.ds(start + j, 1), :] * back_pos).astype(BF16) for j in range(inner)]
+        outers = []
+        for j in range(inner):
+            one, other = gated[:, lanes[j]], turned[:, lanes[j]]
+            left = [jnp.where((lane_group == i) | (lane_group == i + half), other, zero) for i in range(half)]
+            right = [jnp.where(lane_group < half, one, zero), jnp.where(lane_group >= half, one, zero)]
+            outers.append(mxu_t(jnp.concatenate(left, axis=0), jnp.concatenate(right, axis=0)))
+        for j in range(inner):
+            totals = []
+            for g in range(per_block):
+                i, h = g % half, g // half
+                tile = outers[j][i * tokens : (i + 1) * tokens, h * tokens : (h + 1) * tokens]
+                tile = jnp.where(causal, tile, 0.0)
+                total = None
+                for a in range(tokens // 8):
+                    shift = (8 * (a - g)) % tokens
+                    piece = tile[8 * a : 8 * a + 8]
+                    piece = pltpu.roll(piece, shift, 1) if shift else piece
+                    total = piece if total is None else total + piece
+                totals.append(total)
+            total = pltpu.roll(jnp.concatenate(totals, axis=0), 0, 1, stride=1, stride_axis=0)
+            lag = jnp.sum(total.reshape(per_block, 8, tokens), axis=1)
+            stack = jnp.concatenate([split(lag, 2), split(lag * back_lane, 2)], axis=0)
+            local = mxu(stack, lows[j])
+            for n in range(2):
+                part = join(local[2 * n * per_block : 2 * (n + 1) * per_block], per_block)
+                row = jnp.sum(jnp.where(own_rows, part, 0.0), axis=0, keepdims=True)
+                near_ref[n, pl.ds(start + j, 1), :] = row
+        return carry
+
+    lax.fori_loop(0, blocks // inner, body, 0)
     pick = iota((poles, LANES), 0) == within(iota((poles, LANES), 1), poles)
     terms = []
     for b in range(blocks):
         near = [jnp.where(pick, near_ref[n, b : b + 1, :], 0.0) for n in range(2)]
         terms.append(split(jnp.concatenate(near, axis=0), 2))
     sums = mxu_t(jnp.concatenate(terms, axis=1), members(groups, 0, poles, blocks * LANES))
-    sums = join(sums, 2 * poles)
-    tail = half_blocks * 4 * poles
-    for turn, msg_ref in enumerate((send_ref, keep_ref)):
-        half = lax.rem(core + 1 + turn, 2)
-        msg_ref[tail : tail + 2 * poles, :] = pack_half(sums, half)
-        skip = skip_ref[pl.ds(pl.multiple_of(half * half_blocks, 8), half_blocks), :]
-        msg_ref[tail + 2 * poles :, :] = split(skip, 2)
+    sums_ref[: 4 * poles, :] = split(join(sums, 2 * poles), 2)
+    sums_ref[4 * poles :, :] = split(skip_ref[...], 2)
 
 
 def tables_kernel(logs_ref, res_ref, _, rates_ref, taps_ref, tables_ref, *, group, poles, inner):
@@ -226,7 +224,7 @@
             tables_ref[here] = table[:, lanes]
 
 
-def conv_kernel(rows_ref, skip_ref, rates_ref, taps_ref, tables_ref, gated_ref, turned_ref, conv_ref,
+def conv_kernel(rows_ref, skip_ref, rates_ref, taps_ref, tables_ref, gated_ref, turned_ref, _, conv_ref,
                 *, group, poles, inner):
     tokens, _ = gated_ref.shape
     per_block = LANES // group
@@ -295,10 +293,11 @@
         if level > 1:
             held_ref = rest.pop(0)
         else:
+            own_sums_ref, got_sums_ref = rest.pop(0), rest.pop(0)
+        if level == min(2, levels - 1):
             rest.pop(0)
         if last:
-            near_ref, logs_ref, res_ref = rest[:3]
-            mine_ref, out_ref = rest[3:]
+            near_ref, mine_ref, out_ref = rest
         else:
             out_ref, new_held_ref = rest[:2]
             rest = rest[2:]
@@ -381,41 +380,36 @@
                 slim_ref[b * slim_rows : (b + 1) * slim_rows, :] = chosen.astype(BF16)
     own_tail, got_tail = blocks * own_rows, blocks * got_rows
     cross = mxu_t(jnp.concatenate(wide_terms, axis=1), members(groups, 0, group, blocks * LANES))
-    total = (
-        join(cross, 2 * poles)
-        + open_half(own_ref[own_tail : own_tail + 2 * poles, :])
-        + open_half(got_ref[got_tail : got_tail + 2 * poles, :])
-    )
-    skip = join(own_ref[own_tail + 2 * poles :, :], blocks) + join(got_ref[got_tail + 2 * poles :, :], blocks)
-    if last:
-        start = shard_start(groups)
-        rate = jnp.exp(logs_ref[:, pl.ds(start, groups)])
-        factor = -rate * res_ref[:, pl.ds(start, groups)]
-        factor = jnp.where(core > 0, pltpu.roll(factor, LANES // 2, 1), factor)
-        length = 2 * span
-        total = jnp.concatenate(
-            [total[:poles] / length, factor * total[poles:] / math.sqrt(length)], axis=0
-        )
-        skip = skip / math.sqrt(length)
-    rests = jnp.concatenate([pack_half(total, 0), split(skip, 2)], axis=0)
-    if last:
-        out_ref[blocks * 2 * poles :, :] = rests
+    cross = join(cross, 2 * poles)
+    total = jnp.where(core > 0, pltpu.roll(cross, groups // 2, 1), cross)
+    if level:
+        own_tail, got_tail = own_ref[own_tail:, :], got_ref[got_tail:, :]
+        tails = [own_tail, got_tail]
+        if level == 1:
+            tails += [own_sums_ref[...], got_sums_ref[...]]
+        for part in tails:
+            total = total + join(part[: 4 * poles], 2 * poles)
+        skip = sum(join(part[4 * poles :], all_blocks) for part in tails if part.shape[0] > 4 * poles)
+        rests = jnp.concatenate([split(total, 2), split(skip, 2)], axis=0)
     else:
-        out_ref[own_tail:, :] = rests
-        if slim_ref is not None:
-            slim_ref[blocks * slim_rows :, :] = rests
-
-
-def merge_kernel(own_ref, got_ref, out_ref, *, poles):
-    core = lax.rem(lax.axis_index("ctx"), 2)
-    blocks = (out_ref.shape[0] - 2 * poles) // 2
-    rows = own_ref.shape[0] - 2 * poles - 2 * blocks
-    own, got = open_half(own_ref[rows : rows + 2 * poles, :]), open_half(got_ref[rows : rows + 2 * poles, :])
-    left, right = jnp.where(core > 0, got, own), jnp.where(core > 0, own, got)
-    out_ref[: 2 * poles, :] = jnp.where(iota(own.shape, 1) < LANES // 2, left, pltpu.roll(right, LANES // 2, 1))
-    own, got = join(own_ref[rows + 2 * poles :, :], blocks), join(got_ref[rows + 2 * poles :, :], blocks)
-    out_ref[2 * poles : 2 * poles + blocks, :] = jnp.where(core > 0, got, own)
-    out_ref[2 * poles + blocks :, :] = jnp.where(core > 0, own, got)
+        rests = split(total, 2)
+    out_ref[blocks * (2 * poles if last else own_rows) :, :] = rests
+    if slim_ref is not None:
+        slim_ref[blocks * slim_rows :, :] = rests
+
+
+def merge_kernel(logs_ref, res_ref, own_ref, got_ref, out_ref, *, poles, length):
+    blocks = out_ref.shape[0] - 2 * poles
+    groups = out_ref.shape[1]
+    start = own_ref.shape[0] - 4 * poles - 2 * blocks
+    own, got = own_ref[start:, :], got_ref[start:, :]
+    total = join(own[: 4 * poles], 2 * poles) + join(got[: 4 * poles], 2 * poles)
+    skip = join(own[4 * poles :], blocks) + join(got[4 * poles :], blocks)
+    first = shard_start(groups)
+    factor = -jnp.exp(logs_ref[:, pl.ds(first, groups)]) * res_ref[:, pl.ds(first, groups)]
+    out_ref[:poles, :] = total[:poles] / length
+    out_ref[poles : 2 * poles, :] = factor * total[poles:] / math.sqrt(length)
+    out_ref[2 * poles :, :] = skip / math.sqrt(length)
 
 
 def output_kernel(rows_ref, conv_ref, mine_ref, got_ref, k_ref, v_ref, c_ref, gq_ref, gk_ref, gv_ref,
@@ -483,8 +477,8 @@
     half_blocks = blocks // 2
     lag_width = LANES // group * SUB
     sizes = dict(group=group, poles=poles)
-    tail = 2 * poles + blocks
-    full_rows, slim_rows = half_blocks * 4 * poles + tail, half_blocks * 2 * poles + tail
+    near_tail, tail = 4 * poles, 4 * poles + 2 * blocks
+    full_rows, half_rows = half_blocks * 4 * poles, half_blocks * 2 * poles
 
     vmem = pl.BlockSpec(memory_space=pltpu.VMEM)
     anywhere = pl.BlockSpec(memory_space=pl.ANY)
@@ -508,7 +502,6 @@
             shape(tokens, width, dtype=BF16),
             shape(2, blocks, LANES),
         ],
-        scratch_shapes=[pltpu.VMEM((blocks, LANES), F32), pltpu.VMEM((2, blocks, LANES), F32)],
         compiler_params=PARAMS,
         name="states",
     )(log_rates, residues, gated, dgate)
@@ -527,18 +520,33 @@
         name="tables",
     )(log_rates, residues, rows)
 
-    skip_rows = skip_gain.reshape(-1, LANES)
-    conv = pl.pallas_call(
-        lambda *refs: conv_kernel(*refs, inner=inner, **sizes),
-        in_specs=[vmem] * 7,
-        out_specs=vmem,
-        out_shape=shape(tokens, 2 * width),
-        compiler_params=PARAMS,
-        cost_estimate=pl.CostEstimate(
-            flops=16 * tokens * tokens * width, bytes_accessed=12 * tokens * width, transcendentals=tokens * width
-        ),
-        name="conv",
-    )(rows, skip_rows, rates, taps, tables, gated, turned)
+    def local_sums(after):
+        return pl.pallas_call(
+            lambda *refs: lags_kernel(*refs, inner=inner, **sizes),
+            in_specs=[vmem] * 4 + [anywhere],
+            out_specs=vmem,
+            out_shape=shape(tail, LANES, dtype=BF16),
+            scratch_shapes=[pltpu.VMEM((blocks, LANES), F32), pltpu.VMEM((2, blocks, LANES), F32)],
+            compiler_params=PARAMS,
+            cost_estimate=pl.CostEstimate(
+                flops=16 * tokens * tokens * width, bytes_accessed=12 * tokens * width, transcendentals=tokens * width
+            ),
+            name="lags",
+        )(rows, gated, dgate, turned, after)
+
+    def convolve(after):
+        skip_rows = skip_gain.reshape(-1, LANES)
+        return pl.pallas_call(
+            lambda *refs: conv_kernel(*refs, inner=inner, **sizes),
+            in_specs=[vmem] * 7 + [anywhere],
+            out_specs=vmem,
+            out_shape=shape(tokens, 2 * width),
+            compiler_params=PARAMS,
+            cost_estimate=pl.CostEstimate(
+                flops=16 * tokens * tokens * width, bytes_accessed=12 * tokens * width, transcendentals=tokens * width
+            ),
+            name="conv",
+        )(rows, skip_rows, rates, taps, tables, gated, turned, after)
 
     held = near = None
     for level in range(levels):
@@ -546,19 +554,27 @@
         got = swap(outgoing, level)
         operands, specs = [rates, message, got], [vmem] * 3
         if level == 1:
-            operands.append(conv)
-            specs.append(anywhere)
+            sums = local_sums(near)
+            operands += [sums, swap(sums, level)]
+            specs += [vmem] * 2
         elif level > 1:
             operands.append(held)
             specs.append(vmem)
+        if level == min(2, levels - 1):
+            conv = convolve(near if held is None else held)
+            operands.append(conv)
+            specs.append(anywhere)
         if last:
-            operands += [near, log_rates, residues]
-            specs += [vmem] * 3
-            outs = [shape(half_blocks, 2 * poles, LANES, dtype=BF16), shape(slim_rows, LANES, dtype=BF16)]
+            operands.append(near)
+            specs.append(vmem)
+            outs = [shape(half_blocks, 2 * poles, LANES, dtype=BF16), shape(half_rows + tail, LANES, dtype=BF16)]
         else:
-            outs = [shape(full_rows, LANES, dtype=BF16), shape(half_blocks, 2 * poles, LANES)]
+            outs = [
+                shape(full_rows + (tail if level else near_tail), LANES, dtype=BF16),
+                shape(half_blocks, 2 * poles, LANES),
+            ]
         if level == levels - 2:
-            outs.append(shape(slim_rows, LANES, dtype=BF16))
+            outs.append(shape(half_rows + (tail if level else near_tail), LANES, dtype=BF16))
         results = pl.pallas_call(
             lambda *refs, level=level: combine_kernel(*refs, level=level, levels=levels, tokens=tokens, **sizes),
             in_specs=specs,
@@ -578,13 +594,13 @@
                 held = results[1]
     got = swap(outgoing, 0)
     merged = pl.pallas_call(
-        lambda *refs: merge_kernel(*refs, poles=poles),
-        in_specs=[vmem] * 2,
+        lambda *refs: merge_kernel(*refs, poles=poles, length=tokens * parts),
+        in_specs=[vmem] * 4,
         out_specs=vmem,
         out_shape=shape(2 * poles + blocks, LANES),
         compiler_params=PARAMS,
         name="merge",
-    )(outgoing, got)
+    )(log_rates, residues, outgoing, got)
 
     gathered = [merged]
     for shift in range(1, shards):

time: 33.9 us -> 34.2 us (level)
    pallas_call x2 -> x3, Pallas kernels: 2.94 us -> 6.96 us  [the longest x1 4.15 us: local_sums(): pl.pallas_call(lambda *refs: lags_kernel(*refs, inner=inner, **sizes), in...]
    pallas_call x1, Pallas kernels: 5.75 us -> 2.16 us  [local(): pl.pallas_call(lambda *refs: states_kernel(*refs, inner=inner, **sizes),...]
    ppermute x4 -> x5, waiting for transfers between devices: 5.56 us -> 5.68 us  [swap(): lax.ppermute(value, 'ctx', [(i, i ^ 1 << level) for i in range(parts)])]
    ppermute x4 -> x5, starting transfers between devices: 5.16 us -> 5.17 us  [swap(): lax.ppermute(value, 'ctx', [(i, i ^ 1 << level) for i in range(parts)])]
  transfers between devices with their start and end apart: 7 -> 8, of which waited for: 6 -> 6; matrix products, arithmetic and copies ran while one was open for 0% -> 0% of each run, Pallas kernels for 18% -> 30%
where the time goes in v6:
time: 34.2 us; the launch traced here: 34.1 us
  Pallas kernels  13.8 us (40%)
  starting transfers between devices  9.84 us (29%)
  waiting for transfers between devices  7.68 us (22%)
  other arithmetic  1.92 us (6%)
  between operations  0.82 us (2%)
    ppermute x5, waiting for transfers between devices, swap(): lax.ppermute(value, 'ctx', [(i, i ^ 1 << level) for i in range(parts)])  5.68 us
    ppermute x5, starting transfers between devices, swap(): lax.ppermute(value, 'ctx', [(i, i ^ 1 << level) for i in range(parts)])  5.17 us
    ppermute x3, starting transfers between devices, local(): lax.ppermute(merged, 'ch', [(i, (i + shift) % shards) for i in range(shar...  4.67 us
    pallas_call x1, Pallas kernels, local_sums(): pl.pallas_call(lambda *refs: lags_kernel(*refs, inner=inner, **sizes), in...  4.15 us
    pallas_call x1, Pallas kernels, convolve(): pl.pallas_call(lambda *refs: conv_kernel(*refs, inner=inner, **sizes), in...  2.8 us
    pallas_call x1, Pallas kernels, local(): pl.pallas_call(lambda *refs: output_kernel(*refs, **sizes), grid=(steps,)...  2.6 us
    pallas_call x1, Pallas kernels, local(): pl.pallas_call(lambda *refs: states_kernel(*refs, inner=inner, **sizes),...  2.16 us
    ppermute x3, waiting for transfers between devices, local(): lax.ppermute(merged, 'ch', [(i, (i + shift) % shards) for i in range(shar...  2 us
  transfers between devices with their start and end apart: 8, of which 6 were waited for; matrix products, arithmetic and copies ran while one was open for 0% of the time, Pallas kernels for 30%

profile of v6, /device:TPU:0, one launch (start us, length us, event | category | flops | bytes accessed | tf_op | source)
XLA Modules:
  0.0 34.1 jit_solution(14353452621414165548)
XLA Ops:
  0.6 0.0 copy-start.3
  0.6 0.0 copy-start.4
  0.7 1.9 %multiply_convert_fusion = (bf16[128,2048]{1,0:T(8,128)(2,1)S(1)}, bf16[128,2048]{1,0:T(8,128)(2,1)S(1)}) fusion(bf16[128,2048]{1,0:T(8,128)(2,1)} %param.7, bf16[128,2048]{1,0:T(8,128)(2,1)} %refs_6_.1, bf16[128,2048]{1,0:T(8,128)(2,1)} %refs_5_.1, bf16[128,2048]{1,0:T(8,128)(2,1)} %refs_4_.1), kind=kLoop, calls=%fused_computation | loop fusion | flops 2097152 | bytes 3145728 | tf_op jit(solution)/shard_map/convert_element_type | solution.py:44
  2.6 0.0 copy-done.3
  2.6 0.0 copy-done.4
  2.6 2.2 %states.1 = (bf16[512,128]{1,0:T(8,128)(2,1)S(1)}, bf16[512,128]{1,0:T(8,128)(2,1)S(1)}, bf16[128,2048]{1,0:T(8,128)(2,1)S(1)}, f32[2,16,128]{2,1,0:T(8,128)S(1)}) custom-call(f32[16,512]{1,0:T(8,128)S(1)} %bitcast.6, f32[16,512]{1,0:T(8,128)S(1)} %bitcast.9, bf16[128,2048]{1,0:T(8,128)(2,1)S(1)} %get-tuple-element.47.refs_2_.refs_1_.refs_5_, ...), custom_call_target="tpu_custom_call" | custom-call | tf_op jit(solution)/shard_map/states/pallas_call | solution.py:495
  4.8 0.5 %collective-permute-start = (bf16[512,128]{1,0:T(8,128)(2,1)S(1)}, bf16[512,128]{1,0:T(8,128)(2,1)S(1)}, u32[]{:S(2)}, u32[]{:S(2)}) collective-permute-start(bf16[512,128]{1,0:T(8,128)(2,1)S(1)} %get-tuple-element.32), channel_id=1, source_target_pairs={{0,4},{4,0},{8,12},{12,8},{16,20},{20,16},{24,28},{28,24},{1,5},{5... | collective-permute-start | bytes 393224 | tf_op jit(solution)/shard_map/ppermute | solution.py:492
  5.3 0.5 %tables.1 = (f32[16,16,128]{2,1,0:T(8,128)S(1)}, f32[16,256]{1,0:T(8,128)S(1)}, bf16[16,16,256]{2,1,0:T(8,128)(2,1)S(1)}) custom-call(f32[16,512]{1,0:T(8,128)S(1)} %bitcast.7, f32[16,512]{1,0:T(8,128)S(1)} %bitcast.10, f32[2,16,128]{2,1,0:T(8,128)S(1)} %get-tuple-element.26.refs_2_.refs_0_), custom_call_target="tpu_custom_call" | custom-call | flops 1000000000 | bytes 1000000 | tf_op jit(solution)/shard_map/tables/pallas_call | solution.py:509
  5.8 0.0 copy-start.5
  5.8 0.4 %collective-permute-done.refs_2_ = bf16[512,128]{1,0:T(8,128)(2,1)S(1)} collective-permute-done((bf16[512,128]{1,0:T(8,128)(2,1)S(1)}, bf16[512,128]{1,0:T(8,128)(2,1)S(1)}, u32[]{:S(2)}, u32[]{:S(2)}) %collective-permute-start) | collective-permute-done | bytes 131104 | tf_op jit(solution)/shard_map/ppermute | solution.py:492
  6.3 0.3 combine.3
  6.5 2.9 %collective-permute-start.1 = (bf16[576,128]{1,0:T(8,128)(2,1)S(1)}, bf16[576,128]{1,0:T(8,128)(2,1)S(1)}, u32[]{:S(2)}, u32[]{:S(2)}) collective-permute-start(bf16[576,128]{1,0:T(8,128)(2,1)S(1)} %get-tuple-element.33.refs_1_), channel_id=1, source_target_pairs={{0,8},{4,12},{8,0},{12,4},{16,24},{20,28},{24,16},{28,20},{1,9},{5... | collective-permute-start | bytes 442376 | tf_op jit(solution)/shard_map/ppermute | solution.py:492
  9.5 4.1 %lags.1.refs_3_ = bf16[96,128]{1,0:T(8,128)(2,1)S(1)} custom-call(f32[2,16,128]{2,1,0:T(8,128)S(1)} %get-tuple-element.26.refs_2_.refs_0_, bf16[128,2048]{1,0:T(8,128)(2,1)S(1)} %get-tuple-element.47.refs_2_.refs_1_.refs_5_, bf16[128,2048]{1,0:T(8,128)(2,1)S(1)} %get-tuple-element.46.refs_3_.refs_2_, ...), custom_call_target="tpu_custom_call" | custom-call | flops 536870912 | bytes 3145728 | tf_op jit(solution)/shard_map/lags/pallas_call | solution.py:524
  13.6 0.1 collective-permute-start.2
  13.7 3.8 %collective-permute-done.2.refs_4_ = bf16[96,128]{1,0:T(8,128)(2,1)S(1)} collective-permute-done((bf16[96,128]{1,0:T(8,128)(2,1)S(1)}, bf16[96,128]{1,0:T(8,128)(2,1)S(1)}, u32[]{:S(2)}, u32[]{:S(2)}) %collective-permute-start.2) | collective-permute-done | bytes 24608 | tf_op jit(solution)/shard_map/ppermute | solution.py:492
  17.5 0.0 collective-permute-done.1.refs_2_
  17.5 0.3 combine.4
  17.9 1.6 %collective-permute-start.3 = (bf16[352,128]{1,0:T(8,128)(2,1)S(1)}, bf16[352,128]{1,0:T(8,128)(2,1)S(1)}, u32[]{:S(2)}, u32[]{:S(2)}) collective-permute-start(bf16[352,128]{1,0:T(8,128)(2,1)S(1)} %get-tuple-element.37), channel_id=1, source_target_pairs={{0,16},{4,20},{8,24},{12,28},{16,0},{20,4},{24,8},{28,12},{1,17},{... | collective-permute-start | bytes 270344 | tf_op jit(solution)/shard_map/ppermute | solution.py:492
  19.4 0.0 copy-done.5
  19.4 2.8 %conv.1.refs_4_.refs_1_ = f32[128,4096]{1,0:T(8,128)S(1)} custom-call(f32[2,16,128]{2,1,0:T(8,128)S(1)} %get-tuple-element.26.refs_2_.refs_0_, f32[64,128]{1,0:T(8,128)S(1)} %bitcast.12, f32[16,16,128]{2,1,0:T(8,128)S(1)} %get-tuple-element.27.refs_0_.refs_2_, f32[16,256]{1,0:T(8,128)S(1)} %get-tuple-element.28.refs_3_, ...), custom_call_target="tpu_custom_call" | custom-call | flops 536870912 | bytes 3145728 | tf_op jit(solution)/shard_map/conv/pallas_call | solution.py:539
  22.3 0.0 copy-start
  22.3 0.0 copy-start.1
  22.3 0.0 copy-start.2
  22.3 0.2 collective-permute-done.3.refs_2_
  22.5 0.3 combine.5
  22.8 0.1 collective-permute-start.4
  22.8 1.3 %collective-permute-done.4.refs_3_ = bf16[352,128]{1,0:T(8,128)(2,1)S(1)} collective-permute-done((bf16[352,128]{1,0:T(8,128)(2,1)S(1)}, bf16[352,128]{1,0:T(8,128)(2,1)S(1)}, u32[]{:S(2)}, u32[]{:S(2)}) %collective-permute-start.4) | collective-permute-done | bytes 90144 | tf_op jit(solution)/shard_map/ppermute | solution.py:492
  24.1 3.7 %collective-permute-start.7 = (f32[48,128]{1,0:T(8,128)S(1)}, f32[48,128]{1,0:T(8,128)S(1)}, u32[]{:S(2)}, u32[]{:S(2)}) collective-permute-start(f32[48,128]{1,0:T(8,128)S(1)} %merge.1.refs_0_), channel_id=1, source_target_pairs={{0,3},{1,0},{2,1},{3,2},{4,7},{5,4},{6,5},{7,6},{8,11},{9,8},{10,9... | collective-permute-start | bytes 73736 | tf_op jit(solution)/shard_map/ppermute | solution.py:607
  27.8 0.0 collective-permute-start.6
  27.8 1.0 %collective-permute-start.5 = (f32[48,128]{1,0:T(8,128)S(1)}, f32[48,128]{1,0:T(8,128)S(1)}, u32[]{:S(2)}, u32[]{:S(2)}) collective-permute-start(f32[48,128]{1,0:T(8,128)S(1)} %merge.1.refs_0_), channel_id=1, source_target_pairs={{0,1},{1,2},{2,3},{3,0},{4,5},{5,6},{6,7},{7,4},{8,9},{9,10},{10,1... | collective-permute-start | bytes 73736 | tf_op jit(solution)/shard_map/ppermute | solution.py:607
  28.8 0.0 copy-done
  28.8 0.0 copy-done.1
  28.8 0.0 copy-done.2
  28.8 2.6 %outputs.1 = (bf16[128,2048]{1,0:T(8,128)(2,1)}, bf16[128,2048]{1,0:T(8,128)(2,1)}, bf16[128,2048]{1,0:T(8,128)(2,1)}) custom-call(f32[2,16,128]{2,1,0:T(8,128)S(1)} %get-tuple-element.26.refs_2_.refs_0_, f32[128,4096]{1,0:T(8,128)S(1)} %conv.1.refs_4_.refs_1_, bf16[8,32,128]{2,1,0:T(8,128)(2,1)S(1)} %get-tuple-element.38.refs_2_, ...), custom_call_target="tpu_custom_call" | custom-call | tf_op jit(solution)/shard_map/outputs/pallas_call | solution.py:609
  31.4 0.0 collective-permute-done.7.refs_3_
  31.4 1.2 %collective-permute-done.6.refs_2_ = f32[48,128]{1,0:T(8,128)S(1)} collective-permute-done((f32[48,128]{1,0:T(8,128)S(1)}, f32[48,128]{1,0:T(8,128)S(1)}, u32[]{:S(2)}, u32[]{:S(2)}) %collective-permute-start.6) | collective-permute-done | bytes 24608 | tf_op jit(solution)/shard_map/ppermute | solution.py:607
  32.6 0.8 %collective-permute-done.5.refs_1_ = f32[48,128]{1,0:T(8,128)S(1)} collective-permute-done((f32[48,128]{1,0:T(8,128)S(1)}, f32[48,128]{1,0:T(8,128)S(1)}, u32[]{:S(2)}, u32[]{:S(2)}) %collective-permute-start.5) | collective-permute-done | bytes 24608 | tf_op jit(solution)/shard_map/ppermute | solution.py:607
  33.4 0.6 %assemble.1 = (f32[16,512]{1,0:T(8,128)}, f32[16,512]{1,0:T(8,128)}, f32[64,128]{1,0:T(8,128)}) custom-call(f32[48,128]{1,0:T(8,128)S(1)} %merge.1.refs_0_, f32[48,128]{1,0:T(8,128)S(1)} %collective-permute-done.5.refs_1_, f32[48,128]{1,0:T(8,128)S(1)} %collective-permute-done.6.refs_2_, f32[48,128]{1,0:T(8,128)S(1)} %collective-permute-done.7.refs_3_), custom_call_target="tpu_custom_call" | custom-call | tf_op jit(solution)/shard_map/assemble/pallas_call | solution.py:619
  (1 shorter events, 0.0 us)
Async XLA Ops:
  0.6 1.9 %copy-start.3 = (f32[512,16]{0,1:T(8,128)S(1)}, f32[512,16]{0,1:T(8,128)}, u32[]{:S(2)}) copy-start(f32[512,16]{0,1:T(8,128)} %param.12) | copy-start | bytes 98308
  0.6 1.9 %copy-start.4 = (f32[512,16]{0,1:T(8,128)S(1)}, f32[512,16]{0,1:T(8,128)}, u32[]{:S(2)}) copy-start(f32[512,16]{0,1:T(8,128)} %param.11) | copy-start | bytes 98308
  4.8 1.5 %collective-permute-start = (bf16[512,128]{1,0:T(8,128)(2,1)S(1)}, bf16[512,128]{1,0:T(8,128)(2,1)S(1)}, u32[]{:S(2)}, u32[]{:S(2)}) collective-permute-start(bf16[512,128]{1,0:T(8,128)(2,1)S(1)} %get-tuple-element.32), channel_id=1, source_target_pairs={{0,4},{4,0},{8,12},{12,8},{16,20},{20,16},{24,28},{28,24},{1,5},{5... | collective-permute-start | bytes 393224 | tf_op jit(solution)/shard_map/ppermute | solution.py:492
  5.8 13.6 %copy-start.5 = (f32[8192]{0:T(1024)S(1)}, f32[8192]{0:T(1024)}, u32[]{:S(2)}) copy-start(f32[8192]{0:T(1024)} %param.13) | copy-start | bytes 98308
  6.5 11.0 %collective-permute-start.1 = (bf16[576,128]{1,0:T(8,128)(2,1)S(1)}, bf16[576,128]{1,0:T(8,128)(2,1)S(1)}, u32[]{:S(2)}, u32[]{:S(2)}) collective-permute-start(bf16[576,128]{1,0:T(8,128)(2,1)S(1)} %get-tuple-element.33.refs_1_), channel_id=1, source_target_pairs={{0,8},{4,12},{8,0},{12,4},{16,24},{20,28},{24,16},{28,20},{1,9},{5... | collective-permute-start | bytes 442376 | tf_op jit(solution)/shard_map/ppermute | solution.py:492
  13.6 3.9 %collective-permute-start.2 = (bf16[96,128]{1,0:T(8,128)(2,1)S(1)}, bf16[96,128]{1,0:T(8,128)(2,1)S(1)}, u32[]{:S(2)}, u32[]{:S(2)}) collective-permute-start(bf16[96,128]{1,0:T(8,128)(2,1)S(1)} %lags.1.refs_3_), channel_id=1, source_target_pairs={{0,8},{4,12},{8,0},{12,4},{16,24},{20,28},{24,16},{28,20},{1,9},{5... | collective-permute-start | bytes 73736 | tf_op jit(solution)/shard_map/ppermute | solution.py:492
  17.9 4.6 %collective-permute-start.3 = (bf16[352,128]{1,0:T(8,128)(2,1)S(1)}, bf16[352,128]{1,0:T(8,128)(2,1)S(1)}, u32[]{:S(2)}, u32[]{:S(2)}) collective-permute-start(bf16[352,128]{1,0:T(8,128)(2,1)S(1)} %get-tuple-element.37), channel_id=1, source_target_pairs={{0,16},{4,20},{8,24},{12,28},{16,0},{20,4},{24,8},{28,12},{1,17},{... | collective-permute-start | bytes 270344 | tf_op jit(solution)/shard_map/ppermute | solution.py:492
  22.3 6.6 %copy-start = (bf16[128,2048]{1,0:T(8,128)(2,1)S(1)}, bf16[128,2048]{1,0:T(8,128)(2,1)}, u32[]{:S(2)}) copy-start(bf16[128,2048]{1,0:T(8,128)(2,1)} %refs_6_.1) | copy-start | bytes 1572868
  22.3 6.6 %copy-start.1 = (bf16[128,2048]{1,0:T(8,128)(2,1)S(1)}, bf16[128,2048]{1,0:T(8,128)(2,1)}, u32[]{:S(2)}) copy-start(bf16[128,2048]{1,0:T(8,128)(2,1)} %refs_5_.1) | copy-start | bytes 1572868
  22.3 6.5 %copy-start.2 = (bf16[128,2048]{1,0:T(8,128)(2,1)S(1)}, bf16[128,2048]{1,0:T(8,128)(2,1)}, u32[]{:S(2)}) copy-start(bf16[128,2048]{1,0:T(8,128)(2,1)} %refs_4_.1) | copy-start | bytes 1572868
  22.8 1.4 %collective-permute-start.4 = (bf16[352,128]{1,0:T(8,128)(2,1)S(1)}, bf16[352,128]{1,0:T(8,128)(2,1)S(1)}, u32[]{:S(2)}, u32[]{:S(2)}) collective-permute-start(bf16[352,128]{1,0:T(8,128)(2,1)S(1)} %get-tuple-element.39.refs_2_), channel_id=1, source_target_pairs={{0,4},{4,0},{8,12},{12,8},{16,20},{20,16},{24,28},{28,24},{1,5},{5... | collective-permute-start | bytes 270344 | tf_op jit(solution)/shard_map/ppermute | solution.py:492
  24.1 7.3 %collective-permute-start.7 = (f32[48,128]{1,0:T(8,128)S(1)}, f32[48,128]{1,0:T(8,128)S(1)}, u32[]{:S(2)}, u32[]{:S(2)}) collective-permute-start(f32[48,128]{1,0:T(8,128)S(1)} %merge.1.refs_0_), channel_id=1, source_target_pairs={{0,3},{1,0},{2,1},{3,2},{4,7},{5,4},{6,5},{7,6},{8,11},{9,8},{10,9... | collective-permute-start | bytes 73736 | tf_op jit(solution)/shard_map/ppermute | solution.py:607
  27.8 4.8 %collective-permute-start.6 = (f32[48,128]{1,0:T(8,128)S(1)}, f32[48,128]{1,0:T(8,128)S(1)}, u32[]{:S(2)}, u32[]{:S(2)}) collective-permute-start(f32[48,128]{1,0:T(8,128)S(1)} %merge.1.refs_0_), channel_id=1, source_target_pairs={{0,2},{1,3},{2,0},{3,1},{4,6},{5,7},{6,4},{7,5},{8,10},{9,11},{10,... | collective-permute-start | bytes 73736 | tf_op jit(solution)/shard_map/ppermute | solution.py:607
  27.8 5.6 %collective-permute-start.5 = (f32[48,128]{1,0:T(8,128)S(1)}, f32[48,128]{1,0:T(8,128)S(1)}, u32[]{:S(2)}, u32[]{:S(2)}) collective-permute-start(f32[48,128]{1,0:T(8,128)S(1)} %merge.1.refs_0_), channel_id=1, source_target_pairs={{0,1},{1,2},{2,3},{3,0},{4,5},{5,6},{6,7},{7,4},{8,9},{9,10},{10,1... | collective-permute-start | bytes 73736 | tf_op jit(solution)/shard_map/ppermute | solution.py:607

commit v7 on v6

--- a/solution.py
+++ b/solution.py
@@ -133,12 +133,11 @@
         lax.fori_loop(0, half_blocks // inner, body, 0)
 
 
-def lags_kernel(rows_ref, gated_ref, dgate_ref, turned_ref, _, sums_ref, skip_ref, near_ref, *, group, poles, inner):
+def lags_kernel(rows_ref, gated_ref, dgate_ref, turned_ref, _, sums_ref, skip_ref, near_ref, lag_ref, *, group, poles):
     tokens, _ = gated_ref.shape
     per_block = LANES // group
     _, blocks, _ = rows_ref.shape
     groups = blocks * per_block
-    wide = inner * LANES
     back_pos = (tokens - 1 - iota((tokens, LANES), 0)).astype(F32)
     back_lane = (tokens - 1 - iota((per_block, tokens), 1)).astype(F32)
     lane_group = over(iota((tokens, LANES), 1), group)
@@ -146,46 +145,46 @@
     own_rows = iota((per_block, LANES), 0) == over(iota((per_block, LANES), 1), poles)
     half = per_block // 2
     zero = jnp.zeros((tokens, LANES), BF16)
-    lanes = [slice(j * LANES, (j + 1) * LANES) for j in range(inner)]
-
-    def body(step, carry):
-        start = step * inner
-        cut = pl.ds(pl.multiple_of(start * LANES, LANES), wide)
-        gated, turned = gated_ref[:, cut], turned_ref[:, cut]
-        skip = jnp.sum(gated.astype(F32) * dgate_ref[:, cut].astype(F32), axis=0, keepdims=True)
-        for j in range(inner):
-            skip_ref[pl.ds(start + j, 1), :] = skip[:, lanes[j]]
-        lows = [jnp.exp(-rows_ref[0, pl.ds(start + j, 1), :] * back_pos).astype(BF16) for j in range(inner)]
-        outers = []
-        for j in range(inner):
-            one, other = gated[:, lanes[j]], turned[:, lanes[j]]
-            left = [jnp.where((lane_group == i) | (lane_group == i + half), other, zero) for i in range(half)]
-            right = [jnp.where(lane_group < half, one, zero), jnp.where(lane_group >= half, one, zero)]
-            outers.append(mxu_t(jnp.concatenate(left, axis=0), jnp.concatenate(right, axis=0)))
-        for j in range(inner):
-            totals = []
-            for g in range(per_block):
-                i, h = g % half, g // half
-                tile = outers[j][i * tokens : (i + 1) * tokens, h * tokens : (h + 1) * tokens]
-                tile = jnp.where(causal, tile, 0.0)
-                total = None
-                for a in range(tokens // 8):
-                    shift = (8 * (a - g)) % tokens
-                    piece = tile[8 * a : 8 * a + 8]
-                    piece = pltpu.roll(piece, shift, 1) if shift else piece
-                    total = piece if total is None else total + piece
-                totals.append(total)
-            total = pltpu.roll(jnp.concatenate(totals, axis=0), 0, 1, stride=1, stride_axis=0)
-            lag = jnp.sum(total.reshape(per_block, 8, tokens), axis=1)
-            stack = jnp.concatenate([split(lag, 2), split(lag * back_lane, 2)], axis=0)
-            local = mxu(stack, lows[j])
-            for n in range(2):
-                part = join(local[2 * n * per_block : 2 * (n + 1) * per_block], per_block)
-                row = jnp.sum(jnp.where(own_rows, part, 0.0), axis=0, keepdims=True)
-                near_ref[n, pl.ds(start + j, 1), :] = row
-        return carry
-
-    lax.fori_loop(0, blocks // inner, body, 0)
+    lanes = [slice(b * LANES, (b + 1) * LANES) for b in range(blocks)]
+
+    def outer_of(b):
+        one, other = gated_ref[:, lanes[b]], turned_ref[:, lanes[b]]
+        left = [jnp.where((lane_group == i) | (lane_group == i + half), other, zero) for i in range(half)]
+        right = [jnp.where(lane_group < half, one, zero), jnp.where(lane_group >= half, one, zero)]
+        return mxu_t(jnp.concatenate(left, axis=0), jnp.concatenate(right, axis=0))
+
+    def diagonals(b, outer):
+        totals = []
+        for g in range(per_block):
+            i, h = g % half, g // half
+            total = None
+            for a in range(tokens // 8):
+                rows = slice(i * tokens + 8 * a, i * tokens + 8 * a + 8)
+                piece = jnp.where(causal[8 * a : 8 * a + 8], outer[rows, h * tokens : (h + 1) * tokens], 0.0)
+                shift = (8 * (a - g)) % tokens
+                piece = pltpu.roll(piece, shift, 1) if shift else piece
+                total = piece if total is None else total + piece
+            totals.append(total)
+        total = pltpu.roll(jnp.concatenate(totals, axis=0), 0, 1, stride=1, stride_axis=0)
+        lag_ref[b * per_block : (b + 1) * per_block, :] = jnp.sum(total.reshape(per_block, 8, tokens), axis=1)
+
+    ahead = outer_of(0)
+    for b in range(blocks):
+        outer, ahead = ahead, outer_of(b + 1) if b + 1 < blocks else None
+        diagonals(b, outer)
+    for b in range(blocks):
+        product = gated_ref[:, lanes[b]].astype(F32) * dgate_ref[:, lanes[b]].astype(F32)
+        skip_ref[b : b + 1, :] = jnp.sum(product, axis=0, keepdims=True)
+    locals_ = []
+    for b in range(blocks):
+        lag = lag_ref[b * per_block : (b + 1) * per_block, :]
+        stack = jnp.concatenate([split(lag, 2), split(lag * back_lane, 2)], axis=0)
+        low = jnp.exp(-rows_ref[0, b : b + 1, :] * back_pos).astype(BF16)
+        locals_.append(mxu(stack, low))
+    for b in range(blocks):
+        for n in range(2):
+            part = join(locals_[b][2 * n * per_block : 2 * (n + 1) * per_block], per_block)
+            near_ref[n, b : b + 1, :] = jnp.sum(jnp.where(own_rows, part, 0.0), axis=0, keepdims=True)
     pick = iota((poles, LANES), 0) == within(iota((poles, LANES), 1), poles)
     terms = []
     for b in range(blocks):
@@ -522,11 +521,15 @@
 
     def local_sums(after):
         return pl.pallas_call(
-            lambda *refs: lags_kernel(*refs, inner=inner, **sizes),
+            lambda *refs: lags_kernel(*refs, **sizes),
             in_specs=[vmem] * 4 + [anywhere],
             out_specs=vmem,
             out_shape=shape(tail, LANES, dtype=BF16),
-            scratch_shapes=[pltpu.VMEM((blocks, LANES), F32), pltpu.VMEM((2, blocks, LANES), F32)],
+            scratch_shapes=[
+                pltpu.VMEM((blocks, LANES), F32),
+                pltpu.VMEM((2, blocks, LANES), F32),
+                pltpu.VMEM((groups, tokens), F32),
+            ],
             compiler_params=PARAMS,
             cost_estimate=pl.CostEstimate(
                 flops=16 * tokens * tokens * width, bytes_accessed=12 * tokens * width, transcendentals=tokens * width

time: 34.2 us -> 33.6 us (0.982)
  Pallas kernels: 13.8 us -> 13.1 us
    pallas_call x1, Pallas kernels: 4.15 us -> 3.49 us  [local_sums(): pl.pallas_call(lambda *refs: lags_kernel(*refs, **sizes), in_specs=[vmem]...]
  transfers between devices with their start and end apart: 8 -> 8, of which waited for: 6 -> 6; matrix products, arithmetic and copies ran while one was open for 0% -> 0% of each run, Pallas kernels for 30% -> 28%
where the time goes in v7:
time: 33.6 us; the launch traced here: 33.4 us
  Pallas kernels  13.1 us (39%)
  starting transfers between devices  9.84 us (29%)
  waiting for transfers between devices  7.67 us (23%)
  other arithmetic  1.92 us (6%)
  between operations  0.81 us (2%)
    ppermute x5, waiting for transfers between devices, swap(): lax.ppermute(value, 'ctx', [(i, i ^ 1 << level) for i in range(parts)])  5.67 us
    ppermute x5, starting transfers between devices, swap(): lax.ppermute(value, 'ctx', [(i, i ^ 1 << level) for i in range(parts)])  5.17 us
    ppermute x3, starting transfers between devices, local(): lax.ppermute(merged, 'ch', [(i, (i + shift) % shards) for i in range(shar...  4.67 us
    pallas_call x1, Pallas kernels, local_sums(): pl.pallas_call(lambda *refs: lags_kernel(*refs, **sizes), in_specs=[vmem]...  3.49 us
    pallas_call x1, Pallas kernels, convolve(): pl.pallas_call(lambda *refs: conv_kernel(*refs, inner=inner, **sizes), in...  2.81 us
    pallas_call x1, Pallas kernels, local(): pl.pallas_call(lambda *refs: output_kernel(*refs, **sizes), grid=(steps,)...  2.6 us
    pallas_call x1, Pallas kernels, local(): pl.pallas_call(lambda *refs: states_kernel(*refs, inner=inner, **sizes),...  2.16 us
    ppermute x3, waiting for transfers between devices, local(): lax.ppermute(merged, 'ch', [(i, (i + shift) % shards) for i in range(shar...  2 us
  transfers between devices with their start and end apart: 8, of which 6 were waited for; matrix products, arithmetic and copies ran while one was open for 0% of the time, Pallas kernels for 28%

profile of v7, /device:TPU:0, one launch (start us, length us, event | category | flops | bytes accessed | tf_op | source)
XLA Modules:
  0.0 33.4 jit_solution(8016093719938506042)
XLA Ops:
  0.6 0.0 copy-start.3
  0.6 0.0 copy-start.4
  0.7 1.9 %multiply_convert_fusion = (bf16[128,2048]{1,0:T(8,128)(2,1)S(1)}, bf16[128,2048]{1,0:T(8,128)(2,1)S(1)}) fusion(bf16[128,2048]{1,0:T(8,128)(2,1)} %param.7, bf16[128,2048]{1,0:T(8,128)(2,1)} %refs_6_.1, bf16[128,2048]{1,0:T(8,128)(2,1)} %refs_5_.1, bf16[128,2048]{1,0:T(8,128)(2,1)} %refs_4_.1), kind=kLoop, calls=%fused_computation | loop fusion | flops 2097152 | bytes 3145728 | tf_op jit(solution)/shard_map/convert_element_type | solution.py:44
  2.6 0.0 copy-done.3
  2.6 0.0 copy-done.4
  2.6 2.2 %states.1 = (bf16[512,128]{1,0:T(8,128)(2,1)S(1)}, bf16[512,128]{1,0:T(8,128)(2,1)S(1)}, bf16[128,2048]{1,0:T(8,128)(2,1)S(1)}, f32[2,16,128]{2,1,0:T(8,128)S(1)}) custom-call(f32[16,512]{1,0:T(8,128)S(1)} %bitcast.6, f32[16,512]{1,0:T(8,128)S(1)} %bitcast.9, bf16[128,2048]{1,0:T(8,128)(2,1)S(1)} %get-tuple-element.47.refs_2_.refs_1_.refs_5_, ...), custom_call_target="tpu_custom_call" | custom-call | tf_op jit(solution)/shard_map/states/pallas_call | solution.py:494
  4.8 0.5 %collective-permute-start = (bf16[512,128]{1,0:T(8,128)(2,1)S(1)}, bf16[512,128]{1,0:T(8,128)(2,1)S(1)}, u32[]{:S(2)}, u32[]{:S(2)}) collective-permute-start(bf16[512,128]{1,0:T(8,128)(2,1)S(1)} %get-tuple-element.32), channel_id=1, source_target_pairs={{0,4},{4,0},{8,12},{12,8},{16,20},{20,16},{24,28},{28,24},{1,5},{5... | collective-permute-start | bytes 393224 | tf_op jit(solution)/shard_map/ppermute | solution.py:491
  5.3 0.5 %tables.1 = (f32[16,16,128]{2,1,0:T(8,128)S(1)}, f32[16,256]{1,0:T(8,128)S(1)}, bf16[16,16,256]{2,1,0:T(8,128)(2,1)S(1)}) custom-call(f32[16,512]{1,0:T(8,128)S(1)} %bitcast.7, f32[16,512]{1,0:T(8,128)S(1)} %bitcast.10, f32[2,16,128]{2,1,0:T(8,128)S(1)} %get-tuple-element.26.refs_2_.refs_0_), custom_call_target="tpu_custom_call" | custom-call | flops 1000000000 | bytes 1000000 | tf_op jit(solution)/shard_map/tables/pallas_call | solution.py:508
  5.8 0.0 copy-start.5
  5.8 0.4 %collective-permute-done.refs_2_ = bf16[512,128]{1,0:T(8,128)(2,1)S(1)} collective-permute-done((bf16[512,128]{1,0:T(8,128)(2,1)S(1)}, bf16[512,128]{1,0:T(8,128)(2,1)S(1)}, u32[]{:S(2)}, u32[]{:S(2)}) %collective-permute-start) | collective-permute-done | bytes 131104 | tf_op jit(solution)/shard_map/ppermute | solution.py:491
  6.3 0.3 combine.3
  6.5 2.9 %collective-permute-start.1 = (bf16[576,128]{1,0:T(8,128)(2,1)S(1)}, bf16[576,128]{1,0:T(8,128)(2,1)S(1)}, u32[]{:S(2)}, u32[]{:S(2)}) collective-permute-start(bf16[576,128]{1,0:T(8,128)(2,1)S(1)} %get-tuple-element.33.refs_1_), channel_id=1, source_target_pairs={{0,8},{4,12},{8,0},{12,4},{16,24},{20,28},{24,16},{28,20},{1,9},{5... | collective-permute-start | bytes 442376 | tf_op jit(solution)/shard_map/ppermute | solution.py:491
  9.5 3.5 %lags.1.refs_3_ = bf16[96,128]{1,0:T(8,128)(2,1)S(1)} custom-call(f32[2,16,128]{2,1,0:T(8,128)S(1)} %get-tuple-element.26.refs_2_.refs_0_, bf16[128,2048]{1,0:T(8,128)(2,1)S(1)} %get-tuple-element.47.refs_2_.refs_1_.refs_5_, bf16[128,2048]{1,0:T(8,128)(2,1)S(1)} %get-tuple-element.46.refs_3_.refs_2_, ...), custom_call_target="tpu_custom_call" | custom-call | flops 536870912 | bytes 3145728 | tf_op jit(solution)/shard_map/lags/pallas_call | solution.py:523
  12.9 0.1 collective-permute-start.2
  13.0 3.8 %collective-permute-done.2.refs_4_ = bf16[96,128]{1,0:T(8,128)(2,1)S(1)} collective-permute-done((bf16[96,128]{1,0:T(8,128)(2,1)S(1)}, bf16[96,128]{1,0:T(8,128)(2,1)S(1)}, u32[]{:S(2)}, u32[]{:S(2)}) %collective-permute-start.2) | collective-permute-done | bytes 24608 | tf_op jit(solution)/shard_map/ppermute | solution.py:491
  16.8 0.0 collective-permute-done.1.refs_2_
  16.8 0.3 %combine.4 = (bf16[608,128]{1,0:T(8,128)(2,1)S(1)}, f32[8,32,128]{2,1,0:T(8,128)S(1)}, bf16[352,128]{1,0:T(8,128)(2,1)S(1)}) custom-call(f32[16,16,128]{2,1,0:T(8,128)S(1)} %get-tuple-element.27.refs_0_.refs_2_, bf16[576,128]{1,0:T(8,128)(2,1)S(1)} %get-tuple-element.33.refs_1_, bf16[576,128]{1,0:T(8,128)(2,1)S(1)} %collective-permute-done.1.refs_2_, ...), custom_call_target="tpu_custom_call" | custom-call | tf_op jit(solution)/shard_map/combine/pallas_call | solution.py:581
  17.2 1.6 %collective-permute-start.3 = (bf16[352,128]{1,0:T(8,128)(2,1)S(1)}, bf16[352,128]{1,0:T(8,128)(2,1)S(1)}, u32[]{:S(2)}, u32[]{:S(2)}) collective-permute-start(bf16[352,128]{1,0:T(8,128)(2,1)S(1)} %get-tuple-element.37), channel_id=1, source_target_pairs={{0,16},{4,20},{8,24},{12,28},{16,0},{20,4},{24,8},{28,12},{1,17},{... | collective-permute-start | bytes 270344 | tf_op jit(solution)/shard_map/ppermute | solution.py:491
  18.8 0.0 copy-done.5
  18.8 2.8 %conv.1.refs_4_.refs_1_ = f32[128,4096]{1,0:T(8,128)S(1)} custom-call(f32[2,16,128]{2,1,0:T(8,128)S(1)} %get-tuple-element.26.refs_2_.refs_0_, f32[64,128]{1,0:T(8,128)S(1)} %bitcast.12, f32[16,16,128]{2,1,0:T(8,128)S(1)} %get-tuple-element.27.refs_0_.refs_2_, f32[16,256]{1,0:T(8,128)S(1)} %get-tuple-element.28.refs_3_, ...), custom_call_target="tpu_custom_call" | custom-call | flops 536870912 | bytes 3145728 | tf_op jit(solution)/shard_map/conv/pallas_call | solution.py:542
  21.6 0.0 copy-start
  21.6 0.0 copy-start.1
  21.6 0.0 copy-start.2
  21.6 0.2 collective-permute-done.3.refs_2_
  21.8 0.3 combine.5
  22.1 0.1 collective-permute-start.4
  22.2 1.3 %collective-permute-done.4.refs_3_ = bf16[352,128]{1,0:T(8,128)(2,1)S(1)} collective-permute-done((bf16[352,128]{1,0:T(8,128)(2,1)S(1)}, bf16[352,128]{1,0:T(8,128)(2,1)S(1)}, u32[]{:S(2)}, u32[]{:S(2)}) %collective-permute-start.4) | collective-permute-done | bytes 90144 | tf_op jit(solution)/shard_map/ppermute | solution.py:491
  23.5 3.7 %collective-permute-start.7 = (f32[48,128]{1,0:T(8,128)S(1)}, f32[48,128]{1,0:T(8,128)S(1)}, u32[]{:S(2)}, u32[]{:S(2)}) collective-permute-start(f32[48,128]{1,0:T(8,128)S(1)} %merge.1.refs_0_), channel_id=1, source_target_pairs={{0,3},{1,0},{2,1},{3,2},{4,7},{5,4},{6,5},{7,6},{8,11},{9,8},{10,9... | collective-permute-start | bytes 73736 | tf_op jit(solution)/shard_map/ppermute | solution.py:610
  27.1 0.0 collective-permute-start.6
  27.1 1.0 %collective-permute-start.5 = (f32[48,128]{1,0:T(8,128)S(1)}, f32[48,128]{1,0:T(8,128)S(1)}, u32[]{:S(2)}, u32[]{:S(2)}) collective-permute-start(f32[48,128]{1,0:T(8,128)S(1)} %merge.1.refs_0_), channel_id=1, source_target_pairs={{0,1},{1,2},{2,3},{3,0},{4,5},{5,6},{6,7},{7,4},{8,9},{9,10},{10,1... | collective-permute-start | bytes 73736 | tf_op jit(solution)/shard_map/ppermute | solution.py:610
  28.1 0.0 copy-done
  28.1 0.0 copy-done.1
  28.1 0.0 copy-done.2
  28.1 2.6 %outputs.1 = (bf16[128,2048]{1,0:T(8,128)(2,1)}, bf16[128,2048]{1,0:T(8,128)(2,1)}, bf16[128,2048]{1,0:T(8,128)(2,1)}) custom-call(f32[2,16,128]{2,1,0:T(8,128)S(1)} %get-tuple-element.26.refs_2_.refs_0_, f32[128,4096]{1,0:T(8,128)S(1)} %conv.1.refs_4_.refs_1_, bf16[8,32,128]{2,1,0:T(8,128)(2,1)S(1)} %get-tuple-element.38.refs_2_, ...), custom_call_target="tpu_custom_call" | custom-call | tf_op jit(solution)/shard_map/outputs/pallas_call | solution.py:612
  30.7 0.0 collective-permute-done.7.refs_3_
  30.8 1.2 %collective-permute-done.6.refs_2_ = f32[48,128]{1,0:T(8,128)S(1)} collective-permute-done((f32[48,128]{1,0:T(8,128)S(1)}, f32[48,128]{1,0:T(8,128)S(1)}, u32[]{:S(2)}, u32[]{:S(2)}) %collective-permute-start.6) | collective-permute-done | bytes 24608 | tf_op jit(solution)/shard_map/ppermute | solution.py:610
  31.9 0.8 %collective-permute-done.5.refs_1_ = f32[48,128]{1,0:T(8,128)S(1)} collective-permute-done((f32[48,128]{1,0:T(8,128)S(1)}, f32[48,128]{1,0:T(8,128)S(1)}, u32[]{:S(2)}, u32[]{:S(2)}) %collective-permute-start.5) | collective-permute-done | bytes 24608 | tf_op jit(solution)/shard_map/ppermute | solution.py:610
  32.8 0.6 %assemble.1 = (f32[16,512]{1,0:T(8,128)}, f32[16,512]{1,0:T(8,128)}, f32[64,128]{1,0:T(8,128)}) custom-call(f32[48,128]{1,0:T(8,128)S(1)} %merge.1.refs_0_, f32[48,128]{1,0:T(8,128)S(1)} %collective-permute-done.5.refs_1_, f32[48,128]{1,0:T(8,128)S(1)} %collective-permute-done.6.refs_2_, f32[48,128]{1,0:T(8,128)S(1)} %collective-permute-done.7.refs_3_), custom_call_target="tpu_custom_call" | custom-call | tf_op jit(solution)/shard_map/assemble/pallas_call | solution.py:622
  (1 shorter events, 0.0 us)
Async XLA Ops:
  0.6 1.9 %copy-start.3 = (f32[512,16]{0,1:T(8,128)S(1)}, f32[512,16]{0,1:T(8,128)}, u32[]{:S(2)}) copy-start(f32[512,16]{0,1:T(8,128)} %param.12) | copy-start | bytes 98308
  0.6 1.9 %copy-start.4 = (f32[512,16]{0,1:T(8,128)S(1)}, f32[512,16]{0,1:T(8,128)}, u32[]{:S(2)}) copy-start(f32[512,16]{0,1:T(8,128)} %param.11) | copy-start | bytes 98308
  4.8 1.5 %collective-permute-start = (bf16[512,128]{1,0:T(8,128)(2,1)S(1)}, bf16[512,128]{1,0:T(8,128)(2,1)S(1)}, u32[]{:S(2)}, u32[]{:S(2)}) collective-permute-start(bf16[512,128]{1,0:T(8,128)(2,1)S(1)} %get-tuple-element.32), channel_id=1, source_target_pairs={{0,4},{4,0},{8,12},{12,8},{16,20},{20,16},{24,28},{28,24},{1,5},{5... | collective-permute-start | bytes 393224 | tf_op jit(solution)/shard_map/ppermute | solution.py:491
  5.8 12.9 %copy-start.5 = (f32[8192]{0:T(1024)S(1)}, f32[8192]{0:T(1024)}, u32[]{:S(2)}) copy-start(f32[8192]{0:T(1024)} %param.13) | copy-start | bytes 98308
  6.5 10.3 %collective-permute-start.1 = (bf16[576,128]{1,0:T(8,128)(2,1)S(1)}, bf16[576,128]{1,0:T(8,128)(2,1)S(1)}, u32[]{:S(2)}, u32[]{:S(2)}) collective-permute-start(bf16[576,128]{1,0:T(8,128)(2,1)S(1)} %get-tuple-element.33.refs_1_), channel_id=1, source_target_pairs={{0,8},{4,12},{8,0},{12,4},{16,24},{20,28},{24,16},{28,20},{1,9},{5... | collective-permute-start | bytes 442376 | tf_op jit(solution)/shard_map/ppermute | solution.py:491
  12.9 3.9 %collective-permute-start.2 = (bf16[96,128]{1,0:T(8,128)(2,1)S(1)}, bf16[96,128]{1,0:T(8,128)(2,1)S(1)}, u32[]{:S(2)}, u32[]{:S(2)}) collective-permute-start(bf16[96,128]{1,0:T(8,128)(2,1)S(1)} %lags.1.refs_3_), channel_id=1, source_target_pairs={{0,8},{4,12},{8,0},{12,4},{16,24},{20,28},{24,16},{28,20},{1,9},{5... | collective-permute-start | bytes 73736 | tf_op jit(solution)/shard_map/ppermute | solution.py:491
  17.2 4.6 %collective-permute-start.3 = (bf16[352,128]{1,0:T(8,128)(2,1)S(1)}, bf16[352,128]{1,0:T(8,128)(2,1)S(1)}, u32[]{:S(2)}, u32[]{:S(2)}) collective-permute-start(bf16[352,128]{1,0:T(8,128)(2,1)S(1)} %get-tuple-element.37), channel_id=1, source_target_pairs={{0,16},{4,20},{8,24},{12,28},{16,0},{20,4},{24,8},{28,12},{1,17},{... | collective-permute-start | bytes 270344 | tf_op jit(solution)/shard_map/ppermute | solution.py:491
  21.6 6.6 %copy-start = (bf16[128,2048]{1,0:T(8,128)(2,1)S(1)}, bf16[128,2048]{1,0:T(8,128)(2,1)}, u32[]{:S(2)}) copy-start(bf16[128,2048]{1,0:T(8,128)(2,1)} %refs_6_.1) | copy-start | bytes 1572868
  21.6 6.5 %copy-start.1 = (bf16[128,2048]{1,0:T(8,128)(2,1)S(1)}, bf16[128,2048]{1,0:T(8,128)(2,1)}, u32[]{:S(2)}) copy-start(bf16[128,2048]{1,0:T(8,128)(2,1)} %refs_5_.1) | copy-start | bytes 1572868
  21.6 6.5 %copy-start.2 = (bf16[128,2048]{1,0:T(8,128)(2,1)S(1)}, bf16[128,2048]{1,0:T(8,128)(2,1)}, u32[]{:S(2)}) copy-start(bf16[128,2048]{1,0:T(8,128)(2,1)} %refs_4_.1) | copy-start | bytes 1572868
  22.1 1.4 %collective-permute-start.4 = (bf16[352,128]{1,0:T(8,128)(2,1)S(1)}, bf16[352,128]{1,0:T(8,128)(2,1)S(1)}, u32[]{:S(2)}, u32[]{:S(2)}) collective-permute-start(bf16[352,128]{1,0:T(8,128)(2,1)S(1)} %get-tuple-element.39.refs_2_), channel_id=1, source_target_pairs={{0,4},{4,0},{8,12},{12,8},{16,20},{20,16},{24,28},{28,24},{1,5},{5... | collective-permute-start | bytes 270344 | tf_op jit(solution)/shard_map/ppermute | solution.py:491
  23.5 7.3 %collective-permute-start.7 = (f32[48,128]{1,0:T(8,128)S(1)}, f32[48,128]{1,0:T(8,128)S(1)}, u32[]{:S(2)}, u32[]{:S(2)}) collective-permute-start(f32[48,128]{1,0:T(8,128)S(1)} %merge.1.refs_0_), channel_id=1, source_target_pairs={{0,3},{1,0},{2,1},{3,2},{4,7},{5,4},{6,5},{7,6},{8,11},{9,8},{10,9... | collective-permute-start | bytes 73736 | tf_op jit(solution)/shard_map/ppermute | solution.py:610
  27.1 4.8 %collective-permute-start.6 = (f32[48,128]{1,0:T(8,128)S(1)}, f32[48,128]{1,0:T(8,128)S(1)}, u32[]{:S(2)}, u32[]{:S(2)}) collective-permute-start(f32[48,128]{1,0:T(8,128)S(1)} %merge.1.refs_0_), channel_id=1, source_target_pairs={{0,2},{1,3},{2,0},{3,1},{4,6},{5,7},{6,4},{7,5},{8,10},{9,11},{10,... | collective-permute-start | bytes 73736 | tf_op jit(solution)/shard_map/ppermute | solution.py:610
  27.1 5.6 %collective-permute-start.5 = (f32[48,128]{1,0:T(8,128)S(1)}, f32[48,128]{1,0:T(8,128)S(1)}, u32[]{:S(2)}, u32[]{:S(2)}) collective-permute-start(f32[48,128]{1,0:T(8,128)S(1)} %merge.1.refs_0_), channel_id=1, source_target_pairs={{0,1},{1,2},{2,3},{3,0},{4,5},{5,6},{6,7},{7,4},{8,9},{9,10},{10,1... | collective-permute-start | bytes 73736 | tf_op jit(solution)/shard_map/ppermute | solution.py:610

commit v8 on v6

--- a/solution.py
+++ b/solution.py
@@ -133,70 +133,65 @@
         lax.fori_loop(0, half_blocks // inner, body, 0)
 
 
-def lags_kernel(rows_ref, gated_ref, dgate_ref, turned_ref, _, sums_ref, skip_ref, near_ref, *, group, poles, inner):
+def lags_kernel(lag_rates_ref, gated_ref, dgate_ref, turned_ref, _, sums_ref, skip_ref, *, group, poles, inner):
     tokens, _ = gated_ref.shape
     per_block = LANES // group
-    _, blocks, _ = rows_ref.shape
-    groups = blocks * per_block
-    wide = inner * LANES
-    back_pos = (tokens - 1 - iota((tokens, LANES), 0)).astype(F32)
-    back_lane = (tokens - 1 - iota((per_block, tokens), 1)).astype(F32)
-    lane_group = over(iota((tokens, LANES), 1), group)
-    causal = iota((tokens, tokens), 0) + iota((tokens, tokens), 1) <= tokens - 1
-    own_rows = iota((per_block, LANES), 0) == over(iota((per_block, LANES), 1), poles)
-    half = per_block // 2
-    zero = jnp.zeros((tokens, LANES), BF16)
-    lanes = [slice(j * LANES, (j + 1) * LANES) for j in range(inner)]
-
-    def body(step, carry):
-        start = step * inner
-        cut = pl.ds(pl.multiple_of(start * LANES, LANES), wide)
-        gated, turned = gated_ref[:, cut], turned_ref[:, cut]
-        skip = jnp.sum(gated.astype(F32) * dgate_ref[:, cut].astype(F32), axis=0, keepdims=True)
-        for j in range(inner):
-            skip_ref[pl.ds(start + j, 1), :] = skip[:, lanes[j]]
-        lows = [jnp.exp(-rows_ref[0, pl.ds(start + j, 1), :] * back_pos).astype(BF16) for j in range(inner)]
+    blocks, _, lag_width = lag_rates_ref.shape
+    subs = tokens // SUB
+    step_groups = inner * per_block
+    lane_group = over(iota((SUB, LANES), 1), group)
+    row, lane = iota((SUB, lag_width), 0), within(iota((SUB, lag_width), 1), SUB)
+    near_side, no_wrap = row + lane <= SUB - 1, lane >= row
+    lag = (SUB - 1 - within(iota((poles, lag_width), 1), SUB)).astype(F32)
+    spread = members(step_groups, 0, SUB, inner * lag_width)
+    sums = []
+    for step in range(blocks // inner):
         outers = []
         for j in range(inner):
-            one, other = gated[:, lanes[j]], turned[:, lanes[j]]
-            left = [jnp.where((lane_group == i) | (lane_group == i + half), other, zero) for i in range(half)]
-            right = [jnp.where(lane_group < half, one, zero), jnp.where(lane_group >= half, one, zero)]
-            outers.append(mxu_t(jnp.concatenate(left, axis=0), jnp.concatenate(right, axis=0)))
+            lanes = slice((step * inner + j) * LANES, (step * inner + j + 1) * LANES)
+            found = [None] * subs
+            for k in range(subs):
+                part = gated_ref[k * SUB : (k + 1) * SUB, lanes]
+                stack = jnp.concatenate(
+                    [jnp.where(lane_group == g, part, jnp.zeros_like(part)) for g in range(per_block)], axis=0
+                )
+                outer = mxu_t(turned_ref[: (subs - k) * SUB, lanes], stack)
+                for n in range(subs - k):
+                    far = subs - 1 - k - n
+                    piece = outer[n * SUB : (n + 1) * SUB]
+                    found[far] = piece if found[far] is None else found[far] + piece
+            outers.append(found)
+        terms = []
         for j in range(inner):
-            totals = []
-            for g in range(per_block):
-                i, h = g % half, g // half
-                tile = outers[j][i * tokens : (i + 1) * tokens, h * tokens : (h + 1) * tokens]
-                tile = jnp.where(causal, tile, 0.0)
-                total = None
-                for a in range(tokens // 8):
-                    shift = (8 * (a - g)) % tokens
-                    piece = tile[8 * a : 8 * a + 8]
-                    piece = pltpu.roll(piece, shift, 1) if shift else piece
-                    total = piece if total is None else total + piece
-                totals.append(total)
-            total = pltpu.roll(jnp.concatenate(totals, axis=0), 0, 1, stride=1, stride_axis=0)
-            lag = jnp.sum(total.reshape(per_block, 8, tokens), axis=1)
-            stack = jnp.concatenate([split(lag, 2), split(lag * back_lane, 2)], axis=0)
-            local = mxu(stack, lows[j])
-            for n in range(2):
-                part = join(local[2 * n * per_block : 2 * (n + 1) * per_block], per_block)
-                row = jnp.sum(jnp.where(own_rows, part, 0.0), axis=0, keepdims=True)
-                near_ref[n, pl.ds(start + j, 1), :] = row
-        return carry
-
-    lax.fori_loop(0, blocks // inner, body, 0)
-    pick = iota((poles, LANES), 0) == within(iota((poles, LANES), 1), poles)
-    terms = []
+            found = outers[j] + [jnp.zeros((SUB, lag_width), F32)]
+            lags = []
+            for far in range(subs):
+                total = jnp.where(near_side, found[far], found[far + 1])
+                straight = pltpu.roll(total, 0, 1, stride=1, stride_axis=0)
+                wrapped = pltpu.roll(total, lag_width - SUB, 1, stride=1, stride_axis=0)
+                lags.append(jnp.sum(jnp.where(no_wrap, straight, wrapped), axis=0, keepdims=True))
+            rate = lag_rates_ref[step * inner + j]
+            decay = jnp.exp(-rate * SUB)
+            total = jnp.zeros((poles, lag_width), F32)
+            weighted = total
+            for far in reversed(range(subs)):
+                weighted = decay * weighted + far * lags[far]
+                total = decay * total + lags[far]
+            table = jnp.exp(-rate * lag)
+            terms.append(
+                split(jnp.concatenate([table * total, table * (lag * total + SUB * weighted)], axis=0), 2)
+            )
+        sums.append(mxu_t(jnp.concatenate(terms, axis=1), spread))
     for b in range(blocks):
-        near = [jnp.where(pick, near_ref[n, b : b + 1, :], 0.0) for n in range(2)]
-        terms.append(split(jnp.concatenate(near, axis=0), 2))
-    sums = mxu_t(jnp.concatenate(terms, axis=1), members(groups, 0, poles, blocks * LANES))
+        lanes = slice(b * LANES, (b + 1) * LANES)
+        product = gated_ref[:, lanes].astype(F32) * dgate_ref[:, lanes].astype(F32)
+        skip_ref[b : b + 1, :] = jnp.sum(product, axis=0, keepdims=True)
+    sums = jnp.concatenate(sums, axis=1)
     sums_ref[: 4 * poles, :] = split(join(sums, 2 * poles), 2)
     sums_ref[4 * poles :, :] = split(skip_ref[...], 2)
 
 
-def tables_kernel(logs_ref, res_ref, _, rates_ref, taps_ref, tables_ref, *, group, poles, inner):
+def tables_kernel(logs_ref, res_ref, _, rates_ref, lag_rates_ref, taps_ref, tables_ref, *, group, poles, inner):
     blocks, _, lag_width = tables_ref.shape
     per_block = LANES // group
     groups = blocks * per_block
@@ -220,6 +215,7 @@
             here = step * inner + j
             lanes = slice(j * lag_width, (j + 1) * lag_width)
             rates_ref[here] = rate[:, j * LANES : (j + 1) * LANES]
+            lag_rates_ref[here] = rates[:, lanes]
             taps_ref[here : here + 1, :] = taps[:, lanes]
             tables_ref[here] = table[:, lanes]
 
@@ -506,12 +502,13 @@
         name="states",
     )(log_rates, residues, gated, dgate)
 
-    rates, taps, tables = pl.pallas_call(
+    rates, lag_rates, taps, tables = pl.pallas_call(
         lambda *refs: tables_kernel(*refs, inner=inner, **sizes),
         in_specs=[vmem, vmem, anywhere],
-        out_specs=[vmem] * 3,
+        out_specs=[vmem] * 4,
         out_shape=[
             shape(blocks, poles, LANES),
+            shape(blocks, poles, lag_width),
             shape(blocks, lag_width),
             shape(blocks, poles, lag_width, dtype=BF16),
         ],
@@ -526,13 +523,13 @@
             in_specs=[vmem] * 4 + [anywhere],
             out_specs=vmem,
             out_shape=shape(tail, LANES, dtype=BF16),
-            scratch_shapes=[pltpu.VMEM((blocks, LANES), F32), pltpu.VMEM((2, blocks, LANES), F32)],
+            scratch_shapes=[pltpu.VMEM((blocks, LANES), F32)],
             compiler_params=PARAMS,
             cost_estimate=pl.CostEstimate(
                 flops=16 * tokens * tokens * width, bytes_accessed=12 * tokens * width, transcendentals=tokens * width
             ),
             name="lags",
-        )(rows, gated, dgate, turned, after)
+        )(lag_rates, gated, dgate, turned, after)
 
     def convolve(after):
         skip_rows = skip_gain.reshape(-1, LANES)

time: 34.2 us -> 32.6 us (0.953)
  Pallas kernels: 13.8 us -> 12.2 us
    pallas_call x1, Pallas kernels: 4.15 us -> 2.51 us  [local_sums(): pl.pallas_call(lambda *refs: lags_kernel(*refs, inner=inner, **sizes), in...]
  transfers between devices with their start and end apart: 8 -> 8, of which waited for: 6 -> 6; matrix products, arithmetic and copies ran while one was open for 0% -> 0% of each run, Pallas kernels for 30% -> 26%
where the time goes in v8:
time: 32.6 us; the launch traced here: 32.4 us
  Pallas kernels  12.2 us (37%)
  starting transfers between devices  9.84 us (30%)
  waiting for transfers between devices  7.68 us (24%)
  other arithmetic  1.91 us (6%)
  between operations  0.81 us (2%)
    ppermute x5, waiting for transfers between devices, swap(): lax.ppermute(value, 'ctx', [(i, i ^ 1 << level) for i in range(parts)])  5.67 us
    ppermute x5, starting transfers between devices, swap(): lax.ppermute(value, 'ctx', [(i, i ^ 1 << level) for i in range(parts)])  5.17 us
    ppermute x3, starting transfers between devices, local(): lax.ppermute(merged, 'ch', [(i, (i + shift) % shards) for i in range(shar...  4.67 us
    pallas_call x1, Pallas kernels, convolve(): pl.pallas_call(lambda *refs: conv_kernel(*refs, inner=inner, **sizes), in...  2.8 us
    pallas_call x1, Pallas kernels, local(): pl.pallas_call(lambda *refs: output_kernel(*refs, **sizes), grid=(steps,)...  2.6 us
    pallas_call x1, Pallas kernels, local_sums(): pl.pallas_call(lambda *refs: lags_kernel(*refs, inner=inner, **sizes), in...  2.51 us
    pallas_call x1, Pallas kernels, local(): pl.pallas_call(lambda *refs: states_kernel(*refs, inner=inner, **sizes),...  2.16 us
    ppermute x3, waiting for transfers between devices, local(): lax.ppermute(merged, 'ch', [(i, (i + shift) % shards) for i in range(shar...  2 us
  transfers between devices with their start and end apart: 8, of which 6 were waited for; matrix products, arithmetic and copies ran while one was open for 0% of the time, Pallas kernels for 26%

profile of v8, /device:TPU:0, one launch (start us, length us, event | category | flops | bytes accessed | tf_op | source)
XLA Modules:
  0.0 32.4 jit_solution(11894436717979199302)
XLA Ops:
  0.6 0.0 copy-start.3
  0.6 0.0 copy-start.4
  0.7 1.9 %multiply_convert_fusion = (bf16[128,2048]{1,0:T(8,128)(2,1)S(1)}, bf16[128,2048]{1,0:T(8,128)(2,1)S(1)}) fusion(bf16[128,2048]{1,0:T(8,128)(2,1)} %param.7, bf16[128,2048]{1,0:T(8,128)(2,1)} %refs_6_.1, bf16[128,2048]{1,0:T(8,128)(2,1)} %refs_5_.1, bf16[128,2048]{1,0:T(8,128)(2,1)} %refs_4_.1), kind=kLoop, calls=%fused_computation | loop fusion | flops 2097152 | bytes 3145728 | tf_op jit(solution)/shard_map/convert_element_type | solution.py:44
  2.6 0.0 copy-done.3
  2.6 0.0 copy-done.4
  2.6 2.2 %states.1 = (bf16[512,128]{1,0:T(8,128)(2,1)S(1)}, bf16[512,128]{1,0:T(8,128)(2,1)S(1)}, bf16[128,2048]{1,0:T(8,128)(2,1)S(1)}, f32[2,16,128]{2,1,0:T(8,128)S(1)}) custom-call(f32[16,512]{1,0:T(8,128)S(1)} %bitcast.6, f32[16,512]{1,0:T(8,128)S(1)} %bitcast.9, bf16[128,2048]{1,0:T(8,128)(2,1)S(1)} %get-tuple-element.49.refs_2_.refs_1_.refs_5_, ...), custom_call_target="tpu_custom_call" | custom-call | tf_op jit(solution)/shard_map/states/pallas_call | solution.py:491
  4.8 0.5 %collective-permute-start = (bf16[512,128]{1,0:T(8,128)(2,1)S(1)}, bf16[512,128]{1,0:T(8,128)(2,1)S(1)}, u32[]{:S(2)}, u32[]{:S(2)}) collective-permute-start(bf16[512,128]{1,0:T(8,128)(2,1)S(1)} %get-tuple-element.33), channel_id=1, source_target_pairs={{0,4},{4,0},{8,12},{12,8},{16,20},{20,16},{24,28},{28,24},{1,5},{5... | collective-permute-start | bytes 393224 | tf_op jit(solution)/shard_map/ppermute | solution.py:488
  5.3 0.5 %tables.1 = (f32[16,16,128]{2,1,0:T(8,128)S(1)}, f32[16,16,256]{2,1,0:T(8,128)S(1)}, f32[16,256]{1,0:T(8,128)S(1)}, bf16[16,16,256]{2,1,0:T(8,128)(2,1)S(1)}) custom-call(f32[16,512]{1,0:T(8,128)S(1)} %bitcast.7, f32[16,512]{1,0:T(8,128)S(1)} %bitcast.10, f32[2,16,128]{2,1,0:T(8,128)S(1)} %get-tuple-element.27.refs_2_.refs_0_), custom_call_target="tpu_custom_call" | custom-call | flops 1000000000 | bytes 1000000 | tf_op jit(solution)/shard_map/tables/pallas_call | solution.py:505
  5.8 0.0 copy-start.5
  5.8 0.4 %collective-permute-done.refs_2_ = bf16[512,128]{1,0:T(8,128)(2,1)S(1)} collective-permute-done((bf16[512,128]{1,0:T(8,128)(2,1)S(1)}, bf16[512,128]{1,0:T(8,128)(2,1)S(1)}, u32[]{:S(2)}, u32[]{:S(2)}) %collective-permute-start) | collective-permute-done | bytes 131104 | tf_op jit(solution)/shard_map/ppermute | solution.py:488
  6.3 0.3 combine.3
  6.5 2.9 %collective-permute-start.1 = (bf16[576,128]{1,0:T(8,128)(2,1)S(1)}, bf16[576,128]{1,0:T(8,128)(2,1)S(1)}, u32[]{:S(2)}, u32[]{:S(2)}) collective-permute-start(bf16[576,128]{1,0:T(8,128)(2,1)S(1)} %get-tuple-element.34.refs_1_), channel_id=1, source_target_pairs={{0,8},{4,12},{8,0},{12,4},{16,24},{20,28},{24,16},{28,20},{1,9},{5... | collective-permute-start | bytes 442376 | tf_op jit(solution)/shard_map/ppermute | solution.py:488
  9.5 2.5 %lags.1.refs_3_ = bf16[96,128]{1,0:T(8,128)(2,1)S(1)} custom-call(f32[16,16,256]{2,1,0:T(8,128)S(1)} %get-tuple-element.35.refs_0_, bf16[128,2048]{1,0:T(8,128)(2,1)S(1)} %get-tuple-element.49.refs_2_.refs_1_.refs_5_, bf16[128,2048]{1,0:T(8,128)(2,1)S(1)} %get-tuple-element.48.refs_3_.refs_2_, bf16[128,2048]{1,0:T(8,128)(2,1)S(1)} %get-tuple-element.31.refs_3_.refs_6_, ...), custom_call_target="tpu_custom_call" | custom-call | flops 536870912 | bytes 3145728 | tf_op jit(solution)/shard_map/lags/pallas_call | solution.py:521
  12.0 0.1 collective-permute-start.2
  12.0 3.8 %collective-permute-done.2.refs_4_ = bf16[96,128]{1,0:T(8,128)(2,1)S(1)} collective-permute-done((bf16[96,128]{1,0:T(8,128)(2,1)S(1)}, bf16[96,128]{1,0:T(8,128)(2,1)S(1)}, u32[]{:S(2)}, u32[]{:S(2)}) %collective-permute-start.2) | collective-permute-done | bytes 24608 | tf_op jit(solution)/shard_map/ppermute | solution.py:488
  15.9 0.0 collective-permute-done.1.refs_2_
  15.9 0.3 %combine.4 = (bf16[608,128]{1,0:T(8,128)(2,1)S(1)}, f32[8,32,128]{2,1,0:T(8,128)S(1)}, bf16[352,128]{1,0:T(8,128)(2,1)S(1)}) custom-call(f32[16,16,128]{2,1,0:T(8,128)S(1)} %get-tuple-element.28.refs_0_.refs_2_, bf16[576,128]{1,0:T(8,128)(2,1)S(1)} %get-tuple-element.34.refs_1_, bf16[576,128]{1,0:T(8,128)(2,1)S(1)} %collective-permute-done.1.refs_2_, ...), custom_call_target="tpu_custom_call" | custom-call | tf_op jit(solution)/shard_map/combine/pallas_call | solution.py:575
  16.2 1.6 %collective-permute-start.3 = (bf16[352,128]{1,0:T(8,128)(2,1)S(1)}, bf16[352,128]{1,0:T(8,128)(2,1)S(1)}, u32[]{:S(2)}, u32[]{:S(2)}) collective-permute-start(bf16[352,128]{1,0:T(8,128)(2,1)S(1)} %get-tuple-element.39), channel_id=1, source_target_pairs={{0,16},{4,20},{8,24},{12,28},{16,0},{20,4},{24,8},{28,12},{1,17},{... | collective-permute-start | bytes 270344 | tf_op jit(solution)/shard_map/ppermute | solution.py:488
  17.8 0.0 copy-done.5
  17.8 2.8 %conv.1.refs_4_.refs_1_ = f32[128,4096]{1,0:T(8,128)S(1)} custom-call(f32[2,16,128]{2,1,0:T(8,128)S(1)} %get-tuple-element.27.refs_2_.refs_0_, f32[64,128]{1,0:T(8,128)S(1)} %bitcast.12, f32[16,16,128]{2,1,0:T(8,128)S(1)} %get-tuple-element.28.refs_0_.refs_2_, f32[16,256]{1,0:T(8,128)S(1)} %get-tuple-element.29.refs_3_, ...), custom_call_target="tpu_custom_call" | custom-call | flops 536870912 | bytes 3145728 | tf_op jit(solution)/shard_map/conv/pallas_call | solution.py:536
  20.6 0.0 copy-start
  20.6 0.0 copy-start.1
  20.6 0.0 copy-start.2
  20.6 0.2 collective-permute-done.3.refs_2_
  20.8 0.3 combine.5
  21.1 0.1 collective-permute-start.4
  21.2 1.3 %collective-permute-done.4.refs_3_ = bf16[352,128]{1,0:T(8,128)(2,1)S(1)} collective-permute-done((bf16[352,128]{1,0:T(8,128)(2,1)S(1)}, bf16[352,128]{1,0:T(8,128)(2,1)S(1)}, u32[]{:S(2)}, u32[]{:S(2)}) %collective-permute-start.4) | collective-permute-done | bytes 90144 | tf_op jit(solution)/shard_map/ppermute | solution.py:488
  22.5 3.7 %collective-permute-start.7 = (f32[48,128]{1,0:T(8,128)S(1)}, f32[48,128]{1,0:T(8,128)S(1)}, u32[]{:S(2)}, u32[]{:S(2)}) collective-permute-start(f32[48,128]{1,0:T(8,128)S(1)} %merge.1.refs_0_), channel_id=1, source_target_pairs={{0,3},{1,0},{2,1},{3,2},{4,7},{5,4},{6,5},{7,6},{8,11},{9,8},{10,9... | collective-permute-start | bytes 73736 | tf_op jit(solution)/shard_map/ppermute | solution.py:604
  26.1 0.0 collective-permute-start.6
  26.2 1.0 %collective-permute-start.5 = (f32[48,128]{1,0:T(8,128)S(1)}, f32[48,128]{1,0:T(8,128)S(1)}, u32[]{:S(2)}, u32[]{:S(2)}) collective-permute-start(f32[48,128]{1,0:T(8,128)S(1)} %merge.1.refs_0_), channel_id=1, source_target_pairs={{0,1},{1,2},{2,3},{3,0},{4,5},{5,6},{6,7},{7,4},{8,9},{9,10},{10,1... | collective-permute-start | bytes 73736 | tf_op jit(solution)/shard_map/ppermute | solution.py:604
  27.2 0.0 copy-done
  27.2 0.0 copy-done.1
  27.2 0.0 copy-done.2
  27.2 2.6 %outputs.1 = (bf16[128,2048]{1,0:T(8,128)(2,1)}, bf16[128,2048]{1,0:T(8,128)(2,1)}, bf16[128,2048]{1,0:T(8,128)(2,1)}) custom-call(f32[2,16,128]{2,1,0:T(8,128)S(1)} %get-tuple-element.27.refs_2_.refs_0_, f32[128,4096]{1,0:T(8,128)S(1)} %conv.1.refs_4_.refs_1_, bf16[8,32,128]{2,1,0:T(8,128)(2,1)S(1)} %get-tuple-element.40.refs_2_, ...), custom_call_target="tpu_custom_call" | custom-call | tf_op jit(solution)/shard_map/outputs/pallas_call | solution.py:606
  29.8 0.0 collective-permute-done.7.refs_3_
  29.8 1.2 %collective-permute-done.6.refs_2_ = f32[48,128]{1,0:T(8,128)S(1)} collective-permute-done((f32[48,128]{1,0:T(8,128)S(1)}, f32[48,128]{1,0:T(8,128)S(1)}, u32[]{:S(2)}, u32[]{:S(2)}) %collective-permute-start.6) | collective-permute-done | bytes 24608 | tf_op jit(solution)/shard_map/ppermute | solution.py:604
  30.9 0.8 %collective-permute-done.5.refs_1_ = f32[48,128]{1,0:T(8,128)S(1)} collective-permute-done((f32[48,128]{1,0:T(8,128)S(1)}, f32[48,128]{1,0:T(8,128)S(1)}, u32[]{:S(2)}, u32[]{:S(2)}) %collective-permute-start.5) | collective-permute-done | bytes 24608 | tf_op jit(solution)/shard_map/ppermute | solution.py:604
  31.8 0.6 %assemble.1 = (f32[16,512]{1,0:T(8,128)}, f32[16,512]{1,0:T(8,128)}, f32[64,128]{1,0:T(8,128)}) custom-call(f32[48,128]{1,0:T(8,128)S(1)} %merge.1.refs_0_, f32[48,128]{1,0:T(8,128)S(1)} %collective-permute-done.5.refs_1_, f32[48,128]{1,0:T(8,128)S(1)} %collective-permute-done.6.refs_2_, f32[48,128]{1,0:T(8,128)S(1)} %collective-permute-done.7.refs_3_), custom_call_target="tpu_custom_call" | custom-call | tf_op jit(solution)/shard_map/assemble/pallas_call | solution.py:616
  (1 shorter events, 0.0 us)
Async XLA Ops:
  0.6 1.9 %copy-start.3 = (f32[512,16]{0,1:T(8,128)S(1)}, f32[512,16]{0,1:T(8,128)}, u32[]{:S(2)}) copy-start(f32[512,16]{0,1:T(8,128)} %param.12) | copy-start | bytes 98308
  0.6 1.9 %copy-start.4 = (f32[512,16]{0,1:T(8,128)S(1)}, f32[512,16]{0,1:T(8,128)}, u32[]{:S(2)}) copy-start(f32[512,16]{0,1:T(8,128)} %param.11) | copy-start | bytes 98308
  4.8 1.5 %collective-permute-start = (bf16[512,128]{1,0:T(8,128)(2,1)S(1)}, bf16[512,128]{1,0:T(8,128)(2,1)S(1)}, u32[]{:S(2)}, u32[]{:S(2)}) collective-permute-start(bf16[512,128]{1,0:T(8,128)(2,1)S(1)} %get-tuple-element.33), channel_id=1, source_target_pairs={{0,4},{4,0},{8,12},{12,8},{16,20},{20,16},{24,28},{28,24},{1,5},{5... | collective-permute-start | bytes 393224 | tf_op jit(solution)/shard_map/ppermute | solution.py:488
  5.8 12.0 %copy-start.5 = (f32[8192]{0:T(1024)S(1)}, f32[8192]{0:T(1024)}, u32[]{:S(2)}) copy-start(f32[8192]{0:T(1024)} %param.13) | copy-start | bytes 98308
  6.5 9.3 %collective-permute-start.1 = (bf16[576,128]{1,0:T(8,128)(2,1)S(1)}, bf16[576,128]{1,0:T(8,128)(2,1)S(1)}, u32[]{:S(2)}, u32[]{:S(2)}) collective-permute-start(bf16[576,128]{1,0:T(8,128)(2,1)S(1)} %get-tuple-element.34.refs_1_), channel_id=1, source_target_pairs={{0,8},{4,12},{8,0},{12,4},{16,24},{20,28},{24,16},{28,20},{1,9},{5... | collective-permute-start | bytes 442376 | tf_op jit(solution)/shard_map/ppermute | solution.py:488
  12.0 3.9 %collective-permute-start.2 = (bf16[96,128]{1,0:T(8,128)(2,1)S(1)}, bf16[96,128]{1,0:T(8,128)(2,1)S(1)}, u32[]{:S(2)}, u32[]{:S(2)}) collective-permute-start(bf16[96,128]{1,0:T(8,128)(2,1)S(1)} %lags.1.refs_3_), channel_id=1, source_target_pairs={{0,8},{4,12},{8,0},{12,4},{16,24},{20,28},{24,16},{28,20},{1,9},{5... | collective-permute-start | bytes 73736 | tf_op jit(solution)/shard_map/ppermute | solution.py:488
  16.2 4.6 %collective-permute-start.3 = (bf16[352,128]{1,0:T(8,128)(2,1)S(1)}, bf16[352,128]{1,0:T(8,128)(2,1)S(1)}, u32[]{:S(2)}, u32[]{:S(2)}) collective-permute-start(bf16[352,128]{1,0:T(8,128)(2,1)S(1)} %get-tuple-element.39), channel_id=1, source_target_pairs={{0,16},{4,20},{8,24},{12,28},{16,0},{20,4},{24,8},{28,12},{1,17},{... | collective-permute-start | bytes 270344 | tf_op jit(solution)/shard_map/ppermute | solution.py:488
  20.6 6.6 %copy-start = (bf16[128,2048]{1,0:T(8,128)(2,1)S(1)}, bf16[128,2048]{1,0:T(8,128)(2,1)}, u32[]{:S(2)}) copy-start(bf16[128,2048]{1,0:T(8,128)(2,1)} %refs_6_.1) | copy-start | bytes 1572868
  20.6 6.5 %copy-start.1 = (bf16[128,2048]{1,0:T(8,128)(2,1)S(1)}, bf16[128,2048]{1,0:T(8,128)(2,1)}, u32[]{:S(2)}) copy-start(bf16[128,2048]{1,0:T(8,128)(2,1)} %refs_5_.1) | copy-start | bytes 1572868
  20.6 6.5 %copy-start.2 = (bf16[128,2048]{1,0:T(8,128)(2,1)S(1)}, bf16[128,2048]{1,0:T(8,128)(2,1)}, u32[]{:S(2)}) copy-start(bf16[128,2048]{1,0:T(8,128)(2,1)} %refs_4_.1) | copy-start | bytes 1572868
  21.1 1.4 %collective-permute-start.4 = (bf16[352,128]{1,0:T(8,128)(2,1)S(1)}, bf16[352,128]{1,0:T(8,128)(2,1)S(1)}, u32[]{:S(2)}, u32[]{:S(2)}) collective-permute-start(bf16[352,128]{1,0:T(8,128)(2,1)S(1)} %get-tuple-element.41.refs_2_), channel_id=1, source_target_pairs={{0,4},{4,0},{8,12},{12,8},{16,20},{20,16},{24,28},{28,24},{1,5},{5... | collective-permute-start | bytes 270344 | tf_op jit(solution)/shard_map/ppermute | solution.py:488
  22.5 7.3 %collective-permute-start.7 = (f32[48,128]{1,0:T(8,128)S(1)}, f32[48,128]{1,0:T(8,128)S(1)}, u32[]{:S(2)}, u32[]{:S(2)}) collective-permute-start(f32[48,128]{1,0:T(8,128)S(1)} %merge.1.refs_0_), channel_id=1, source_target_pairs={{0,3},{1,0},{2,1},{3,2},{4,7},{5,4},{6,5},{7,6},{8,11},{9,8},{10,9... | collective-permute-start | bytes 73736 | tf_op jit(solution)/shard_map/ppermute | solution.py:604
  26.1 4.8 %collective-permute-start.6 = (f32[48,128]{1,0:T(8,128)S(1)}, f32[48,128]{1,0:T(8,128)S(1)}, u32[]{:S(2)}, u32[]{:S(2)}) collective-permute-start(f32[48,128]{1,0:T(8,128)S(1)} %merge.1.refs_0_), channel_id=1, source_target_pairs={{0,2},{1,3},{2,0},{3,1},{4,6},{5,7},{6,4},{7,5},{8,10},{9,11},{10,... | collective-permute-start | bytes 73736 | tf_op jit(solution)/shard_map/ppermute | solution.py:604
  26.2 5.6 %collective-permute-start.5 = (f32[48,128]{1,0:T(8,128)S(1)}, f32[48,128]{1,0:T(8,128)S(1)}, u32[]{:S(2)}, u32[]{:S(2)}) collective-permute-start(f32[48,128]{1,0:T(8,128)S(1)} %merge.1.refs_0_), channel_id=1, source_target_pairs={{0,1},{1,2},{2,3},{3,0},{4,5},{5,6},{6,7},{7,4},{8,9},{9,10},{10,1... | collective-permute-start | bytes 73736 | tf_op jit(solution)/shard_map/ppermute | solution.py:604

commit v9 on v8

--- a/solution.py
+++ b/solution.py
@@ -133,7 +133,7 @@
         lax.fori_loop(0, half_blocks // inner, body, 0)
 
 
-def lags_kernel(lag_rates_ref, gated_ref, dgate_ref, turned_ref, _, sums_ref, skip_ref, *, group, poles, inner):
+def lags_kernel(lag_rates_ref, gated_ref, dgate_ref, turned_ref, _, sums_ref, skip_ref, *, second, group, poles, inner):
     tokens, _ = gated_ref.shape
     per_block = LANES // group
     blocks, _, lag_width = lag_rates_ref.shape
@@ -144,8 +144,9 @@
     near_side, no_wrap = row + lane <= SUB - 1, lane >= row
     lag = (SUB - 1 - within(iota((poles, lag_width), 1), SUB)).astype(F32)
     spread = members(step_groups, 0, SUB, inner * lag_width)
+    half_steps = blocks // inner // 2
     sums = []
-    for step in range(blocks // inner):
+    for step in range(half_steps * second, half_steps * (second + 1)):
         outers = []
         for j in range(inner):
             lanes = slice((step * inner + j) * LANES, (step * inner + j + 1) * LANES)
@@ -182,13 +183,16 @@
                 split(jnp.concatenate([table * total, table * (lag * total + SUB * weighted)], axis=0), 2)
             )
         sums.append(mxu_t(jnp.concatenate(terms, axis=1), spread))
-    for b in range(blocks):
-        lanes = slice(b * LANES, (b + 1) * LANES)
-        product = gated_ref[:, lanes].astype(F32) * dgate_ref[:, lanes].astype(F32)
-        skip_ref[b : b + 1, :] = jnp.sum(product, axis=0, keepdims=True)
     sums = jnp.concatenate(sums, axis=1)
+    zeros = jnp.zeros_like(sums)
+    sums = jnp.concatenate([zeros, sums] if second else [sums, zeros], axis=1)
     sums_ref[: 4 * poles, :] = split(join(sums, 2 * poles), 2)
-    sums_ref[4 * poles :, :] = split(skip_ref[...], 2)
+    if second:
+        for b in range(blocks):
+            lanes = slice(b * LANES, (b + 1) * LANES)
+            product = gated_ref[:, lanes].astype(F32) * dgate_ref[:, lanes].astype(F32)
+            skip_ref[b : b + 1, :] = jnp.sum(product, axis=0, keepdims=True)
+        sums_ref[4 * poles :, :] = split(skip_ref[...], 2)
 
 
 def tables_kernel(logs_ref, res_ref, _, rates_ref, lag_rates_ref, taps_ref, tables_ref, *, group, poles, inner):
@@ -283,8 +287,8 @@
     rest = refs[3:]
     near_ref = held_ref = slim_ref = None
     if level == 0:
-        out_ref, near_ref = rest[:2]
-        rest = rest[2:]
+        own_sums_ref, out_ref, near_ref = rest[:3]
+        rest = rest[3:]
     else:
         if level > 1:
             held_ref = rest.pop(0)
@@ -388,7 +392,7 @@
         skip = sum(join(part[4 * poles :], all_blocks) for part in tails if part.shape[0] > 4 * poles)
         rests = jnp.concatenate([split(total, 2), split(skip, 2)], axis=0)
     else:
-        rests = split(total, 2)
+        rests = split(total + join(own_sums_ref[...], 2 * poles), 2)
     out_ref[blocks * (2 * poles if last else own_rows) :, :] = rests
     if slim_ref is not None:
         slim_ref[blocks * slim_rows :, :] = rests
@@ -408,11 +412,12 @@
     out_ref[2 * poles :, :] = skip / math.sqrt(length)
 
 
-def output_kernel(rows_ref, conv_ref, mine_ref, got_ref, k_ref, v_ref, c_ref, gq_ref, gk_ref, gv_ref,
-                  *, group, poles):
+def output_kernel(rows_ref, conv_ref, mine_ref, got_ref, k_ref, v_ref, c_ref, *rest, offset, group, poles):
+    gq_ref, gk_ref, gv_ref, mark_ref = rest[-4:]
+    mark_ref[...] = jnp.zeros_like(mark_ref)
     tokens, width = gq_ref.shape
     per_block = LANES // group
-    step = pl.program_id(0)
+    step = pl.program_id(0) + offset
     inner = width // LANES
     half_blocks = mine_ref.shape[0]
     core = lax.rem(lax.axis_index("ctx"), 2)
@@ -445,18 +450,25 @@
     gv_ref[...] = (flow * k_ref[:, cut].astype(F32)).astype(BF16)
 
 
-def assemble_kernel(*refs, shards, poles):
-    slots = refs[:shards]
-    res_ref, log_ref, skip_ref = refs[shards:]
+def stack_kernel(own_ref, got_ref, _, out_ref):
+    rows = own_ref.shape[0]
+    out_ref[:rows, :] = own_ref[...]
+    out_ref[rows:, :] = got_ref[...]
+
+
+def assemble_kernel(own_ref, got_ref, res_ref, log_ref, skip_ref, *, shards, poles):
     me = lax.axis_index("ch")
-    groups = slots[0].shape[1]
-    rows = slots[0].shape[0] - 2 * poles
-    for shift, slot in enumerate(slots):
-        source = lax.rem(me - shift + shards, shards)
+    groups = own_ref.shape[1]
+    half = shards // 2
+    piece = own_ref.shape[0] // half
+    rows = piece - 2 * poles
+    for k in range(shards):
+        source = lax.bitwise_xor(me, k)
+        value = (own_ref if k < half else got_ref)[k % half * piece : (k % half + 1) * piece, :]
         cut = pl.ds(pl.multiple_of(source * groups, LANES), groups)
-        res_ref[:, cut] = slot[:poles, :]
-        log_ref[:, cut] = slot[poles : 2 * poles, :]
-        skip_ref[pl.ds(pl.multiple_of(source * rows, 8), rows), :] = slot[2 * poles :, :]
+        res_ref[:, cut] = value[:poles]
+        log_ref[:, cut] = value[poles : 2 * poles]
+        skip_ref[pl.ds(pl.multiple_of(source * rows, 8), rows), :] = value[2 * poles :]
 
 
 def local(queries, key_input, value_input, cotangent, residues, log_rates, skip_gain):
@@ -479,8 +491,6 @@
     vmem = pl.BlockSpec(memory_space=pltpu.VMEM)
     anywhere = pl.BlockSpec(memory_space=pl.ANY)
     log_rates, residues = log_rates.T, residues.T
-    main = pl.BlockSpec((tokens, inner * LANES), lambda i: (0, i))
-
     def shape(*dims, dtype=F32):
         return jax.ShapeDtypeStruct(dims, dtype)
 
@@ -517,12 +527,12 @@
         name="tables",
     )(log_rates, residues, rows)
 
-    def local_sums(after):
+    def local_sums(after, second):
         return pl.pallas_call(
-            lambda *refs: lags_kernel(*refs, inner=inner, **sizes),
+            lambda *refs: lags_kernel(*refs, second=second, inner=inner, **sizes),
             in_specs=[vmem] * 4 + [anywhere],
             out_specs=vmem,
-            out_shape=shape(tail, LANES, dtype=BF16),
+            out_shape=shape(tail if second else near_tail, LANES, dtype=BF16),
             scratch_shapes=[pltpu.VMEM((blocks, LANES), F32)],
             compiler_params=PARAMS,
             cost_estimate=pl.CostEstimate(
@@ -550,11 +560,14 @@
         last = level == levels - 1
         got = swap(outgoing, level)
         operands, specs = [rates, message, got], [vmem] * 3
-        if level == 1:
-            sums = local_sums(near)
+        if level == 0:
+            operands.append(local_sums(rows, 0))
+            specs.append(vmem)
+        elif level == 1:
+            sums = local_sums(near, 1)
             operands += [sums, swap(sums, level)]
             specs += [vmem] * 2
-        elif level > 1:
+        else:
             operands.append(held)
             specs.append(vmem)
         if level == min(2, levels - 1):
@@ -599,32 +612,48 @@
         name="merge",
     )(log_rates, residues, outgoing, got)
 
-    gathered = [merged]
-    for shift in range(1, shards):
-        gathered.append(lax.ppermute(merged, "ch", [(i, (i + shift) % shards) for i in range(shards)]))
-
-    grad_query, grad_key, grad_value = pl.pallas_call(
-        lambda *refs: output_kernel(*refs, **sizes),
-        grid=(steps,),
-        in_specs=[vmem] * 7,
-        out_specs=[main, main, main],
-        out_shape=[jax.ShapeDtypeStruct((tokens, width), BF16)] * 3,
-        compiler_params=PARAMS,
-        name="outputs",
-    )(rows, conv, mine, got, key_input, value_input, cotangent)
+    def emit(offset, before):
+        count = steps // 2
+        main = pl.BlockSpec((tokens, inner * LANES), lambda i: (0, i + offset))
+        return pl.pallas_call(
+            lambda *refs: output_kernel(*refs, offset=offset, **sizes),
+            grid=(count,),
+            in_specs=[vmem] * 7 + [anywhere] * len(before),
+            out_specs=[main] * 3 + [pl.BlockSpec((8, LANES), lambda i: (0, 0))],
+            out_shape=[shape(tokens, width, dtype=BF16)] * 3 + [shape(8, LANES)],
+            input_output_aliases={7 + n: n for n in range(3)} if offset else {},
+            compiler_params=PARAMS,
+            cost_estimate=pl.CostEstimate(
+                flops=4 * tokens * tokens * width, bytes_accessed=8 * tokens * width, transcendentals=tokens * width
+            ),
+            name="outputs",
+        )(rows, conv, mine, got, key_input, value_input, cotangent, *before)
+
+    own, after = merged, []
+    for level in range(shards.bit_length() - 1):
+        other = lax.ppermute(own, "ch", [(i, i ^ (1 << level)) for i in range(shards)])
+        if level == shards.bit_length() - 2:
+            break
+        if not after:
+            after = emit(0, [])
+        own = pl.pallas_call(
+            stack_kernel,
+            in_specs=[vmem, vmem, anywhere],
+            out_specs=vmem,
+            out_shape=shape(2 * own.shape[0], LANES),
+            compiler_params=PARAMS,
+            name="stack",
+        )(own, other, after[3])
+    grad_query, grad_key, grad_value, _ = emit(steps // 2, [*after[:3], own])
 
     grad_residue, grad_lograte, grad_skip = pl.pallas_call(
         lambda *refs: assemble_kernel(*refs, shards=shards, poles=poles),
-        in_specs=[vmem] * shards,
+        in_specs=[vmem] * 2,
         out_specs=[vmem] * 3,
-        out_shape=[
-            jax.ShapeDtypeStruct((poles, all_groups), F32),
-            jax.ShapeDtypeStruct((poles, all_groups), F32),
-            jax.ShapeDtypeStruct((shards * blocks, LANES), F32),
-        ],
+        out_shape=[shape(poles, all_groups), shape(poles, all_groups), shape(shards * blocks, LANES)],
         compiler_params=PARAMS,
         name="assemble",
-    )(*gathered)
+    )(own, other)
     return (grad_query, grad_key, grad_value, grad_residue.T, grad_lograte.T, grad_skip.reshape(-1))
 
 

time: 32.6 us -> 31.8 us (0.975)
  waiting for transfers between devices: 7.68 us -> 6.88 us
  starting transfers between devices: 9.84 us -> 9.08 us
  Pallas kernels: 12.2 us -> 12.9 us
    pallas_call x2 -> x5, Pallas kernels: 5.12 us -> 5.83 us  [the longest x2 3.01 us: emit(): pl.pallas_call(lambda *refs: output_kernel(*refs, offset=offset, **sizes)...]
    ppermute x3 -> x2, starting transfers between devices: 4.67 us -> 4.23 us  [local(): lax.ppermute(own, 'ch', [(i, i ^ 1 << level) for i in range(shards)])]
    ppermute x5, waiting for transfers between devices: 5.67 us -> 5.25 us  [swap(): lax.ppermute(value, 'ctx', [(i, i ^ 1 << level) for i in range(parts)])]
    ppermute x3 -> x2, waiting for transfers between devices: 2 us -> 1.63 us  [local(): lax.ppermute(own, 'ch', [(i, i ^ 1 << level) for i in range(shards)])]
  transfers between devices with their start and end apart: 8 -> 7, of which waited for: 6 -> 5; matrix products, arithmetic and copies ran while one was open for 0% -> 0% of each run, Pallas kernels for 26% -> 29%
where the time goes in v9:
time: 31.8 us; the launch traced here: 31.6 us
  Pallas kernels  12.9 us (41%)
  starting transfers between devices  9.08 us (29%)
  waiting for transfers between devices  6.88 us (22%)
  other arithmetic  1.91 us (6%)
  between operations  0.82 us (3%)
    ppermute x5, waiting for transfers between devices, swap(): lax.ppermute(value, 'ctx', [(i, i ^ 1 << level) for i in range(parts)])  5.25 us
    ppermute x5, starting transfers between devices, swap(): lax.ppermute(value, 'ctx', [(i, i ^ 1 << level) for i in range(parts)])  4.86 us
    ppermute x2, starting transfers between devices, local(): lax.ppermute(own, 'ch', [(i, i ^ 1 << level) for i in range(shards)])  4.23 us
    pallas_call x2, Pallas kernels, emit(): pl.pallas_call(lambda *refs: output_kernel(*refs, offset=offset, **sizes)...  3.01 us
    pallas_call x2, Pallas kernels, local_sums(): pl.pallas_call(lambda *refs: lags_kernel(*refs, second=second, inner=inne...  2.81 us
    pallas_call x1, Pallas kernels, convolve(): pl.pallas_call(lambda *refs: conv_kernel(*refs, inner=inner, **sizes), in...  2.8 us
    pallas_call x1, Pallas kernels, local(): pl.pallas_call(lambda *refs: states_kernel(*refs, inner=inner, **sizes),...  2.16 us
    convert_element_type x1, other arithmetic, gate(): return (left.astype(F32) * right.astype(F32)).astype(BF16)  1.91 us
  transfers between devices with their start and end apart: 7, of which 5 were waited for; matrix products, arithmetic and copies ran while one was open for 0% of the time, Pallas kernels for 29%

profile of v9, /device:TPU:0, one launch (start us, length us, event | category | flops | bytes accessed | tf_op | source)
XLA Modules:
  0.0 31.6 jit_solution(5833990196573809215)
XLA Ops:
  0.6 0.0 copy-start.3
  0.6 0.0 copy-start.4
  0.7 1.9 %multiply_convert_fusion = (bf16[128,2048]{1,0:T(8,128)(2,1)S(1)}, bf16[128,2048]{1,0:T(8,128)(2,1)S(1)}) fusion(bf16[128,2048]{1,0:T(8,128)(2,1)} %param.7, bf16[128,2048]{1,0:T(8,128)(2,1)} %refs_6_.3, bf16[128,2048]{1,0:T(8,128)(2,1)} %refs_5_.3, bf16[128,2048]{1,0:T(8,128)(2,1)} %refs_4_.3), kind=kLoop, calls=%fused_computation | loop fusion | flops 2097152 | bytes 3145728 | tf_op jit(solution)/shard_map/convert_element_type | solution.py:44
  2.6 0.0 copy-done.3
  2.6 0.0 copy-done.4
  2.6 2.2 %states.1 = (bf16[512,128]{1,0:T(8,128)(2,1)S(1)}, bf16[512,128]{1,0:T(8,128)(2,1)S(1)}, bf16[128,2048]{1,0:T(8,128)(2,1)S(1)}, f32[2,16,128]{2,1,0:T(8,128)S(1)}) custom-call(f32[16,512]{1,0:T(8,128)S(1)} %bitcast.6, f32[16,512]{1,0:T(8,128)S(1)} %bitcast.9, bf16[128,2048]{1,0:T(8,128)(2,1)S(1)} %get-tuple-element.57.refs_2_.refs_1_.refs_5_, ...), custom_call_target="tpu_custom_call" | custom-call | tf_op jit(solution)/shard_map/states/pallas_call | solution.py:501
  4.8 0.5 %collective-permute-start = (bf16[512,128]{1,0:T(8,128)(2,1)S(1)}, bf16[512,128]{1,0:T(8,128)(2,1)S(1)}, u32[]{:S(2)}, u32[]{:S(2)}) collective-permute-start(bf16[512,128]{1,0:T(8,128)(2,1)S(1)} %get-tuple-element.37), channel_id=1, source_target_pairs={{0,4},{4,0},{8,12},{12,8},{16,20},{20,16},{24,28},{28,24},{1,5},{5... | collective-permute-start | bytes 393224 | tf_op jit(solution)/shard_map/ppermute | solution.py:498
  5.3 0.5 %tables.1 = (f32[16,16,128]{2,1,0:T(8,128)S(1)}, f32[16,16,256]{2,1,0:T(8,128)S(1)}, f32[16,256]{1,0:T(8,128)S(1)}, bf16[16,16,256]{2,1,0:T(8,128)(2,1)S(1)}) custom-call(f32[16,512]{1,0:T(8,128)S(1)} %bitcast.7, f32[16,512]{1,0:T(8,128)S(1)} %bitcast.10, f32[2,16,128]{2,1,0:T(8,128)S(1)} %get-tuple-element.31.refs_2_.refs_4_.refs_0_), custom_call_target="tpu_custom_call" | custom-call | flops 1000000000 | bytes 1000000 | tf_op jit(solution)/shard_map/tables/pallas_call | solution.py:515
  5.8 0.0 copy-start.5
  5.8 1.3 %lags.2.refs_3_ = bf16[64,128]{1,0:T(8,128)(2,1)S(1)} custom-call(f32[16,16,256]{2,1,0:T(8,128)S(1)} %get-tuple-element.38.refs_0_, bf16[128,2048]{1,0:T(8,128)(2,1)S(1)} %get-tuple-element.57.refs_2_.refs_1_.refs_5_, bf16[128,2048]{1,0:T(8,128)(2,1)S(1)} %get-tuple-element.56.refs_3_.refs_2_, bf16[128,2048]{1,0:T(8,128)(2,1)S(1)} %get-tuple-element.35.refs_3_.refs_6_, ...), custom_call_target="tpu_custom_call" | custom-call | flops 536870912 | bytes 3145728 | tf_op jit(solution)/shard_map/lags/pallas_call | solution.py:531
  7.2 0.0 collective-permute-done.refs_2_
  7.2 0.3 combine.3
  7.4 2.6 %collective-permute-start.1 = (bf16[576,128]{1,0:T(8,128)(2,1)S(1)}, bf16[576,128]{1,0:T(8,128)(2,1)S(1)}, u32[]{:S(2)}, u32[]{:S(2)}) collective-permute-start(bf16[576,128]{1,0:T(8,128)(2,1)S(1)} %get-tuple-element.39.refs_1_), channel_id=1, source_target_pairs={{0,8},{4,12},{8,0},{12,4},{16,24},{20,28},{24,16},{28,20},{1,9},{5... | collective-permute-start | bytes 442376 | tf_op jit(solution)/shard_map/ppermute | solution.py:498
  10.1 1.5 %lags.3.refs_3_ = bf16[96,128]{1,0:T(8,128)(2,1)S(1)} custom-call(f32[16,16,256]{2,1,0:T(8,128)S(1)} %get-tuple-element.38.refs_0_, bf16[128,2048]{1,0:T(8,128)(2,1)S(1)} %get-tuple-element.57.refs_2_.refs_1_.refs_5_, bf16[128,2048]{1,0:T(8,128)(2,1)S(1)} %get-tuple-element.56.refs_3_.refs_2_, bf16[128,2048]{1,0:T(8,128)(2,1)S(1)} %get-tuple-element.35.refs_3_.refs_6_, ...), custom_call_target="tpu_custom_call" | custom-call | flops 536870912 | bytes 3145728 | tf_op jit(solution)/shard_map/lags/pallas_call | solution.py:531
  11.6 0.1 collective-permute-start.2
  11.6 3.8 %collective-permute-done.2.refs_4_ = bf16[96,128]{1,0:T(8,128)(2,1)S(1)} collective-permute-done((bf16[96,128]{1,0:T(8,128)(2,1)S(1)}, bf16[96,128]{1,0:T(8,128)(2,1)S(1)}, u32[]{:S(2)}, u32[]{:S(2)}) %collective-permute-start.2) | collective-permute-done | bytes 24608 | tf_op jit(solution)/shard_map/ppermute | solution.py:498
  15.4 0.0 collective-permute-done.1.refs_2_
  15.4 0.3 %combine.4 = (bf16[608,128]{1,0:T(8,128)(2,1)S(1)}, f32[8,32,128]{2,1,0:T(8,128)S(1)}, bf16[352,128]{1,0:T(8,128)(2,1)S(1)}) custom-call(f32[16,16,128]{2,1,0:T(8,128)S(1)} %get-tuple-element.32.refs_0_.refs_2_, bf16[576,128]{1,0:T(8,128)(2,1)S(1)} %get-tuple-element.39.refs_1_, bf16[576,128]{1,0:T(8,128)(2,1)S(1)} %collective-permute-done.1.refs_2_, ...), custom_call_target="tpu_custom_call" | custom-call | tf_op jit(solution)/shard_map/combine/pallas_call | solution.py:588
  15.8 1.6 %collective-permute-start.3 = (bf16[352,128]{1,0:T(8,128)(2,1)S(1)}, bf16[352,128]{1,0:T(8,128)(2,1)S(1)}, u32[]{:S(2)}, u32[]{:S(2)}) collective-permute-start(bf16[352,128]{1,0:T(8,128)(2,1)S(1)} %get-tuple-element.43), channel_id=1, source_target_pairs={{0,16},{4,20},{8,24},{12,28},{16,0},{20,4},{24,8},{28,12},{1,17},{... | collective-permute-start | bytes 270344 | tf_op jit(solution)/shard_map/ppermute | solution.py:498
  17.4 0.0 copy-done.5
  17.4 2.8 %conv.1.refs_4_.refs_1_ = f32[128,4096]{1,0:T(8,128)S(1)} custom-call(f32[2,16,128]{2,1,0:T(8,128)S(1)} %get-tuple-element.31.refs_2_.refs_4_.refs_0_, f32[64,128]{1,0:T(8,128)S(1)} %bitcast.12, f32[16,16,128]{2,1,0:T(8,128)S(1)} %get-tuple-element.32.refs_0_.refs_2_, f32[16,256]{1,0:T(8,128)S(1)} %get-tuple-element.33.refs_3_, ...), custom_call_target="tpu_custom_call" | custom-call | flops 536870912 | bytes 3145728 | tf_op jit(solution)/shard_map/conv/pallas_call | solution.py:546
  20.2 0.0 copy-start
  20.2 0.0 copy-start.1
  20.2 0.0 copy-start.2
  20.2 0.2 collective-permute-done.3.refs_2_
  20.4 0.3 combine.5
  20.7 0.1 collective-permute-start.4
  20.8 1.3 %collective-permute-done.4.refs_3_ = bf16[352,128]{1,0:T(8,128)(2,1)S(1)} collective-permute-done((bf16[352,128]{1,0:T(8,128)(2,1)S(1)}, bf16[352,128]{1,0:T(8,128)(2,1)S(1)}, u32[]{:S(2)}, u32[]{:S(2)}) %collective-permute-start.4) | collective-permute-done | bytes 90144 | tf_op jit(solution)/shard_map/ppermute | solution.py:498
  22.1 1.6 %collective-permute-start.5 = (f32[48,128]{1,0:T(8,128)S(1)}, f32[48,128]{1,0:T(8,128)S(1)}, u32[]{:S(2)}, u32[]{:S(2)}) collective-permute-start(f32[48,128]{1,0:T(8,128)S(1)} %merge.1.own_ref), channel_id=1, source_target_pairs={{0,1},{1,0},{2,3},{3,2},{4,5},{5,4},{6,7},{7,6},{8,9},{9,8},{10,11... | collective-permute-start | bytes 73736 | tf_op jit(solution)/shard_map/ppermute | solution.py:634
  23.7 0.0 copy-done
  23.7 0.0 copy-done.1
  23.7 0.0 copy-done.2
  23.7 1.5 %outputs.2 = (bf16[128,2048]{1,0:T(8,128)(2,1)}, bf16[128,2048]{1,0:T(8,128)(2,1)}, bf16[128,2048]{1,0:T(8,128)(2,1)}, f32[8,128]{1,0:T(8,128)S(1)}) custom-call(f32[2,16,128]{2,1,0:T(8,128)S(1)} %get-tuple-element.31.refs_2_.refs_4_.refs_0_, f32[128,4096]{1,0:T(8,128)S(1)} %conv.1.refs_4_.refs_1_, bf16[8,32,128]{2,1,0:T(8,128)(2,1)S(1)} %get-tuple-element.44.refs_2_, ...), custom_call_target="tpu_custom_call" | custom-call | flops 134217728 | bytes 2097152 | tf_op jit(solution)/shard_map/outputs/pallas_call | solution.py:618
  25.2 0.7 %collective-permute-done.5.got_ref = f32[48,128]{1,0:T(8,128)S(1)} collective-permute-done((f32[48,128]{1,0:T(8,128)S(1)}, f32[48,128]{1,0:T(8,128)S(1)}, u32[]{:S(2)}, u32[]{:S(2)}) %collective-permute-start.5) | collective-permute-done | bytes 24608 | tf_op jit(solution)/shard_map/ppermute | solution.py:634
  26.0 2.6 %collective-permute-start.6 = (f32[96,128]{1,0:T(8,128)S(1)}, f32[96,128]{1,0:T(8,128)S(1)}, u32[]{:S(2)}, u32[]{:S(2)}) collective-permute-start(f32[96,128]{1,0:T(8,128)S(1)} %stack.1.refs_10_.refs_0_), channel_id=1, source_target_pairs={{0,2},{1,3},{2,0},{3,1},{4,6},{5,7},{6,4},{7,5},{8,10},{9,11},{10,... | collective-permute-start | bytes 147464 | tf_op jit(solution)/shard_map/ppermute | solution.py:634
  28.6 1.5 %outputs.3 = (bf16[128,2048]{1,0:T(8,128)(2,1)}, bf16[128,2048]{1,0:T(8,128)(2,1)}, bf16[128,2048]{1,0:T(8,128)(2,1)}, f32[8,128]{1,0:T(8,128)}) custom-call(f32[2,16,128]{2,1,0:T(8,128)S(1)} %get-tuple-element.31.refs_2_.refs_4_.refs_0_, f32[128,4096]{1,0:T(8,128)S(1)} %conv.1.refs_4_.refs_1_, ...), custom_call_target="tpu_custom_call", output_to_operand_aliasing={{0}: (7, {}), {1}: (8, {}), {2}: (9, {})} | custom-call | flops 134217728 | bytes 2097152 | tf_op jit(solution)/shard_map/outputs/pallas_call | solution.py:618
  30.1 0.9 %collective-permute-done.6.refs_1_ = f32[96,128]{1,0:T(8,128)S(1)} collective-permute-done((f32[96,128]{1,0:T(8,128)S(1)}, f32[96,128]{1,0:T(8,128)S(1)}, u32[]{:S(2)}, u32[]{:S(2)}) %collective-permute-start.6) | collective-permute-done | bytes 49184 | tf_op jit(solution)/shard_map/ppermute | solution.py:634
  31.0 0.6 %assemble.1 = (f32[16,512]{1,0:T(8,128)}, f32[16,512]{1,0:T(8,128)}, f32[64,128]{1,0:T(8,128)}) custom-call(f32[96,128]{1,0:T(8,128)S(1)} %stack.1.refs_10_.refs_0_, f32[96,128]{1,0:T(8,128)S(1)} %collective-permute-done.6.refs_1_), custom_call_target="tpu_custom_call" | custom-call | tf_op jit(solution)/shard_map/assemble/pallas_call | solution.py:649
  (2 shorter events, 0.0 us)
Async XLA Ops:
  0.6 1.9 %copy-start.3 = (f32[512,16]{0,1:T(8,128)S(1)}, f32[512,16]{0,1:T(8,128)}, u32[]{:S(2)}) copy-start(f32[512,16]{0,1:T(8,128)} %param.12) | copy-start | bytes 98308
  0.6 1.9 %copy-start.4 = (f32[512,16]{0,1:T(8,128)S(1)}, f32[512,16]{0,1:T(8,128)}, u32[]{:S(2)}) copy-start(f32[512,16]{0,1:T(8,128)} %param.11) | copy-start | bytes 98308
  4.8 2.4 %collective-permute-start = (bf16[512,128]{1,0:T(8,128)(2,1)S(1)}, bf16[512,128]{1,0:T(8,128)(2,1)S(1)}, u32[]{:S(2)}, u32[]{:S(2)}) collective-permute-start(bf16[512,128]{1,0:T(8,128)(2,1)S(1)} %get-tuple-element.37), channel_id=1, source_target_pairs={{0,4},{4,0},{8,12},{12,8},{16,20},{20,16},{24,28},{28,24},{1,5},{5... | collective-permute-start | bytes 393224 | tf_op jit(solution)/shard_map/ppermute | solution.py:498
  5.8 11.6 %copy-start.5 = (f32[8192]{0:T(1024)S(1)}, f32[8192]{0:T(1024)}, u32[]{:S(2)}) copy-start(f32[8192]{0:T(1024)} %param.13) | copy-start | bytes 98308
  7.4 8.0 %collective-permute-start.1 = (bf16[576,128]{1,0:T(8,128)(2,1)S(1)}, bf16[576,128]{1,0:T(8,128)(2,1)S(1)}, u32[]{:S(2)}, u32[]{:S(2)}) collective-permute-start(bf16[576,128]{1,0:T(8,128)(2,1)S(1)} %get-tuple-element.39.refs_1_), channel_id=1, source_target_pairs={{0,8},{4,12},{8,0},{12,4},{16,24},{20,28},{24,16},{28,20},{1,9},{5... | collective-permute-start | bytes 442376 | tf_op jit(solution)/shard_map/ppermute | solution.py:498
  11.6 3.9 %collective-permute-start.2 = (bf16[96,128]{1,0:T(8,128)(2,1)S(1)}, bf16[96,128]{1,0:T(8,128)(2,1)S(1)}, u32[]{:S(2)}, u32[]{:S(2)}) collective-permute-start(bf16[96,128]{1,0:T(8,128)(2,1)S(1)} %lags.3.refs_3_), channel_id=1, source_target_pairs={{0,8},{4,12},{8,0},{12,4},{16,24},{20,28},{24,16},{28,20},{1,9},{5... | collective-permute-start | bytes 73736 | tf_op jit(solution)/shard_map/ppermute | solution.py:498
  15.8 4.6 %collective-permute-start.3 = (bf16[352,128]{1,0:T(8,128)(2,1)S(1)}, bf16[352,128]{1,0:T(8,128)(2,1)S(1)}, u32[]{:S(2)}, u32[]{:S(2)}) collective-permute-start(bf16[352,128]{1,0:T(8,128)(2,1)S(1)} %get-tuple-element.43), channel_id=1, source_target_pairs={{0,16},{4,20},{8,24},{12,28},{16,0},{20,4},{24,8},{28,12},{1,17},{... | collective-permute-start | bytes 270344 | tf_op jit(solution)/shard_map/ppermute | solution.py:498
  20.2 3.5 %copy-start = (bf16[128,2048]{1,0:T(8,128)(2,1)S(1)}, bf16[128,2048]{1,0:T(8,128)(2,1)}, u32[]{:S(2)}) copy-start(bf16[128,2048]{1,0:T(8,128)(2,1)} %refs_6_.3) | copy-start | bytes 1572868
  20.2 3.5 %copy-start.1 = (bf16[128,2048]{1,0:T(8,128)(2,1)S(1)}, bf16[128,2048]{1,0:T(8,128)(2,1)}, u32[]{:S(2)}) copy-start(bf16[128,2048]{1,0:T(8,128)(2,1)} %refs_5_.3) | copy-start | bytes 1572868
  20.2 3.5 %copy-start.2 = (bf16[128,2048]{1,0:T(8,128)(2,1)S(1)}, bf16[128,2048]{1,0:T(8,128)(2,1)}, u32[]{:S(2)}) copy-start(bf16[128,2048]{1,0:T(8,128)(2,1)} %refs_4_.3) | copy-start | bytes 1572868
  20.7 1.4 %collective-permute-start.4 = (bf16[352,128]{1,0:T(8,128)(2,1)S(1)}, bf16[352,128]{1,0:T(8,128)(2,1)S(1)}, u32[]{:S(2)}, u32[]{:S(2)}) collective-permute-start(bf16[352,128]{1,0:T(8,128)(2,1)S(1)} %get-tuple-element.45.refs_2_), channel_id=1, source_target_pairs={{0,4},{4,0},{8,12},{12,8},{16,20},{20,16},{24,28},{28,24},{1,5},{5... | collective-permute-start | bytes 270344 | tf_op jit(solution)/shard_map/ppermute | solution.py:498
  22.1 3.9 %collective-permute-start.5 = (f32[48,128]{1,0:T(8,128)S(1)}, f32[48,128]{1,0:T(8,128)S(1)}, u32[]{:S(2)}, u32[]{:S(2)}) collective-permute-start(f32[48,128]{1,0:T(8,128)S(1)} %merge.1.own_ref), channel_id=1, source_target_pairs={{0,1},{1,0},{2,3},{3,2},{4,5},{5,4},{6,7},{7,6},{8,9},{9,8},{10,11... | collective-permute-start | bytes 73736 | tf_op jit(solution)/shard_map/ppermute | solution.py:634
  26.0 5.0 %collective-permute-start.6 = (f32[96,128]{1,0:T(8,128)S(1)}, f32[96,128]{1,0:T(8,128)S(1)}, u32[]{:S(2)}, u32[]{:S(2)}) collective-permute-start(f32[96,128]{1,0:T(8,128)S(1)} %stack.1.refs_10_.refs_0_), channel_id=1, source_target_pairs={{0,2},{1,3},{2,0},{3,1},{4,6},{5,7},{6,4},{7,5},{8,10},{9,11},{10,... | collective-permute-start | bytes 147464 | tf_op jit(solution)/shard_map/ppermute | solution.py:634

commit v10 on v9

--- a/solution.py
+++ b/solution.py
@@ -133,7 +133,11 @@
         lax.fori_loop(0, half_blocks // inner, body, 0)
 
 
-def lags_kernel(lag_rates_ref, gated_ref, dgate_ref, turned_ref, _, sums_ref, skip_ref, *, second, group, poles, inner):
+def lags_kernel(lag_rates_ref, gated_ref, dgate_ref, turned_ref, *rest, second, group, poles, inner):
+    if second:
+        first_ref, out_ref, skip_ref = rest
+    else:
+        (out_ref,) = rest
     tokens, _ = gated_ref.shape
     per_block = LANES // group
     blocks, _, lag_width = lag_rates_ref.shape
@@ -186,45 +190,38 @@
     sums = jnp.concatenate(sums, axis=1)
     zeros = jnp.zeros_like(sums)
     sums = jnp.concatenate([zeros, sums] if second else [sums, zeros], axis=1)
-    sums_ref[: 4 * poles, :] = split(join(sums, 2 * poles), 2)
-    if second:
-        for b in range(blocks):
-            lanes = slice(b * LANES, (b + 1) * LANES)
-            product = gated_ref[:, lanes].astype(F32) * dgate_ref[:, lanes].astype(F32)
-            skip_ref[b : b + 1, :] = jnp.sum(product, axis=0, keepdims=True)
-        sums_ref[4 * poles :, :] = split(skip_ref[...], 2)
-
-
-def tables_kernel(logs_ref, res_ref, _, rates_ref, lag_rates_ref, taps_ref, tables_ref, *, group, poles, inner):
-    blocks, _, lag_width = tables_ref.shape
+    sums = join(sums, 2 * poles)
+    if not second:
+        out_ref[...] = sums
+        return
+    for b in range(blocks):
+        lanes = slice(b * LANES, (b + 1) * LANES)
+        product = gated_ref[:, lanes].astype(F32) * dgate_ref[:, lanes].astype(F32)
+        skip_ref[b : b + 1, :] = jnp.sum(product, axis=0, keepdims=True)
+    out_ref[: 2 * poles, :] = (first_ref[...] + sums).astype(BF16)
+    out_ref[2 * poles :, :] = skip_ref[...].astype(BF16)
+
+
+def tables_kernel(logs_ref, _, rates_ref, lag_rates_ref, *, group, poles, inner):
+    blocks, _, lag_width = lag_rates_ref.shape
     per_block = LANES // group
     groups = blocks * per_block
     step_groups = inner * per_block
-    wide, lag_wide = inner * LANES, inner * lag_width
-    first = shard_start(groups)
-    logs = logs_ref[:, pl.ds(first, groups)]
-    res = res_ref[:, pl.ds(first, groups)]
-    pieces = jnp.concatenate([split(logs, 3), split(res, 3)], axis=0)
-    spread = jnp.concatenate([members(step_groups, 0, SUB, lag_wide), members(step_groups, 0, group, wide)], axis=1)
-    lag = (SUB - 1 - within(iota((poles, lag_wide), 1), SUB)).astype(F32)
+    lag_wide = inner * lag_width
+    pieces = split(logs_ref[:, pl.ds(shard_start(groups), groups)], 3)
+    spread = jnp.concatenate(
+        [members(step_groups, 0, SUB, lag_wide), members(step_groups, 0, group, inner * LANES)], axis=1
+    )
     for step in range(blocks // inner):
         spreads = mxu(pieces[:, step * step_groups : (step + 1) * step_groups], spread)
-        rates = jnp.exp(join(spreads[: 3 * poles], poles))
-        res_lag = join(spreads[3 * poles :, :lag_wide], poles)
-        rate = rates[:, lag_wide:]
-        table = jnp.exp(-rates[:, :lag_wide] * lag)
-        taps = jnp.sum(res_lag * table, axis=0, keepdims=True)
-        table = table.astype(BF16)
+        rates = jnp.exp(join(spreads, poles))
         for j in range(inner):
             here = step * inner + j
-            lanes = slice(j * lag_width, (j + 1) * lag_width)
-            rates_ref[here] = rate[:, j * LANES : (j + 1) * LANES]
-            lag_rates_ref[here] = rates[:, lanes]
-            taps_ref[here : here + 1, :] = taps[:, lanes]
-            tables_ref[here] = table[:, lanes]
-
-
-def conv_kernel(rows_ref, skip_ref, rates_ref, taps_ref, tables_ref, gated_ref, turned_ref, _, conv_ref,
+            lag_rates_ref[here] = rates[:, j * lag_width : (j + 1) * lag_width]
+            rates_ref[here] = rates[:, lag_wide + j * LANES : lag_wide + (j + 1) * LANES]
+
+
+def conv_kernel(res_ref, rows_ref, skip_ref, rates_ref, lag_rates_ref, gated_ref, turned_ref, _, conv_ref,
                 *, group, poles, inner):
     tokens, _ = gated_ref.shape
     per_block = LANES // group
@@ -236,16 +233,24 @@
     wide_group = over(within(iota((SUB, 2 * LANES), 1), LANES), group)
     state_group = over(within(iota((poles, 2 * LANES), 1), LANES), group)
     causal = iota((SUB, lag_width), 0) >= within(iota((SUB, lag_width), 1), SUB)
+    lag = (SUB - 1 - within(iota((poles, lag_width), 1), SUB)).astype(F32)
+    groups = blocks * per_block
+    pieces = split(res_ref[:, pl.ds(shard_start(groups), groups)], 3).astype(F32)
+    spread = members(groups, 0, SUB, inner * lag_width)
 
     def body(step, carry):
         start = step * inner
+        moved = pltpu.roll(pieces, groups - start * per_block, 1).astype(BF16)
+        lag_res = join(mxu(moved, spread), poles)
         lefts, lead_tables, decays, pairs, gains = [], [], [], [], []
         for j in range(inner):
             here = start + j
-            taps = jnp.broadcast_to(taps_ref[pl.ds(here, 1), :], (SUB, lag_width))
+            table = jnp.exp(-lag_rates_ref[here] * lag)
+            taps = jnp.sum(lag_res[:, j * lag_width : (j + 1) * lag_width] * table, axis=0, keepdims=True)
+            taps = jnp.broadcast_to(taps, (SUB, lag_width))
             taps = pltpu.roll(taps, lag_width - SUB + 1, 1, stride=1, stride_axis=0)
             taps = jnp.where(causal, taps, 0.0).astype(BF16)
-            lefts.append(jnp.concatenate([taps, tables_ref[here]], axis=0))
+            lefts.append(jnp.concatenate([taps, table.astype(BF16)], axis=0))
             rate = rows_ref[0, pl.ds(here, 1), :]
             res = rows_ref[1, pl.ds(here, 1), :]
             lead_tables.append((res * jnp.exp(-rate * lead)).astype(BF16))
@@ -283,30 +288,25 @@
 def combine_kernel(*refs, level, levels, group, poles, tokens):
     last = level == levels - 1
     refs = list(refs)
-    rates_ref, own_ref, got_ref = refs[:3]
-    rest = refs[3:]
-    near_ref = held_ref = slim_ref = None
-    if level == 0:
-        own_sums_ref, out_ref, near_ref = rest[:3]
-        rest = rest[3:]
-    else:
-        if level > 1:
-            held_ref = rest.pop(0)
-        else:
-            own_sums_ref, got_sums_ref = rest.pop(0), rest.pop(0)
-        if level == min(2, levels - 1):
-            rest.pop(0)
-        if last:
-            near_ref, mine_ref, out_ref = rest
-        else:
-            out_ref, new_held_ref = rest[:2]
-            rest = rest[2:]
-    if level == levels - 2:
-        slim_ref = rest[0]
+    rates_ref = refs.pop(0)
     all_blocks = rates_ref.shape[0]
     blocks = all_blocks // 2
     per_block = LANES // group
     groups = all_blocks * per_block
+    rows = 2 * poles
+    if level == 0:
+        own_ref, got_ref, sums_ref, states_ref, total_ref, near_ref = refs
+    else:
+        own_ref, own_tail_ref, got_ref = refs.pop(0), refs.pop(0), refs.pop(0)
+        got_tail_ref = None if last else refs.pop(0)
+        held_ref = refs.pop(0) if level > 1 else None
+        if level == min(2, levels - 1):
+            refs.pop(0)
+        if last:
+            near_ref, mine_ref, out_ref = refs
+        else:
+            states_ref, tail_ref, new_held_ref = refs[:3]
+            slim_ref = refs[3] if level == levels - 2 else None
     me = lax.axis_index("ctx")
     core = lax.rem(me, 2)
     is_right = lax.rem(lax.shift_right_logical(me, level), 2) == 1
@@ -316,23 +316,21 @@
     gap = jnp.where(is_right, gap_left, gap_right)
     span = float(tokens * 2**level)
     next_right = lax.rem(lax.shift_right_logical(me, level + 1), 2) == 1
-    own_rows = 4 * poles
-    got_rows = 2 * poles if last else 4 * poles
-    slim_rows = 2 * poles
-
-    def thirds(value):
+
+    def quarters(ref, b):
+        value = ref[2 * b * rows : 2 * (b + 1) * rows].astype(F32)
         return [value[n * poles : (n + 1) * poles] for n in range(4)]
 
     wide_terms = []
     for b in range(blocks):
         rate = rates_ref[core * blocks + b]
-        own_f, own_b, own_fm, own_bm = thirds(own_ref[b * own_rows : (b + 1) * own_rows].astype(F32))
-        got = got_ref[b * got_rows : (b + 1) * got_rows].astype(F32)
+        own_f, own_b, own_fm, own_bm = quarters(own_ref, b)
         if last:
+            got = got_ref[b * rows : (b + 1) * rows].astype(F32)
             got_f = got_b = got[:poles]
             got_fm = got_bm = got[poles:]
         else:
-            got_f, got_b, got_fm, got_bm = thirds(got)
+            got_f, got_b, got_fm, got_bm = quarters(got_ref, b)
         left_f = jnp.where(is_right, got_f, own_f)
         left_fm = jnp.where(is_right, got_fm, own_fm)
         right_b = jnp.where(is_right, own_b, got_b)
@@ -355,9 +353,7 @@
                 first_core = jnp.concatenate([hold[:poles], near[poles:] + step * hold[poles:]], axis=0)
                 second_core = jnp.concatenate([near[:poles] + step * hold[:poles], hold[poles:]], axis=0)
                 mine_ref[b] = jnp.where(core > 0, second_core, first_core).astype(BF16)
-                out_ref[b * 2 * poles : (b + 1) * 2 * poles, :] = jnp.where(
-                    core > 0, first_core, second_core
-                ).astype(BF16)
+                out_ref[b * rows : (b + 1) * rows, :] = jnp.where(core > 0, first_core, second_core).astype(BF16)
             else:
                 new_held_ref[b] = hold
         if not last:
@@ -366,50 +362,44 @@
             left_b = jnp.where(is_right, got_b, own_b)
             left_bm = jnp.where(is_right, got_bm, own_bm)
             decay = jnp.exp(-rate * span)
-            new = [
-                decay * left_f + right_f,
-                left_b + decay * right_b,
-                decay * (left_fm + span * left_f) + right_fm,
-                left_bm + decay * (right_bm + span * right_b),
-            ]
-            out_ref[b * own_rows : (b + 1) * own_rows, :] = jnp.concatenate(new, axis=0).astype(BF16)
-            if slim_ref is not None:
-                chosen = jnp.concatenate(
-                    [jnp.where(next_right, new[1], new[0]), jnp.where(next_right, new[3], new[2])], axis=0
-                )
-                slim_ref[b * slim_rows : (b + 1) * slim_rows, :] = chosen.astype(BF16)
-    own_tail, got_tail = blocks * own_rows, blocks * got_rows
-    cross = mxu_t(jnp.concatenate(wide_terms, axis=1), members(groups, 0, group, blocks * LANES))
-    cross = join(cross, 2 * poles)
-    total = jnp.where(core > 0, pltpu.roll(cross, groups // 2, 1), cross)
-    if level:
-        own_tail, got_tail = own_ref[own_tail:, :], got_ref[got_tail:, :]
-        tails = [own_tail, got_tail]
-        if level == 1:
-            tails += [own_sums_ref[...], got_sums_ref[...]]
-        for part in tails:
-            total = total + join(part[: 4 * poles], 2 * poles)
-        skip = sum(join(part[4 * poles :], all_blocks) for part in tails if part.shape[0] > 4 * poles)
-        rests = jnp.concatenate([split(total, 2), split(skip, 2)], axis=0)
+            new_f, new_b = decay * left_f + right_f, left_b + decay * right_b
+            new_fm = decay * (left_fm + span * left_f) + right_fm
+            new_bm = left_bm + decay * (right_bm + span * right_b)
+            here = slice(b * rows, (b + 1) * rows)
+            new = jnp.concatenate([new_f, new_b, new_fm, new_bm], axis=0).astype(BF16)
+            states_ref[2 * b * rows : 2 * (b + 1) * rows, :] = new
+            if level == levels - 2 and level:
+                chosen = [jnp.where(next_right, new_b, new_f), jnp.where(next_right, new_bm, new_fm)]
+                slim_ref[here, :] = jnp.concatenate(chosen, axis=0).astype(BF16)
+    cross = join(mxu_t(jnp.concatenate(wide_terms, axis=1), members(groups, 0, group, blocks * LANES)), rows)
+    cross = jnp.where(core > 0, pltpu.roll(cross, groups // 2, 1), cross)
+    tail = blocks * rows
+    if level == 0:
+        total_ref[...] = cross + sums_ref[...]
+        return
+    got_tail = got_ref[tail:, :] if last else got_tail_ref[...]
+    both = own_tail_ref[...].astype(F32) + got_tail.astype(F32)
+    rests = jnp.concatenate([both[:rows] + cross, both[rows:]], axis=0).astype(BF16)
+    if last:
+        out_ref[tail:, :] = rests
     else:
-        rests = split(total + join(own_sums_ref[...], 2 * poles), 2)
-    out_ref[blocks * (2 * poles if last else own_rows) :, :] = rests
-    if slim_ref is not None:
-        slim_ref[blocks * slim_rows :, :] = rests
+        tail_ref[...] = rests
+        if slim_ref is not None:
+            slim_ref[tail:, :] = rests
 
 
 def merge_kernel(logs_ref, res_ref, own_ref, got_ref, out_ref, *, poles, length):
-    blocks = out_ref.shape[0] - 2 * poles
     groups = out_ref.shape[1]
-    start = own_ref.shape[0] - 4 * poles - 2 * blocks
-    own, got = own_ref[start:, :], got_ref[start:, :]
-    total = join(own[: 4 * poles], 2 * poles) + join(got[: 4 * poles], 2 * poles)
-    skip = join(own[4 * poles :], blocks) + join(got[4 * poles :], blocks)
+    start = own_ref.shape[0] - out_ref.shape[0]
+    both = own_ref[start:, :].astype(F32) + got_ref[start:, :].astype(F32)
     first = shard_start(groups)
     factor = -jnp.exp(logs_ref[:, pl.ds(first, groups)]) * res_ref[:, pl.ds(first, groups)]
-    out_ref[:poles, :] = total[:poles] / length
-    out_ref[poles : 2 * poles, :] = factor * total[poles:] / math.sqrt(length)
-    out_ref[2 * poles :, :] = skip / math.sqrt(length)
+    scaled = [
+        both[:poles] / length,
+        factor * both[poles : 2 * poles] / math.sqrt(length),
+        both[2 * poles :] / math.sqrt(length),
+    ]
+    out_ref[...] = jnp.concatenate(scaled, axis=0).astype(BF16)
 
 
 def output_kernel(rows_ref, conv_ref, mine_ref, got_ref, k_ref, v_ref, c_ref, *rest, offset, group, poles):
@@ -456,15 +446,16 @@
     out_ref[rows:, :] = got_ref[...]
 
 
-def assemble_kernel(own_ref, got_ref, res_ref, log_ref, skip_ref, *, shards, poles):
+def assemble_kernel(own_ref, got_ref, res_ref, log_ref, skip_ref, *, masks, poles):
+    shards = len(masks)
     me = lax.axis_index("ch")
     groups = own_ref.shape[1]
     half = shards // 2
     piece = own_ref.shape[0] // half
     rows = piece - 2 * poles
-    for k in range(shards):
-        source = lax.bitwise_xor(me, k)
-        value = (own_ref if k < half else got_ref)[k % half * piece : (k % half + 1) * piece, :]
+    for k, mask in enumerate(masks):
+        source = lax.bitwise_xor(me, mask)
+        value = (own_ref if k < half else got_ref)[k % half * piece : (k % half + 1) * piece, :].astype(F32)
         cut = pl.ds(pl.multiple_of(source * groups, LANES), groups)
         res_ref[:, cut] = value[:poles]
         log_ref[:, cut] = value[poles : 2 * poles]
@@ -485,8 +476,7 @@
     half_blocks = blocks // 2
     lag_width = LANES // group * SUB
     sizes = dict(group=group, poles=poles)
-    near_tail, tail = 4 * poles, 4 * poles + 2 * blocks
-    full_rows, half_rows = half_blocks * 4 * poles, half_blocks * 2 * poles
+    half_rows, tail = half_blocks * 2 * poles, 2 * poles + blocks
 
     vmem = pl.BlockSpec(memory_space=pltpu.VMEM)
     anywhere = pl.BlockSpec(memory_space=pl.ANY)
@@ -503,8 +493,8 @@
         in_specs=[vmem] * 4,
         out_specs=[vmem] * 4,
         out_shape=[
-            shape(full_rows, LANES, dtype=BF16),
-            shape(full_rows, LANES, dtype=BF16),
+            shape(2 * half_rows, LANES, dtype=BF16),
+            shape(2 * half_rows, LANES, dtype=BF16),
             shape(tokens, width, dtype=BF16),
             shape(2, blocks, LANES),
         ],
@@ -512,34 +502,31 @@
         name="states",
     )(log_rates, residues, gated, dgate)
 
-    rates, lag_rates, taps, tables = pl.pallas_call(
+    rates, lag_rates = pl.pallas_call(
         lambda *refs: tables_kernel(*refs, inner=inner, **sizes),
-        in_specs=[vmem, vmem, anywhere],
-        out_specs=[vmem] * 4,
-        out_shape=[
-            shape(blocks, poles, LANES),
-            shape(blocks, poles, lag_width),
-            shape(blocks, lag_width),
-            shape(blocks, poles, lag_width, dtype=BF16),
-        ],
+        in_specs=[vmem, anywhere],
+        out_specs=[vmem] * 2,
+        out_shape=[shape(blocks, poles, LANES), shape(blocks, poles, lag_width)],
         compiler_params=PARAMS,
         cost_estimate=pl.CostEstimate(flops=10**9, bytes_accessed=10**6, transcendentals=10**5),
         name="tables",
-    )(log_rates, residues, rows)
-
-    def local_sums(after, second):
+    )(log_rates, rows)
+
+    work = pl.CostEstimate(
+        flops=16 * tokens * tokens * width, bytes_accessed=12 * tokens * width, transcendentals=tokens * width
+    )
+
+    def local_sums(second, *more):
         return pl.pallas_call(
             lambda *refs: lags_kernel(*refs, second=second, inner=inner, **sizes),
-            in_specs=[vmem] * 4 + [anywhere],
+            in_specs=[vmem] * (4 + len(more)),
             out_specs=vmem,
-            out_shape=shape(tail if second else near_tail, LANES, dtype=BF16),
-            scratch_shapes=[pltpu.VMEM((blocks, LANES), F32)],
+            out_shape=shape(tail, LANES, dtype=BF16) if second else shape(2 * poles, LANES),
+            scratch_shapes=[pltpu.VMEM((blocks, LANES), F32)] if second else [],
             compiler_params=PARAMS,
-            cost_estimate=pl.CostEstimate(
-                flops=16 * tokens * tokens * width, bytes_accessed=12 * tokens * width, transcendentals=tokens * width
-            ),
+            cost_estimate=work,
             name="lags",
-        )(lag_rates, gated, dgate, turned, after)
+        )(lag_rates, gated, dgate, turned, *more)
 
     def convolve(after):
         skip_rows = skip_gain.reshape(-1, LANES)
@@ -549,65 +536,60 @@
             out_specs=vmem,
             out_shape=shape(tokens, 2 * width),
             compiler_params=PARAMS,
-            cost_estimate=pl.CostEstimate(
-                flops=16 * tokens * tokens * width, bytes_accessed=12 * tokens * width, transcendentals=tokens * width
-            ),
+            cost_estimate=work,
             name="conv",
-        )(rows, skip_rows, rates, taps, tables, gated, turned, after)
-
-    held = near = None
-    for level in range(levels):
-        last = level == levels - 1
-        got = swap(outgoing, level)
-        operands, specs = [rates, message, got], [vmem] * 3
-        if level == 0:
-            operands.append(local_sums(rows, 0))
-            specs.append(vmem)
-        elif level == 1:
-            sums = local_sums(near, 1)
-            operands += [sums, swap(sums, level)]
-            specs += [vmem] * 2
-        else:
-            operands.append(held)
-            specs.append(vmem)
-        if level == min(2, levels - 1):
-            conv = convolve(near if held is None else held)
-            operands.append(conv)
-            specs.append(anywhere)
-        if last:
-            operands.append(near)
-            specs.append(vmem)
-            outs = [shape(half_blocks, 2 * poles, LANES, dtype=BF16), shape(half_rows + tail, LANES, dtype=BF16)]
-        else:
-            outs = [
-                shape(full_rows + (tail if level else near_tail), LANES, dtype=BF16),
-                shape(half_blocks, 2 * poles, LANES),
-            ]
-        if level == levels - 2:
-            outs.append(shape(half_rows + (tail if level else near_tail), LANES, dtype=BF16))
-        results = pl.pallas_call(
-            lambda *refs, level=level: combine_kernel(*refs, level=level, levels=levels, tokens=tokens, **sizes),
-            in_specs=specs,
+        )(residues, rows, skip_rows, rates, lag_rates, gated, turned, after)
+
+    def combine(level, operands, outs):
+        return pl.pallas_call(
+            lambda *refs: combine_kernel(*refs, level=level, levels=levels, tokens=tokens, **sizes),
+            in_specs=[anywhere if x is conv else vmem for x in operands],
             out_specs=[vmem] * len(outs),
             out_shape=outs,
             compiler_params=PARAMS,
             name="combine",
         )(*operands)
+
+    conv = None
+    states_shape = shape(2 * half_rows, LANES, dtype=BF16)
+    tail_shape = shape(tail, LANES, dtype=BF16)
+    slim_shape = shape(half_rows + tail, LANES, dtype=BF16)
+    held_shape = shape(half_blocks, 2 * poles, LANES)
+    got = swap(outgoing, 0)
+    states, total, near = combine(
+        0, [rates, message, got, local_sums(0)], [states_shape, shape(2 * poles, LANES), held_shape]
+    )
+    held = slim = None
+    for level in range(1, levels):
+        last = level == levels - 1
+        if last and slim is not None:
+            received = [swap(slim, level)]
+        else:
+            received = [swap(states, level)]
+            if level == 1:
+                carried = local_sums(1, total)
+            received.append(swap(carried, level))
+        operands = [rates, states, carried, *received]
+        if level > 1:
+            operands.append(held)
+        if level == min(2, levels - 1):
+            conv = convolve(near if held is None else held)
+            operands.append(conv)
         if last:
-            mine, outgoing = results
+            outs = [shape(half_blocks, 2 * poles, LANES, dtype=BF16), slim_shape]
+            mine, outgoing = combine(level, [*operands, near], outs)
         else:
-            message = results[0]
-            outgoing = results[-1] if level == levels - 2 else message
-            if level == 0:
-                near = results[1]
-            else:
-                held = results[1]
+            outs = [states_shape, tail_shape, held_shape]
+            if level == levels - 2:
+                outs.append(slim_shape)
+            states, carried, held, *more = combine(level, operands, outs)
+            slim = more[0] if more else None
     got = swap(outgoing, 0)
     merged = pl.pallas_call(
         lambda *refs: merge_kernel(*refs, poles=poles, length=tokens * parts),
         in_specs=[vmem] * 4,
         out_specs=vmem,
-        out_shape=shape(2 * poles + blocks, LANES),
+        out_shape=shape(tail, LANES, dtype=BF16),
         compiler_params=PARAMS,
         name="merge",
     )(log_rates, residues, outgoing, got)
@@ -629,10 +611,11 @@
             name="outputs",
         )(rows, conv, mine, got, key_input, value_input, cotangent, *before)
 
-    own, after = merged, []
-    for level in range(shards.bit_length() - 1):
+    own, after, masks = merged, [], [0]
+    for level in reversed(range(shards.bit_length() - 1)):
         other = lax.ppermute(own, "ch", [(i, i ^ (1 << level)) for i in range(shards)])
-        if level == shards.bit_length() - 2:
+        masks += [mask ^ (1 << level) for mask in masks]
+        if level == 0:
             break
         if not after:
             after = emit(0, [])
@@ -640,14 +623,14 @@
             stack_kernel,
             in_specs=[vmem, vmem, anywhere],
             out_specs=vmem,
-            out_shape=shape(2 * own.shape[0], LANES),
+            out_shape=shape(2 * own.shape[0], LANES, dtype=BF16),
             compiler_params=PARAMS,
             name="stack",
         )(own, other, after[3])
     grad_query, grad_key, grad_value, _ = emit(steps // 2, [*after[:3], own])
 
     grad_residue, grad_lograte, grad_skip = pl.pallas_call(
-        lambda *refs: assemble_kernel(*refs, shards=shards, poles=poles),
+        lambda *refs: assemble_kernel(*refs, masks=masks, poles=poles),
         in_specs=[vmem] * 2,
         out_specs=[vmem] * 3,
         out_shape=[shape(poles, all_groups), shape(poles, all_groups), shape(shards * blocks, LANES)],

time: 31.8 us -> 31.5 us (level)
  waiting for transfers between devices: 6.88 us -> 6.17 us
  Pallas kernels: 12.9 us -> 13.5 us
    pallas_call x1, Pallas kernels: 2.8 us -> 3.64 us  [convolve(): pl.pallas_call(lambda *refs: conv_kernel(*refs, inner=inner, **sizes), in...]
    ppermute x2, waiting for transfers between devices: 1.63 us -> 1.23 us  [local(): lax.ppermute(own, 'ch', [(i, i ^ 1 << level) for i in range(shards)])]
  transfers between devices with their start and end apart: 7 -> 7, of which waited for: 5 -> 4; matrix products, arithmetic and copies ran while one was open for 0% -> 0% of each run, Pallas kernels for 29% -> 31%
where the time goes in v10:
time: 31.5 us; the launch traced here: 31.4 us
  Pallas kernels  13.5 us (43%)
  starting transfers between devices  9.02 us (29%)
  waiting for transfers between devices  6.17 us (20%)
  other arithmetic  1.92 us (6%)
  between operations  0.77 us (2%)
    ppermute x5, waiting for transfers between devices, swap(): lax.ppermute(value, 'ctx', [(i, i ^ 1 << level) for i in range(parts)])  4.95 us
    ppermute x5, starting transfers between devices, swap(): lax.ppermute(value, 'ctx', [(i, i ^ 1 << level) for i in range(parts)])  4.78 us
    ppermute x2, starting transfers between devices, local(): lax.ppermute(own, 'ch', [(i, i ^ 1 << level) for i in range(shards)])  4.24 us
    pallas_call x1, Pallas kernels, convolve(): pl.pallas_call(lambda *refs: conv_kernel(*refs, inner=inner, **sizes), in...  3.64 us
    pallas_call x2, Pallas kernels, emit(): pl.pallas_call(lambda *refs: output_kernel(*refs, offset=offset, **sizes)...  3.01 us
    pallas_call x2, Pallas kernels, local_sums(): pl.pallas_call(lambda *refs: lags_kernel(*refs, second=second, inner=inne...  2.79 us
    pallas_call x1, Pallas kernels, local(): pl.pallas_call(lambda *refs: states_kernel(*refs, inner=inner, **sizes),...  2.16 us
    convert_element_type x1, other arithmetic, gate(): return (left.astype(F32) * right.astype(F32)).astype(BF16)  1.92 us
  transfers between devices with their start and end apart: 7, of which 4 were waited for; matrix products, arithmetic and copies ran while one was open for 0% of the time, Pallas kernels for 31%

profile of v10, /device:TPU:0, one launch (start us, length us, event | category | flops | bytes accessed | tf_op | source)
XLA Modules:
  0.0 31.4 jit_solution(8042489944126535850)
XLA Ops:
  0.6 0.0 copy-start.4
  0.6 0.0 copy-start.3
  0.7 1.9 %multiply_convert_fusion = (bf16[128,2048]{1,0:T(8,128)(2,1)S(1)}, bf16[128,2048]{1,0:T(8,128)(2,1)S(1)}) fusion(bf16[128,2048]{1,0:T(8,128)(2,1)} %param.7, bf16[128,2048]{1,0:T(8,128)(2,1)} %refs_6_.3, bf16[128,2048]{1,0:T(8,128)(2,1)} %refs_5_.3, bf16[128,2048]{1,0:T(8,128)(2,1)} %refs_4_.3), kind=kLoop, calls=%fused_computation | loop fusion | flops 2097152 | bytes 3145728 | tf_op jit(solution)/shard_map/convert_element_type | solution.py:44
  2.6 0.0 copy-done.4
  2.6 0.0 copy-done.3
  2.6 2.2 %states.1 = (bf16[512,128]{1,0:T(8,128)(2,1)S(1)}, bf16[512,128]{1,0:T(8,128)(2,1)S(1)}, bf16[128,2048]{1,0:T(8,128)(2,1)S(1)}, f32[2,16,128]{2,1,0:T(8,128)S(1)}) custom-call(f32[16,512]{1,0:T(8,128)S(1)} %bitcast.9, f32[16,512]{1,0:T(8,128)S(1)} %bitcast.6, bf16[128,2048]{1,0:T(8,128)(2,1)S(1)} %get-tuple-element.57.refs_2_.refs_1_.refs_5_, ...), custom_call_target="tpu_custom_call" | custom-call | tf_op jit(solution)/shard_map/states/pallas_call | solution.py:491
  4.8 0.5 %collective-permute-start = (bf16[512,128]{1,0:T(8,128)(2,1)S(1)}, bf16[512,128]{1,0:T(8,128)(2,1)S(1)}, u32[]{:S(2)}, u32[]{:S(2)}) collective-permute-start(bf16[512,128]{1,0:T(8,128)(2,1)S(1)} %get-tuple-element.36), channel_id=1, source_target_pairs={{0,4},{4,0},{8,12},{12,8},{16,20},{20,16},{24,28},{28,24},{1,5},{5... | collective-permute-start | bytes 393224 | tf_op jit(solution)/shard_map/ppermute | solution.py:488
  5.3 0.4 %tables.1 = (f32[16,16,128]{2,1,0:T(8,128)S(1)}, f32[16,16,256]{2,1,0:T(8,128)S(1)}) custom-call(f32[16,512]{1,0:T(8,128)S(1)} %bitcast.10, f32[2,16,128]{2,1,0:T(8,128)S(1)} %get-tuple-element.31.refs_1_.refs_0_), custom_call_target="tpu_custom_call" | custom-call | flops 1000000000 | bytes 1000000 | tf_op jit(solution)/shard_map/tables/pallas_call | solution.py:505
  5.6 0.0 copy-start.5
  5.7 1.3 %lags.2.refs_3_ = f32[32,128]{1,0:T(8,128)S(1)} custom-call(f32[16,16,256]{2,1,0:T(8,128)S(1)} %get-tuple-element.33.refs_0_.refs_4_, bf16[128,2048]{1,0:T(8,128)(2,1)S(1)} %get-tuple-element.57.refs_2_.refs_1_.refs_5_, bf16[128,2048]{1,0:T(8,128)(2,1)S(1)} %get-tuple-element.56.refs_3_.refs_2_, bf16[128,2048]{1,0:T(8,128)(2,1)S(1)} %get-tuple-element.34.refs_3_.refs_6_), custom_call_target="tpu_custom_call" | custom-call | flops 536870912 | bytes 3145728 | tf_op jit(solution)/shard_map/lags/pallas_call | solution.py:520
  7.0 0.0 collective-permute-done.refs_2_
  7.0 0.3 combine.3
  7.3 2.6 %collective-permute-start.1 = (bf16[512,128]{1,0:T(8,128)(2,1)S(1)}, bf16[512,128]{1,0:T(8,128)(2,1)S(1)}, u32[]{:S(2)}, u32[]{:S(2)}) collective-permute-start(bf16[512,128]{1,0:T(8,128)(2,1)S(1)} %get-tuple-element.37.refs_1_), channel_id=1, source_target_pairs={{0,8},{4,12},{8,0},{12,4},{16,24},{20,28},{24,16},{28,20},{1,9},{5... | collective-permute-start | bytes 393224 | tf_op jit(solution)/shard_map/ppermute | solution.py:488
  9.8 1.5 %lags.3.refs_2_ = bf16[48,128]{1,0:T(8,128)(2,1)S(1)} custom-call(f32[16,16,256]{2,1,0:T(8,128)S(1)} %get-tuple-element.33.refs_0_.refs_4_, bf16[128,2048]{1,0:T(8,128)(2,1)S(1)} %get-tuple-element.57.refs_2_.refs_1_.refs_5_, bf16[128,2048]{1,0:T(8,128)(2,1)S(1)} %get-tuple-element.56.refs_3_.refs_2_, ...), custom_call_target="tpu_custom_call" | custom-call | flops 536870912 | bytes 3145728 | tf_op jit(solution)/shard_map/lags/pallas_call | solution.py:520
  11.3 0.1 collective-permute-start.2
  11.4 3.7 %collective-permute-done.2.refs_4_ = bf16[48,128]{1,0:T(8,128)(2,1)S(1)} collective-permute-done((bf16[48,128]{1,0:T(8,128)(2,1)S(1)}, bf16[48,128]{1,0:T(8,128)(2,1)S(1)}, u32[]{:S(2)}, u32[]{:S(2)}) %collective-permute-start.2) | collective-permute-done | bytes 12320 | tf_op jit(solution)/shard_map/ppermute | solution.py:488
  15.1 0.0 collective-permute-done.1.refs_3_
  15.1 0.3 combine.4
  15.4 1.6 %collective-permute-start.3 = (bf16[304,128]{1,0:T(8,128)(2,1)S(1)}, bf16[304,128]{1,0:T(8,128)(2,1)S(1)}, u32[]{:S(2)}, u32[]{:S(2)}) collective-permute-start(bf16[304,128]{1,0:T(8,128)(2,1)S(1)} %get-tuple-element.42), channel_id=1, source_target_pairs={{0,16},{4,20},{8,24},{12,28},{16,0},{20,4},{24,8},{28,12},{1,17},{... | collective-permute-start | bytes 233480 | tf_op jit(solution)/shard_map/ppermute | solution.py:488
  16.9 0.0 copy-done.5
  16.9 3.6 %conv.1.refs_5_.refs_1_ = f32[128,4096]{1,0:T(8,128)S(1)} custom-call(f32[16,512]{1,0:T(8,128)S(1)} %bitcast.7, f32[2,16,128]{2,1,0:T(8,128)S(1)} %get-tuple-element.31.refs_1_.refs_0_, f32[64,128]{1,0:T(8,128)S(1)} %bitcast.12, f32[16,16,128]{2,1,0:T(8,128)S(1)} %get-tuple-element.32.refs_0_.refs_3_, f32[16,16,256]{2,1,0:T(8,128)S(1)} %get-tuple-element.33.refs_0_.refs_4_, ...), custom_call_target="tpu_custom_call" | custom-call | flops 536870912 | bytes 3145728 | tf_op jit(solution)/shard_map/conv/pallas_call | solution.py:533
  20.6 0.0 copy-start
  20.6 0.0 copy-start.1
  20.6 0.0 copy-start.2
  20.6 0.0 collective-permute-done.3.refs_3_
  20.6 0.3 combine.5
  20.9 0.1 collective-permute-start.4
  21.0 1.3 %collective-permute-done.4.refs_3_ = bf16[304,128]{1,0:T(8,128)(2,1)S(1)} collective-permute-done((bf16[304,128]{1,0:T(8,128)(2,1)S(1)}, bf16[304,128]{1,0:T(8,128)(2,1)S(1)}, u32[]{:S(2)}, u32[]{:S(2)}) %collective-permute-start.4) | collective-permute-done | bytes 77856 | tf_op jit(solution)/shard_map/ppermute | solution.py:488
  22.2 2.7 %collective-permute-start.5 = (bf16[48,128]{1,0:T(8,128)(2,1)S(1)}, bf16[48,128]{1,0:T(8,128)(2,1)S(1)}, u32[]{:S(2)}, u32[]{:S(2)}) collective-permute-start(bf16[48,128]{1,0:T(8,128)(2,1)S(1)} %merge.1.own_ref), channel_id=1, source_target_pairs={{0,2},{1,3},{2,0},{3,1},{4,6},{5,7},{6,4},{7,5},{8,10},{9,11},{10,... | collective-permute-start | bytes 36872 | tf_op jit(solution)/shard_map/ppermute | solution.py:616
  24.9 0.0 copy-done
  24.9 0.0 copy-done.1
  24.9 0.0 copy-done.2
  24.9 1.5 %outputs.2 = (bf16[128,2048]{1,0:T(8,128)(2,1)}, bf16[128,2048]{1,0:T(8,128)(2,1)}, bf16[128,2048]{1,0:T(8,128)(2,1)}, f32[8,128]{1,0:T(8,128)S(1)}) custom-call(f32[2,16,128]{2,1,0:T(8,128)S(1)} %get-tuple-element.31.refs_1_.refs_0_, f32[128,4096]{1,0:T(8,128)S(1)} %conv.1.refs_5_.refs_1_, bf16[8,32,128]{2,1,0:T(8,128)(2,1)S(1)} %get-tuple-element.44.refs_2_, ...), custom_call_target="tpu_custom_call" | custom-call | flops 134217728 | bytes 2097152 | tf_op jit(solution)/shard_map/outputs/pallas_call | solution.py:600
  26.4 0.5 %collective-permute-done.5.got_ref = bf16[48,128]{1,0:T(8,128)(2,1)S(1)} collective-permute-done((bf16[48,128]{1,0:T(8,128)(2,1)S(1)}, bf16[48,128]{1,0:T(8,128)(2,1)S(1)}, u32[]{:S(2)}, u32[]{:S(2)}) %collective-permute-start.5) | collective-permute-done | bytes 12320 | tf_op jit(solution)/shard_map/ppermute | solution.py:616
  26.9 1.6 %collective-permute-start.6 = (bf16[96,128]{1,0:T(8,128)(2,1)S(1)}, bf16[96,128]{1,0:T(8,128)(2,1)S(1)}, u32[]{:S(2)}, u32[]{:S(2)}) collective-permute-start(bf16[96,128]{1,0:T(8,128)(2,1)S(1)} %stack.1.refs_10_.refs_0_), channel_id=1, source_target_pairs={{0,1},{1,0},{2,3},{3,2},{4,5},{5,4},{6,7},{7,6},{8,9},{9,8},{10,11... | collective-permute-start | bytes 73736 | tf_op jit(solution)/shard_map/ppermute | solution.py:616
  28.5 1.5 %outputs.3 = (bf16[128,2048]{1,0:T(8,128)(2,1)}, bf16[128,2048]{1,0:T(8,128)(2,1)}, bf16[128,2048]{1,0:T(8,128)(2,1)}, f32[8,128]{1,0:T(8,128)}) custom-call(f32[2,16,128]{2,1,0:T(8,128)S(1)} %get-tuple-element.31.refs_1_.refs_0_, f32[128,4096]{1,0:T(8,128)S(1)} %conv.1.refs_5_.refs_1_, ...), custom_call_target="tpu_custom_call", output_to_operand_aliasing={{0}: (7, {}), {1}: (8, {}), {2}: (9, {})} | custom-call | flops 134217728 | bytes 2097152 | tf_op jit(solution)/shard_map/outputs/pallas_call | solution.py:600
  30.0 0.8 %collective-permute-done.6.refs_1_ = bf16[96,128]{1,0:T(8,128)(2,1)S(1)} collective-permute-done((bf16[96,128]{1,0:T(8,128)(2,1)S(1)}, bf16[96,128]{1,0:T(8,128)(2,1)S(1)}, u32[]{:S(2)}, u32[]{:S(2)}) %collective-permute-start.6) | collective-permute-done | bytes 24608 | tf_op jit(solution)/shard_map/ppermute | solution.py:616
  30.7 0.6 %assemble.1 = (f32[16,512]{1,0:T(8,128)}, f32[16,512]{1,0:T(8,128)}, f32[64,128]{1,0:T(8,128)}) custom-call(bf16[96,128]{1,0:T(8,128)(2,1)S(1)} %stack.1.refs_10_.refs_0_, bf16[96,128]{1,0:T(8,128)(2,1)S(1)} %collective-permute-done.6.refs_1_), custom_call_target="tpu_custom_call" | custom-call | tf_op jit(solution)/shard_map/assemble/pallas_call | solution.py:632
  (2 shorter events, 0.0 us)
Async XLA Ops:
  0.6 1.9 %copy-start.4 = (f32[512,16]{0,1:T(8,128)S(1)}, f32[512,16]{0,1:T(8,128)}, u32[]{:S(2)}) copy-start(f32[512,16]{0,1:T(8,128)} %param.12) | copy-start | bytes 98308
  0.6 1.9 %copy-start.3 = (f32[512,16]{0,1:T(8,128)S(1)}, f32[512,16]{0,1:T(8,128)}, u32[]{:S(2)}) copy-start(f32[512,16]{0,1:T(8,128)} %param.11) | copy-start | bytes 98308
  4.8 2.2 %collective-permute-start = (bf16[512,128]{1,0:T(8,128)(2,1)S(1)}, bf16[512,128]{1,0:T(8,128)(2,1)S(1)}, u32[]{:S(2)}, u32[]{:S(2)}) collective-permute-start(bf16[512,128]{1,0:T(8,128)(2,1)S(1)} %get-tuple-element.36), channel_id=1, source_target_pairs={{0,4},{4,0},{8,12},{12,8},{16,20},{20,16},{24,28},{28,24},{1,5},{5... | collective-permute-start | bytes 393224 | tf_op jit(solution)/shard_map/ppermute | solution.py:488
  5.6 11.3 %copy-start.5 = (f32[8192]{0:T(1024)S(1)}, f32[8192]{0:T(1024)}, u32[]{:S(2)}) copy-start(f32[8192]{0:T(1024)} %param.13) | copy-start | bytes 98308
  7.3 7.8 %collective-permute-start.1 = (bf16[512,128]{1,0:T(8,128)(2,1)S(1)}, bf16[512,128]{1,0:T(8,128)(2,1)S(1)}, u32[]{:S(2)}, u32[]{:S(2)}) collective-permute-start(bf16[512,128]{1,0:T(8,128)(2,1)S(1)} %get-tuple-element.37.refs_1_), channel_id=1, source_target_pairs={{0,8},{4,12},{8,0},{12,4},{16,24},{20,28},{24,16},{28,20},{1,9},{5... | collective-permute-start | bytes 393224 | tf_op jit(solution)/shard_map/ppermute | solution.py:488
  11.3 3.8 %collective-permute-start.2 = (bf16[48,128]{1,0:T(8,128)(2,1)S(1)}, bf16[48,128]{1,0:T(8,128)(2,1)S(1)}, u32[]{:S(2)}, u32[]{:S(2)}) collective-permute-start(bf16[48,128]{1,0:T(8,128)(2,1)S(1)} %lags.3.refs_2_), channel_id=1, source_target_pairs={{0,8},{4,12},{8,0},{12,4},{16,24},{20,28},{24,16},{28,20},{1,9},{5... | collective-permute-start | bytes 36872 | tf_op jit(solution)/shard_map/ppermute | solution.py:488
  15.4 5.3 %collective-permute-start.3 = (bf16[304,128]{1,0:T(8,128)(2,1)S(1)}, bf16[304,128]{1,0:T(8,128)(2,1)S(1)}, u32[]{:S(2)}, u32[]{:S(2)}) collective-permute-start(bf16[304,128]{1,0:T(8,128)(2,1)S(1)} %get-tuple-element.42), channel_id=1, source_target_pairs={{0,16},{4,20},{8,24},{12,28},{16,0},{20,4},{24,8},{28,12},{1,17},{... | collective-permute-start | bytes 233480 | tf_op jit(solution)/shard_map/ppermute | solution.py:488
  20.6 4.3 %copy-start = (bf16[128,2048]{1,0:T(8,128)(2,1)S(1)}, bf16[128,2048]{1,0:T(8,128)(2,1)}, u32[]{:S(2)}) copy-start(bf16[128,2048]{1,0:T(8,128)(2,1)} %refs_6_.3) | copy-start | bytes 1572868
  20.6 4.3 %copy-start.1 = (bf16[128,2048]{1,0:T(8,128)(2,1)S(1)}, bf16[128,2048]{1,0:T(8,128)(2,1)}, u32[]{:S(2)}) copy-start(bf16[128,2048]{1,0:T(8,128)(2,1)} %refs_5_.3) | copy-start | bytes 1572868
  20.6 4.3 %copy-start.2 = (bf16[128,2048]{1,0:T(8,128)(2,1)S(1)}, bf16[128,2048]{1,0:T(8,128)(2,1)}, u32[]{:S(2)}) copy-start(bf16[128,2048]{1,0:T(8,128)(2,1)} %refs_4_.3) | copy-start | bytes 1572868
  20.9 1.3 %collective-permute-start.4 = (bf16[304,128]{1,0:T(8,128)(2,1)S(1)}, bf16[304,128]{1,0:T(8,128)(2,1)S(1)}, u32[]{:S(2)}, u32[]{:S(2)}) collective-permute-start(bf16[304,128]{1,0:T(8,128)(2,1)S(1)} %get-tuple-element.45.refs_2_), channel_id=1, source_target_pairs={{0,4},{4,0},{8,12},{12,8},{16,20},{20,16},{24,28},{28,24},{1,5},{5... | collective-permute-start | bytes 233480 | tf_op jit(solution)/shard_map/ppermute | solution.py:488
  22.2 4.7 %collective-permute-start.5 = (bf16[48,128]{1,0:T(8,128)(2,1)S(1)}, bf16[48,128]{1,0:T(8,128)(2,1)S(1)}, u32[]{:S(2)}, u32[]{:S(2)}) collective-permute-start(bf16[48,128]{1,0:T(8,128)(2,1)S(1)} %merge.1.own_ref), channel_id=1, source_target_pairs={{0,2},{1,3},{2,0},{3,1},{4,6},{5,7},{6,4},{7,5},{8,10},{9,11},{10,... | collective-permute-start | bytes 36872 | tf_op jit(solution)/shard_map/ppermute | solution.py:616
  26.9 3.8 %collective-permute-start.6 = (bf16[96,128]{1,0:T(8,128)(2,1)S(1)}, bf16[96,128]{1,0:T(8,128)(2,1)S(1)}, u32[]{:S(2)}, u32[]{:S(2)}) collective-permute-start(bf16[96,128]{1,0:T(8,128)(2,1)S(1)} %stack.1.refs_10_.refs_0_), channel_id=1, source_target_pairs={{0,1},{1,0},{2,3},{3,2},{4,5},{5,4},{6,7},{7,6},{8,9},{9,8},{10,11... | collective-permute-start | bytes 73736 | tf_op jit(solution)/shard_map/ppermute | solution.py:616

commit v11 on v10

--- a/solution.py
+++ b/solution.py
@@ -389,8 +389,8 @@
 
 
 def merge_kernel(logs_ref, res_ref, own_ref, got_ref, out_ref, *, poles, length):
-    groups = out_ref.shape[1]
-    start = own_ref.shape[0] - out_ref.shape[0]
+    groups = out_ref.shape[2]
+    start = own_ref.shape[0] - out_ref.shape[1]
     both = own_ref[start:, :].astype(F32) + got_ref[start:, :].astype(F32)
     first = shard_start(groups)
     factor = -jnp.exp(logs_ref[:, pl.ds(first, groups)]) * res_ref[:, pl.ds(first, groups)]
@@ -399,15 +399,17 @@
         factor * both[poles : 2 * poles] / math.sqrt(length),
         both[2 * poles :] / math.sqrt(length),
     ]
-    out_ref[...] = jnp.concatenate(scaled, axis=0).astype(BF16)
-
-
-def output_kernel(rows_ref, conv_ref, mine_ref, got_ref, k_ref, v_ref, c_ref, *rest, offset, group, poles):
-    gq_ref, gk_ref, gv_ref, mark_ref = rest[-4:]
+    scaled = jnp.concatenate(scaled, axis=0).astype(BF16)
+    for n in range(out_ref.shape[0]):
+        out_ref[n] = scaled
+
+
+def output_kernel(rows_ref, conv_ref, mine_ref, got_ref, k_ref, v_ref, c_ref, gq_ref, gk_ref, gv_ref,
+                  mark_ref, *, group, poles):
     mark_ref[...] = jnp.zeros_like(mark_ref)
     tokens, width = gq_ref.shape
     per_block = LANES // group
-    step = pl.program_id(0) + offset
+    step = pl.program_id(0)
     inner = width // LANES
     half_blocks = mine_ref.shape[0]
     core = lax.rem(lax.axis_index("ctx"), 2)
@@ -440,26 +442,15 @@
     gv_ref[...] = (flow * k_ref[:, cut].astype(F32)).astype(BF16)
 
 
-def stack_kernel(own_ref, got_ref, _, out_ref):
-    rows = own_ref.shape[0]
-    out_ref[:rows, :] = own_ref[...]
-    out_ref[rows:, :] = got_ref[...]
-
-
-def assemble_kernel(own_ref, got_ref, res_ref, log_ref, skip_ref, *, masks, poles):
-    shards = len(masks)
-    me = lax.axis_index("ch")
-    groups = own_ref.shape[1]
-    half = shards // 2
-    piece = own_ref.shape[0] // half
-    rows = piece - 2 * poles
-    for k, mask in enumerate(masks):
-        source = lax.bitwise_xor(me, mask)
-        value = (own_ref if k < half else got_ref)[k % half * piece : (k % half + 1) * piece, :].astype(F32)
-        cut = pl.ds(pl.multiple_of(source * groups, LANES), groups)
+def assemble_kernel(pieces_ref, _, res_ref, log_ref, skip_ref, *, poles):
+    shards, rows, groups = pieces_ref.shape
+    rows -= 2 * poles
+    for n in range(shards):
+        value = pieces_ref[n].astype(F32)
+        cut = slice(n * groups, (n + 1) * groups)
         res_ref[:, cut] = value[:poles]
         log_ref[:, cut] = value[poles : 2 * poles]
-        skip_ref[pl.ds(pl.multiple_of(source * rows, 8), rows), :] = value[2 * poles :]
+        skip_ref[n * rows : (n + 1) * rows, :] = value[2 * poles :]
 
 
 def local(queries, key_input, value_input, cotangent, residues, log_rates, skip_gain):
@@ -589,54 +580,33 @@
         lambda *refs: merge_kernel(*refs, poles=poles, length=tokens * parts),
         in_specs=[vmem] * 4,
         out_specs=vmem,
-        out_shape=shape(tail, LANES, dtype=BF16),
+        out_shape=shape(shards, tail, LANES, dtype=BF16),
         compiler_params=PARAMS,
         name="merge",
     )(log_rates, residues, outgoing, got)
 
-    def emit(offset, before):
-        count = steps // 2
-        main = pl.BlockSpec((tokens, inner * LANES), lambda i: (0, i + offset))
-        return pl.pallas_call(
-            lambda *refs: output_kernel(*refs, offset=offset, **sizes),
-            grid=(count,),
-            in_specs=[vmem] * 7 + [anywhere] * len(before),
-            out_specs=[main] * 3 + [pl.BlockSpec((8, LANES), lambda i: (0, 0))],
-            out_shape=[shape(tokens, width, dtype=BF16)] * 3 + [shape(8, LANES)],
-            input_output_aliases={7 + n: n for n in range(3)} if offset else {},
-            compiler_params=PARAMS,
-            cost_estimate=pl.CostEstimate(
-                flops=4 * tokens * tokens * width, bytes_accessed=8 * tokens * width, transcendentals=tokens * width
-            ),
-            name="outputs",
-        )(rows, conv, mine, got, key_input, value_input, cotangent, *before)
-
-    own, after, masks = merged, [], [0]
-    for level in reversed(range(shards.bit_length() - 1)):
-        other = lax.ppermute(own, "ch", [(i, i ^ (1 << level)) for i in range(shards)])
-        masks += [mask ^ (1 << level) for mask in masks]
-        if level == 0:
-            break
-        if not after:
-            after = emit(0, [])
-        own = pl.pallas_call(
-            stack_kernel,
-            in_specs=[vmem, vmem, anywhere],
-            out_specs=vmem,
-            out_shape=shape(2 * own.shape[0], LANES, dtype=BF16),
-            compiler_params=PARAMS,
-            name="stack",
-        )(own, other, after[3])
-    grad_query, grad_key, grad_value, _ = emit(steps // 2, [*after[:3], own])
+    pieces = lax.all_to_all(merged, "ch", split_axis=0, concat_axis=0, tiled=True)
+
+    main = pl.BlockSpec((tokens, inner * LANES), lambda i: (0, i))
+    grad_query, grad_key, grad_value, mark = pl.pallas_call(
+        lambda *refs: output_kernel(*refs, **sizes),
+        grid=(steps,),
+        in_specs=[vmem] * 7,
+        out_specs=[main] * 3 + [pl.BlockSpec((8, LANES), lambda i: (0, 0))],
+        out_shape=[shape(tokens, width, dtype=BF16)] * 3 + [shape(8, LANES)],
+        compiler_params=PARAMS,
+        cost_estimate=work,
+        name="outputs",
+    )(rows, conv, mine, got, key_input, value_input, cotangent)
 
     grad_residue, grad_lograte, grad_skip = pl.pallas_call(
-        lambda *refs: assemble_kernel(*refs, masks=masks, poles=poles),
+        lambda *refs: assemble_kernel(*refs, poles=poles),
         in_specs=[vmem] * 2,
         out_specs=[vmem] * 3,
         out_shape=[shape(poles, all_groups), shape(poles, all_groups), shape(shards * blocks, LANES)],
         compiler_params=PARAMS,
         name="assemble",
-    )(own, other)
+    )(pieces, mark)
     return (grad_query, grad_key, grad_value, grad_residue.T, grad_lograte.T, grad_skip.reshape(-1))
 
 

time: 31.5 us -> 34.3 us (1.089)
  local copies, waits for them, and re-layouts: 0.03 us -> 1.06 us
  waiting for transfers between devices: 6.17 us -> 7.02 us
  starting transfers between devices: 9.02 us -> 9.66 us
    all_to_all x0 -> x1, starting transfers between devices: none -> 4.88 us  [local(): lax.all_to_all(merged, 'ch', split_axis=0, concat_axis=0, tiled=True)]
    ppermute x2 -> x0, starting transfers between devices: 4.24 us -> none  [local(): lax.ppermute(own, 'ch', [(i, i ^ 1 << level) for i in range(shards)])]
    all_to_all x0 -> x1, waiting for transfers between devices: none -> 2.07 us  [local(): lax.all_to_all(merged, 'ch', split_axis=0, concat_axis=0, tiled=True)]
    ppermute x2 -> x0, waiting for transfers between devices: 1.23 us -> none  [local(): lax.ppermute(own, 'ch', [(i, i ^ 1 << level) for i in range(shards)])]
    unnamed x12, local copies, waits for them, and re-layouts: 0.03 us -> 1.06 us
    pallas_call x1, Pallas kernels: 0.02 us -> 0.63 us  [local(): pl.pallas_call(lambda *refs: merge_kernel(*refs, poles=poles, length=toke...]
    pallas_call x4 -> x2, Pallas kernels: 3.66 us -> 3.22 us  [the longest x1 2.58 us: local(): pl.pallas_call(lambda *refs: output_kernel(*refs, **sizes), grid=(steps,)...]
  transfers between devices with their start and end apart: 7 -> 6, of which waited for: 4 -> 3; matrix products, arithmetic and copies ran while one was open for 0% -> 0% of each run, Pallas kernels for 31% -> 27%
where the time goes in v11:
time: 34.3 us; the launch traced here: 34.1 us
  Pallas kernels  13.6 us (40%)
  starting transfers between devices  9.66 us (28%)
  waiting for transfers between devices  7.02 us (20%)
  other arithmetic  1.92 us (6%)
  local copies, waits for them, and re-layouts  1.06 us (3%)
  between operations  0.76 us (2%)
    ppermute x5, waiting for transfers between devices, swap(): lax.ppermute(value, 'ctx', [(i, i ^ 1 << level) for i in range(parts)])  4.95 us
    all_to_all x1, starting transfers between devices, local(): lax.all_to_all(merged, 'ch', split_axis=0, concat_axis=0, tiled=True)  4.88 us
    ppermute x5, starting transfers between devices, swap(): lax.ppermute(value, 'ctx', [(i, i ^ 1 << level) for i in range(parts)])  4.78 us
    pallas_call x1, Pallas kernels, convolve(): pl.pallas_call(lambda *refs: conv_kernel(*refs, inner=inner, **sizes), in...  3.64 us
    pallas_call x2, Pallas kernels, local_sums(): pl.pallas_call(lambda *refs: lags_kernel(*refs, second=second, inner=inne...  2.79 us
    pallas_call x1, Pallas kernels, local(): pl.pallas_call(lambda *refs: output_kernel(*refs, **sizes), grid=(steps,)...  2.58 us
    pallas_call x1, Pallas kernels, local(): pl.pallas_call(lambda *refs: states_kernel(*refs, inner=inner, **sizes),...  2.16 us
    all_to_all x1, waiting for transfers between devices, local(): lax.all_to_all(merged, 'ch', split_axis=0, concat_axis=0, tiled=True)  2.07 us
  transfers between devices with their start and end apart: 6, of which 3 were waited for; matrix products, arithmetic and copies ran while one was open for 0% of the time, Pallas kernels for 27%

profile of v11, /device:TPU:0, one launch (start us, length us, event | category | flops | bytes accessed | tf_op | source)
XLA Modules:
  0.0 34.1 jit_solution(1245786726479900817)
XLA Ops:
  0.6 0.0 copy-start.4
  0.6 0.0 copy-start.3
  0.7 1.9 %multiply_convert_fusion = (bf16[128,2048]{1,0:T(8,128)(2,1)S(1)}, bf16[128,2048]{1,0:T(8,128)(2,1)S(1)}) fusion(bf16[128,2048]{1,0:T(8,128)(2,1)} %param.7, bf16[128,2048]{1,0:T(8,128)(2,1)} %refs_6_.1, bf16[128,2048]{1,0:T(8,128)(2,1)} %refs_5_.1, bf16[128,2048]{1,0:T(8,128)(2,1)} %refs_4_.1), kind=kLoop, calls=%fused_computation | loop fusion | flops 2097152 | bytes 3145728 | tf_op jit(solution)/shard_map/convert_element_type | solution.py:44
  2.6 0.0 copy-done.4
  2.6 0.0 copy-done.3
  2.6 2.2 %states.1 = (bf16[512,128]{1,0:T(8,128)(2,1)S(1)}, bf16[512,128]{1,0:T(8,128)(2,1)S(1)}, bf16[128,2048]{1,0:T(8,128)(2,1)S(1)}, f32[2,16,128]{2,1,0:T(8,128)S(1)}) custom-call(f32[16,512]{1,0:T(8,128)S(1)} %bitcast.9, f32[16,512]{1,0:T(8,128)S(1)} %bitcast.6, bf16[128,2048]{1,0:T(8,128)(2,1)S(1)} %get-tuple-element.51.refs_2_.refs_1_.refs_5_, ...), custom_call_target="tpu_custom_call" | custom-call | tf_op jit(solution)/shard_map/states/pallas_call | solution.py:482
  4.8 0.5 %collective-permute-start = (bf16[512,128]{1,0:T(8,128)(2,1)S(1)}, bf16[512,128]{1,0:T(8,128)(2,1)S(1)}, u32[]{:S(2)}, u32[]{:S(2)}) collective-permute-start(bf16[512,128]{1,0:T(8,128)(2,1)S(1)} %get-tuple-element.33), channel_id=1, source_target_pairs={{0,4},{4,0},{8,12},{12,8},{16,20},{20,16},{24,28},{28,24},{1,5},{5... | collective-permute-start | bytes 393224 | tf_op jit(solution)/shard_map/ppermute | solution.py:479
  5.3 0.4 %tables.1 = (f32[16,16,128]{2,1,0:T(8,128)S(1)}, f32[16,16,256]{2,1,0:T(8,128)S(1)}) custom-call(f32[16,512]{1,0:T(8,128)S(1)} %bitcast.10, f32[2,16,128]{2,1,0:T(8,128)S(1)} %get-tuple-element.28.refs_1_.refs_0_), custom_call_target="tpu_custom_call" | custom-call | flops 1000000000 | bytes 1000000 | tf_op jit(solution)/shard_map/tables/pallas_call | solution.py:496
  5.6 0.0 copy-start.5
  5.7 1.3 %lags.2.refs_3_ = f32[32,128]{1,0:T(8,128)S(1)} custom-call(f32[16,16,256]{2,1,0:T(8,128)S(1)} %get-tuple-element.30.refs_0_.refs_4_, bf16[128,2048]{1,0:T(8,128)(2,1)S(1)} %get-tuple-element.51.refs_2_.refs_1_.refs_5_, bf16[128,2048]{1,0:T(8,128)(2,1)S(1)} %get-tuple-element.50.refs_3_.refs_2_, bf16[128,2048]{1,0:T(8,128)(2,1)S(1)} %get-tuple-element.31.refs_3_.refs_6_), custom_call_target="tpu_custom_call" | custom-call | flops 536870912 | bytes 3145728 | tf_op jit(solution)/shard_map/lags/pallas_call | solution.py:511
  7.0 0.0 collective-permute-done.refs_2_
  7.0 0.3 combine.3
  7.3 2.6 %collective-permute-start.1 = (bf16[512,128]{1,0:T(8,128)(2,1)S(1)}, bf16[512,128]{1,0:T(8,128)(2,1)S(1)}, u32[]{:S(2)}, u32[]{:S(2)}) collective-permute-start(bf16[512,128]{1,0:T(8,128)(2,1)S(1)} %get-tuple-element.34.refs_1_), channel_id=1, source_target_pairs={{0,8},{4,12},{8,0},{12,4},{16,24},{20,28},{24,16},{28,20},{1,9},{5... | collective-permute-start | bytes 393224 | tf_op jit(solution)/shard_map/ppermute | solution.py:479
  9.8 1.5 %lags.3.refs_2_ = bf16[48,128]{1,0:T(8,128)(2,1)S(1)} custom-call(f32[16,16,256]{2,1,0:T(8,128)S(1)} %get-tuple-element.30.refs_0_.refs_4_, bf16[128,2048]{1,0:T(8,128)(2,1)S(1)} %get-tuple-element.51.refs_2_.refs_1_.refs_5_, bf16[128,2048]{1,0:T(8,128)(2,1)S(1)} %get-tuple-element.50.refs_3_.refs_2_, ...), custom_call_target="tpu_custom_call" | custom-call | flops 536870912 | bytes 3145728 | tf_op jit(solution)/shard_map/lags/pallas_call | solution.py:511
  11.3 0.1 collective-permute-start.2
  11.4 3.7 %collective-permute-done.2.refs_4_ = bf16[48,128]{1,0:T(8,128)(2,1)S(1)} collective-permute-done((bf16[48,128]{1,0:T(8,128)(2,1)S(1)}, bf16[48,128]{1,0:T(8,128)(2,1)S(1)}, u32[]{:S(2)}, u32[]{:S(2)}) %collective-permute-start.2) | collective-permute-done | bytes 12320 | tf_op jit(solution)/shard_map/ppermute | solution.py:479
  15.1 0.0 collective-permute-done.1.refs_3_
  15.1 0.3 combine.4
  15.4 1.6 %collective-permute-start.3 = (bf16[304,128]{1,0:T(8,128)(2,1)S(1)}, bf16[304,128]{1,0:T(8,128)(2,1)S(1)}, u32[]{:S(2)}, u32[]{:S(2)}) collective-permute-start(bf16[304,128]{1,0:T(8,128)(2,1)S(1)} %get-tuple-element.39), channel_id=1, source_target_pairs={{0,16},{4,20},{8,24},{12,28},{16,0},{20,4},{24,8},{28,12},{1,17},{... | collective-permute-start | bytes 233480 | tf_op jit(solution)/shard_map/ppermute | solution.py:479
  16.9 0.0 copy-done.5
  16.9 3.6 %conv.1.refs_5_.refs_1_ = f32[128,4096]{1,0:T(8,128)S(1)} custom-call(f32[16,512]{1,0:T(8,128)S(1)} %bitcast.7, f32[2,16,128]{2,1,0:T(8,128)S(1)} %get-tuple-element.28.refs_1_.refs_0_, f32[64,128]{1,0:T(8,128)S(1)} %bitcast.12, f32[16,16,128]{2,1,0:T(8,128)S(1)} %get-tuple-element.29.refs_0_.refs_3_, f32[16,16,256]{2,1,0:T(8,128)S(1)} %get-tuple-element.30.refs_0_.refs_4_, ...), custom_call_target="tpu_custom_call" | custom-call | flops 536870912 | bytes 3145728 | tf_op jit(solution)/shard_map/conv/pallas_call | solution.py:524
  20.6 0.0 copy-start
  20.6 0.0 copy-start.1
  20.6 0.0 collective-permute-done.3.refs_3_
  20.6 0.3 combine.5
  20.9 0.1 collective-permute-start.4
  20.9 1.3 %collective-permute-done.4.refs_3_ = bf16[304,128]{1,0:T(8,128)(2,1)S(1)} collective-permute-done((bf16[304,128]{1,0:T(8,128)(2,1)S(1)}, bf16[304,128]{1,0:T(8,128)(2,1)S(1)}, u32[]{:S(2)}, u32[]{:S(2)}) %collective-permute-start.4) | collective-permute-done | bytes 77856 | tf_op jit(solution)/shard_map/ppermute | solution.py:479
  22.2 0.6 %merge.1 = bf16[4,48,128]{2,1,0:T(8,128)(2,1)} custom-call(f32[16,512]{1,0:T(8,128)S(1)} %bitcast.11, f32[16,512]{1,0:T(8,128)S(1)} %bitcast.8, bf16[304,128]{1,0:T(8,128)(2,1)S(1)} %get-tuple-element.42.refs_2_, bf16[304,128]{1,0:T(8,128)(2,1)S(1)} %collective-permute-done.4.refs_3_), custom_call_target="tpu_custom_call" | custom-call | tf_op jit(solution)/shard_map/merge/pallas_call | solution.py:579
  22.8 4.9 %all-to-all-start = ((bf16[4,48,128]{2,1,0:T(8,128)(2,1)}), bf16[4,48,128]{2,1,0:T(8,128)(2,1)S(1)}, u32[]{:S(2)}, u32[]{:S(2)}) async-start(bf16[4,48,128]{2,1,0:T(8,128)(2,1)} %merge.1), calls=%async_computation | async-start | bytes 98304 | tf_op jit(solution)/shard_map/all_to_all | solution.py:588
  27.7 0.0 copy-done
  27.7 0.0 copy-done.1
  27.7 0.0 copy-start.2
  27.7 1.0 %copy-done.2 = bf16[128,2048]{1,0:T(8,128)(2,1)S(1)} copy-done((bf16[128,2048]{1,0:T(8,128)(2,1)S(1)}, bf16[128,2048]{1,0:T(8,128)(2,1)}, u32[]{:S(2)}) %copy-start.2) | copy-done | bytes 524312
  28.8 2.6 %outputs.1 = (bf16[128,2048]{1,0:T(8,128)(2,1)}, bf16[128,2048]{1,0:T(8,128)(2,1)}, bf16[128,2048]{1,0:T(8,128)(2,1)}, f32[8,128]{1,0:T(8,128)S(1)}) custom-call(f32[2,16,128]{2,1,0:T(8,128)S(1)} %get-tuple-element.28.refs_1_.refs_0_, f32[128,4096]{1,0:T(8,128)S(1)} %conv.1.refs_5_.refs_1_, bf16[8,32,128]{2,1,0:T(8,128)(2,1)S(1)} %get-tuple-element.41.refs_2_, ...), custom_call_target="tpu_custom_call" | custom-call | flops 536870912 | bytes 3145728 | tf_op jit(solution)/shard_map/outputs/pallas_call | solution.py:591
  31.3 2.1 %all-to-all-done.refs_0_ = bf16[4,48,128]{2,1,0:T(8,128)(2,1)S(1)} async-done(((bf16[4,48,128]{2,1,0:T(8,128)(2,1)}), bf16[4,48,128]{2,1,0:T(8,128)(2,1)S(1)}, u32[]{:S(2)}, u32[]{:S(2)}) %all-to-all-start) | async-done | bytes 49184 | tf_op jit(solution)/shard_map/all_to_all | solution.py:588
  33.4 0.6 %assemble.1 = (f32[16,512]{1,0:T(8,128)}, f32[16,512]{1,0:T(8,128)}, f32[64,128]{1,0:T(8,128)}) custom-call(bf16[4,48,128]{2,1,0:T(8,128)(2,1)S(1)} %all-to-all-done.refs_0_, f32[8,128]{1,0:T(8,128)S(1)} %get-tuple-element.46.refs_1_), custom_call_target="tpu_custom_call" | custom-call | tf_op jit(solution)/shard_map/assemble/pallas_call | solution.py:602
Async XLA Ops:
  0.6 1.9 %copy-start.4 = (f32[512,16]{0,1:T(8,128)S(1)}, f32[512,16]{0,1:T(8,128)}, u32[]{:S(2)}) copy-start(f32[512,16]{0,1:T(8,128)} %param.12) | copy-start | bytes 98308
  0.6 1.9 %copy-start.3 = (f32[512,16]{0,1:T(8,128)S(1)}, f32[512,16]{0,1:T(8,128)}, u32[]{:S(2)}) copy-start(f32[512,16]{0,1:T(8,128)} %param.11) | copy-start | bytes 98308
  4.8 2.2 %collective-permute-start = (bf16[512,128]{1,0:T(8,128)(2,1)S(1)}, bf16[512,128]{1,0:T(8,128)(2,1)S(1)}, u32[]{:S(2)}, u32[]{:S(2)}) collective-permute-start(bf16[512,128]{1,0:T(8,128)(2,1)S(1)} %get-tuple-element.33), channel_id=1, source_target_pairs={{0,4},{4,0},{8,12},{12,8},{16,20},{20,16},{24,28},{28,24},{1,5},{5... | collective-permute-start | bytes 393224 | tf_op jit(solution)/shard_map/ppermute | solution.py:479
  5.6 11.3 %copy-start.5 = (f32[8192]{0:T(1024)S(1)}, f32[8192]{0:T(1024)}, u32[]{:S(2)}) copy-start(f32[8192]{0:T(1024)} %param.13) | copy-start | bytes 98308
  7.3 7.8 %collective-permute-start.1 = (bf16[512,128]{1,0:T(8,128)(2,1)S(1)}, bf16[512,128]{1,0:T(8,128)(2,1)S(1)}, u32[]{:S(2)}, u32[]{:S(2)}) collective-permute-start(bf16[512,128]{1,0:T(8,128)(2,1)S(1)} %get-tuple-element.34.refs_1_), channel_id=1, source_target_pairs={{0,8},{4,12},{8,0},{12,4},{16,24},{20,28},{24,16},{28,20},{1,9},{5... | collective-permute-start | bytes 393224 | tf_op jit(solution)/shard_map/ppermute | solution.py:479
  11.3 3.8 %collective-permute-start.2 = (bf16[48,128]{1,0:T(8,128)(2,1)S(1)}, bf16[48,128]{1,0:T(8,128)(2,1)S(1)}, u32[]{:S(2)}, u32[]{:S(2)}) collective-permute-start(bf16[48,128]{1,0:T(8,128)(2,1)S(1)} %lags.3.refs_2_), channel_id=1, source_target_pairs={{0,8},{4,12},{8,0},{12,4},{16,24},{20,28},{24,16},{28,20},{1,9},{5... | collective-permute-start | bytes 36872 | tf_op jit(solution)/shard_map/ppermute | solution.py:479
  15.4 5.2 %collective-permute-start.3 = (bf16[304,128]{1,0:T(8,128)(2,1)S(1)}, bf16[304,128]{1,0:T(8,128)(2,1)S(1)}, u32[]{:S(2)}, u32[]{:S(2)}) collective-permute-start(bf16[304,128]{1,0:T(8,128)(2,1)S(1)} %get-tuple-element.39), channel_id=1, source_target_pairs={{0,16},{4,20},{8,24},{12,28},{16,0},{20,4},{24,8},{28,12},{1,17},{... | collective-permute-start | bytes 233480 | tf_op jit(solution)/shard_map/ppermute | solution.py:479
  20.6 7.1 %copy-start = (bf16[128,2048]{1,0:T(8,128)(2,1)S(1)}, bf16[128,2048]{1,0:T(8,128)(2,1)}, u32[]{:S(2)}) copy-start(bf16[128,2048]{1,0:T(8,128)(2,1)} %refs_6_.1) | copy-start | bytes 1572868
  20.6 7.1 %copy-start.1 = (bf16[128,2048]{1,0:T(8,128)(2,1)S(1)}, bf16[128,2048]{1,0:T(8,128)(2,1)}, u32[]{:S(2)}) copy-start(bf16[128,2048]{1,0:T(8,128)(2,1)} %refs_5_.1) | copy-start | bytes 1572868
  20.9 1.3 %collective-permute-start.4 = (bf16[304,128]{1,0:T(8,128)(2,1)S(1)}, bf16[304,128]{1,0:T(8,128)(2,1)S(1)}, u32[]{:S(2)}, u32[]{:S(2)}) collective-permute-start(bf16[304,128]{1,0:T(8,128)(2,1)S(1)} %get-tuple-element.42.refs_2_), channel_id=1, source_target_pairs={{0,4},{4,0},{8,12},{12,8},{16,20},{20,16},{24,28},{28,24},{1,5},{5... | collective-permute-start | bytes 233480 | tf_op jit(solution)/shard_map/ppermute | solution.py:479
  22.8 10.6 %all-to-all-start = ((bf16[4,48,128]{2,1,0:T(8,128)(2,1)}), bf16[4,48,128]{2,1,0:T(8,128)(2,1)S(1)}, u32[]{:S(2)}, u32[]{:S(2)}) async-start(bf16[4,48,128]{2,1,0:T(8,128)(2,1)} %merge.1), calls=%async_computation | async-start | bytes 98304 | tf_op jit(solution)/shard_map/all_to_all | solution.py:588
  27.7 1.0 %copy-start.2 = (bf16[128,2048]{1,0:T(8,128)(2,1)S(1)}, bf16[128,2048]{1,0:T(8,128)(2,1)}, u32[]{:S(2)}) copy-start(bf16[128,2048]{1,0:T(8,128)(2,1)} %refs_4_.1) | copy-start | bytes 1572868

commit v12 on v11

--- a/solution.py
+++ b/solution.py
@@ -148,9 +148,9 @@
     near_side, no_wrap = row + lane <= SUB - 1, lane >= row
     lag = (SUB - 1 - within(iota((poles, lag_width), 1), SUB)).astype(F32)
     spread = members(step_groups, 0, SUB, inner * lag_width)
-    half_steps = blocks // inner // 2
+    steps = blocks // inner
     sums = []
-    for step in range(half_steps * second, half_steps * (second + 1)):
+    for step in range(1, steps) if second else range(1):
         outers = []
         for j in range(inner):
             lanes = slice((step * inner + j) * LANES, (step * inner + j + 1) * LANES)
@@ -188,7 +188,7 @@
             )
         sums.append(mxu_t(jnp.concatenate(terms, axis=1), spread))
     sums = jnp.concatenate(sums, axis=1)
-    zeros = jnp.zeros_like(sums)
+    zeros = jnp.zeros((sums.shape[0], blocks * per_block - sums.shape[1]), F32)
     sums = jnp.concatenate([zeros, sums] if second else [sums, zeros], axis=1)
     sums = join(sums, 2 * poles)
     if not second:
@@ -222,7 +222,7 @@
 
 
 def conv_kernel(res_ref, rows_ref, skip_ref, rates_ref, lag_rates_ref, gated_ref, turned_ref, _, conv_ref,
-                *, group, poles, inner):
+                *, first_step, group, poles, inner):
     tokens, _ = gated_ref.shape
     per_block = LANES // group
     blocks, _, _ = rates_ref.shape
@@ -239,7 +239,7 @@
     spread = members(groups, 0, SUB, inner * lag_width)
 
     def body(step, carry):
-        start = step * inner
+        start = (step + first_step) * inner
         moved = pltpu.roll(pieces, groups - start * per_block, 1).astype(BF16)
         lag_res = join(mxu(moved, spread), poles)
         lefts, lead_tables, decays, pairs, gains = [], [], [], [], []
@@ -278,11 +278,11 @@
                 totals[j].append(total)
             states = [decays[j] * states[j] + found[j][SUB:] for j in range(inner)]
         for j in range(inner):
-            cut = pl.ds(pl.multiple_of(2 * (start + j) * LANES, LANES), 2 * LANES)
+            cut = pl.ds(pl.multiple_of(2 * (step * inner + j) * LANES, LANES), 2 * LANES)
             conv_ref[:, cut] = jnp.concatenate(totals[j], axis=0)
         return carry
 
-    lax.fori_loop(0, blocks // inner, body, 0)
+    lax.fori_loop(0, conv_ref.shape[1] // (2 * inner * LANES), body, 0)
 
 
 def combine_kernel(*refs, level, levels, group, poles, tokens):
@@ -388,9 +388,9 @@
             slim_ref[tail:, :] = rests
 
 
-def merge_kernel(logs_ref, res_ref, own_ref, got_ref, out_ref, *, poles, length):
-    groups = out_ref.shape[2]
-    start = own_ref.shape[0] - out_ref.shape[1]
+def merge_kernel(logs_ref, res_ref, own_ref, got_ref, _, out_ref, *, poles, length):
+    groups = out_ref.shape[1]
+    start = own_ref.shape[0] - out_ref.shape[0]
     both = own_ref[start:, :].astype(F32) + got_ref[start:, :].astype(F32)
     first = shard_start(groups)
     factor = -jnp.exp(logs_ref[:, pl.ds(first, groups)]) * res_ref[:, pl.ds(first, groups)]
@@ -399,17 +399,15 @@
         factor * both[poles : 2 * poles] / math.sqrt(length),
         both[2 * poles :] / math.sqrt(length),
     ]
-    scaled = jnp.concatenate(scaled, axis=0).astype(BF16)
-    for n in range(out_ref.shape[0]):
-        out_ref[n] = scaled
-
-
-def output_kernel(rows_ref, conv_ref, mine_ref, got_ref, k_ref, v_ref, c_ref, gq_ref, gk_ref, gv_ref,
-                  mark_ref, *, group, poles):
-    mark_ref[...] = jnp.zeros_like(mark_ref)
+    out_ref[...] = jnp.concatenate(scaled, axis=0).astype(BF16)
+
+
+def output_kernel(rows_ref, conv_ref, last_ref, mine_ref, got_ref, k_ref, v_ref, c_ref, gq_ref, gk_ref, gv_ref,
+                  *, group, poles):
     tokens, width = gq_ref.shape
     per_block = LANES // group
     step = pl.program_id(0)
+    steps = pl.num_programs(0)
     inner = width // LANES
     half_blocks = mine_ref.shape[0]
     core = lax.rem(lax.axis_index("ctx"), 2)
@@ -418,39 +416,53 @@
     state_group = over(within(iota((poles, 2 * LANES), 1), LANES), group)
     start = step * inner
     is_mine = over(start, half_blocks) == core
-    totals = []
-    for j in range(inner):
-        here = start + j
-        rate = rows_ref[0, pl.ds(here, 1), :]
-        res = rows_ref[1, pl.ds(here, 1), :]
-        table = (res * jnp.exp(-rate * ahead)).astype(BF16)
-        place = within(here, half_blocks)
-        held = jnp.where(
-            is_mine, mine_ref[place], got_ref[pl.ds(pl.multiple_of(place * 2 * poles, 2 * poles), 2 * poles), :]
-        )
-        states = jnp.concatenate([held[:poles], held[poles:]], axis=1)
-        stack = jnp.concatenate(
-            [jnp.where(state_group == g, states, jnp.zeros_like(states)) for g in range(per_block)], axis=0
-        )
-        both = pl.ds(pl.multiple_of(2 * here * LANES, LANES), 2 * LANES)
-        totals.append((conv_ref[:, both] + mxu(table, stack)).astype(BF16))
-    hidden = jnp.concatenate([t[:, :LANES] for t in totals], axis=1)
-    flow = mxu(flip, jnp.concatenate([t[:, LANES:] for t in totals], axis=1))
     cut = pl.ds(pl.multiple_of(start * LANES, LANES), width)
-    gq_ref[...] = (c_ref[:, cut].astype(F32) * hidden.astype(F32)).astype(BF16)
-    gk_ref[...] = (flow * v_ref[:, cut].astype(F32)).astype(BF16)
-    gv_ref[...] = (flow * k_ref[:, cut].astype(F32)).astype(BF16)
-
-
-def assemble_kernel(pieces_ref, _, res_ref, log_ref, skip_ref, *, poles):
-    shards, rows, groups = pieces_ref.shape
-    rows -= 2 * poles
-    for n in range(shards):
-        value = pieces_ref[n].astype(F32)
-        cut = slice(n * groups, (n + 1) * groups)
+
+    def emit(conv_ref, base):
+        totals = []
+        for j in range(inner):
+            here = start + j
+            rate = rows_ref[0, pl.ds(here, 1), :]
+            res = rows_ref[1, pl.ds(here, 1), :]
+            table = (res * jnp.exp(-rate * ahead)).astype(BF16)
+            place = within(here, half_blocks)
+            held = jnp.where(
+                is_mine, mine_ref[place], got_ref[pl.ds(pl.multiple_of(place * 2 * poles, 2 * poles), 2 * poles), :]
+            )
+            states = jnp.concatenate([held[:poles], held[poles:]], axis=1)
+            stack = jnp.concatenate(
+                [jnp.where(state_group == g, states, jnp.zeros_like(states)) for g in range(per_block)], axis=0
+            )
+            both = pl.ds(pl.multiple_of(2 * (here - base) * LANES, LANES), 2 * LANES)
+            totals.append((conv_ref[:, both] + mxu(table, stack)).astype(BF16))
+        hidden = jnp.concatenate([t[:, :LANES] for t in totals], axis=1)
+        flow = mxu(flip, jnp.concatenate([t[:, LANES:] for t in totals], axis=1))
+        gq_ref[...] = (c_ref[:, cut].astype(F32) * hidden.astype(F32)).astype(BF16)
+        gk_ref[...] = (flow * v_ref[:, cut].astype(F32)).astype(BF16)
+        gv_ref[...] = (flow * k_ref[:, cut].astype(F32)).astype(BF16)
+
+    @pl.when(step < steps - 1)
+    def _():
+        emit(conv_ref, 0)
+
+    @pl.when(step == steps - 1)
+    def _():
+        emit(last_ref, (steps - 1) * inner)
+
+
+def assemble_kernel(*refs, poles):
+    *slots, res_ref, log_ref, skip_ref = refs
+    shards = len(slots)
+    me = lax.axis_index("ch")
+    groups = slots[0].shape[1]
+    rows = slots[0].shape[0] - 2 * poles
+    for shift, slot in enumerate(slots):
+        source = lax.rem(me - shift + shards, shards)
+        value = slot[...].astype(F32)
+        cut = pl.ds(pl.multiple_of(source * groups, LANES), groups)
         res_ref[:, cut] = value[:poles]
         log_ref[:, cut] = value[poles : 2 * poles]
-        skip_ref[n * rows : (n + 1) * rows, :] = value[2 * poles :]
+        skip_ref[pl.ds(pl.multiple_of(source * rows, 8), rows), :] = value[2 * poles :]
 
 
 def local(queries, key_input, value_input, cotangent, residues, log_rates, skip_gain):
@@ -519,13 +531,13 @@
             name="lags",
         )(lag_rates, gated, dgate, turned, *more)
 
-    def convolve(after):
+    def convolve(first_step, count, after):
         skip_rows = skip_gain.reshape(-1, LANES)
         return pl.pallas_call(
-            lambda *refs: conv_kernel(*refs, inner=inner, **sizes),
+            lambda *refs: conv_kernel(*refs, first_step=first_step, inner=inner, **sizes),
             in_specs=[vmem] * 7 + [anywhere],
             out_specs=vmem,
-            out_shape=shape(tokens, 2 * width),
+            out_shape=shape(tokens, 2 * count * inner * LANES),
             compiler_params=PARAMS,
             cost_estimate=work,
             name="conv",
@@ -564,7 +576,7 @@
         if level > 1:
             operands.append(held)
         if level == min(2, levels - 1):
-            conv = convolve(near if held is None else held)
+            conv = convolve(0, steps - 1, near if held is None else held)
             operands.append(conv)
         if last:
             outs = [shape(half_blocks, 2 * poles, LANES, dtype=BF16), slim_shape]
@@ -576,37 +588,40 @@
             states, carried, held, *more = combine(level, operands, outs)
             slim = more[0] if more else None
     got = swap(outgoing, 0)
+    last_conv = convolve(steps - 1, 1, outgoing)
     merged = pl.pallas_call(
         lambda *refs: merge_kernel(*refs, poles=poles, length=tokens * parts),
-        in_specs=[vmem] * 4,
+        in_specs=[vmem] * 4 + [anywhere],
         out_specs=vmem,
-        out_shape=shape(shards, tail, LANES, dtype=BF16),
+        out_shape=shape(tail, LANES, dtype=BF16),
         compiler_params=PARAMS,
         name="merge",
-    )(log_rates, residues, outgoing, got)
-
-    pieces = lax.all_to_all(merged, "ch", split_axis=0, concat_axis=0, tiled=True)
+    )(log_rates, residues, outgoing, got, last_conv)
+
+    gathered = [merged]
+    for shift in range(1, shards):
+        gathered.append(lax.ppermute(merged, "ch", [(i, (i + shift) % shards) for i in range(shards)]))
 
     main = pl.BlockSpec((tokens, inner * LANES), lambda i: (0, i))
-    grad_query, grad_key, grad_value, mark = pl.pallas_call(
+    grad_query, grad_key, grad_value = pl.pallas_call(
         lambda *refs: output_kernel(*refs, **sizes),
         grid=(steps,),
-        in_specs=[vmem] * 7,
-        out_specs=[main] * 3 + [pl.BlockSpec((8, LANES), lambda i: (0, 0))],
-        out_shape=[shape(tokens, width, dtype=BF16)] * 3 + [shape(8, LANES)],
+        in_specs=[vmem] * 8,
+        out_specs=[main] * 3,
+        out_shape=[shape(tokens, width, dtype=BF16)] * 3,
         compiler_params=PARAMS,
         cost_estimate=work,
         name="outputs",
-    )(rows, conv, mine, got, key_input, value_input, cotangent)
+    )(rows, conv, last_conv, mine, got, key_input, value_input, cotangent)
 
     grad_residue, grad_lograte, grad_skip = pl.pallas_call(
         lambda *refs: assemble_kernel(*refs, poles=poles),
-        in_specs=[vmem] * 2,
+        in_specs=[vmem] * shards,
         out_specs=[vmem] * 3,
         out_shape=[shape(poles, all_groups), shape(poles, all_groups), shape(shards * blocks, LANES)],
         compiler_params=PARAMS,
         name="assemble",
-    )(pieces, mark)
+    )(*gathered)
     return (grad_query, grad_key, grad_value, grad_residue.T, grad_lograte.T, grad_skip.reshape(-1))
 
 

time: 34.3 us -> 31.7 us (0.924)
  waiting for transfers between devices: 7.02 us -> 5.89 us
  local copies, waits for them, and re-layouts: 1.06 us -> 0.03 us
  Pallas kernels: 13.6 us -> 13.1 us
    all_to_all x1 -> x0, starting transfers between devices: 4.88 us -> none  [local(): lax.all_to_all(merged, 'ch', split_axis=0, concat_axis=0, tiled=True)]
    ppermute x0 -> x3, starting transfers between devices: none -> 4.66 us  [local(): lax.ppermute(merged, 'ch', [(i, (i + shift) % shards) for i in range(shar...]
    all_to_all x1 -> x0, waiting for transfers between devices: 2.07 us -> none  [local(): lax.all_to_all(merged, 'ch', split_axis=0, concat_axis=0, tiled=True)]
    ppermute x0 -> x3, waiting for transfers between devices: none -> 1.74 us  [local(): lax.ppermute(merged, 'ch', [(i, (i + shift) % shards) for i in range(shar...]
    unnamed x12, local copies, waits for them, and re-layouts: 1.06 us -> 0.03 us
    ppermute x5, waiting for transfers between devices: 4.95 us -> 4.15 us  [swap(): lax.ppermute(value, 'ctx', [(i, i ^ 1 << level) for i in range(parts)])]
    pallas_call x1, Pallas kernels: 0.63 us -> 0.02 us  [local(): pl.pallas_call(lambda *refs: merge_kernel(*refs, poles=poles, length=toke...]
    pallas_call x1 -> x2, Pallas kernels: 3.64 us -> 3.65 us  [convolve(): pl.pallas_call(lambda *refs: conv_kernel(*refs, first_step=first_step, in...]
  transfers between devices with their start and end apart: 6 -> 8, of which waited for: 3 -> 5; matrix products, arithmetic and copies ran while one was open for 0% -> 0% of each run, Pallas kernels for 27% -> 30%
where the time goes in v12:
time: 31.7 us; the launch traced here: 31.5 us
  Pallas kernels  13.1 us (41%)
  starting transfers between devices  9.7 us (31%)
  waiting for transfers between devices  5.89 us (19%)
  other arithmetic  1.99 us (6%)
  between operations  0.82 us (3%)
    ppermute x5, starting transfers between devices, swap(): lax.ppermute(value, 'ctx', [(i, i ^ 1 << level) for i in range(parts)])  5.04 us
    ppermute x3, starting transfers between devices, local(): lax.ppermute(merged, 'ch', [(i, (i + shift) % shards) for i in range(shar...  4.66 us
    ppermute x5, waiting for transfers between devices, swap(): lax.ppermute(value, 'ctx', [(i, i ^ 1 << level) for i in range(parts)])  4.15 us
    pallas_call x2, Pallas kernels, convolve(): pl.pallas_call(lambda *refs: conv_kernel(*refs, first_step=first_step, in...  3.65 us
    pallas_call x1, Pallas kernels, local(): pl.pallas_call(lambda *refs: output_kernel(*refs, **sizes), grid=(steps,)...  2.74 us
    pallas_call x2, Pallas kernels, local_sums(): pl.pallas_call(lambda *refs: lags_kernel(*refs, second=second, inner=inne...  2.71 us
    pallas_call x1, Pallas kernels, local(): pl.pallas_call(lambda *refs: states_kernel(*refs, inner=inner, **sizes),...  2.16 us
    convert_element_type x1, other arithmetic, gate(): return (left.astype(F32) * right.astype(F32)).astype(BF16)  1.99 us
  transfers between devices with their start and end apart: 8, of which 5 were waited for; matrix products, arithmetic and copies ran while one was open for 0% of the time, Pallas kernels for 30%

profile of v12, /device:TPU:0, one launch (start us, length us, event | category | flops | bytes accessed | tf_op | source)
XLA Modules:
  0.0 31.5 jit_solution(872514162915054770)
XLA Ops:
  0.6 0.0 copy-start.5
  0.6 0.0 copy-start.3
  0.7 2.0 %multiply_convert_fusion = (bf16[128,2048]{1,0:T(8,128)(2,1)S(1)}, bf16[128,2048]{1,0:T(8,128)(2,1)S(1)}) fusion(bf16[128,2048]{1,0:T(8,128)(2,1)} %param.7, bf16[128,2048]{1,0:T(8,128)(2,1)} %refs_7_.1, bf16[128,2048]{1,0:T(8,128)(2,1)} %refs_6_.1, bf16[128,2048]{1,0:T(8,128)(2,1)} %refs_5_.1), kind=kLoop, calls=%fused_computation | loop fusion | flops 2097152 | bytes 3145728 | tf_op jit(solution)/shard_map/convert_element_type | solution.py:44
  2.6 0.0 copy-done.5
  2.7 0.0 copy-done.3
  2.7 2.2 %states.1 = (bf16[512,128]{1,0:T(8,128)(2,1)S(1)}, bf16[512,128]{1,0:T(8,128)(2,1)S(1)}, bf16[128,2048]{1,0:T(8,128)(2,1)S(1)}, f32[2,16,128]{2,1,0:T(8,128)S(1)}) custom-call(f32[16,512]{1,0:T(8,128)S(1)} %bitcast.12, f32[16,512]{1,0:T(8,128)S(1)} %bitcast.6, bf16[128,2048]{1,0:T(8,128)(2,1)S(1)} %get-tuple-element.49.refs_2_.refs_1_.refs_5_, ...), custom_call_target="tpu_custom_call" | custom-call | tf_op jit(solution)/shard_map/states/pallas_call | solution.py:494
  4.8 0.5 %collective-permute-start = (bf16[512,128]{1,0:T(8,128)(2,1)S(1)}, bf16[512,128]{1,0:T(8,128)(2,1)S(1)}, u32[]{:S(2)}, u32[]{:S(2)}) collective-permute-start(bf16[512,128]{1,0:T(8,128)(2,1)S(1)} %get-tuple-element.32), channel_id=1, source_target_pairs={{0,4},{4,0},{8,12},{12,8},{16,20},{20,16},{24,28},{28,24},{1,5},{5... | collective-permute-start | bytes 393224 | tf_op jit(solution)/shard_map/ppermute | solution.py:491
  5.3 0.4 %tables.1 = (f32[16,16,128]{2,1,0:T(8,128)S(1)}, f32[16,16,256]{2,1,0:T(8,128)S(1)}) custom-call(f32[16,512]{1,0:T(8,128)S(1)} %bitcast.13, f32[2,16,128]{2,1,0:T(8,128)S(1)} %get-tuple-element.27.refs_1_.refs_0_), custom_call_target="tpu_custom_call" | custom-call | flops 1000000000 | bytes 1000000 | tf_op jit(solution)/shard_map/tables/pallas_call | solution.py:508
  5.7 0.7 %lags.2.refs_3_ = f32[32,128]{1,0:T(8,128)S(1)} custom-call(f32[16,16,256]{2,1,0:T(8,128)S(1)} %get-tuple-element.29.refs_0_.refs_4_, bf16[128,2048]{1,0:T(8,128)(2,1)S(1)} %get-tuple-element.49.refs_2_.refs_1_.refs_5_, bf16[128,2048]{1,0:T(8,128)(2,1)S(1)} %get-tuple-element.48.refs_3_.refs_2_, bf16[128,2048]{1,0:T(8,128)(2,1)S(1)} %get-tuple-element.30.refs_3_.refs_6_), custom_call_target="tpu_custom_call" | custom-call | flops 536870912 | bytes 3145728 | tf_op jit(solution)/shard_map/lags/pallas_call | solution.py:523
  6.4 0.0 copy-start.4
  6.4 0.0 collective-permute-done.refs_2_
  6.4 0.3 combine.3
  6.7 2.8 %collective-permute-start.1 = (bf16[512,128]{1,0:T(8,128)(2,1)S(1)}, bf16[512,128]{1,0:T(8,128)(2,1)S(1)}, u32[]{:S(2)}, u32[]{:S(2)}) collective-permute-start(bf16[512,128]{1,0:T(8,128)(2,1)S(1)} %get-tuple-element.33.refs_1_), channel_id=1, source_target_pairs={{0,8},{4,12},{8,0},{12,4},{16,24},{20,28},{24,16},{28,20},{1,9},{5... | collective-permute-start | bytes 393224 | tf_op jit(solution)/shard_map/ppermute | solution.py:491
  9.5 2.0 %lags.3.refs_2_ = bf16[48,128]{1,0:T(8,128)(2,1)S(1)} custom-call(f32[16,16,256]{2,1,0:T(8,128)S(1)} %get-tuple-element.29.refs_0_.refs_4_, bf16[128,2048]{1,0:T(8,128)(2,1)S(1)} %get-tuple-element.49.refs_2_.refs_1_.refs_5_, bf16[128,2048]{1,0:T(8,128)(2,1)S(1)} %get-tuple-element.48.refs_3_.refs_2_, ...), custom_call_target="tpu_custom_call" | custom-call | flops 536870912 | bytes 3145728 | tf_op jit(solution)/shard_map/lags/pallas_call | solution.py:523
  11.5 0.1 collective-permute-start.2
  11.6 3.7 %collective-permute-done.2.refs_4_ = bf16[48,128]{1,0:T(8,128)(2,1)S(1)} collective-permute-done((bf16[48,128]{1,0:T(8,128)(2,1)S(1)}, bf16[48,128]{1,0:T(8,128)(2,1)S(1)}, u32[]{:S(2)}, u32[]{:S(2)}) %collective-permute-start.2) | collective-permute-done | bytes 12320 | tf_op jit(solution)/shard_map/ppermute | solution.py:491
  15.3 0.0 collective-permute-done.1.refs_3_
  15.3 0.3 combine.4
  15.6 1.6 %collective-permute-start.3 = (bf16[304,128]{1,0:T(8,128)(2,1)S(1)}, bf16[304,128]{1,0:T(8,128)(2,1)S(1)}, u32[]{:S(2)}, u32[]{:S(2)}) collective-permute-start(bf16[304,128]{1,0:T(8,128)(2,1)S(1)} %get-tuple-element.38), channel_id=1, source_target_pairs={{0,16},{4,20},{8,24},{12,28},{16,0},{20,4},{24,8},{28,12},{1,17},{... | collective-permute-start | bytes 233480 | tf_op jit(solution)/shard_map/ppermute | solution.py:491
  17.2 0.0 copy-done.4
  17.2 2.7 %conv.2.refs_5_.refs_1_ = f32[128,3072]{1,0:T(8,128)S(1)} custom-call(f32[16,512]{1,0:T(8,128)S(1)} %bitcast.7, f32[2,16,128]{2,1,0:T(8,128)S(1)} %get-tuple-element.27.refs_1_.refs_0_, f32[64,128]{1,0:T(8,128)S(1)} %bitcast.10, f32[16,16,128]{2,1,0:T(8,128)S(1)} %get-tuple-element.28.refs_0_.refs_3_, f32[16,16,256]{2,1,0:T(8,128)S(1)} %get-tuple-element.29.refs_0_.refs_4_, ...), custom_call_target="tpu_custom_call" | custom-call | flops 536870912 | bytes 3145728 | tf_op jit(solution)/shard_map/conv/pallas_call | solution.py:536
  19.9 0.1 collective-permute-done.3.refs_3_
  20.1 0.3 combine.5
  20.3 0.0 copy-start
  20.4 0.0 copy-start.1
  20.4 0.0 copy-start.2
  20.4 0.1 collective-permute-start.4
  20.5 0.9 %conv.3.refs_2_.refs_4_ = f32[128,1024]{1,0:T(8,128)S(1)} custom-call(f32[16,512]{1,0:T(8,128)S(1)} %bitcast.8, f32[2,16,128]{2,1,0:T(8,128)S(1)} %get-tuple-element.27.refs_1_.refs_0_, f32[64,128]{1,0:T(8,128)S(1)} %bitcast.11, f32[16,16,128]{2,1,0:T(8,128)S(1)} %get-tuple-element.28.refs_0_.refs_3_, f32[16,16,256]{2,1,0:T(8,128)S(1)} %get-tuple-element.29.refs_0_.refs_4_, ...), custom_call_target="tpu_custom_call" | custom-call | flops 536870912 | bytes 3145728 | tf_op jit(solution)/shard_map/conv/pallas_call | solution.py:536
  21.4 0.3 %collective-permute-done.4.refs_4_.refs_3_ = bf16[304,128]{1,0:T(8,128)(2,1)S(1)} collective-permute-done((bf16[304,128]{1,0:T(8,128)(2,1)S(1)}, bf16[304,128]{1,0:T(8,128)(2,1)S(1)}, u32[]{:S(2)}, u32[]{:S(2)}) %collective-permute-start.4) | collective-permute-done | bytes 77856 | tf_op jit(solution)/shard_map/ppermute | solution.py:491
  21.8 3.7 %collective-permute-start.7 = (bf16[48,128]{1,0:T(8,128)(2,1)S(1)}, bf16[48,128]{1,0:T(8,128)(2,1)S(1)}, u32[]{:S(2)}, u32[]{:S(2)}) collective-permute-start(bf16[48,128]{1,0:T(8,128)(2,1)S(1)} %merge.1.refs_0_), channel_id=1, source_target_pairs={{0,3},{1,0},{2,1},{3,2},{4,7},{5,4},{6,5},{7,6},{8,11},{9,8},{10,9... | collective-permute-start | bytes 36872 | tf_op jit(solution)/shard_map/ppermute | solution.py:603
  25.4 0.0 collective-permute-start.6
  25.4 1.0 %collective-permute-start.5 = (bf16[48,128]{1,0:T(8,128)(2,1)S(1)}, bf16[48,128]{1,0:T(8,128)(2,1)S(1)}, u32[]{:S(2)}, u32[]{:S(2)}) collective-permute-start(bf16[48,128]{1,0:T(8,128)(2,1)S(1)} %merge.1.refs_0_), channel_id=1, source_target_pairs={{0,1},{1,2},{2,3},{3,0},{4,5},{5,6},{6,7},{7,4},{8,9},{9,10},{10,1... | collective-permute-start | bytes 36872 | tf_op jit(solution)/shard_map/ppermute | solution.py:603
  26.4 0.0 copy-done
  26.4 0.0 copy-done.1
  26.4 0.0 copy-done.2
  26.4 2.7 %outputs.1 = (bf16[128,2048]{1,0:T(8,128)(2,1)}, bf16[128,2048]{1,0:T(8,128)(2,1)}, bf16[128,2048]{1,0:T(8,128)(2,1)}) custom-call(f32[2,16,128]{2,1,0:T(8,128)S(1)} %get-tuple-element.27.refs_1_.refs_0_, f32[128,3072]{1,0:T(8,128)S(1)} %conv.2.refs_5_.refs_1_, f32[128,1024]{1,0:T(8,128)S(1)} %conv.3.refs_2_.refs_4_, ...), custom_call_target="tpu_custom_call" | custom-call | flops 536870912 | bytes 3145728 | tf_op jit(solution)/shard_map/outputs/pallas_call | solution.py:606
  29.2 0.0 collective-permute-done.7.refs_3_
  29.2 0.8 %collective-permute-done.6.refs_2_ = bf16[48,128]{1,0:T(8,128)(2,1)S(1)} collective-permute-done((bf16[48,128]{1,0:T(8,128)(2,1)S(1)}, bf16[48,128]{1,0:T(8,128)(2,1)S(1)}, u32[]{:S(2)}, u32[]{:S(2)}) %collective-permute-start.6) | collective-permute-done | bytes 12320 | tf_op jit(solution)/shard_map/ppermute | solution.py:603
  30.0 0.9 %collective-permute-done.5.refs_1_ = bf16[48,128]{1,0:T(8,128)(2,1)S(1)} collective-permute-done((bf16[48,128]{1,0:T(8,128)(2,1)S(1)}, bf16[48,128]{1,0:T(8,128)(2,1)S(1)}, u32[]{:S(2)}, u32[]{:S(2)}) %collective-permute-start.5) | collective-permute-done | bytes 12320 | tf_op jit(solution)/shard_map/ppermute | solution.py:603
  30.9 0.6 %assemble.1 = (f32[16,512]{1,0:T(8,128)}, f32[16,512]{1,0:T(8,128)}, f32[64,128]{1,0:T(8,128)}) custom-call(bf16[48,128]{1,0:T(8,128)(2,1)S(1)} %merge.1.refs_0_, bf16[48,128]{1,0:T(8,128)(2,1)S(1)} %collective-permute-done.5.refs_1_, bf16[48,128]{1,0:T(8,128)(2,1)S(1)} %collective-permute-done.6.refs_2_, bf16[48,128]{1,0:T(8,128)(2,1)S(1)} %collective-permute-done.7.refs_3_), custom_call_target="tpu_custom_call" | custom-call | tf_op jit(solution)/shard_map/assemble/pallas_call | solution.py:617
  (1 shorter events, 0.0 us)
Async XLA Ops:
  0.6 2.0 %copy-start.5 = (f32[512,16]{0,1:T(8,128)S(1)}, f32[512,16]{0,1:T(8,128)}, u32[]{:S(2)}) copy-start(f32[512,16]{0,1:T(8,128)} %param.12) | copy-start | bytes 98308
  0.6 2.0 %copy-start.3 = (f32[512,16]{0,1:T(8,128)S(1)}, f32[512,16]{0,1:T(8,128)}, u32[]{:S(2)}) copy-start(f32[512,16]{0,1:T(8,128)} %param.11) | copy-start | bytes 98308
  4.8 1.6 %collective-permute-start = (bf16[512,128]{1,0:T(8,128)(2,1)S(1)}, bf16[512,128]{1,0:T(8,128)(2,1)S(1)}, u32[]{:S(2)}, u32[]{:S(2)}) collective-permute-start(bf16[512,128]{1,0:T(8,128)(2,1)S(1)} %get-tuple-element.32), channel_id=1, source_target_pairs={{0,4},{4,0},{8,12},{12,8},{16,20},{20,16},{24,28},{28,24},{1,5},{5... | collective-permute-start | bytes 393224 | tf_op jit(solution)/shard_map/ppermute | solution.py:491
  6.4 10.8 %copy-start.4 = (f32[8192]{0:T(1024)S(1)}, f32[8192]{0:T(1024)}, u32[]{:S(2)}) copy-start(f32[8192]{0:T(1024)} %param.13) | copy-start | bytes 98308
  6.7 8.6 %collective-permute-start.1 = (bf16[512,128]{1,0:T(8,128)(2,1)S(1)}, bf16[512,128]{1,0:T(8,128)(2,1)S(1)}, u32[]{:S(2)}, u32[]{:S(2)}) collective-permute-start(bf16[512,128]{1,0:T(8,128)(2,1)S(1)} %get-tuple-element.33.refs_1_), channel_id=1, source_target_pairs={{0,8},{4,12},{8,0},{12,4},{16,24},{20,28},{24,16},{28,20},{1,9},{5... | collective-permute-start | bytes 393224 | tf_op jit(solution)/shard_map/ppermute | solution.py:491
  11.5 3.8 %collective-permute-start.2 = (bf16[48,128]{1,0:T(8,128)(2,1)S(1)}, bf16[48,128]{1,0:T(8,128)(2,1)S(1)}, u32[]{:S(2)}, u32[]{:S(2)}) collective-permute-start(bf16[48,128]{1,0:T(8,128)(2,1)S(1)} %lags.3.refs_2_), channel_id=1, source_target_pairs={{0,8},{4,12},{8,0},{12,4},{16,24},{20,28},{24,16},{28,20},{1,9},{5... | collective-permute-start | bytes 36872 | tf_op jit(solution)/shard_map/ppermute | solution.py:491
  15.6 4.4 %collective-permute-start.3 = (bf16[304,128]{1,0:T(8,128)(2,1)S(1)}, bf16[304,128]{1,0:T(8,128)(2,1)S(1)}, u32[]{:S(2)}, u32[]{:S(2)}) collective-permute-start(bf16[304,128]{1,0:T(8,128)(2,1)S(1)} %get-tuple-element.38), channel_id=1, source_target_pairs={{0,16},{4,20},{8,24},{12,28},{16,0},{20,4},{24,8},{28,12},{1,17},{... | collective-permute-start | bytes 233480 | tf_op jit(solution)/shard_map/ppermute | solution.py:491
  20.3 6.1 %copy-start = (bf16[128,2048]{1,0:T(8,128)(2,1)S(1)}, bf16[128,2048]{1,0:T(8,128)(2,1)}, u32[]{:S(2)}) copy-start(bf16[128,2048]{1,0:T(8,128)(2,1)} %refs_7_.1) | copy-start | bytes 1572868
  20.4 6.0 %copy-start.1 = (bf16[128,2048]{1,0:T(8,128)(2,1)S(1)}, bf16[128,2048]{1,0:T(8,128)(2,1)}, u32[]{:S(2)}) copy-start(bf16[128,2048]{1,0:T(8,128)(2,1)} %refs_6_.1) | copy-start | bytes 1572868
  20.4 6.0 %copy-start.2 = (bf16[128,2048]{1,0:T(8,128)(2,1)S(1)}, bf16[128,2048]{1,0:T(8,128)(2,1)}, u32[]{:S(2)}) copy-start(bf16[128,2048]{1,0:T(8,128)(2,1)} %refs_5_.1) | copy-start | bytes 1572868
  20.4 1.3 %collective-permute-start.4 = (bf16[304,128]{1,0:T(8,128)(2,1)S(1)}, bf16[304,128]{1,0:T(8,128)(2,1)S(1)}, u32[]{:S(2)}, u32[]{:S(2)}) collective-permute-start(bf16[304,128]{1,0:T(8,128)(2,1)S(1)} %get-tuple-element.40.refs_7_.refs_2_), channel_id=1, source_target_pairs={{0,4},{4,0},{8,12},{12,8},{16,20},{20,16},{24,28},{28,24},{1,5},{5... | collective-permute-start | bytes 233480 | tf_op jit(solution)/shard_map/ppermute | solution.py:491
  21.8 7.4 %collective-permute-start.7 = (bf16[48,128]{1,0:T(8,128)(2,1)S(1)}, bf16[48,128]{1,0:T(8,128)(2,1)S(1)}, u32[]{:S(2)}, u32[]{:S(2)}) collective-permute-start(bf16[48,128]{1,0:T(8,128)(2,1)S(1)} %merge.1.refs_0_), channel_id=1, source_target_pairs={{0,3},{1,0},{2,1},{3,2},{4,7},{5,4},{6,5},{7,6},{8,11},{9,8},{10,9... | collective-permute-start | bytes 36872 | tf_op jit(solution)/shard_map/ppermute | solution.py:603
  25.4 4.6 %collective-permute-start.6 = (bf16[48,128]{1,0:T(8,128)(2,1)S(1)}, bf16[48,128]{1,0:T(8,128)(2,1)S(1)}, u32[]{:S(2)}, u32[]{:S(2)}) collective-permute-start(bf16[48,128]{1,0:T(8,128)(2,1)S(1)} %merge.1.refs_0_), channel_id=1, source_target_pairs={{0,2},{1,3},{2,0},{3,1},{4,6},{5,7},{6,4},{7,5},{8,10},{9,11},{10,... | collective-permute-start | bytes 36872 | tf_op jit(solution)/shard_map/ppermute | solution.py:603
  25.4 5.5 %collective-permute-start.5 = (bf16[48,128]{1,0:T(8,128)(2,1)S(1)}, bf16[48,128]{1,0:T(8,128)(2,1)S(1)}, u32[]{:S(2)}, u32[]{:S(2)}) collective-permute-start(bf16[48,128]{1,0:T(8,128)(2,1)S(1)} %merge.1.refs_0_), channel_id=1, source_target_pairs={{0,1},{1,2},{2,3},{3,0},{4,5},{5,6},{6,7},{7,4},{8,9},{9,10},{10,1... | collective-permute-start | bytes 36872 | tf_op jit(solution)/shard_map/ppermute | solution.py:603

commit v13 on v12

--- a/solution.py
+++ b/solution.py
@@ -452,12 +452,11 @@
 
 def assemble_kernel(*refs, poles):
     *slots, res_ref, log_ref, skip_ref = refs
-    shards = len(slots)
     me = lax.axis_index("ch")
     groups = slots[0].shape[1]
     rows = slots[0].shape[0] - 2 * poles
-    for shift, slot in enumerate(slots):
-        source = lax.rem(me - shift + shards, shards)
+    for mask, slot in enumerate(slots):
+        source = lax.bitwise_xor(me, mask)
         value = slot[...].astype(F32)
         cut = pl.ds(pl.multiple_of(source * groups, LANES), groups)
         res_ref[:, cut] = value[:poles]
@@ -599,8 +598,8 @@
     )(log_rates, residues, outgoing, got, last_conv)
 
     gathered = [merged]
-    for shift in range(1, shards):
-        gathered.append(lax.ppermute(merged, "ch", [(i, (i + shift) % shards) for i in range(shards)]))
+    for mask in range(1, shards):
+        gathered.append(lax.ppermute(merged, "ch", [(i, i ^ mask) for i in range(shards)]))
 
     main = pl.BlockSpec((tokens, inner * LANES), lambda i: (0, i))
     grad_query, grad_key, grad_value = pl.pallas_call(

time: 31.7 us -> 30.8 us (0.972)
  waiting for transfers between devices: 5.89 us -> 5.22 us
    ppermute x3, waiting for transfers between devices: 1.74 us -> 1.06 us  [local(): lax.ppermute(merged, 'ch', [(i, i ^ mask) for i in range(shards)])]
  transfers between devices with their start and end apart: 8 -> 8, of which waited for: 5 -> 4; matrix products, arithmetic and copies ran while one was open for 0% -> 0% of each run, Pallas kernels for 30% -> 31%
where the time goes in v13:
time: 30.8 us; the launch traced here: 30.7 us
  Pallas kernels  13.1 us (43%)
  starting transfers between devices  9.49 us (31%)
  waiting for transfers between devices  5.22 us (17%)
  other arithmetic  1.99 us (6%)
  between operations  0.82 us (3%)
    ppermute x5, starting transfers between devices, swap(): lax.ppermute(value, 'ctx', [(i, i ^ 1 << level) for i in range(parts)])  5.04 us
    ppermute x3, starting transfers between devices, local(): lax.ppermute(merged, 'ch', [(i, i ^ mask) for i in range(shards)])  4.45 us
    ppermute x5, waiting for transfers between devices, swap(): lax.ppermute(value, 'ctx', [(i, i ^ 1 << level) for i in range(parts)])  4.15 us
    pallas_call x2, Pallas kernels, convolve(): pl.pallas_call(lambda *refs: conv_kernel(*refs, first_step=first_step, in...  3.65 us
    pallas_call x1, Pallas kernels, local(): pl.pallas_call(lambda *refs: output_kernel(*refs, **sizes), grid=(steps,)...  2.74 us
    pallas_call x2, Pallas kernels, local_sums(): pl.pallas_call(lambda *refs: lags_kernel(*refs, second=second, inner=inne...  2.71 us
    pallas_call x1, Pallas kernels, local(): pl.pallas_call(lambda *refs: states_kernel(*refs, inner=inner, **sizes),...  2.16 us
    convert_element_type x1, other arithmetic, gate(): return (left.astype(F32) * right.astype(F32)).astype(BF16)  1.99 us
  transfers between devices with their start and end apart: 8, of which 4 were waited for; matrix products, arithmetic and copies ran while one was open for 0% of the time, Pallas kernels for 31%

profile of v13, /device:TPU:0, one launch (start us, length us, event | category | flops | bytes accessed | tf_op | source)
XLA Modules:
  0.0 30.7 jit_solution(15200776420741152819)
XLA Ops:
  0.6 0.0 copy-start.5
  0.6 0.0 copy-start.3
  0.7 2.0 %multiply_convert_fusion = (bf16[128,2048]{1,0:T(8,128)(2,1)S(1)}, bf16[128,2048]{1,0:T(8,128)(2,1)S(1)}) fusion(bf16[128,2048]{1,0:T(8,128)(2,1)} %param.7, bf16[128,2048]{1,0:T(8,128)(2,1)} %refs_7_.1, bf16[128,2048]{1,0:T(8,128)(2,1)} %refs_6_.1, bf16[128,2048]{1,0:T(8,128)(2,1)} %refs_5_.1), kind=kLoop, calls=%fused_computation | loop fusion | flops 2097152 | bytes 3145728 | tf_op jit(solution)/shard_map/convert_element_type | solution.py:44
  2.6 0.0 copy-done.5
  2.7 0.0 copy-done.3
  2.7 2.2 %states.1 = (bf16[512,128]{1,0:T(8,128)(2,1)S(1)}, bf16[512,128]{1,0:T(8,128)(2,1)S(1)}, bf16[128,2048]{1,0:T(8,128)(2,1)S(1)}, f32[2,16,128]{2,1,0:T(8,128)S(1)}) custom-call(f32[16,512]{1,0:T(8,128)S(1)} %bitcast.12, f32[16,512]{1,0:T(8,128)S(1)} %bitcast.6, bf16[128,2048]{1,0:T(8,128)(2,1)S(1)} %get-tuple-element.49.refs_2_.refs_1_.refs_5_, ...), custom_call_target="tpu_custom_call" | custom-call | tf_op jit(solution)/shard_map/states/pallas_call | solution.py:493
  4.8 0.5 %collective-permute-start = (bf16[512,128]{1,0:T(8,128)(2,1)S(1)}, bf16[512,128]{1,0:T(8,128)(2,1)S(1)}, u32[]{:S(2)}, u32[]{:S(2)}) collective-permute-start(bf16[512,128]{1,0:T(8,128)(2,1)S(1)} %get-tuple-element.32), channel_id=1, source_target_pairs={{0,4},{4,0},{8,12},{12,8},{16,20},{20,16},{24,28},{28,24},{1,5},{5... | collective-permute-start | bytes 393224 | tf_op jit(solution)/shard_map/ppermute | solution.py:490
  5.3 0.4 %tables.1 = (f32[16,16,128]{2,1,0:T(8,128)S(1)}, f32[16,16,256]{2,1,0:T(8,128)S(1)}) custom-call(f32[16,512]{1,0:T(8,128)S(1)} %bitcast.13, f32[2,16,128]{2,1,0:T(8,128)S(1)} %get-tuple-element.27.refs_1_.refs_0_), custom_call_target="tpu_custom_call" | custom-call | flops 1000000000 | bytes 1000000 | tf_op jit(solution)/shard_map/tables/pallas_call | solution.py:507
  5.7 0.7 %lags.2.refs_3_ = f32[32,128]{1,0:T(8,128)S(1)} custom-call(f32[16,16,256]{2,1,0:T(8,128)S(1)} %get-tuple-element.29.refs_0_.refs_4_, bf16[128,2048]{1,0:T(8,128)(2,1)S(1)} %get-tuple-element.49.refs_2_.refs_1_.refs_5_, bf16[128,2048]{1,0:T(8,128)(2,1)S(1)} %get-tuple-element.48.refs_3_.refs_2_, bf16[128,2048]{1,0:T(8,128)(2,1)S(1)} %get-tuple-element.30.refs_3_.refs_6_), custom_call_target="tpu_custom_call" | custom-call | flops 536870912 | bytes 3145728 | tf_op jit(solution)/shard_map/lags/pallas_call | solution.py:522
  6.4 0.0 copy-start.4
  6.4 0.0 collective-permute-done.refs_2_
  6.4 0.3 combine.3
  6.7 2.8 %collective-permute-start.1 = (bf16[512,128]{1,0:T(8,128)(2,1)S(1)}, bf16[512,128]{1,0:T(8,128)(2,1)S(1)}, u32[]{:S(2)}, u32[]{:S(2)}) collective-permute-start(bf16[512,128]{1,0:T(8,128)(2,1)S(1)} %get-tuple-element.33.refs_1_), channel_id=1, source_target_pairs={{0,8},{4,12},{8,0},{12,4},{16,24},{20,28},{24,16},{28,20},{1,9},{5... | collective-permute-start | bytes 393224 | tf_op jit(solution)/shard_map/ppermute | solution.py:490
  9.5 2.0 %lags.3.refs_2_ = bf16[48,128]{1,0:T(8,128)(2,1)S(1)} custom-call(f32[16,16,256]{2,1,0:T(8,128)S(1)} %get-tuple-element.29.refs_0_.refs_4_, bf16[128,2048]{1,0:T(8,128)(2,1)S(1)} %get-tuple-element.49.refs_2_.refs_1_.refs_5_, bf16[128,2048]{1,0:T(8,128)(2,1)S(1)} %get-tuple-element.48.refs_3_.refs_2_, ...), custom_call_target="tpu_custom_call" | custom-call | flops 536870912 | bytes 3145728 | tf_op jit(solution)/shard_map/lags/pallas_call | solution.py:522
  11.5 0.1 collective-permute-start.2
  11.6 3.7 %collective-permute-done.2.refs_4_ = bf16[48,128]{1,0:T(8,128)(2,1)S(1)} collective-permute-done((bf16[48,128]{1,0:T(8,128)(2,1)S(1)}, bf16[48,128]{1,0:T(8,128)(2,1)S(1)}, u32[]{:S(2)}, u32[]{:S(2)}) %collective-permute-start.2) | collective-permute-done | bytes 12320 | tf_op jit(solution)/shard_map/ppermute | solution.py:490
  15.3 0.0 collective-permute-done.1.refs_3_
  15.3 0.3 combine.4
  15.6 1.6 %collective-permute-start.3 = (bf16[304,128]{1,0:T(8,128)(2,1)S(1)}, bf16[304,128]{1,0:T(8,128)(2,1)S(1)}, u32[]{:S(2)}, u32[]{:S(2)}) collective-permute-start(bf16[304,128]{1,0:T(8,128)(2,1)S(1)} %get-tuple-element.38), channel_id=1, source_target_pairs={{0,16},{4,20},{8,24},{12,28},{16,0},{20,4},{24,8},{28,12},{1,17},{... | collective-permute-start | bytes 233480 | tf_op jit(solution)/shard_map/ppermute | solution.py:490
  17.2 0.0 copy-done.4
  17.2 2.7 %conv.2.refs_5_.refs_1_ = f32[128,3072]{1,0:T(8,128)S(1)} custom-call(f32[16,512]{1,0:T(8,128)S(1)} %bitcast.7, f32[2,16,128]{2,1,0:T(8,128)S(1)} %get-tuple-element.27.refs_1_.refs_0_, f32[64,128]{1,0:T(8,128)S(1)} %bitcast.10, f32[16,16,128]{2,1,0:T(8,128)S(1)} %get-tuple-element.28.refs_0_.refs_3_, f32[16,16,256]{2,1,0:T(8,128)S(1)} %get-tuple-element.29.refs_0_.refs_4_, ...), custom_call_target="tpu_custom_call" | custom-call | flops 536870912 | bytes 3145728 | tf_op jit(solution)/shard_map/conv/pallas_call | solution.py:535
  19.9 0.1 collective-permute-done.3.refs_3_
  20.1 0.3 combine.5
  20.3 0.0 copy-start
  20.4 0.0 copy-start.1
  20.4 0.0 copy-start.2
  20.4 0.1 collective-permute-start.4
  20.5 0.9 %conv.3.refs_2_.refs_4_ = f32[128,1024]{1,0:T(8,128)S(1)} custom-call(f32[16,512]{1,0:T(8,128)S(1)} %bitcast.8, f32[2,16,128]{2,1,0:T(8,128)S(1)} %get-tuple-element.27.refs_1_.refs_0_, f32[64,128]{1,0:T(8,128)S(1)} %bitcast.11, f32[16,16,128]{2,1,0:T(8,128)S(1)} %get-tuple-element.28.refs_0_.refs_3_, f32[16,16,256]{2,1,0:T(8,128)S(1)} %get-tuple-element.29.refs_0_.refs_4_, ...), custom_call_target="tpu_custom_call" | custom-call | flops 536870912 | bytes 3145728 | tf_op jit(solution)/shard_map/conv/pallas_call | solution.py:535
  21.4 0.3 %collective-permute-done.4.refs_4_.refs_3_ = bf16[304,128]{1,0:T(8,128)(2,1)S(1)} collective-permute-done((bf16[304,128]{1,0:T(8,128)(2,1)S(1)}, bf16[304,128]{1,0:T(8,128)(2,1)S(1)}, u32[]{:S(2)}, u32[]{:S(2)}) %collective-permute-start.4) | collective-permute-done | bytes 77856 | tf_op jit(solution)/shard_map/ppermute | solution.py:490
  21.8 3.7 %collective-permute-start.7 = (bf16[48,128]{1,0:T(8,128)(2,1)S(1)}, bf16[48,128]{1,0:T(8,128)(2,1)S(1)}, u32[]{:S(2)}, u32[]{:S(2)}) collective-permute-start(bf16[48,128]{1,0:T(8,128)(2,1)S(1)} %merge.1.refs_0_), channel_id=1, source_target_pairs={{0,3},{1,2},{2,1},{3,0},{4,7},{5,6},{6,5},{7,4},{8,11},{9,10},{10,... | collective-permute-start | bytes 36872 | tf_op jit(solution)/shard_map/ppermute | solution.py:602
  25.4 0.0 collective-permute-start.6
  25.4 0.8 %collective-permute-start.5 = (bf16[48,128]{1,0:T(8,128)(2,1)S(1)}, bf16[48,128]{1,0:T(8,128)(2,1)S(1)}, u32[]{:S(2)}, u32[]{:S(2)}) collective-permute-start(bf16[48,128]{1,0:T(8,128)(2,1)S(1)} %merge.1.refs_0_), channel_id=1, source_target_pairs={{0,1},{1,0},{2,3},{3,2},{4,5},{5,4},{6,7},{7,6},{8,9},{9,8},{10,11... | collective-permute-start | bytes 36872 | tf_op jit(solution)/shard_map/ppermute | solution.py:602
  26.2 0.0 copy-done
  26.2 0.0 copy-done.1
  26.2 0.0 copy-done.2
  26.2 2.7 %outputs.1 = (bf16[128,2048]{1,0:T(8,128)(2,1)}, bf16[128,2048]{1,0:T(8,128)(2,1)}, bf16[128,2048]{1,0:T(8,128)(2,1)}) custom-call(f32[2,16,128]{2,1,0:T(8,128)S(1)} %get-tuple-element.27.refs_1_.refs_0_, f32[128,3072]{1,0:T(8,128)S(1)} %conv.2.refs_5_.refs_1_, f32[128,1024]{1,0:T(8,128)S(1)} %conv.3.refs_2_.refs_4_, ...), custom_call_target="tpu_custom_call" | custom-call | flops 536870912 | bytes 3145728 | tf_op jit(solution)/shard_map/outputs/pallas_call | solution.py:605
  28.9 0.0 collective-permute-done.7.refs_3_
  29.0 1.1 %collective-permute-done.6.refs_2_ = bf16[48,128]{1,0:T(8,128)(2,1)S(1)} collective-permute-done((bf16[48,128]{1,0:T(8,128)(2,1)S(1)}, bf16[48,128]{1,0:T(8,128)(2,1)S(1)}, u32[]{:S(2)}, u32[]{:S(2)}) %collective-permute-start.6) | collective-permute-done | bytes 12320 | tf_op jit(solution)/shard_map/ppermute | solution.py:602
  30.0 0.0 collective-permute-done.5.refs_1_
  30.0 0.6 %assemble.1 = (f32[16,512]{1,0:T(8,128)}, f32[16,512]{1,0:T(8,128)}, f32[64,128]{1,0:T(8,128)}) custom-call(bf16[48,128]{1,0:T(8,128)(2,1)S(1)} %merge.1.refs_0_, bf16[48,128]{1,0:T(8,128)(2,1)S(1)} %collective-permute-done.5.refs_1_, bf16[48,128]{1,0:T(8,128)(2,1)S(1)} %collective-permute-done.6.refs_2_, bf16[48,128]{1,0:T(8,128)(2,1)S(1)} %collective-permute-done.7.refs_3_), custom_call_target="tpu_custom_call" | custom-call | tf_op jit(solution)/shard_map/assemble/pallas_call | solution.py:616
  (1 shorter events, 0.0 us)
Async XLA Ops:
  0.6 2.0 %copy-start.5 = (f32[512,16]{0,1:T(8,128)S(1)}, f32[512,16]{0,1:T(8,128)}, u32[]{:S(2)}) copy-start(f32[512,16]{0,1:T(8,128)} %param.12) | copy-start | bytes 98308
  0.6 2.0 %copy-start.3 = (f32[512,16]{0,1:T(8,128)S(1)}, f32[512,16]{0,1:T(8,128)}, u32[]{:S(2)}) copy-start(f32[512,16]{0,1:T(8,128)} %param.11) | copy-start | bytes 98308
  4.8 1.6 %collective-permute-start = (bf16[512,128]{1,0:T(8,128)(2,1)S(1)}, bf16[512,128]{1,0:T(8,128)(2,1)S(1)}, u32[]{:S(2)}, u32[]{:S(2)}) collective-permute-start(bf16[512,128]{1,0:T(8,128)(2,1)S(1)} %get-tuple-element.32), channel_id=1, source_target_pairs={{0,4},{4,0},{8,12},{12,8},{16,20},{20,16},{24,28},{28,24},{1,5},{5... | collective-permute-start | bytes 393224 | tf_op jit(solution)/shard_map/ppermute | solution.py:490
  6.4 10.8 %copy-start.4 = (f32[8192]{0:T(1024)S(1)}, f32[8192]{0:T(1024)}, u32[]{:S(2)}) copy-start(f32[8192]{0:T(1024)} %param.13) | copy-start | bytes 98308
  6.7 8.6 %collective-permute-start.1 = (bf16[512,128]{1,0:T(8,128)(2,1)S(1)}, bf16[512,128]{1,0:T(8,128)(2,1)S(1)}, u32[]{:S(2)}, u32[]{:S(2)}) collective-permute-start(bf16[512,128]{1,0:T(8,128)(2,1)S(1)} %get-tuple-element.33.refs_1_), channel_id=1, source_target_pairs={{0,8},{4,12},{8,0},{12,4},{16,24},{20,28},{24,16},{28,20},{1,9},{5... | collective-permute-start | bytes 393224 | tf_op jit(solution)/shard_map/ppermute | solution.py:490
  11.5 3.8 %collective-permute-start.2 = (bf16[48,128]{1,0:T(8,128)(2,1)S(1)}, bf16[48,128]{1,0:T(8,128)(2,1)S(1)}, u32[]{:S(2)}, u32[]{:S(2)}) collective-permute-start(bf16[48,128]{1,0:T(8,128)(2,1)S(1)} %lags.3.refs_2_), channel_id=1, source_target_pairs={{0,8},{4,12},{8,0},{12,4},{16,24},{20,28},{24,16},{28,20},{1,9},{5... | collective-permute-start | bytes 36872 | tf_op jit(solution)/shard_map/ppermute | solution.py:490
  15.6 4.4 %collective-permute-start.3 = (bf16[304,128]{1,0:T(8,128)(2,1)S(1)}, bf16[304,128]{1,0:T(8,128)(2,1)S(1)}, u32[]{:S(2)}, u32[]{:S(2)}) collective-permute-start(bf16[304,128]{1,0:T(8,128)(2,1)S(1)} %get-tuple-element.38), channel_id=1, source_target_pairs={{0,16},{4,20},{8,24},{12,28},{16,0},{20,4},{24,8},{28,12},{1,17},{... | collective-permute-start | bytes 233480 | tf_op jit(solution)/shard_map/ppermute | solution.py:490
  20.3 5.9 %copy-start = (bf16[128,2048]{1,0:T(8,128)(2,1)S(1)}, bf16[128,2048]{1,0:T(8,128)(2,1)}, u32[]{:S(2)}) copy-start(bf16[128,2048]{1,0:T(8,128)(2,1)} %refs_7_.1) | copy-start | bytes 1572868
  20.4 5.8 %copy-start.1 = (bf16[128,2048]{1,0:T(8,128)(2,1)S(1)}, bf16[128,2048]{1,0:T(8,128)(2,1)}, u32[]{:S(2)}) copy-start(bf16[128,2048]{1,0:T(8,128)(2,1)} %refs_6_.1) | copy-start | bytes 1572868
  20.4 5.8 %copy-start.2 = (bf16[128,2048]{1,0:T(8,128)(2,1)S(1)}, bf16[128,2048]{1,0:T(8,128)(2,1)}, u32[]{:S(2)}) copy-start(bf16[128,2048]{1,0:T(8,128)(2,1)} %refs_5_.1) | copy-start | bytes 1572868
  20.4 1.3 %collective-permute-start.4 = (bf16[304,128]{1,0:T(8,128)(2,1)S(1)}, bf16[304,128]{1,0:T(8,128)(2,1)S(1)}, u32[]{:S(2)}, u32[]{:S(2)}) collective-permute-start(bf16[304,128]{1,0:T(8,128)(2,1)S(1)} %get-tuple-element.40.refs_7_.refs_2_), channel_id=1, source_target_pairs={{0,4},{4,0},{8,12},{12,8},{16,20},{20,16},{24,28},{28,24},{1,5},{5... | collective-permute-start | bytes 233480 | tf_op jit(solution)/shard_map/ppermute | solution.py:490
  21.8 7.2 %collective-permute-start.7 = (bf16[48,128]{1,0:T(8,128)(2,1)S(1)}, bf16[48,128]{1,0:T(8,128)(2,1)S(1)}, u32[]{:S(2)}, u32[]{:S(2)}) collective-permute-start(bf16[48,128]{1,0:T(8,128)(2,1)S(1)} %merge.1.refs_0_), channel_id=1, source_target_pairs={{0,3},{1,2},{2,1},{3,0},{4,7},{5,6},{6,5},{7,4},{8,11},{9,10},{10,... | collective-permute-start | bytes 36872 | tf_op jit(solution)/shard_map/ppermute | solution.py:602
  25.4 4.6 %collective-permute-start.6 = (bf16[48,128]{1,0:T(8,128)(2,1)S(1)}, bf16[48,128]{1,0:T(8,128)(2,1)S(1)}, u32[]{:S(2)}, u32[]{:S(2)}) collective-permute-start(bf16[48,128]{1,0:T(8,128)(2,1)S(1)} %merge.1.refs_0_), channel_id=1, source_target_pairs={{0,2},{1,3},{2,0},{3,1},{4,6},{5,7},{6,4},{7,5},{8,10},{9,11},{10,... | collective-permute-start | bytes 36872 | tf_op jit(solution)/shard_map/ppermute | solution.py:602
  25.4 4.6 %collective-permute-start.5 = (bf16[48,128]{1,0:T(8,128)(2,1)S(1)}, bf16[48,128]{1,0:T(8,128)(2,1)S(1)}, u32[]{:S(2)}, u32[]{:S(2)}) collective-permute-start(bf16[48,128]{1,0:T(8,128)(2,1)S(1)} %merge.1.refs_0_), channel_id=1, source_target_pairs={{0,1},{1,0},{2,3},{3,2},{4,5},{5,4},{6,7},{7,6},{8,9},{9,8},{10,11... | collective-permute-start | bytes 36872 | tf_op jit(solution)/shard_map/ppermute | solution.py:602

commit v14 on v13

--- a/solution.py
+++ b/solution.py
@@ -82,8 +82,8 @@
     return pl.multiple_of(lax.axis_index("ch") * groups, LANES)
 
 
-def states_kernel(logs_ref, res_ref, gated_ref, dgate_ref, send_ref, keep_ref, turned_ref, rows_ref,
-                  *, group, poles, inner):
+def states_kernel(all_params_ref, q_any, k_any, v_any, c_any, send_ref, keep_ref, gated_ref, dgate_ref, turned_ref,
+                  rows_ref, table_ref, q_ref, k_ref, v_ref, c_ref, sems, *, group, poles, inner):
     tokens, _ = gated_ref.shape
     per_block = LANES // group
     _, blocks, _ = rows_ref.shape
@@ -91,10 +91,26 @@
     groups = blocks * per_block
     wide = inner * LANES
     core = lax.rem(lax.axis_index("ctx"), 2)
+    sources = ((k_any, k_ref), (v_any, v_ref), (c_any, c_ref), (q_any, q_ref))
+    half_steps = half_blocks // inner
+
+    def copies(turn, step):
+        start = lax.rem(core + 1 + turn, 2) * half_blocks + step * inner
+        cut = pl.ds(pl.multiple_of(start * LANES, LANES), wide)
+        return [
+            pltpu.make_async_copy(far.at[:, cut], near.at[:, cut], sems.at[n, turn * half_steps + step])
+            for n, (far, near) in enumerate(sources)
+        ]
 
     first = shard_start(groups)
-    rows_ref[0] = jnp.exp(flat_rows(logs_ref[:, pl.ds(first, groups)], poles))
-    rows_ref[1] = flat_rows(res_ref[:, pl.ds(first, groups)], poles)
+    for turn in range(2):
+        for step in range(half_steps):
+            for copy in copies(turn, step):
+                copy.start()
+    for n in range(2):
+        table_ref[n] = all_params_ref[n, :, pl.ds(first, groups)]
+    rows_ref[0] = jnp.exp(flat_rows(table_ref[0], poles))
+    rows_ref[1] = flat_rows(table_ref[1], poles)
 
     flip = reversal(tokens)
     back_pos = (tokens - 1 - iota((tokens, LANES), 0)).astype(F32)
@@ -105,10 +121,14 @@
     for turn, msg_ref in enumerate((send_ref, keep_ref)):
         base = lax.rem(core + 1 + turn, 2) * half_blocks
 
-        def body(step, carry, base=base, msg_ref=msg_ref):
+        def body(step, carry, base=base, msg_ref=msg_ref, turn=turn):
             start = base + step * inner
             cut = pl.ds(pl.multiple_of(start * LANES, LANES), wide)
-            gated, dgate = gated_ref[:, cut], dgate_ref[:, cut]
+            for copy in copies(turn, step):
+                copy.wait()
+            gated, dgate = gate(k_ref[:, cut], v_ref[:, cut]), gate(c_ref[:, cut], q_ref[:, cut])
+            gated_ref[:, cut] = gated
+            dgate_ref[:, cut] = dgate
             turned = mxu(flip, dgate).astype(BF16)
             turned_ref[:, cut] = turned
             tables = [jnp.exp(-rows_ref[0, pl.ds(start + j, 1), :] * back_pos).T for j in range(inner)]
@@ -202,13 +222,12 @@
     out_ref[2 * poles :, :] = skip_ref[...].astype(BF16)
 
 
-def tables_kernel(logs_ref, _, rates_ref, lag_rates_ref, *, group, poles, inner):
+def tables_kernel(params_ref, rates_ref, lag_rates_ref, *, group, poles, inner):
     blocks, _, lag_width = lag_rates_ref.shape
     per_block = LANES // group
-    groups = blocks * per_block
     step_groups = inner * per_block
     lag_wide = inner * lag_width
-    pieces = split(logs_ref[:, pl.ds(shard_start(groups), groups)], 3)
+    pieces = split(params_ref[0], 3)
     spread = jnp.concatenate(
         [members(step_groups, 0, SUB, lag_wide), members(step_groups, 0, group, inner * LANES)], axis=1
     )
@@ -221,7 +240,7 @@
             rates_ref[here] = rates[:, lag_wide + j * LANES : lag_wide + (j + 1) * LANES]
 
 
-def conv_kernel(res_ref, rows_ref, skip_ref, rates_ref, lag_rates_ref, gated_ref, turned_ref, _, conv_ref,
+def conv_kernel(params_ref, rows_ref, skip_ref, rates_ref, lag_rates_ref, gated_ref, turned_ref, _, conv_ref,
                 *, first_step, group, poles, inner):
     tokens, _ = gated_ref.shape
     per_block = LANES // group
@@ -235,7 +254,7 @@
     causal = iota((SUB, lag_width), 0) >= within(iota((SUB, lag_width), 1), SUB)
     lag = (SUB - 1 - within(iota((poles, lag_width), 1), SUB)).astype(F32)
     groups = blocks * per_block
-    pieces = split(res_ref[:, pl.ds(shard_start(groups), groups)], 3).astype(F32)
+    pieces = split(params_ref[1], 3).astype(F32)
     spread = members(groups, 0, SUB, inner * lag_width)
 
     def body(step, carry):
@@ -388,12 +407,11 @@
             slim_ref[tail:, :] = rests
 
 
-def merge_kernel(logs_ref, res_ref, own_ref, got_ref, _, out_ref, *, poles, length):
+def merge_kernel(params_ref, own_ref, got_ref, _, out_ref, *, poles, length):
     groups = out_ref.shape[1]
     start = own_ref.shape[0] - out_ref.shape[0]
     both = own_ref[start:, :].astype(F32) + got_ref[start:, :].astype(F32)
-    first = shard_start(groups)
-    factor = -jnp.exp(logs_ref[:, pl.ds(first, groups)]) * res_ref[:, pl.ds(first, groups)]
+    factor = -jnp.exp(params_ref[0]) * params_ref[1]
     scaled = [
         both[:poles] / length,
         factor * both[poles : 2 * poles] / math.sqrt(length),
@@ -489,30 +507,35 @@
     def swap(value, level):
         return lax.ppermute(value, "ctx", [(i, i ^ (1 << level)) for i in range(parts)])
 
-    gated, dgate = gate(key_input, value_input), gate(cotangent, queries)
-    outgoing, message, turned, rows = pl.pallas_call(
+    far = pl.BlockSpec(memory_space=pl.ANY)
+    outgoing, message, gated, dgate, turned, rows, params = pl.pallas_call(
         lambda *refs: states_kernel(*refs, inner=inner, **sizes),
-        in_specs=[vmem] * 4,
-        out_specs=[vmem] * 4,
+        in_specs=[vmem] + [far] * 4,
+        out_specs=[vmem] * 7,
         out_shape=[
             shape(2 * half_rows, LANES, dtype=BF16),
             shape(2 * half_rows, LANES, dtype=BF16),
             shape(tokens, width, dtype=BF16),
+            shape(tokens, width, dtype=BF16),
+            shape(tokens, width, dtype=BF16),
             shape(2, blocks, LANES),
+            shape(2, poles, groups),
         ],
-        compiler_params=PARAMS,
+        scratch_shapes=[pltpu.VMEM((tokens, width), BF16)] * 4
+        + [pltpu.SemaphoreType.DMA((4, steps))],
+        compiler_params=pltpu.CompilerParams(vmem_limit_bytes=53000 * 1024),
         name="states",
-    )(log_rates, residues, gated, dgate)
+    )(jnp.stack([log_rates, residues]), queries, key_input, value_input, cotangent)
 
     rates, lag_rates = pl.pallas_call(
         lambda *refs: tables_kernel(*refs, inner=inner, **sizes),
-        in_specs=[vmem, anywhere],
+        in_specs=[vmem],
         out_specs=[vmem] * 2,
         out_shape=[shape(blocks, poles, LANES), shape(blocks, poles, lag_width)],
         compiler_params=PARAMS,
         cost_estimate=pl.CostEstimate(flops=10**9, bytes_accessed=10**6, transcendentals=10**5),
         name="tables",
-    )(log_rates, rows)
+    )(params)
 
     work = pl.CostEstimate(
         flops=16 * tokens * tokens * width, bytes_accessed=12 * tokens * width, transcendentals=tokens * width
@@ -540,7 +563,7 @@
             compiler_params=PARAMS,
             cost_estimate=work,
             name="conv",
-        )(residues, rows, skip_rows, rates, lag_rates, gated, turned, after)
+        )(params, rows, skip_rows, rates, lag_rates, gated, turned, after)
 
     def combine(level, operands, outs):
         return pl.pallas_call(
@@ -590,12 +613,12 @@
     last_conv = convolve(steps - 1, 1, outgoing)
     merged = pl.pallas_call(
         lambda *refs: merge_kernel(*refs, poles=poles, length=tokens * parts),
-        in_specs=[vmem] * 4 + [anywhere],
+        in_specs=[vmem] * 3 + [anywhere],
         out_specs=vmem,
         out_shape=shape(tail, LANES, dtype=BF16),
         compiler_params=PARAMS,
         name="merge",
-    )(log_rates, residues, outgoing, got, last_conv)
+    )(params, outgoing, got, last_conv)
 
     gathered = [merged]
     for mask in range(1, shards):

time: 30.8 us -> 30.5 us (level)
  other arithmetic: 1.99 us -> 0.78 us
  Pallas kernels: 13.1 us -> 14 us
    convert_element_type x1 -> x0, other arithmetic: 1.99 us -> none  [gate(): return (left.astype(F32) * right.astype(F32)).astype(BF16)]
    pallas_call x1, Pallas kernels: 2.16 us -> 3.1 us  [local(): pl.pallas_call(lambda *refs: states_kernel(*refs, inner=inner, **sizes),...]
    another operation x0 -> x1, other arithmetic: none -> 0.78 us  [local(): jnp.stack([log_rates, residues])]
where the time goes in v14:
time: 30.5 us; the launch traced here: 30.3 us
  Pallas kernels  14 us (46%)
  starting transfers between devices  9.49 us (31%)
  waiting for transfers between devices  5.23 us (17%)
  other arithmetic  0.78 us (3%)
  between operations  0.78 us (3%)
    ppermute x5, starting transfers between devices, swap(): lax.ppermute(value, 'ctx', [(i, i ^ 1 << level) for i in range(parts)])  5.04 us
    ppermute x3, starting transfers between devices, local(): lax.ppermute(merged, 'ch', [(i, i ^ mask) for i in range(shards)])  4.45 us
    ppermute x5, waiting for transfers between devices, swap(): lax.ppermute(value, 'ctx', [(i, i ^ 1 << level) for i in range(parts)])  4.17 us
    pallas_call x2, Pallas kernels, convolve(): pl.pallas_call(lambda *refs: conv_kernel(*refs, first_step=first_step, in...  3.64 us
    pallas_call x1, Pallas kernels, local(): pl.pallas_call(lambda *refs: states_kernel(*refs, inner=inner, **sizes),...  3.1 us
    pallas_call x1, Pallas kernels, local(): pl.pallas_call(lambda *refs: output_kernel(*refs, **sizes), grid=(steps,)...  2.74 us
    pallas_call x2, Pallas kernels, local_sums(): pl.pallas_call(lambda *refs: lags_kernel(*refs, second=second, inner=inne...  2.71 us
    ppermute x3, waiting for transfers between devices, local(): lax.ppermute(merged, 'ch', [(i, i ^ mask) for i in range(shards)])  1.07 us
  transfers between devices with their start and end apart: 8, of which 4 were waited for; matrix products, arithmetic and copies ran while one was open for 0% of the time, Pallas kernels for 31%

profile of v14, /device:TPU:0, one launch (start us, length us, event | category | flops | bytes accessed | tf_op | source)
XLA Modules:
  0.0 30.3 jit_solution(17161130661862228870)
XLA Ops:
  0.6 0.8 %pad_maximum_fusion.refs_0_ = f32[2,16,512]{2,1,0:T(8,128)S(1)} fusion(f32[1,16,512]{2,1,0:T(8,128)} %bitcast.12, f32[1,16,512]{2,1,0:T(8,128)} %bitcast.13), kind=kLoop, calls=%fused_computation | loop fusion | flops 16384 | bytes 131072 | tf_op jit(solution)/shard_map/stack | solution.py:528
  1.4 3.1 %states.1 = (bf16[512,128]{1,0:T(8,128)(2,1)S(1)}, bf16[512,128]{1,0:T(8,128)(2,1)S(1)}, bf16[128,2048]{1,0:T(8,128)(2,1)S(1)}, bf16[128,2048]{1,0:T(8,128)(2,1)...) custom-call(f32[2,16,512]{2,1,0:T(8,128)S(1)} %pad_maximum_fusion.refs_0_, ...), custom_call_target="tpu_custom_call" | custom-call | tf_op jit(solution)/shard_map/states/pallas_call | solution.py:511
  4.5 0.5 %collective-permute-start = (bf16[512,128]{1,0:T(8,128)(2,1)S(1)}, bf16[512,128]{1,0:T(8,128)(2,1)S(1)}, u32[]{:S(2)}, u32[]{:S(2)}) collective-permute-start(bf16[512,128]{1,0:T(8,128)(2,1)S(1)} %get-tuple-element.37), channel_id=1, source_target_pairs={{0,4},{4,0},{8,12},{12,8},{16,20},{20,16},{24,28},{28,24},{1,5},{5... | collective-permute-start | bytes 393224 | tf_op jit(solution)/shard_map/ppermute | solution.py:508
  5.0 0.4 %tables.1 = (f32[16,16,128]{2,1,0:T(8,128)S(1)}, f32[16,16,256]{2,1,0:T(8,128)S(1)}) custom-call(f32[2,16,128]{2,1,0:T(8,128)S(1)} %get-tuple-element.31.refs_0_), custom_call_target="tpu_custom_call" | custom-call | flops 1000000000 | bytes 1000000 | tf_op jit(solution)/shard_map/tables/pallas_call | solution.py:530
  5.4 0.7 %lags.2.refs_3_ = f32[32,128]{1,0:T(8,128)S(1)} custom-call(f32[16,16,256]{2,1,0:T(8,128)S(1)} %get-tuple-element.33.refs_0_.refs_4_, bf16[128,2048]{1,0:T(8,128)(2,1)S(1)} %get-tuple-element.34.refs_1_.refs_5_, bf16[128,2048]{1,0:T(8,128)(2,1)S(1)} %get-tuple-element.38.refs_2_, bf16[128,2048]{1,0:T(8,128)(2,1)S(1)} %get-tuple-element.35.refs_3_.refs_6_), custom_call_target="tpu_custom_call" | custom-call | flops 536870912 | bytes 3145728 | tf_op jit(solution)/shard_map/lags/pallas_call | solution.py:545
  6.1 0.0 copy-start.3
  6.1 0.0 collective-permute-done.refs_2_
  6.1 0.3 combine.3
  6.4 2.8 %collective-permute-start.1 = (bf16[512,128]{1,0:T(8,128)(2,1)S(1)}, bf16[512,128]{1,0:T(8,128)(2,1)S(1)}, u32[]{:S(2)}, u32[]{:S(2)}) collective-permute-start(bf16[512,128]{1,0:T(8,128)(2,1)S(1)} %get-tuple-element.39.refs_1_), channel_id=1, source_target_pairs={{0,8},{4,12},{8,0},{12,4},{16,24},{20,28},{24,16},{28,20},{1,9},{5... | collective-permute-start | bytes 393224 | tf_op jit(solution)/shard_map/ppermute | solution.py:508
  9.2 2.0 %lags.3.refs_2_ = bf16[48,128]{1,0:T(8,128)(2,1)S(1)} custom-call(f32[16,16,256]{2,1,0:T(8,128)S(1)} %get-tuple-element.33.refs_0_.refs_4_, bf16[128,2048]{1,0:T(8,128)(2,1)S(1)} %get-tuple-element.34.refs_1_.refs_5_, bf16[128,2048]{1,0:T(8,128)(2,1)S(1)} %get-tuple-element.38.refs_2_, bf16[128,2048]{1,0:T(8,128)(2,1)S(1)} %get-tuple-element.35.refs_3_.refs_6_, ...), custom_call_target="tpu_custom_call" | custom-call | flops 536870912 | bytes 3145728 | tf_op jit(solution)/shard_map/lags/pallas_call | solution.py:545
  11.2 0.1 collective-permute-start.2
  11.3 3.7 %collective-permute-done.2.refs_4_ = bf16[48,128]{1,0:T(8,128)(2,1)S(1)} collective-permute-done((bf16[48,128]{1,0:T(8,128)(2,1)S(1)}, bf16[48,128]{1,0:T(8,128)(2,1)S(1)}, u32[]{:S(2)}, u32[]{:S(2)}) %collective-permute-start.2) | collective-permute-done | bytes 12320 | tf_op jit(solution)/shard_map/ppermute | solution.py:508
  15.0 0.0 collective-permute-done.1.refs_3_
  15.0 0.3 combine.4
  15.3 1.6 %collective-permute-start.3 = (bf16[304,128]{1,0:T(8,128)(2,1)S(1)}, bf16[304,128]{1,0:T(8,128)(2,1)S(1)}, u32[]{:S(2)}, u32[]{:S(2)}) collective-permute-start(bf16[304,128]{1,0:T(8,128)(2,1)S(1)} %get-tuple-element.44), channel_id=1, source_target_pairs={{0,16},{4,20},{8,24},{12,28},{16,0},{20,4},{24,8},{28,12},{1,17},{... | collective-permute-start | bytes 233480 | tf_op jit(solution)/shard_map/ppermute | solution.py:508
  16.9 0.0 copy-done.3
  16.9 2.7 %conv.2.refs_5_.refs_1_ = f32[128,3072]{1,0:T(8,128)S(1)} custom-call(f32[2,16,128]{2,1,0:T(8,128)S(1)} %get-tuple-element.31.refs_0_, f32[2,16,128]{2,1,0:T(8,128)S(1)} %get-tuple-element.30.refs_1_.refs_0_, f32[64,128]{1,0:T(8,128)S(1)} %bitcast.10, f32[16,16,128]{2,1,0:T(8,128)S(1)} %get-tuple-element.32.refs_0_.refs_3_, ...), custom_call_target="tpu_custom_call" | custom-call | flops 536870912 | bytes 3145728 | tf_op jit(solution)/shard_map/conv/pallas_call | solution.py:558
  19.6 0.1 collective-permute-done.3.refs_3_
  19.7 0.3 combine.5
  20.0 0.0 copy-start
  20.0 0.0 copy-start.1
  20.1 0.0 copy-start.2
  20.1 0.1 collective-permute-start.4
  20.1 0.9 %conv.3.refs_2_.refs_3_ = f32[128,1024]{1,0:T(8,128)S(1)} custom-call(f32[2,16,128]{2,1,0:T(8,128)S(1)} %get-tuple-element.31.refs_0_, f32[2,16,128]{2,1,0:T(8,128)S(1)} %get-tuple-element.30.refs_1_.refs_0_, f32[64,128]{1,0:T(8,128)S(1)} %bitcast.11, f32[16,16,128]{2,1,0:T(8,128)S(1)} %get-tuple-element.32.refs_0_.refs_3_, ...), custom_call_target="tpu_custom_call" | custom-call | flops 536870912 | bytes 3145728 | tf_op jit(solution)/shard_map/conv/pallas_call | solution.py:558
  21.1 0.3 %collective-permute-done.4.refs_4_.refs_2_ = bf16[304,128]{1,0:T(8,128)(2,1)S(1)} collective-permute-done((bf16[304,128]{1,0:T(8,128)(2,1)S(1)}, bf16[304,128]{1,0:T(8,128)(2,1)S(1)}, u32[]{:S(2)}, u32[]{:S(2)}) %collective-permute-start.4) | collective-permute-done | bytes 77856 | tf_op jit(solution)/shard_map/ppermute | solution.py:508
  21.4 3.7 %collective-permute-start.7 = (bf16[48,128]{1,0:T(8,128)(2,1)S(1)}, bf16[48,128]{1,0:T(8,128)(2,1)S(1)}, u32[]{:S(2)}, u32[]{:S(2)}) collective-permute-start(bf16[48,128]{1,0:T(8,128)(2,1)S(1)} %merge.1.refs_0_), channel_id=1, source_target_pairs={{0,3},{1,2},{2,1},{3,0},{4,7},{5,6},{6,5},{7,4},{8,11},{9,10},{10,... | collective-permute-start | bytes 36872 | tf_op jit(solution)/shard_map/ppermute | solution.py:625
  25.1 0.0 collective-permute-start.6
  25.1 0.8 %collective-permute-start.5 = (bf16[48,128]{1,0:T(8,128)(2,1)S(1)}, bf16[48,128]{1,0:T(8,128)(2,1)S(1)}, u32[]{:S(2)}, u32[]{:S(2)}) collective-permute-start(bf16[48,128]{1,0:T(8,128)(2,1)S(1)} %merge.1.refs_0_), channel_id=1, source_target_pairs={{0,1},{1,0},{2,3},{3,2},{4,5},{5,4},{6,7},{7,6},{8,9},{9,8},{10,11... | collective-permute-start | bytes 36872 | tf_op jit(solution)/shard_map/ppermute | solution.py:625
  25.9 0.0 copy-done
  25.9 0.0 copy-done.1
  25.9 0.0 copy-done.2
  25.9 2.7 %outputs.1 = (bf16[128,2048]{1,0:T(8,128)(2,1)}, bf16[128,2048]{1,0:T(8,128)(2,1)}, bf16[128,2048]{1,0:T(8,128)(2,1)}) custom-call(f32[2,16,128]{2,1,0:T(8,128)S(1)} %get-tuple-element.30.refs_1_.refs_0_, f32[128,3072]{1,0:T(8,128)S(1)} %conv.2.refs_5_.refs_1_, f32[128,1024]{1,0:T(8,128)S(1)} %conv.3.refs_2_.refs_3_, ...), custom_call_target="tpu_custom_call" | custom-call | flops 536870912 | bytes 3145728 | tf_op jit(solution)/shard_map/outputs/pallas_call | solution.py:628
  28.6 0.0 collective-permute-done.7.refs_3_
  28.6 1.1 %collective-permute-done.6.refs_2_ = bf16[48,128]{1,0:T(8,128)(2,1)S(1)} collective-permute-done((bf16[48,128]{1,0:T(8,128)(2,1)S(1)}, bf16[48,128]{1,0:T(8,128)(2,1)S(1)}, u32[]{:S(2)}, u32[]{:S(2)}) %collective-permute-start.6) | collective-permute-done | bytes 12320 | tf_op jit(solution)/shard_map/ppermute | solution.py:625
  29.7 0.0 collective-permute-done.5.refs_1_
  29.7 0.6 %assemble.1 = (f32[16,512]{1,0:T(8,128)}, f32[16,512]{1,0:T(8,128)}, f32[64,128]{1,0:T(8,128)}) custom-call(bf16[48,128]{1,0:T(8,128)(2,1)S(1)} %merge.1.refs_0_, bf16[48,128]{1,0:T(8,128)(2,1)S(1)} %collective-permute-done.5.refs_1_, bf16[48,128]{1,0:T(8,128)(2,1)S(1)} %collective-permute-done.6.refs_2_, bf16[48,128]{1,0:T(8,128)(2,1)S(1)} %collective-permute-done.7.refs_3_), custom_call_target="tpu_custom_call" | custom-call | tf_op jit(solution)/shard_map/assemble/pallas_call | solution.py:639
  (1 shorter events, 0.0 us)
Async XLA Ops:
  4.5 1.6 %collective-permute-start = (bf16[512,128]{1,0:T(8,128)(2,1)S(1)}, bf16[512,128]{1,0:T(8,128)(2,1)S(1)}, u32[]{:S(2)}, u32[]{:S(2)}) collective-permute-start(bf16[512,128]{1,0:T(8,128)(2,1)S(1)} %get-tuple-element.37), channel_id=1, source_target_pairs={{0,4},{4,0},{8,12},{12,8},{16,20},{20,16},{24,28},{28,24},{1,5},{5... | collective-permute-start | bytes 393224 | tf_op jit(solution)/shard_map/ppermute | solution.py:508
  6.1 10.8 %copy-start.3 = (f32[8192]{0:T(1024)S(1)}, f32[8192]{0:T(1024)}, u32[]{:S(2)}) copy-start(f32[8192]{0:T(1024)} %param.13) | copy-start | bytes 98308
  6.4 8.6 %collective-permute-start.1 = (bf16[512,128]{1,0:T(8,128)(2,1)S(1)}, bf16[512,128]{1,0:T(8,128)(2,1)S(1)}, u32[]{:S(2)}, u32[]{:S(2)}) collective-permute-start(bf16[512,128]{1,0:T(8,128)(2,1)S(1)} %get-tuple-element.39.refs_1_), channel_id=1, source_target_pairs={{0,8},{4,12},{8,0},{12,4},{16,24},{20,28},{24,16},{28,20},{1,9},{5... | collective-permute-start | bytes 393224 | tf_op jit(solution)/shard_map/ppermute | solution.py:508
  11.2 3.8 %collective-permute-start.2 = (bf16[48,128]{1,0:T(8,128)(2,1)S(1)}, bf16[48,128]{1,0:T(8,128)(2,1)S(1)}, u32[]{:S(2)}, u32[]{:S(2)}) collective-permute-start(bf16[48,128]{1,0:T(8,128)(2,1)S(1)} %lags.3.refs_2_), channel_id=1, source_target_pairs={{0,8},{4,12},{8,0},{12,4},{16,24},{20,28},{24,16},{28,20},{1,9},{5... | collective-permute-start | bytes 36872 | tf_op jit(solution)/shard_map/ppermute | solution.py:508
  15.3 4.4 %collective-permute-start.3 = (bf16[304,128]{1,0:T(8,128)(2,1)S(1)}, bf16[304,128]{1,0:T(8,128)(2,1)S(1)}, u32[]{:S(2)}, u32[]{:S(2)}) collective-permute-start(bf16[304,128]{1,0:T(8,128)(2,1)S(1)} %get-tuple-element.44), channel_id=1, source_target_pairs={{0,16},{4,20},{8,24},{12,28},{16,0},{20,4},{24,8},{28,12},{1,17},{... | collective-permute-start | bytes 233480 | tf_op jit(solution)/shard_map/ppermute | solution.py:508
  20.0 5.9 %copy-start = (bf16[128,2048]{1,0:T(8,128)(2,1)S(1)}, bf16[128,2048]{1,0:T(8,128)(2,1)}, u32[]{:S(2)}) copy-start(bf16[128,2048]{1,0:T(8,128)(2,1)} %refs_5_.1) | copy-start | bytes 1572868
  20.0 5.8 %copy-start.1 = (bf16[128,2048]{1,0:T(8,128)(2,1)S(1)}, bf16[128,2048]{1,0:T(8,128)(2,1)}, u32[]{:S(2)}) copy-start(bf16[128,2048]{1,0:T(8,128)(2,1)} %refs_6_.1) | copy-start | bytes 1572868
  20.1 5.8 %copy-start.2 = (bf16[128,2048]{1,0:T(8,128)(2,1)S(1)}, bf16[128,2048]{1,0:T(8,128)(2,1)}, u32[]{:S(2)}) copy-start(bf16[128,2048]{1,0:T(8,128)(2,1)} %refs_7_.1) | copy-start | bytes 1572868
  20.1 1.3 %collective-permute-start.4 = (bf16[304,128]{1,0:T(8,128)(2,1)S(1)}, bf16[304,128]{1,0:T(8,128)(2,1)S(1)}, u32[]{:S(2)}, u32[]{:S(2)}) collective-permute-start(bf16[304,128]{1,0:T(8,128)(2,1)S(1)} %get-tuple-element.46.refs_7_.refs_1_), channel_id=1, source_target_pairs={{0,4},{4,0},{8,12},{12,8},{16,20},{20,16},{24,28},{28,24},{1,5},{5... | collective-permute-start | bytes 233480 | tf_op jit(solution)/shard_map/ppermute | solution.py:508
  21.4 7.2 %collective-permute-start.7 = (bf16[48,128]{1,0:T(8,128)(2,1)S(1)}, bf16[48,128]{1,0:T(8,128)(2,1)S(1)}, u32[]{:S(2)}, u32[]{:S(2)}) collective-permute-start(bf16[48,128]{1,0:T(8,128)(2,1)S(1)} %merge.1.refs_0_), channel_id=1, source_target_pairs={{0,3},{1,2},{2,1},{3,0},{4,7},{5,6},{6,5},{7,4},{8,11},{9,10},{10,... | collective-permute-start | bytes 36872 | tf_op jit(solution)/shard_map/ppermute | solution.py:625
  25.1 4.6 %collective-permute-start.6 = (bf16[48,128]{1,0:T(8,128)(2,1)S(1)}, bf16[48,128]{1,0:T(8,128)(2,1)S(1)}, u32[]{:S(2)}, u32[]{:S(2)}) collective-permute-start(bf16[48,128]{1,0:T(8,128)(2,1)S(1)} %merge.1.refs_0_), channel_id=1, source_target_pairs={{0,2},{1,3},{2,0},{3,1},{4,6},{5,7},{6,4},{7,5},{8,10},{9,11},{10,... | collective-permute-start | bytes 36872 | tf_op jit(solution)/shard_map/ppermute | solution.py:625
  25.1 4.6 %collective-permute-start.5 = (bf16[48,128]{1,0:T(8,128)(2,1)S(1)}, bf16[48,128]{1,0:T(8,128)(2,1)S(1)}, u32[]{:S(2)}, u32[]{:S(2)}) collective-permute-start(bf16[48,128]{1,0:T(8,128)(2,1)S(1)} %merge.1.refs_0_), channel_id=1, source_target_pairs={{0,1},{1,0},{2,3},{3,2},{4,5},{5,4},{6,7},{7,6},{8,9},{9,8},{10,11... | collective-permute-start | bytes 36872 | tf_op jit(solution)/shard_map/ppermute | solution.py:625

commit v15 on v14

--- a/solution.py
+++ b/solution.py
@@ -83,7 +83,8 @@
 
 
 def states_kernel(all_params_ref, q_any, k_any, v_any, c_any, send_ref, keep_ref, gated_ref, dgate_ref, turned_ref,
-                  rows_ref, table_ref, q_ref, k_ref, v_ref, c_ref, sems, *, group, poles, inner):
+                  rows_ref, table_ref, q_ref, k_ref, v_ref, c_ref, both_ref, sems, *,
+                  group, poles, inner):
     tokens, _ = gated_ref.shape
     per_block = LANES // group
     _, blocks, _ = rows_ref.shape
@@ -117,6 +118,10 @@
     back_lane = (tokens - 1 - iota((1, tokens), 1)).astype(F32)
     wide_group = over(within(iota((poles, 2 * LANES), 1), LANES), group)
     lanes = [slice(j * LANES, (j + 1) * LANES) for j in range(inner)]
+    for b in range(blocks):
+        table = jnp.exp(-rows_ref[0, b : b + 1, :] * back_pos).T
+        both_ref[b, :LANES] = table.astype(BF16)
+        both_ref[b, LANES:] = (table * back_lane).astype(BF16)
 
     for turn, msg_ref in enumerate((send_ref, keep_ref)):
         base = lax.rem(core + 1 + turn, 2) * half_blocks
@@ -131,12 +136,10 @@
             dgate_ref[:, cut] = dgate
             turned = mxu(flip, dgate).astype(BF16)
             turned_ref[:, cut] = turned
-            tables = [jnp.exp(-rows_ref[0, pl.ds(start + j, 1), :] * back_pos).T for j in range(inner)]
             found = []
             for j in range(inner):
-                both = jnp.concatenate([tables[j].astype(BF16), (tables[j] * back_lane).astype(BF16)], axis=0)
                 pair = jnp.concatenate([gated[:, lanes[j]], turned[:, lanes[j]]], axis=1)
-                found.append(mxu(both, pair))
+                found.append(mxu(both_ref[start + j], pair))
             for j in range(inner):
                 folded = []
                 for part in range(2):
@@ -522,7 +525,7 @@
             shape(2, poles, groups),
         ],
         scratch_shapes=[pltpu.VMEM((tokens, width), BF16)] * 4
-        + [pltpu.SemaphoreType.DMA((4, steps))],
+        + [pltpu.VMEM((blocks, 2 * LANES, tokens), BF16), pltpu.SemaphoreType.DMA((4, steps))],
         compiler_params=pltpu.CompilerParams(vmem_limit_bytes=53000 * 1024),
         name="states",
     )(jnp.stack([log_rates, residues]), queries, key_input, value_input, cotangent)

time: 30.5 us -> 31.1 us (1.020)
  Pallas kernels: 14 us -> 14.5 us
    pallas_call x1, Pallas kernels: 3.1 us -> 3.61 us  [local(): pl.pallas_call(lambda *refs: states_kernel(*refs, inner=inner, **sizes),...]
where the time goes in v15:
time: 31.1 us; the launch traced here: 30.9 us
  Pallas kernels  14.5 us (47%)
  starting transfers between devices  9.51 us (31%)
  waiting for transfers between devices  5.23 us (17%)
  other arithmetic  0.78 us (3%)
  between operations  0.78 us (3%)
    ppermute x5, starting transfers between devices, swap(): lax.ppermute(value, 'ctx', [(i, i ^ 1 << level) for i in range(parts)])  5.05 us
    ppermute x3, starting transfers between devices, local(): lax.ppermute(merged, 'ch', [(i, i ^ mask) for i in range(shards)])  4.45 us
    ppermute x5, waiting for transfers between devices, swap(): lax.ppermute(value, 'ctx', [(i, i ^ 1 << level) for i in range(parts)])  4.16 us
    pallas_call x2, Pallas kernels, convolve(): pl.pallas_call(lambda *refs: conv_kernel(*refs, first_step=first_step, in...  3.63 us
    pallas_call x1, Pallas kernels, local(): pl.pallas_call(lambda *refs: states_kernel(*refs, inner=inner, **sizes),...  3.61 us
    pallas_call x1, Pallas kernels, local(): pl.pallas_call(lambda *refs: output_kernel(*refs, **sizes), grid=(steps,)...  2.74 us
    pallas_call x2, Pallas kernels, local_sums(): pl.pallas_call(lambda *refs: lags_kernel(*refs, second=second, inner=inne...  2.71 us
    ppermute x3, waiting for transfers between devices, local(): lax.ppermute(merged, 'ch', [(i, i ^ mask) for i in range(shards)])  1.07 us
  transfers between devices with their start and end apart: 8, of which 4 were waited for; matrix products, arithmetic and copies ran while one was open for 0% of the time, Pallas kernels for 31%

profile of v15, /device:TPU:0, one launch (start us, length us, event | category | flops | bytes accessed | tf_op | source)
XLA Modules:
  0.0 30.9 jit_solution(9925764129919712512)
XLA Ops:
  0.6 0.8 %pad_maximum_fusion.refs_0_ = f32[2,16,512]{2,1,0:T(8,128)S(1)} fusion(f32[1,16,512]{2,1,0:T(8,128)} %bitcast.12, f32[1,16,512]{2,1,0:T(8,128)} %bitcast.13), kind=kLoop, calls=%fused_computation | loop fusion | flops 16384 | bytes 131072 | tf_op jit(solution)/shard_map/stack | solution.py:531
  1.4 3.6 %states.1 = (bf16[512,128]{1,0:T(8,128)(2,1)S(1)}, bf16[512,128]{1,0:T(8,128)(2,1)S(1)}, bf16[128,2048]{1,0:T(8,128)(2,1)S(1)}, bf16[128,2048]{1,0:T(8,128)(2,1)...) custom-call(f32[2,16,512]{2,1,0:T(8,128)S(1)} %pad_maximum_fusion.refs_0_, ...), custom_call_target="tpu_custom_call" | custom-call | tf_op jit(solution)/shard_map/states/pallas_call | solution.py:514
  5.0 0.5 %collective-permute-start = (bf16[512,128]{1,0:T(8,128)(2,1)S(1)}, bf16[512,128]{1,0:T(8,128)(2,1)S(1)}, u32[]{:S(2)}, u32[]{:S(2)}) collective-permute-start(bf16[512,128]{1,0:T(8,128)(2,1)S(1)} %get-tuple-element.37), channel_id=1, source_target_pairs={{0,4},{4,0},{8,12},{12,8},{16,20},{20,16},{24,28},{28,24},{1,5},{5... | collective-permute-start | bytes 393224 | tf_op jit(solution)/shard_map/ppermute | solution.py:511
  5.5 0.4 %tables.1 = (f32[16,16,128]{2,1,0:T(8,128)S(1)}, f32[16,16,256]{2,1,0:T(8,128)S(1)}) custom-call(f32[2,16,128]{2,1,0:T(8,128)S(1)} %get-tuple-element.31.refs_0_), custom_call_target="tpu_custom_call" | custom-call | flops 1000000000 | bytes 1000000 | tf_op jit(solution)/shard_map/tables/pallas_call | solution.py:533
  5.9 0.7 %lags.2.refs_3_ = f32[32,128]{1,0:T(8,128)S(1)} custom-call(f32[16,16,256]{2,1,0:T(8,128)S(1)} %get-tuple-element.33.refs_0_.refs_4_, bf16[128,2048]{1,0:T(8,128)(2,1)S(1)} %get-tuple-element.34.refs_1_.refs_5_, bf16[128,2048]{1,0:T(8,128)(2,1)S(1)} %get-tuple-element.38.refs_2_, bf16[128,2048]{1,0:T(8,128)(2,1)S(1)} %get-tuple-element.35.refs_3_.refs_6_), custom_call_target="tpu_custom_call" | custom-call | flops 536870912 | bytes 3145728 | tf_op jit(solution)/shard_map/lags/pallas_call | solution.py:548
  6.6 0.0 copy-start.3
  6.6 0.0 collective-permute-done.refs_2_
  6.6 0.3 combine.3
  6.9 2.8 %collective-permute-start.1 = (bf16[512,128]{1,0:T(8,128)(2,1)S(1)}, bf16[512,128]{1,0:T(8,128)(2,1)S(1)}, u32[]{:S(2)}, u32[]{:S(2)}) collective-permute-start(bf16[512,128]{1,0:T(8,128)(2,1)S(1)} %get-tuple-element.39.refs_1_), channel_id=1, source_target_pairs={{0,8},{4,12},{8,0},{12,4},{16,24},{20,28},{24,16},{28,20},{1,9},{5... | collective-permute-start | bytes 393224 | tf_op jit(solution)/shard_map/ppermute | solution.py:511
  9.7 2.0 %lags.3.refs_2_ = bf16[48,128]{1,0:T(8,128)(2,1)S(1)} custom-call(f32[16,16,256]{2,1,0:T(8,128)S(1)} %get-tuple-element.33.refs_0_.refs_4_, bf16[128,2048]{1,0:T(8,128)(2,1)S(1)} %get-tuple-element.34.refs_1_.refs_5_, bf16[128,2048]{1,0:T(8,128)(2,1)S(1)} %get-tuple-element.38.refs_2_, bf16[128,2048]{1,0:T(8,128)(2,1)S(1)} %get-tuple-element.35.refs_3_.refs_6_, ...), custom_call_target="tpu_custom_call" | custom-call | flops 536870912 | bytes 3145728 | tf_op jit(solution)/shard_map/lags/pallas_call | solution.py:548
  11.7 0.1 collective-permute-start.2
  11.8 3.7 %collective-permute-done.2.refs_4_ = bf16[48,128]{1,0:T(8,128)(2,1)S(1)} collective-permute-done((bf16[48,128]{1,0:T(8,128)(2,1)S(1)}, bf16[48,128]{1,0:T(8,128)(2,1)S(1)}, u32[]{:S(2)}, u32[]{:S(2)}) %collective-permute-start.2) | collective-permute-done | bytes 12320 | tf_op jit(solution)/shard_map/ppermute | solution.py:511
  15.5 0.0 collective-permute-done.1.refs_3_
  15.5 0.3 combine.4
  15.8 1.6 %collective-permute-start.3 = (bf16[304,128]{1,0:T(8,128)(2,1)S(1)}, bf16[304,128]{1,0:T(8,128)(2,1)S(1)}, u32[]{:S(2)}, u32[]{:S(2)}) collective-permute-start(bf16[304,128]{1,0:T(8,128)(2,1)S(1)} %get-tuple-element.44), channel_id=1, source_target_pairs={{0,16},{4,20},{8,24},{12,28},{16,0},{20,4},{24,8},{28,12},{1,17},{... | collective-permute-start | bytes 233480 | tf_op jit(solution)/shard_map/ppermute | solution.py:511
  17.4 0.0 copy-done.3
  17.4 2.7 %conv.2.refs_5_.refs_1_ = f32[128,3072]{1,0:T(8,128)S(1)} custom-call(f32[2,16,128]{2,1,0:T(8,128)S(1)} %get-tuple-element.31.refs_0_, f32[2,16,128]{2,1,0:T(8,128)S(1)} %get-tuple-element.30.refs_1_.refs_0_, f32[64,128]{1,0:T(8,128)S(1)} %bitcast.10, f32[16,16,128]{2,1,0:T(8,128)S(1)} %get-tuple-element.32.refs_0_.refs_3_, ...), custom_call_target="tpu_custom_call" | custom-call | flops 536870912 | bytes 3145728 | tf_op jit(solution)/shard_map/conv/pallas_call | solution.py:561
  20.1 0.1 collective-permute-done.3.refs_3_
  20.2 0.3 combine.5
  20.5 0.0 copy-start
  20.6 0.0 copy-start.1
  20.6 0.0 copy-start.2
  20.6 0.1 collective-permute-start.4
  20.7 0.9 %conv.3.refs_2_.refs_3_ = f32[128,1024]{1,0:T(8,128)S(1)} custom-call(f32[2,16,128]{2,1,0:T(8,128)S(1)} %get-tuple-element.31.refs_0_, f32[2,16,128]{2,1,0:T(8,128)S(1)} %get-tuple-element.30.refs_1_.refs_0_, f32[64,128]{1,0:T(8,128)S(1)} %bitcast.11, f32[16,16,128]{2,1,0:T(8,128)S(1)} %get-tuple-element.32.refs_0_.refs_3_, ...), custom_call_target="tpu_custom_call" | custom-call | flops 536870912 | bytes 3145728 | tf_op jit(solution)/shard_map/conv/pallas_call | solution.py:561
  21.6 0.3 %collective-permute-done.4.refs_4_.refs_2_ = bf16[304,128]{1,0:T(8,128)(2,1)S(1)} collective-permute-done((bf16[304,128]{1,0:T(8,128)(2,1)S(1)}, bf16[304,128]{1,0:T(8,128)(2,1)S(1)}, u32[]{:S(2)}, u32[]{:S(2)}) %collective-permute-start.4) | collective-permute-done | bytes 77856 | tf_op jit(solution)/shard_map/ppermute | solution.py:511
  21.9 3.7 %collective-permute-start.7 = (bf16[48,128]{1,0:T(8,128)(2,1)S(1)}, bf16[48,128]{1,0:T(8,128)(2,1)S(1)}, u32[]{:S(2)}, u32[]{:S(2)}) collective-permute-start(bf16[48,128]{1,0:T(8,128)(2,1)S(1)} %merge.1.refs_0_), channel_id=1, source_target_pairs={{0,3},{1,2},{2,1},{3,0},{4,7},{5,6},{6,5},{7,4},{8,11},{9,10},{10,... | collective-permute-start | bytes 36872 | tf_op jit(solution)/shard_map/ppermute | solution.py:628
  25.6 0.0 collective-permute-start.6
  25.6 0.8 %collective-permute-start.5 = (bf16[48,128]{1,0:T(8,128)(2,1)S(1)}, bf16[48,128]{1,0:T(8,128)(2,1)S(1)}, u32[]{:S(2)}, u32[]{:S(2)}) collective-permute-start(bf16[48,128]{1,0:T(8,128)(2,1)S(1)} %merge.1.refs_0_), channel_id=1, source_target_pairs={{0,1},{1,0},{2,3},{3,2},{4,5},{5,4},{6,7},{7,6},{8,9},{9,8},{10,11... | collective-permute-start | bytes 36872 | tf_op jit(solution)/shard_map/ppermute | solution.py:628
  26.4 0.0 copy-done
  26.4 0.0 copy-done.1
  26.4 0.0 copy-done.2
  26.4 2.7 %outputs.1 = (bf16[128,2048]{1,0:T(8,128)(2,1)}, bf16[128,2048]{1,0:T(8,128)(2,1)}, bf16[128,2048]{1,0:T(8,128)(2,1)}) custom-call(f32[2,16,128]{2,1,0:T(8,128)S(1)} %get-tuple-element.30.refs_1_.refs_0_, f32[128,3072]{1,0:T(8,128)S(1)} %conv.2.refs_5_.refs_1_, f32[128,1024]{1,0:T(8,128)S(1)} %conv.3.refs_2_.refs_3_, ...), custom_call_target="tpu_custom_call" | custom-call | flops 536870912 | bytes 3145728 | tf_op jit(solution)/shard_map/outputs/pallas_call | solution.py:631
  29.1 0.0 collective-permute-done.7.refs_3_
  29.1 1.1 %collective-permute-done.6.refs_2_ = bf16[48,128]{1,0:T(8,128)(2,1)S(1)} collective-permute-done((bf16[48,128]{1,0:T(8,128)(2,1)S(1)}, bf16[48,128]{1,0:T(8,128)(2,1)S(1)}, u32[]{:S(2)}, u32[]{:S(2)}) %collective-permute-start.6) | collective-permute-done | bytes 12320 | tf_op jit(solution)/shard_map/ppermute | solution.py:628
  30.2 0.0 collective-permute-done.5.refs_1_
  30.2 0.6 %assemble.1 = (f32[16,512]{1,0:T(8,128)}, f32[16,512]{1,0:T(8,128)}, f32[64,128]{1,0:T(8,128)}) custom-call(bf16[48,128]{1,0:T(8,128)(2,1)S(1)} %merge.1.refs_0_, bf16[48,128]{1,0:T(8,128)(2,1)S(1)} %collective-permute-done.5.refs_1_, bf16[48,128]{1,0:T(8,128)(2,1)S(1)} %collective-permute-done.6.refs_2_, bf16[48,128]{1,0:T(8,128)(2,1)S(1)} %collective-permute-done.7.refs_3_), custom_call_target="tpu_custom_call" | custom-call | tf_op jit(solution)/shard_map/assemble/pallas_call | solution.py:642
  (1 shorter events, 0.0 us)
Async XLA Ops:
  5.0 1.6 %collective-permute-start = (bf16[512,128]{1,0:T(8,128)(2,1)S(1)}, bf16[512,128]{1,0:T(8,128)(2,1)S(1)}, u32[]{:S(2)}, u32[]{:S(2)}) collective-permute-start(bf16[512,128]{1,0:T(8,128)(2,1)S(1)} %get-tuple-element.37), channel_id=1, source_target_pairs={{0,4},{4,0},{8,12},{12,8},{16,20},{20,16},{24,28},{28,24},{1,5},{5... | collective-permute-start | bytes 393224 | tf_op jit(solution)/shard_map/ppermute | solution.py:511
  6.6 10.8 %copy-start.3 = (f32[8192]{0:T(1024)S(1)}, f32[8192]{0:T(1024)}, u32[]{:S(2)}) copy-start(f32[8192]{0:T(1024)} %param.13) | copy-start | bytes 98308
  6.9 8.6 %collective-permute-start.1 = (bf16[512,128]{1,0:T(8,128)(2,1)S(1)}, bf16[512,128]{1,0:T(8,128)(2,1)S(1)}, u32[]{:S(2)}, u32[]{:S(2)}) collective-permute-start(bf16[512,128]{1,0:T(8,128)(2,1)S(1)} %get-tuple-element.39.refs_1_), channel_id=1, source_target_pairs={{0,8},{4,12},{8,0},{12,4},{16,24},{20,28},{24,16},{28,20},{1,9},{5... | collective-permute-start | bytes 393224 | tf_op jit(solution)/shard_map/ppermute | solution.py:511
  11.7 3.8 %collective-permute-start.2 = (bf16[48,128]{1,0:T(8,128)(2,1)S(1)}, bf16[48,128]{1,0:T(8,128)(2,1)S(1)}, u32[]{:S(2)}, u32[]{:S(2)}) collective-permute-start(bf16[48,128]{1,0:T(8,128)(2,1)S(1)} %lags.3.refs_2_), channel_id=1, source_target_pairs={{0,8},{4,12},{8,0},{12,4},{16,24},{20,28},{24,16},{28,20},{1,9},{5... | collective-permute-start | bytes 36872 | tf_op jit(solution)/shard_map/ppermute | solution.py:511
  15.8 4.4 %collective-permute-start.3 = (bf16[304,128]{1,0:T(8,128)(2,1)S(1)}, bf16[304,128]{1,0:T(8,128)(2,1)S(1)}, u32[]{:S(2)}, u32[]{:S(2)}) collective-permute-start(bf16[304,128]{1,0:T(8,128)(2,1)S(1)} %get-tuple-element.44), channel_id=1, source_target_pairs={{0,16},{4,20},{8,24},{12,28},{16,0},{20,4},{24,8},{28,12},{1,17},{... | collective-permute-start | bytes 233480 | tf_op jit(solution)/shard_map/ppermute | solution.py:511
  20.5 5.9 %copy-start = (bf16[128,2048]{1,0:T(8,128)(2,1)S(1)}, bf16[128,2048]{1,0:T(8,128)(2,1)}, u32[]{:S(2)}) copy-start(bf16[128,2048]{1,0:T(8,128)(2,1)} %refs_5_.1) | copy-start | bytes 1572868
  20.6 5.8 %copy-start.1 = (bf16[128,2048]{1,0:T(8,128)(2,1)S(1)}, bf16[128,2048]{1,0:T(8,128)(2,1)}, u32[]{:S(2)}) copy-start(bf16[128,2048]{1,0:T(8,128)(2,1)} %refs_6_.1) | copy-start | bytes 1572868
  20.6 5.8 %copy-start.2 = (bf16[128,2048]{1,0:T(8,128)(2,1)S(1)}, bf16[128,2048]{1,0:T(8,128)(2,1)}, u32[]{:S(2)}) copy-start(bf16[128,2048]{1,0:T(8,128)(2,1)} %refs_7_.1) | copy-start | bytes 1572868
  20.6 1.3 %collective-permute-start.4 = (bf16[304,128]{1,0:T(8,128)(2,1)S(1)}, bf16[304,128]{1,0:T(8,128)(2,1)S(1)}, u32[]{:S(2)}, u32[]{:S(2)}) collective-permute-start(bf16[304,128]{1,0:T(8,128)(2,1)S(1)} %get-tuple-element.46.refs_7_.refs_1_), channel_id=1, source_target_pairs={{0,4},{4,0},{8,12},{12,8},{16,20},{20,16},{24,28},{28,24},{1,5},{5... | collective-permute-start | bytes 233480 | tf_op jit(solution)/shard_map/ppermute | solution.py:511
  21.9 7.2 %collective-permute-start.7 = (bf16[48,128]{1,0:T(8,128)(2,1)S(1)}, bf16[48,128]{1,0:T(8,128)(2,1)S(1)}, u32[]{:S(2)}, u32[]{:S(2)}) collective-permute-start(bf16[48,128]{1,0:T(8,128)(2,1)S(1)} %merge.1.refs_0_), channel_id=1, source_target_pairs={{0,3},{1,2},{2,1},{3,0},{4,7},{5,6},{6,5},{7,4},{8,11},{9,10},{10,... | collective-permute-start | bytes 36872 | tf_op jit(solution)/shard_map/ppermute | solution.py:628
  25.6 4.6 %collective-permute-start.6 = (bf16[48,128]{1,0:T(8,128)(2,1)S(1)}, bf16[48,128]{1,0:T(8,128)(2,1)S(1)}, u32[]{:S(2)}, u32[]{:S(2)}) collective-permute-start(bf16[48,128]{1,0:T(8,128)(2,1)S(1)} %merge.1.refs_0_), channel_id=1, source_target_pairs={{0,2},{1,3},{2,0},{3,1},{4,6},{5,7},{6,4},{7,5},{8,10},{9,11},{10,... | collective-permute-start | bytes 36872 | tf_op jit(solution)/shard_map/ppermute | solution.py:628
  25.6 4.6 %collective-permute-start.5 = (bf16[48,128]{1,0:T(8,128)(2,1)S(1)}, bf16[48,128]{1,0:T(8,128)(2,1)S(1)}, u32[]{:S(2)}, u32[]{:S(2)}) collective-permute-start(bf16[48,128]{1,0:T(8,128)(2,1)S(1)} %merge.1.refs_0_), channel_id=1, source_target_pairs={{0,1},{1,0},{2,3},{3,2},{4,5},{5,4},{6,7},{7,6},{8,9},{9,8},{10,11... | collective-permute-start | bytes 36872 | tf_op jit(solution)/shard_map/ppermute | solution.py:628

commit v16 on v13

--- a/solution.py
+++ b/solution.py
@@ -13,6 +13,7 @@
 BF16 = jnp.bfloat16
 EXACT = lax.Precision.HIGHEST
 VMEM_LIMIT = 40 * 1024 * 1024
+GATES_LIMIT = 53400 * 1024
 PARAMS = pltpu.CompilerParams(vmem_limit_bytes=VMEM_LIMIT)
 
 
@@ -82,7 +83,29 @@
     return pl.multiple_of(lax.axis_index("ch") * groups, LANES)
 
 
-def states_kernel(logs_ref, res_ref, gated_ref, dgate_ref, send_ref, keep_ref, turned_ref, rows_ref,
+def gates_kernel(q_any, k_any, v_any, c_any, gated_ref, dgate_ref, turned_ref, q_ref, k_ref, v_ref, c_ref, sems, *, steps):
+    tokens, width = q_ref.shape
+    wide = width // steps
+    sources = ((k_any, k_ref), (v_any, v_ref), (c_any, c_ref), (q_any, q_ref))
+    cuts = [slice(step * wide, (step + 1) * wide) for step in range(steps)]
+    copies = [
+        [pltpu.make_async_copy(far.at[:, cut], near.at[:, cut], sems.at[n, step]) for n, (far, near) in enumerate(sources)]
+        for step, cut in enumerate(cuts)
+    ]
+    for step in copies:
+        for copy in step:
+            copy.start()
+    flip = reversal(tokens)
+    for step, cut in enumerate(cuts):
+        for copy in copies[step]:
+            copy.wait()
+        dgate = gate(c_ref[:, cut], q_ref[:, cut])
+        dgate_ref[:, cut] = dgate
+        gated_ref[:, cut] = gate(k_ref[:, cut], v_ref[:, cut])
+        turned_ref[:, cut] = mxu(flip, dgate).astype(BF16)
+
+
+def states_kernel(logs_ref, res_ref, gated_ref, turned_ref, send_ref, keep_ref, rows_ref, table_ref,
                   *, group, poles, inner):
     tokens, _ = gated_ref.shape
     per_block = LANES // group
@@ -91,12 +114,12 @@
     groups = blocks * per_block
     wide = inner * LANES
     core = lax.rem(lax.axis_index("ctx"), 2)
-
     first = shard_start(groups)
-    rows_ref[0] = jnp.exp(flat_rows(logs_ref[:, pl.ds(first, groups)], poles))
-    rows_ref[1] = flat_rows(res_ref[:, pl.ds(first, groups)], poles)
-
-    flip = reversal(tokens)
+    for n, ref in enumerate((logs_ref, res_ref)):
+        table_ref[n] = ref[:, pl.ds(first, groups)]
+    rows_ref[0] = jnp.exp(flat_rows(table_ref[0], poles))
+    rows_ref[1] = flat_rows(table_ref[1], poles)
+
     back_pos = (tokens - 1 - iota((tokens, LANES), 0)).astype(F32)
     back_lane = (tokens - 1 - iota((1, tokens), 1)).astype(F32)
     wide_group = over(within(iota((poles, 2 * LANES), 1), LANES), group)
@@ -108,9 +131,7 @@
         def body(step, carry, base=base, msg_ref=msg_ref):
             start = base + step * inner
             cut = pl.ds(pl.multiple_of(start * LANES, LANES), wide)
-            gated, dgate = gated_ref[:, cut], dgate_ref[:, cut]
-            turned = mxu(flip, dgate).astype(BF16)
-            turned_ref[:, cut] = turned
+            gated, turned = gated_ref[:, cut], turned_ref[:, cut]
             tables = [jnp.exp(-rows_ref[0, pl.ds(start + j, 1), :] * back_pos).T for j in range(inner)]
             found = []
             for j in range(inner):
@@ -202,13 +223,12 @@
     out_ref[2 * poles :, :] = skip_ref[...].astype(BF16)
 
 
-def tables_kernel(logs_ref, _, rates_ref, lag_rates_ref, *, group, poles, inner):
+def tables_kernel(params_ref, rates_ref, lag_rates_ref, *, group, poles, inner):
     blocks, _, lag_width = lag_rates_ref.shape
     per_block = LANES // group
-    groups = blocks * per_block
     step_groups = inner * per_block
     lag_wide = inner * lag_width
-    pieces = split(logs_ref[:, pl.ds(shard_start(groups), groups)], 3)
+    pieces = split(params_ref[0], 3)
     spread = jnp.concatenate(
         [members(step_groups, 0, SUB, lag_wide), members(step_groups, 0, group, inner * LANES)], axis=1
     )
@@ -221,7 +241,7 @@
             rates_ref[here] = rates[:, lag_wide + j * LANES : lag_wide + (j + 1) * LANES]
 
 
-def conv_kernel(res_ref, rows_ref, skip_ref, rates_ref, lag_rates_ref, gated_ref, turned_ref, _, conv_ref,
+def conv_kernel(params_ref, rows_ref, skip_ref, rates_ref, lag_rates_ref, gated_ref, turned_ref, _, conv_ref,
                 *, first_step, group, poles, inner):
     tokens, _ = gated_ref.shape
     per_block = LANES // group
@@ -235,7 +255,7 @@
     causal = iota((SUB, lag_width), 0) >= within(iota((SUB, lag_width), 1), SUB)
     lag = (SUB - 1 - within(iota((poles, lag_width), 1), SUB)).astype(F32)
     groups = blocks * per_block
-    pieces = split(res_ref[:, pl.ds(shard_start(groups), groups)], 3).astype(F32)
+    pieces = split(params_ref[1], 3).astype(F32)
     spread = members(groups, 0, SUB, inner * lag_width)
 
     def body(step, carry):
@@ -388,12 +408,11 @@
             slim_ref[tail:, :] = rests
 
 
-def merge_kernel(logs_ref, res_ref, own_ref, got_ref, _, out_ref, *, poles, length):
+def merge_kernel(params_ref, own_ref, got_ref, _, out_ref, *, poles, length):
     groups = out_ref.shape[1]
     start = own_ref.shape[0] - out_ref.shape[0]
     both = own_ref[start:, :].astype(F32) + got_ref[start:, :].astype(F32)
-    first = shard_start(groups)
-    factor = -jnp.exp(logs_ref[:, pl.ds(first, groups)]) * res_ref[:, pl.ds(first, groups)]
+    factor = -jnp.exp(params_ref[0]) * params_ref[1]
     scaled = [
         both[:poles] / length,
         factor * both[poles : 2 * poles] / math.sqrt(length),
@@ -489,30 +508,39 @@
     def swap(value, level):
         return lax.ppermute(value, "ctx", [(i, i ^ (1 << level)) for i in range(parts)])
 
-    gated, dgate = gate(key_input, value_input), gate(cotangent, queries)
-    outgoing, message, turned, rows = pl.pallas_call(
+    operand = shape(tokens, width, dtype=BF16)
+    gated, dgate, turned = pl.pallas_call(
+        lambda *refs: gates_kernel(*refs, steps=steps),
+        in_specs=[anywhere] * 4,
+        out_specs=[vmem] * 3,
+        out_shape=[operand] * 3,
+        scratch_shapes=[pltpu.VMEM((tokens, width), BF16)] * 4 + [pltpu.SemaphoreType.DMA((4, steps))],
+        compiler_params=pltpu.CompilerParams(vmem_limit_bytes=GATES_LIMIT),
+        name="gates",
+    )(queries, key_input, value_input, cotangent)
+    outgoing, message, rows, params = pl.pallas_call(
         lambda *refs: states_kernel(*refs, inner=inner, **sizes),
         in_specs=[vmem] * 4,
         out_specs=[vmem] * 4,
         out_shape=[
             shape(2 * half_rows, LANES, dtype=BF16),
             shape(2 * half_rows, LANES, dtype=BF16),
-            shape(tokens, width, dtype=BF16),
             shape(2, blocks, LANES),
+            shape(2, poles, groups),
         ],
         compiler_params=PARAMS,
         name="states",
-    )(log_rates, residues, gated, dgate)
+    )(log_rates, residues, gated, turned)
 
     rates, lag_rates = pl.pallas_call(
         lambda *refs: tables_kernel(*refs, inner=inner, **sizes),
-        in_specs=[vmem, anywhere],
+        in_specs=[vmem],
         out_specs=[vmem] * 2,
         out_shape=[shape(blocks, poles, LANES), shape(blocks, poles, lag_width)],
         compiler_params=PARAMS,
         cost_estimate=pl.CostEstimate(flops=10**9, bytes_accessed=10**6, transcendentals=10**5),
         name="tables",
-    )(log_rates, rows)
+    )(params)
 
     work = pl.CostEstimate(
         flops=16 * tokens * tokens * width, bytes_accessed=12 * tokens * width, transcendentals=tokens * width
@@ -540,7 +568,7 @@
             compiler_params=PARAMS,
             cost_estimate=work,
             name="conv",
-        )(residues, rows, skip_rows, rates, lag_rates, gated, turned, after)
+        )(params, rows, skip_rows, rates, lag_rates, gated, turned, after)
 
     def combine(level, operands, outs):
         return pl.pallas_call(
@@ -590,12 +618,12 @@
     last_conv = convolve(steps - 1, 1, outgoing)
     merged = pl.pallas_call(
         lambda *refs: merge_kernel(*refs, poles=poles, length=tokens * parts),
-        in_specs=[vmem] * 4 + [anywhere],
+        in_specs=[vmem] * 3 + [anywhere],
         out_specs=vmem,
         out_shape=shape(tail, LANES, dtype=BF16),
         compiler_params=PARAMS,
         name="merge",
-    )(log_rates, residues, outgoing, got, last_conv)
+    )(params, outgoing, got, last_conv)
 
     gathered = [merged]
     for mask in range(1, shards):

time: 30.8 us -> 30.6 us (level)
  other arithmetic: 1.99 us -> 0 us
  Pallas kernels: 13.1 us -> 14.9 us
    pallas_call x0 -> x1, Pallas kernels: none -> 2.2 us  [local(): pl.pallas_call(lambda *refs: gates_kernel(*refs, steps=steps), in_specs=[...]
    convert_element_type x1 -> x0, other arithmetic: 1.99 us -> none  [gate(): return (left.astype(F32) * right.astype(F32)).astype(BF16)]
    pallas_call x1, Pallas kernels: 2.16 us -> 1.78 us  [local(): pl.pallas_call(lambda *refs: states_kernel(*refs, inner=inner, **sizes),...]
where the time goes in v16:
time: 30.6 us; the launch traced here: 30.5 us
  Pallas kernels  14.9 us (49%)
  starting transfers between devices  9.5 us (31%)
  waiting for transfers between devices  5.23 us (17%)
  between operations  0.81 us (3%)
    ppermute x5, starting transfers between devices, swap(): lax.ppermute(value, 'ctx', [(i, i ^ 1 << level) for i in range(parts)])  5.04 us
    ppermute x3, starting transfers between devices, local(): lax.ppermute(merged, 'ch', [(i, i ^ mask) for i in range(shards)])  4.45 us
    ppermute x5, waiting for transfers between devices, swap(): lax.ppermute(value, 'ctx', [(i, i ^ 1 << level) for i in range(parts)])  4.17 us
    pallas_call x2, Pallas kernels, convolve(): pl.pallas_call(lambda *refs: conv_kernel(*refs, first_step=first_step, in...  3.64 us
    pallas_call x1, Pallas kernels, local(): pl.pallas_call(lambda *refs: output_kernel(*refs, **sizes), grid=(steps,)...  2.74 us
    pallas_call x2, Pallas kernels, local_sums(): pl.pallas_call(lambda *refs: lags_kernel(*refs, second=second, inner=inne...  2.71 us
    pallas_call x1, Pallas kernels, local(): pl.pallas_call(lambda *refs: gates_kernel(*refs, steps=steps), in_specs=[...  2.2 us
    pallas_call x1, Pallas kernels, local(): pl.pallas_call(lambda *refs: states_kernel(*refs, inner=inner, **sizes),...  1.78 us
  transfers between devices with their start and end apart: 8, of which 4 were waited for; matrix products, arithmetic and copies ran while one was open for 0% of the time, Pallas kernels for 31%

profile of v16, /device:TPU:0, one launch (start us, length us, event | category | flops | bytes accessed | tf_op | source)
XLA Modules:
  0.0 30.5 jit_solution(4038227018684581005)
XLA Ops:
  0.6 0.0 copy-start.4
  0.6 0.0 copy-start.5
  0.7 2.2 %gates.1 = (bf16[128,2048]{1,0:T(8,128)(2,1)S(1)}, bf16[128,2048]{1,0:T(8,128)(2,1)S(1)}, bf16[128,2048]{1,0:T(8,128)(2,1)S(1)}) custom-call(bf16[128,2048]{1,0:T(8,128)(2,1)} %refs_0_.1, bf16[128,2048]{1,0:T(8,128)(2,1)} %refs_5_.1, bf16[128,2048]{1,0:T(8,128)(2,1)} %refs_6_.1, bf16[128,2048]{1,0:T(8,128)(2,1)} %refs_7_.1), custom_call_target="tpu_custom_call" | custom-call | tf_op jit(solution)/shard_map/gates/pallas_call | solution.py:512
  2.9 0.0 copy-done.4
  2.9 0.0 copy-done.5
  2.9 1.8 %states.1 = (bf16[512,128]{1,0:T(8,128)(2,1)S(1)}, bf16[512,128]{1,0:T(8,128)(2,1)S(1)}, f32[2,16,128]{2,1,0:T(8,128)S(1)}, f32[2,16,128]{2,1,0:T(8,128)S(1)}) custom-call(f32[16,512]{1,0:T(8,128)S(1)} %bitcast.8, f32[16,512]{1,0:T(8,128)S(1)} %bitcast.9, bf16[128,2048]{1,0:T(8,128)(2,1)S(1)} %get-tuple-element.30.refs_2_.refs_1_.refs_5_, ...), custom_call_target="tpu_custom_call" | custom-call | tf_op jit(solution)/shard_map/states/pallas_call | solution.py:521
  4.7 0.5 %collective-permute-start = (bf16[512,128]{1,0:T(8,128)(2,1)S(1)}, bf16[512,128]{1,0:T(8,128)(2,1)S(1)}, u32[]{:S(2)}, u32[]{:S(2)}) collective-permute-start(bf16[512,128]{1,0:T(8,128)(2,1)S(1)} %get-tuple-element.37), channel_id=1, source_target_pairs={{0,4},{4,0},{8,12},{12,8},{16,20},{20,16},{24,28},{28,24},{1,5},{5... | collective-permute-start | bytes 393224 | tf_op jit(solution)/shard_map/ppermute | solution.py:509
  5.2 0.4 %tables.1 = (f32[16,16,128]{2,1,0:T(8,128)S(1)}, f32[16,16,256]{2,1,0:T(8,128)S(1)}) custom-call(f32[2,16,128]{2,1,0:T(8,128)S(1)} %get-tuple-element.33.refs_0_), custom_call_target="tpu_custom_call" | custom-call | flops 1000000000 | bytes 1000000 | tf_op jit(solution)/shard_map/tables/pallas_call | solution.py:535
  5.5 0.7 %lags.2.refs_3_ = f32[32,128]{1,0:T(8,128)S(1)} custom-call(f32[16,16,256]{2,1,0:T(8,128)S(1)} %get-tuple-element.35.refs_0_.refs_4_, bf16[128,2048]{1,0:T(8,128)(2,1)S(1)} %get-tuple-element.30.refs_2_.refs_1_.refs_5_, bf16[128,2048]{1,0:T(8,128)(2,1)S(1)} %get-tuple-element.38.refs_2_, bf16[128,2048]{1,0:T(8,128)(2,1)S(1)} %get-tuple-element.31.refs_3_.refs_6_), custom_call_target="tpu_custom_call" | custom-call | flops 536870912 | bytes 3145728 | tf_op jit(solution)/shard_map/lags/pallas_call | solution.py:550
  6.2 0.0 copy-start.3
  6.3 0.0 collective-permute-done.refs_2_
  6.3 0.3 combine.3
  6.5 2.8 %collective-permute-start.1 = (bf16[512,128]{1,0:T(8,128)(2,1)S(1)}, bf16[512,128]{1,0:T(8,128)(2,1)S(1)}, u32[]{:S(2)}, u32[]{:S(2)}) collective-permute-start(bf16[512,128]{1,0:T(8,128)(2,1)S(1)} %get-tuple-element.39.refs_1_), channel_id=1, source_target_pairs={{0,8},{4,12},{8,0},{12,4},{16,24},{20,28},{24,16},{28,20},{1,9},{5... | collective-permute-start | bytes 393224 | tf_op jit(solution)/shard_map/ppermute | solution.py:509
  9.4 2.0 %lags.3.refs_2_ = bf16[48,128]{1,0:T(8,128)(2,1)S(1)} custom-call(f32[16,16,256]{2,1,0:T(8,128)S(1)} %get-tuple-element.35.refs_0_.refs_4_, bf16[128,2048]{1,0:T(8,128)(2,1)S(1)} %get-tuple-element.30.refs_2_.refs_1_.refs_5_, bf16[128,2048]{1,0:T(8,128)(2,1)S(1)} %get-tuple-element.38.refs_2_, bf16[128,2048]{1,0:T(8,128)(2,1)S(1)} %get-tuple-element.31.refs_3_.refs_6_, ...), custom_call_target="tpu_custom_call" | custom-call | flops 536870912 | bytes 3145728 | tf_op jit(solution)/shard_map/lags/pallas_call | solution.py:550
  11.4 0.1 collective-permute-start.2
  11.5 3.7 %collective-permute-done.2.refs_4_ = bf16[48,128]{1,0:T(8,128)(2,1)S(1)} collective-permute-done((bf16[48,128]{1,0:T(8,128)(2,1)S(1)}, bf16[48,128]{1,0:T(8,128)(2,1)S(1)}, u32[]{:S(2)}, u32[]{:S(2)}) %collective-permute-start.2) | collective-permute-done | bytes 12320 | tf_op jit(solution)/shard_map/ppermute | solution.py:509
  15.1 0.0 collective-permute-done.1.refs_3_
  15.1 0.3 combine.4
  15.4 1.6 %collective-permute-start.3 = (bf16[304,128]{1,0:T(8,128)(2,1)S(1)}, bf16[304,128]{1,0:T(8,128)(2,1)S(1)}, u32[]{:S(2)}, u32[]{:S(2)}) collective-permute-start(bf16[304,128]{1,0:T(8,128)(2,1)S(1)} %get-tuple-element.44), channel_id=1, source_target_pairs={{0,16},{4,20},{8,24},{12,28},{16,0},{20,4},{24,8},{28,12},{1,17},{... | collective-permute-start | bytes 233480 | tf_op jit(solution)/shard_map/ppermute | solution.py:509
  17.0 0.0 copy-done.3
  17.0 2.7 %conv.2.refs_5_.refs_1_ = f32[128,3072]{1,0:T(8,128)S(1)} custom-call(f32[2,16,128]{2,1,0:T(8,128)S(1)} %get-tuple-element.33.refs_0_, f32[2,16,128]{2,1,0:T(8,128)S(1)} %get-tuple-element.32.refs_1_.refs_0_, f32[64,128]{1,0:T(8,128)S(1)} %bitcast.6, f32[16,16,128]{2,1,0:T(8,128)S(1)} %get-tuple-element.34.refs_0_.refs_3_, ...), custom_call_target="tpu_custom_call" | custom-call | flops 536870912 | bytes 3145728 | tf_op jit(solution)/shard_map/conv/pallas_call | solution.py:563
  19.7 0.1 collective-permute-done.3.refs_3_
  19.9 0.3 combine.5
  20.1 0.0 copy-start
  20.2 0.0 copy-start.1
  20.2 0.0 copy-start.2
  20.2 0.1 collective-permute-start.4
  20.3 0.9 %conv.3.refs_2_.refs_3_ = f32[128,1024]{1,0:T(8,128)S(1)} custom-call(f32[2,16,128]{2,1,0:T(8,128)S(1)} %get-tuple-element.33.refs_0_, f32[2,16,128]{2,1,0:T(8,128)S(1)} %get-tuple-element.32.refs_1_.refs_0_, f32[64,128]{1,0:T(8,128)S(1)} %bitcast.7, f32[16,16,128]{2,1,0:T(8,128)S(1)} %get-tuple-element.34.refs_0_.refs_3_, ...), custom_call_target="tpu_custom_call" | custom-call | flops 536870912 | bytes 3145728 | tf_op jit(solution)/shard_map/conv/pallas_call | solution.py:563
  21.2 0.3 %collective-permute-done.4.refs_4_.refs_2_ = bf16[304,128]{1,0:T(8,128)(2,1)S(1)} collective-permute-done((bf16[304,128]{1,0:T(8,128)(2,1)S(1)}, bf16[304,128]{1,0:T(8,128)(2,1)S(1)}, u32[]{:S(2)}, u32[]{:S(2)}) %collective-permute-start.4) | collective-permute-done | bytes 77856 | tf_op jit(solution)/shard_map/ppermute | solution.py:509
  21.6 3.7 %collective-permute-start.7 = (bf16[48,128]{1,0:T(8,128)(2,1)S(1)}, bf16[48,128]{1,0:T(8,128)(2,1)S(1)}, u32[]{:S(2)}, u32[]{:S(2)}) collective-permute-start(bf16[48,128]{1,0:T(8,128)(2,1)S(1)} %merge.1.refs_0_), channel_id=1, source_target_pairs={{0,3},{1,2},{2,1},{3,0},{4,7},{5,6},{6,5},{7,4},{8,11},{9,10},{10,... | collective-permute-start | bytes 36872 | tf_op jit(solution)/shard_map/ppermute | solution.py:630
  25.2 0.0 collective-permute-start.6
  25.3 0.8 %collective-permute-start.5 = (bf16[48,128]{1,0:T(8,128)(2,1)S(1)}, bf16[48,128]{1,0:T(8,128)(2,1)S(1)}, u32[]{:S(2)}, u32[]{:S(2)}) collective-permute-start(bf16[48,128]{1,0:T(8,128)(2,1)S(1)} %merge.1.refs_0_), channel_id=1, source_target_pairs={{0,1},{1,0},{2,3},{3,2},{4,5},{5,4},{6,7},{7,6},{8,9},{9,8},{10,11... | collective-permute-start | bytes 36872 | tf_op jit(solution)/shard_map/ppermute | solution.py:630
  26.0 0.0 copy-done
  26.0 0.0 copy-done.1
  26.0 0.0 copy-done.2
  26.0 2.7 %outputs.1 = (bf16[128,2048]{1,0:T(8,128)(2,1)}, bf16[128,2048]{1,0:T(8,128)(2,1)}, bf16[128,2048]{1,0:T(8,128)(2,1)}) custom-call(f32[2,16,128]{2,1,0:T(8,128)S(1)} %get-tuple-element.32.refs_1_.refs_0_, f32[128,3072]{1,0:T(8,128)S(1)} %conv.2.refs_5_.refs_1_, f32[128,1024]{1,0:T(8,128)S(1)} %conv.3.refs_2_.refs_3_, ...), custom_call_target="tpu_custom_call" | custom-call | flops 536870912 | bytes 3145728 | tf_op jit(solution)/shard_map/outputs/pallas_call | solution.py:633
  28.8 0.0 collective-permute-done.7.refs_3_
  28.8 1.1 %collective-permute-done.6.refs_2_ = bf16[48,128]{1,0:T(8,128)(2,1)S(1)} collective-permute-done((bf16[48,128]{1,0:T(8,128)(2,1)S(1)}, bf16[48,128]{1,0:T(8,128)(2,1)S(1)}, u32[]{:S(2)}, u32[]{:S(2)}) %collective-permute-start.6) | collective-permute-done | bytes 12320 | tf_op jit(solution)/shard_map/ppermute | solution.py:630
  29.8 0.0 collective-permute-done.5.refs_1_
  29.8 0.6 %assemble.1 = (f32[16,512]{1,0:T(8,128)}, f32[16,512]{1,0:T(8,128)}, f32[64,128]{1,0:T(8,128)}) custom-call(bf16[48,128]{1,0:T(8,128)(2,1)S(1)} %merge.1.refs_0_, bf16[48,128]{1,0:T(8,128)(2,1)S(1)} %collective-permute-done.5.refs_1_, bf16[48,128]{1,0:T(8,128)(2,1)S(1)} %collective-permute-done.6.refs_2_, bf16[48,128]{1,0:T(8,128)(2,1)S(1)} %collective-permute-done.7.refs_3_), custom_call_target="tpu_custom_call" | custom-call | tf_op jit(solution)/shard_map/assemble/pallas_call | solution.py:644
  (1 shorter events, 0.0 us)
Async XLA Ops:
  0.6 2.2 %copy-start.4 = (f32[512,16]{0,1:T(8,128)S(1)}, f32[512,16]{0,1:T(8,128)}, u32[]{:S(2)}) copy-start(f32[512,16]{0,1:T(8,128)} %param.12) | copy-start | bytes 98308
  0.6 2.2 %copy-start.5 = (f32[512,16]{0,1:T(8,128)S(1)}, f32[512,16]{0,1:T(8,128)}, u32[]{:S(2)}) copy-start(f32[512,16]{0,1:T(8,128)} %param.11) | copy-start | bytes 98308
  4.7 1.6 %collective-permute-start = (bf16[512,128]{1,0:T(8,128)(2,1)S(1)}, bf16[512,128]{1,0:T(8,128)(2,1)S(1)}, u32[]{:S(2)}, u32[]{:S(2)}) collective-permute-start(bf16[512,128]{1,0:T(8,128)(2,1)S(1)} %get-tuple-element.37), channel_id=1, source_target_pairs={{0,4},{4,0},{8,12},{12,8},{16,20},{20,16},{24,28},{28,24},{1,5},{5... | collective-permute-start | bytes 393224 | tf_op jit(solution)/shard_map/ppermute | solution.py:509
  6.2 10.8 %copy-start.3 = (f32[8192]{0:T(1024)S(1)}, f32[8192]{0:T(1024)}, u32[]{:S(2)}) copy-start(f32[8192]{0:T(1024)} %param.13) | copy-start | bytes 98308
  6.5 8.6 %collective-permute-start.1 = (bf16[512,128]{1,0:T(8,128)(2,1)S(1)}, bf16[512,128]{1,0:T(8,128)(2,1)S(1)}, u32[]{:S(2)}, u32[]{:S(2)}) collective-permute-start(bf16[512,128]{1,0:T(8,128)(2,1)S(1)} %get-tuple-element.39.refs_1_), channel_id=1, source_target_pairs={{0,8},{4,12},{8,0},{12,4},{16,24},{20,28},{24,16},{28,20},{1,9},{5... | collective-permute-start | bytes 393224 | tf_op jit(solution)/shard_map/ppermute | solution.py:509
  11.4 3.8 %collective-permute-start.2 = (bf16[48,128]{1,0:T(8,128)(2,1)S(1)}, bf16[48,128]{1,0:T(8,128)(2,1)S(1)}, u32[]{:S(2)}, u32[]{:S(2)}) collective-permute-start(bf16[48,128]{1,0:T(8,128)(2,1)S(1)} %lags.3.refs_2_), channel_id=1, source_target_pairs={{0,8},{4,12},{8,0},{12,4},{16,24},{20,28},{24,16},{28,20},{1,9},{5... | collective-permute-start | bytes 36872 | tf_op jit(solution)/shard_map/ppermute | solution.py:509
  15.4 4.4 %collective-permute-start.3 = (bf16[304,128]{1,0:T(8,128)(2,1)S(1)}, bf16[304,128]{1,0:T(8,128)(2,1)S(1)}, u32[]{:S(2)}, u32[]{:S(2)}) collective-permute-start(bf16[304,128]{1,0:T(8,128)(2,1)S(1)} %get-tuple-element.44), channel_id=1, source_target_pairs={{0,16},{4,20},{8,24},{12,28},{16,0},{20,4},{24,8},{28,12},{1,17},{... | collective-permute-start | bytes 233480 | tf_op jit(solution)/shard_map/ppermute | solution.py:509
  20.1 5.9 %copy-start = (bf16[128,2048]{1,0:T(8,128)(2,1)S(1)}, bf16[128,2048]{1,0:T(8,128)(2,1)}, u32[]{:S(2)}) copy-start(bf16[128,2048]{1,0:T(8,128)(2,1)} %refs_5_.1) | copy-start | bytes 1572868
  20.2 5.8 %copy-start.1 = (bf16[128,2048]{1,0:T(8,128)(2,1)S(1)}, bf16[128,2048]{1,0:T(8,128)(2,1)}, u32[]{:S(2)}) copy-start(bf16[128,2048]{1,0:T(8,128)(2,1)} %refs_6_.1) | copy-start | bytes 1572868
  20.2 5.8 %copy-start.2 = (bf16[128,2048]{1,0:T(8,128)(2,1)S(1)}, bf16[128,2048]{1,0:T(8,128)(2,1)}, u32[]{:S(2)}) copy-start(bf16[128,2048]{1,0:T(8,128)(2,1)} %refs_7_.1) | copy-start | bytes 1572868
  20.2 1.3 %collective-permute-start.4 = (bf16[304,128]{1,0:T(8,128)(2,1)S(1)}, bf16[304,128]{1,0:T(8,128)(2,1)S(1)}, u32[]{:S(2)}, u32[]{:S(2)}) collective-permute-start(bf16[304,128]{1,0:T(8,128)(2,1)S(1)} %get-tuple-element.46.refs_7_.refs_1_), channel_id=1, source_target_pairs={{0,4},{4,0},{8,12},{12,8},{16,20},{20,16},{24,28},{28,24},{1,5},{5... | collective-permute-start | bytes 233480 | tf_op jit(solution)/shard_map/ppermute | solution.py:509
  21.6 7.2 %collective-permute-start.7 = (bf16[48,128]{1,0:T(8,128)(2,1)S(1)}, bf16[48,128]{1,0:T(8,128)(2,1)S(1)}, u32[]{:S(2)}, u32[]{:S(2)}) collective-permute-start(bf16[48,128]{1,0:T(8,128)(2,1)S(1)} %merge.1.refs_0_), channel_id=1, source_target_pairs={{0,3},{1,2},{2,1},{3,0},{4,7},{5,6},{6,5},{7,4},{8,11},{9,10},{10,... | collective-permute-start | bytes 36872 | tf_op jit(solution)/shard_map/ppermute | solution.py:630
  25.2 4.6 %collective-permute-start.6 = (bf16[48,128]{1,0:T(8,128)(2,1)S(1)}, bf16[48,128]{1,0:T(8,128)(2,1)S(1)}, u32[]{:S(2)}, u32[]{:S(2)}) collective-permute-start(bf16[48,128]{1,0:T(8,128)(2,1)S(1)} %merge.1.refs_0_), channel_id=1, source_target_pairs={{0,2},{1,3},{2,0},{3,1},{4,6},{5,7},{6,4},{7,5},{8,10},{9,11},{10,... | collective-permute-start | bytes 36872 | tf_op jit(solution)/shard_map/ppermute | solution.py:630
  25.3 4.6 %collective-permute-start.5 = (bf16[48,128]{1,0:T(8,128)(2,1)S(1)}, bf16[48,128]{1,0:T(8,128)(2,1)S(1)}, u32[]{:S(2)}, u32[]{:S(2)}) collective-permute-start(bf16[48,128]{1,0:T(8,128)(2,1)S(1)} %merge.1.refs_0_), channel_id=1, source_target_pairs={{0,1},{1,0},{2,3},{3,2},{4,5},{5,4},{6,7},{7,6},{8,9},{9,8},{10,11... | collective-permute-start | bytes 36872 | tf_op jit(solution)/shard_map/ppermute | solution.py:630

commit v17 on v16

--- a/solution.py
+++ b/solution.py
@@ -13,7 +13,7 @@
 BF16 = jnp.bfloat16
 EXACT = lax.Precision.HIGHEST
 VMEM_LIMIT = 40 * 1024 * 1024
-GATES_LIMIT = 53400 * 1024
+GATES_LIMIT = 53900 * 1024
 PARAMS = pltpu.CompilerParams(vmem_limit_bytes=VMEM_LIMIT)
 
 
@@ -83,7 +83,38 @@
     return pl.multiple_of(lax.axis_index("ch") * groups, LANES)
 
 
-def gates_kernel(q_any, k_any, v_any, c_any, gated_ref, dgate_ref, turned_ref, q_ref, k_ref, v_ref, c_ref, sems, *, steps):
+def diagonals(gated, turned, group):
+    tokens = gated.shape[0]
+    per_block = LANES // group
+    lag_width = per_block * SUB
+    subs = tokens // SUB
+    lane_group = over(iota((SUB, LANES), 1), group)
+    row, lane = iota((SUB, lag_width), 0), within(iota((SUB, lag_width), 1), SUB)
+    near_side, no_wrap = row + lane <= SUB - 1, lane >= row
+    found = [None] * subs + [jnp.zeros((SUB, lag_width), F32)]
+    for k in range(subs):
+        part = gated[k * SUB : (k + 1) * SUB]
+        stack = jnp.concatenate(
+            [jnp.where(lane_group == g, part, jnp.zeros_like(part)) for g in range(per_block)], axis=0
+        )
+        outer = mxu_t(turned[: (subs - k) * SUB], stack)
+        for n in range(subs - k):
+            far = subs - 1 - k - n
+            piece = outer[n * SUB : (n + 1) * SUB]
+            found[far] = piece if found[far] is None else found[far] + piece
+
+    def rows():
+        for far in range(subs):
+            total = jnp.where(near_side, found[far], found[far + 1])
+            straight = pltpu.roll(total, 0, 1, stride=1, stride_axis=0)
+            wrapped = pltpu.roll(total, lag_width - SUB, 1, stride=1, stride_axis=0)
+            yield jnp.sum(jnp.where(no_wrap, straight, wrapped), axis=0, keepdims=True)
+
+    return rows
+
+
+def gates_kernel(q_any, k_any, v_any, c_any, gated_ref, turned_ref, lags_ref, skip_ref, q_ref, k_ref, v_ref, c_ref, sems,
+                 *, steps, group):
     tokens, width = q_ref.shape
     wide = width // steps
     sources = ((k_any, k_ref), (v_any, v_ref), (c_any, c_ref), (q_any, q_ref))
@@ -99,10 +130,18 @@
     for step, cut in enumerate(cuts):
         for copy in copies[step]:
             copy.wait()
-        dgate = gate(c_ref[:, cut], q_ref[:, cut])
-        dgate_ref[:, cut] = dgate
-        gated_ref[:, cut] = gate(k_ref[:, cut], v_ref[:, cut])
-        turned_ref[:, cut] = mxu(flip, dgate).astype(BF16)
+        gated, dgate = gate(k_ref[:, cut], v_ref[:, cut]), gate(c_ref[:, cut], q_ref[:, cut])
+        gated_ref[:, cut] = gated
+        turned = mxu(flip, dgate).astype(BF16)
+        turned_ref[:, cut] = turned
+        skip = jnp.sum(gated.astype(F32) * dgate.astype(F32), axis=0, keepdims=True)
+        lanes = [slice(j * LANES, (j + 1) * LANES) for j in range(wide // LANES)]
+        found = [diagonals(gated[:, here], turned[:, here], group) for here in lanes]
+        for j, here in enumerate(lanes):
+            block = step * len(lanes) + j
+            skip_ref[block : block + 1, :] = skip[:, here]
+            for far, row in enumerate(found[j]()):
+                lags_ref[block, far : far + 1, :] = row
 
 
 def states_kernel(logs_ref, res_ref, gated_ref, turned_ref, send_ref, keep_ref, rows_ref, table_ref,
@@ -154,73 +193,30 @@
         lax.fori_loop(0, half_blocks // inner, body, 0)
 
 
-def lags_kernel(lag_rates_ref, gated_ref, dgate_ref, turned_ref, *rest, second, group, poles, inner):
-    if second:
-        first_ref, out_ref, skip_ref = rest
-    else:
-        (out_ref,) = rest
-    tokens, _ = gated_ref.shape
+def lags_kernel(lag_rates_ref, lags_ref, sums_ref, *, group, poles, inner):
+    blocks, subs, lag_width = lags_ref.shape
     per_block = LANES // group
-    blocks, _, lag_width = lag_rates_ref.shape
-    subs = tokens // SUB
-    step_groups = inner * per_block
-    lane_group = over(iota((SUB, LANES), 1), group)
-    row, lane = iota((SUB, lag_width), 0), within(iota((SUB, lag_width), 1), SUB)
-    near_side, no_wrap = row + lane <= SUB - 1, lane >= row
     lag = (SUB - 1 - within(iota((poles, lag_width), 1), SUB)).astype(F32)
-    spread = members(step_groups, 0, SUB, inner * lag_width)
-    steps = blocks // inner
+    spread = members(inner * per_block, 0, SUB, inner * lag_width)
     sums = []
-    for step in range(1, steps) if second else range(1):
-        outers = []
-        for j in range(inner):
-            lanes = slice((step * inner + j) * LANES, (step * inner + j + 1) * LANES)
-            found = [None] * subs
-            for k in range(subs):
-                part = gated_ref[k * SUB : (k + 1) * SUB, lanes]
-                stack = jnp.concatenate(
-                    [jnp.where(lane_group == g, part, jnp.zeros_like(part)) for g in range(per_block)], axis=0
-                )
-                outer = mxu_t(turned_ref[: (subs - k) * SUB, lanes], stack)
-                for n in range(subs - k):
-                    far = subs - 1 - k - n
-                    piece = outer[n * SUB : (n + 1) * SUB]
-                    found[far] = piece if found[far] is None else found[far] + piece
-            outers.append(found)
+    for step in range(blocks // inner):
         terms = []
         for j in range(inner):
-            found = outers[j] + [jnp.zeros((SUB, lag_width), F32)]
-            lags = []
-            for far in range(subs):
-                total = jnp.where(near_side, found[far], found[far + 1])
-                straight = pltpu.roll(total, 0, 1, stride=1, stride_axis=0)
-                wrapped = pltpu.roll(total, lag_width - SUB, 1, stride=1, stride_axis=0)
-                lags.append(jnp.sum(jnp.where(no_wrap, straight, wrapped), axis=0, keepdims=True))
-            rate = lag_rates_ref[step * inner + j]
+            block = step * inner + j
+            rate = lag_rates_ref[block]
             decay = jnp.exp(-rate * SUB)
             total = jnp.zeros((poles, lag_width), F32)
             weighted = total
             for far in reversed(range(subs)):
-                weighted = decay * weighted + far * lags[far]
-                total = decay * total + lags[far]
+                row = lags_ref[block, far : far + 1, :]
+                weighted = decay * weighted + far * row
+                total = decay * total + row
             table = jnp.exp(-rate * lag)
             terms.append(
                 split(jnp.concatenate([table * total, table * (lag * total + SUB * weighted)], axis=0), 2)
             )
         sums.append(mxu_t(jnp.concatenate(terms, axis=1), spread))
-    sums = jnp.concatenate(sums, axis=1)
-    zeros = jnp.zeros((sums.shape[0], blocks * per_block - sums.shape[1]), F32)
-    sums = jnp.concatenate([zeros, sums] if second else [sums, zeros], axis=1)
-    sums = join(sums, 2 * poles)
-    if not second:
-        out_ref[...] = sums
-        return
-    for b in range(blocks):
-        lanes = slice(b * LANES, (b + 1) * LANES)
-        product = gated_ref[:, lanes].astype(F32) * dgate_ref[:, lanes].astype(F32)
-        skip_ref[b : b + 1, :] = jnp.sum(product, axis=0, keepdims=True)
-    out_ref[: 2 * poles, :] = (first_ref[...] + sums).astype(BF16)
-    out_ref[2 * poles :, :] = skip_ref[...].astype(BF16)
+    sums_ref[...] = join(jnp.concatenate(sums, axis=1), 2 * poles)
 
 
 def tables_kernel(params_ref, rates_ref, lag_rates_ref, *, group, poles, inner):
@@ -315,18 +311,17 @@
     groups = all_blocks * per_block
     rows = 2 * poles
     if level == 0:
-        own_ref, got_ref, sums_ref, states_ref, total_ref, near_ref = refs
+        own_ref, got_ref, sums_ref, skip_ref, states_ref, near_ref = refs
     else:
-        own_ref, own_tail_ref, got_ref = refs.pop(0), refs.pop(0), refs.pop(0)
-        got_tail_ref = None if last else refs.pop(0)
+        own_ref, got_ref = refs.pop(0), refs.pop(0)
         held_ref = refs.pop(0) if level > 1 else None
-        if level == min(2, levels - 1):
+        if level == 1:
             refs.pop(0)
         if last:
             near_ref, mine_ref, out_ref = refs
         else:
-            states_ref, tail_ref, new_held_ref = refs[:3]
-            slim_ref = refs[3] if level == levels - 2 else None
+            states_ref, new_held_ref = refs[:2]
+            slim_ref = refs[2] if level == levels - 2 else None
     me = lax.axis_index("ctx")
     core = lax.rem(me, 2)
     is_right = lax.rem(lax.shift_right_logical(me, level), 2) == 1
@@ -395,17 +390,17 @@
     cross = jnp.where(core > 0, pltpu.roll(cross, groups // 2, 1), cross)
     tail = blocks * rows
     if level == 0:
-        total_ref[...] = cross + sums_ref[...]
-        return
-    got_tail = got_ref[tail:, :] if last else got_tail_ref[...]
-    both = own_tail_ref[...].astype(F32) + got_tail.astype(F32)
-    rests = jnp.concatenate([both[:rows] + cross, both[rows:]], axis=0).astype(BF16)
+        rests = jnp.concatenate([cross + sums_ref[...], skip_ref[...]], axis=0).astype(BF16)
+    else:
+        got_start = tail if last else 2 * tail
+        both = own_ref[2 * tail :, :].astype(F32) + got_ref[got_start:, :].astype(F32)
+        rests = jnp.concatenate([both[:rows] + cross, both[rows:]], axis=0).astype(BF16)
     if last:
         out_ref[tail:, :] = rests
-    else:
-        tail_ref[...] = rests
-        if slim_ref is not None:
-            slim_ref[tail:, :] = rests
+        return
+    states_ref[2 * tail :, :] = rests
+    if level and slim_ref is not None:
+        slim_ref[tail:, :] = rests
 
 
 def merge_kernel(params_ref, own_ref, got_ref, _, out_ref, *, poles, length):
@@ -509,11 +504,11 @@
         return lax.ppermute(value, "ctx", [(i, i ^ (1 << level)) for i in range(parts)])
 
     operand = shape(tokens, width, dtype=BF16)
-    gated, dgate, turned = pl.pallas_call(
-        lambda *refs: gates_kernel(*refs, steps=steps),
+    gated, turned, lags, skips = pl.pallas_call(
+        lambda *refs: gates_kernel(*refs, steps=steps, group=group),
         in_specs=[anywhere] * 4,
-        out_specs=[vmem] * 3,
-        out_shape=[operand] * 3,
+        out_specs=[vmem] * 4,
+        out_shape=[operand, operand, shape(blocks, tokens // SUB, lag_width), shape(blocks, LANES)],
         scratch_shapes=[pltpu.VMEM((tokens, width), BF16)] * 4 + [pltpu.SemaphoreType.DMA((4, steps))],
         compiler_params=pltpu.CompilerParams(vmem_limit_bytes=GATES_LIMIT),
         name="gates",
@@ -546,17 +541,15 @@
         flops=16 * tokens * tokens * width, bytes_accessed=12 * tokens * width, transcendentals=tokens * width
     )
 
-    def local_sums(second, *more):
-        return pl.pallas_call(
-            lambda *refs: lags_kernel(*refs, second=second, inner=inner, **sizes),
-            in_specs=[vmem] * (4 + len(more)),
-            out_specs=vmem,
-            out_shape=shape(tail, LANES, dtype=BF16) if second else shape(2 * poles, LANES),
-            scratch_shapes=[pltpu.VMEM((blocks, LANES), F32)] if second else [],
-            compiler_params=PARAMS,
-            cost_estimate=work,
-            name="lags",
-        )(lag_rates, gated, dgate, turned, *more)
+    sums = pl.pallas_call(
+        lambda *refs: lags_kernel(*refs, inner=inner, **sizes),
+        in_specs=[vmem] * 2,
+        out_specs=vmem,
+        out_shape=shape(2 * poles, LANES),
+        compiler_params=PARAMS,
+        cost_estimate=work,
+        name="lags",
+    )(lag_rates, lags)
 
     def convolve(first_step, count, after):
         skip_rows = skip_gain.reshape(-1, LANES)
@@ -581,39 +574,29 @@
         )(*operands)
 
     conv = None
-    states_shape = shape(2 * half_rows, LANES, dtype=BF16)
-    tail_shape = shape(tail, LANES, dtype=BF16)
+    states_shape = shape(2 * half_rows + tail, LANES, dtype=BF16)
     slim_shape = shape(half_rows + tail, LANES, dtype=BF16)
     held_shape = shape(half_blocks, 2 * poles, LANES)
     got = swap(outgoing, 0)
-    states, total, near = combine(
-        0, [rates, message, got, local_sums(0)], [states_shape, shape(2 * poles, LANES), held_shape]
-    )
-    held = slim = None
+    states, near = combine(0, [rates, message, got, sums, skips], [states_shape, held_shape])
+    held, outgoing = None, states
     for level in range(1, levels):
         last = level == levels - 1
-        if last and slim is not None:
-            received = [swap(slim, level)]
-        else:
-            received = [swap(states, level)]
-            if level == 1:
-                carried = local_sums(1, total)
-            received.append(swap(carried, level))
-        operands = [rates, states, carried, *received]
+        operands = [rates, states, swap(outgoing, level)]
         if level > 1:
             operands.append(held)
-        if level == min(2, levels - 1):
-            conv = convolve(0, steps - 1, near if held is None else held)
+        else:
+            conv = convolve(0, steps - 1, near)
             operands.append(conv)
         if last:
             outs = [shape(half_blocks, 2 * poles, LANES, dtype=BF16), slim_shape]
             mine, outgoing = combine(level, [*operands, near], outs)
         else:
-            outs = [states_shape, tail_shape, held_shape]
+            outs = [states_shape, held_shape]
             if level == levels - 2:
                 outs.append(slim_shape)
-            states, carried, held, *more = combine(level, operands, outs)
-            slim = more[0] if more else None
+            states, held, *slim = combine(level, operands, outs)
+            outgoing = slim[0] if slim else states
     got = swap(outgoing, 0)
     last_conv = convolve(steps - 1, 1, outgoing)
     merged = pl.pallas_call(

time: 30.6 us -> 31 us (1.013)
  starting transfers between devices: 9.5 us -> 9.88 us
  waiting for transfers between devices: 5.23 us -> 5.57 us
    pallas_call x3 -> x2, Pallas kernels: 4.91 us -> 4.59 us  [the longest x1 4.05 us: local(): pl.pallas_call(lambda *refs: gates_kernel(*refs, steps=steps, group=group...]
    ppermute x5 -> x4, starting transfers between devices: 5.04 us -> 5.31 us  [swap(): lax.ppermute(value, 'ctx', [(i, i ^ 1 << level) for i in range(parts)])]
    ppermute x5 -> x4, waiting for transfers between devices: 4.17 us -> 4.37 us  [swap(): lax.ppermute(value, 'ctx', [(i, i ^ 1 << level) for i in range(parts)])]
  transfers between devices with their start and end apart: 8 -> 7, of which waited for: 4 -> 5; matrix products, arithmetic and copies ran while one was open for 0% -> 0% of each run, Pallas kernels for 31% -> 24%
where the time goes in v17:
time: 31 us; the launch traced here: 30.8 us
  Pallas kernels  14.6 us (47%)
  starting transfers between devices  9.88 us (32%)
  waiting for transfers between devices  5.57 us (18%)
  between operations  0.74 us (2%)
    ppermute x4, starting transfers between devices, swap(): lax.ppermute(value, 'ctx', [(i, i ^ 1 << level) for i in range(parts)])  5.31 us
    ppermute x3, starting transfers between devices, local(): lax.ppermute(merged, 'ch', [(i, i ^ mask) for i in range(shards)])  4.56 us
    ppermute x4, waiting for transfers between devices, swap(): lax.ppermute(value, 'ctx', [(i, i ^ 1 << level) for i in range(parts)])  4.37 us
    pallas_call x1, Pallas kernels, local(): pl.pallas_call(lambda *refs: gates_kernel(*refs, steps=steps, group=group...  4.05 us
    pallas_call x2, Pallas kernels, convolve(): pl.pallas_call(lambda *refs: conv_kernel(*refs, first_step=first_step, in...  3.64 us
    pallas_call x1, Pallas kernels, local(): pl.pallas_call(lambda *refs: output_kernel(*refs, **sizes), grid=(steps,)...  2.74 us
    pallas_call x1, Pallas kernels, local(): pl.pallas_call(lambda *refs: states_kernel(*refs, inner=inner, **sizes),...  1.78 us
    ppermute x3, waiting for transfers between devices, local(): lax.ppermute(merged, 'ch', [(i, i ^ mask) for i in range(shards)])  1.21 us
  transfers between devices with their start and end apart: 7, of which 5 were waited for; matrix products, arithmetic and copies ran while one was open for 0% of the time, Pallas kernels for 24%

profile of v17, /device:TPU:0, one launch (start us, length us, event | category | flops | bytes accessed | tf_op | source)
XLA Modules:
  0.0 30.8 jit_solution(12078525434374974875)
XLA Ops:
  0.6 0.0 copy-start.4
  0.6 0.0 copy-start.5
  0.7 4.0 %gates.1 = (bf16[128,2048]{1,0:T(8,128)(2,1)S(1)}, bf16[128,2048]{1,0:T(8,128)(2,1)S(1)}, f32[16,4,256]{2,1,0:T(4,128)S(1)}, f32[16,128]{1,0:T(8,128)S(1)}) custom-call(bf16[128,2048]{1,0:T(8,128)(2,1)} %refs_0_.1, bf16[128,2048]{1,0:T(8,128)(2,1)} %refs_5_.1, bf16[128,2048]{1,0:T(8,128)(2,1)} %refs_6_.1, bf16[128,2048]{1,0:T(8,128)(2,1)} %refs_7_.1), custom_call_target="tpu_custom_call" | custom-call | tf_op jit(solution)/shard_map/gates/pallas_call | solution.py:507
  4.7 0.0 copy-done.4
  4.7 0.0 copy-done.5
  4.7 1.8 %states.1 = (bf16[512,128]{1,0:T(8,128)(2,1)S(1)}, bf16[512,128]{1,0:T(8,128)(2,1)S(1)}, f32[2,16,128]{2,1,0:T(8,128)S(1)}, f32[2,16,128]{2,1,0:T(8,128)S(1)}) custom-call(f32[16,512]{1,0:T(8,128)S(1)} %bitcast.8, f32[16,512]{1,0:T(8,128)S(1)} %bitcast.9, bf16[128,2048]{1,0:T(8,128)(2,1)S(1)} %get-tuple-element.29.refs_2_.refs_5_, ...), custom_call_target="tpu_custom_call" | custom-call | tf_op jit(solution)/shard_map/states/pallas_call | solution.py:516
  6.5 0.5 %collective-permute-start = (bf16[512,128]{1,0:T(8,128)(2,1)S(1)}, bf16[512,128]{1,0:T(8,128)(2,1)S(1)}, u32[]{:S(2)}, u32[]{:S(2)}) collective-permute-start(bf16[512,128]{1,0:T(8,128)(2,1)S(1)} %get-tuple-element.36), channel_id=1, source_target_pairs={{0,4},{4,0},{8,12},{12,8},{16,20},{20,16},{24,28},{28,24},{1,5},{5... | collective-permute-start | bytes 393224 | tf_op jit(solution)/shard_map/ppermute | solution.py:504
  7.0 0.4 %tables.1 = (f32[16,16,128]{2,1,0:T(8,128)S(1)}, f32[16,16,256]{2,1,0:T(8,128)S(1)}) custom-call(f32[2,16,128]{2,1,0:T(8,128)S(1)} %get-tuple-element.32.refs_0_), custom_call_target="tpu_custom_call" | custom-call | flops 1000000000 | bytes 1000000 | tf_op jit(solution)/shard_map/tables/pallas_call | solution.py:530
  7.4 0.0 copy-start.3
  7.4 0.5 %lags.1.refs_3_ = f32[32,128]{1,0:T(8,128)S(1)} custom-call(f32[16,16,256]{2,1,0:T(8,128)S(1)} %get-tuple-element.34.refs_0_.refs_4_, f32[16,4,256]{2,1,0:T(4,128)S(1)} %get-tuple-element.37.refs_1_), custom_call_target="tpu_custom_call" | custom-call | flops 536870912 | bytes 3145728 | tf_op jit(solution)/shard_map/lags/pallas_call | solution.py:544
  7.9 0.1 collective-permute-done.refs_2_
  8.0 0.3 combine.3
  8.3 2.9 %collective-permute-start.1 = (bf16[560,128]{1,0:T(8,128)(2,1)S(1)}, bf16[560,128]{1,0:T(8,128)(2,1)S(1)}, u32[]{:S(2)}, u32[]{:S(2)}) collective-permute-start(bf16[560,128]{1,0:T(8,128)(2,1)S(1)} %get-tuple-element.40.refs_1_), channel_id=1, source_target_pairs={{0,8},{4,12},{8,0},{12,4},{16,24},{20,28},{24,16},{28,20},{1,9},{5... | collective-permute-start | bytes 430088 | tf_op jit(solution)/shard_map/ppermute | solution.py:504
  11.2 0.0 copy-done.3
  11.2 2.7 %conv.2.refs_3_.refs_1_ = f32[128,3072]{1,0:T(8,128)S(1)} custom-call(f32[2,16,128]{2,1,0:T(8,128)S(1)} %get-tuple-element.32.refs_0_, f32[2,16,128]{2,1,0:T(8,128)S(1)} %get-tuple-element.31.refs_1_.refs_0_, f32[64,128]{1,0:T(8,128)S(1)} %bitcast.6, f32[16,16,128]{2,1,0:T(8,128)S(1)} %get-tuple-element.33.refs_0_.refs_3_, ...), custom_call_target="tpu_custom_call" | custom-call | flops 536870912 | bytes 3145728 | tf_op jit(solution)/shard_map/conv/pallas_call | solution.py:556
  13.9 1.3 %collective-permute-done.1.refs_2_ = bf16[560,128]{1,0:T(8,128)(2,1)S(1)} collective-permute-done((bf16[560,128]{1,0:T(8,128)(2,1)S(1)}, bf16[560,128]{1,0:T(8,128)(2,1)S(1)}, u32[]{:S(2)}, u32[]{:S(2)}) %collective-permute-start.1) | collective-permute-done | bytes 143392 | tf_op jit(solution)/shard_map/ppermute | solution.py:504
  15.3 0.3 combine.4
  15.6 1.8 %collective-permute-start.2 = (bf16[304,128]{1,0:T(8,128)(2,1)S(1)}, bf16[304,128]{1,0:T(8,128)(2,1)S(1)}, u32[]{:S(2)}, u32[]{:S(2)}) collective-permute-start(bf16[304,128]{1,0:T(8,128)(2,1)S(1)} %get-tuple-element.42), channel_id=1, source_target_pairs={{0,16},{4,20},{8,24},{12,28},{16,0},{20,4},{24,8},{28,12},{1,17},{... | collective-permute-start | bytes 233480 | tf_op jit(solution)/shard_map/ppermute | solution.py:504
  17.4 2.6 %collective-permute-done.2.refs_2_ = bf16[304,128]{1,0:T(8,128)(2,1)S(1)} collective-permute-done((bf16[304,128]{1,0:T(8,128)(2,1)S(1)}, bf16[304,128]{1,0:T(8,128)(2,1)S(1)}, u32[]{:S(2)}, u32[]{:S(2)}) %collective-permute-start.2) | collective-permute-done | bytes 77856 | tf_op jit(solution)/shard_map/ppermute | solution.py:504
  20.0 0.0 copy-start
  20.0 0.0 copy-start.1
  20.0 0.0 copy-start.2
  20.0 0.3 combine.5
  20.3 0.1 collective-permute-start.3
  20.4 0.9 %conv.3.refs_2_.refs_3_ = f32[128,1024]{1,0:T(8,128)S(1)} custom-call(f32[2,16,128]{2,1,0:T(8,128)S(1)} %get-tuple-element.32.refs_0_, f32[2,16,128]{2,1,0:T(8,128)S(1)} %get-tuple-element.31.refs_1_.refs_0_, f32[64,128]{1,0:T(8,128)S(1)} %bitcast.7, f32[16,16,128]{2,1,0:T(8,128)S(1)} %get-tuple-element.33.refs_0_.refs_3_, ...), custom_call_target="tpu_custom_call" | custom-call | flops 536870912 | bytes 3145728 | tf_op jit(solution)/shard_map/conv/pallas_call | solution.py:556
  21.3 0.3 %collective-permute-done.3.refs_4_.refs_2_ = bf16[304,128]{1,0:T(8,128)(2,1)S(1)} collective-permute-done((bf16[304,128]{1,0:T(8,128)(2,1)S(1)}, bf16[304,128]{1,0:T(8,128)(2,1)S(1)}, u32[]{:S(2)}, u32[]{:S(2)}) %collective-permute-start.3) | collective-permute-done | bytes 77856 | tf_op jit(solution)/shard_map/ppermute | solution.py:504
  21.6 3.9 %collective-permute-start.6 = (bf16[48,128]{1,0:T(8,128)(2,1)S(1)}, bf16[48,128]{1,0:T(8,128)(2,1)S(1)}, u32[]{:S(2)}, u32[]{:S(2)}) collective-permute-start(bf16[48,128]{1,0:T(8,128)(2,1)S(1)} %merge.1.refs_0_), channel_id=1, source_target_pairs={{0,3},{1,2},{2,1},{3,0},{4,7},{5,6},{6,5},{7,4},{8,11},{9,10},{10,... | collective-permute-start | bytes 36872 | tf_op jit(solution)/shard_map/ppermute | solution.py:613
  25.6 0.0 collective-permute-start.5
  25.6 0.6 %collective-permute-start.4 = (bf16[48,128]{1,0:T(8,128)(2,1)S(1)}, bf16[48,128]{1,0:T(8,128)(2,1)S(1)}, u32[]{:S(2)}, u32[]{:S(2)}) collective-permute-start(bf16[48,128]{1,0:T(8,128)(2,1)S(1)} %merge.1.refs_0_), channel_id=1, source_target_pairs={{0,1},{1,0},{2,3},{3,2},{4,5},{5,4},{6,7},{7,6},{8,9},{9,8},{10,11... | collective-permute-start | bytes 36872 | tf_op jit(solution)/shard_map/ppermute | solution.py:613
  26.2 0.0 copy-done
  26.2 0.0 copy-done.1
  26.2 0.0 copy-done.2
  26.2 2.7 %outputs.1 = (bf16[128,2048]{1,0:T(8,128)(2,1)}, bf16[128,2048]{1,0:T(8,128)(2,1)}, bf16[128,2048]{1,0:T(8,128)(2,1)}) custom-call(f32[2,16,128]{2,1,0:T(8,128)S(1)} %get-tuple-element.31.refs_1_.refs_0_, f32[128,3072]{1,0:T(8,128)S(1)} %conv.2.refs_3_.refs_1_, f32[128,1024]{1,0:T(8,128)S(1)} %conv.3.refs_2_.refs_3_, ...), custom_call_target="tpu_custom_call" | custom-call | flops 536870912 | bytes 3145728 | tf_op jit(solution)/shard_map/outputs/pallas_call | solution.py:616
  28.9 0.0 collective-permute-done.6.refs_3_
  29.0 1.2 %collective-permute-done.5.refs_2_ = bf16[48,128]{1,0:T(8,128)(2,1)S(1)} collective-permute-done((bf16[48,128]{1,0:T(8,128)(2,1)S(1)}, bf16[48,128]{1,0:T(8,128)(2,1)S(1)}, u32[]{:S(2)}, u32[]{:S(2)}) %collective-permute-start.5) | collective-permute-done | bytes 12320 | tf_op jit(solution)/shard_map/ppermute | solution.py:613
  30.2 0.0 collective-permute-done.4.refs_1_
  30.2 0.6 %assemble.1 = (f32[16,512]{1,0:T(8,128)}, f32[16,512]{1,0:T(8,128)}, f32[64,128]{1,0:T(8,128)}) custom-call(bf16[48,128]{1,0:T(8,128)(2,1)S(1)} %merge.1.refs_0_, bf16[48,128]{1,0:T(8,128)(2,1)S(1)} %collective-permute-done.4.refs_1_, bf16[48,128]{1,0:T(8,128)(2,1)S(1)} %collective-permute-done.5.refs_2_, bf16[48,128]{1,0:T(8,128)(2,1)S(1)} %collective-permute-done.6.refs_3_), custom_call_target="tpu_custom_call" | custom-call | tf_op jit(solution)/shard_map/assemble/pallas_call | solution.py:627
  (1 shorter events, 0.0 us)
Async XLA Ops:
  0.6 4.1 %copy-start.4 = (f32[512,16]{0,1:T(8,128)S(1)}, f32[512,16]{0,1:T(8,128)}, u32[]{:S(2)}) copy-start(f32[512,16]{0,1:T(8,128)} %param.12) | copy-start | bytes 98308
  0.6 4.1 %copy-start.5 = (f32[512,16]{0,1:T(8,128)S(1)}, f32[512,16]{0,1:T(8,128)}, u32[]{:S(2)}) copy-start(f32[512,16]{0,1:T(8,128)} %param.11) | copy-start | bytes 98308
  6.5 1.5 %collective-permute-start = (bf16[512,128]{1,0:T(8,128)(2,1)S(1)}, bf16[512,128]{1,0:T(8,128)(2,1)S(1)}, u32[]{:S(2)}, u32[]{:S(2)}) collective-permute-start(bf16[512,128]{1,0:T(8,128)(2,1)S(1)} %get-tuple-element.36), channel_id=1, source_target_pairs={{0,4},{4,0},{8,12},{12,8},{16,20},{20,16},{24,28},{28,24},{1,5},{5... | collective-permute-start | bytes 393224 | tf_op jit(solution)/shard_map/ppermute | solution.py:504
  7.4 3.8 %copy-start.3 = (f32[8192]{0:T(1024)S(1)}, f32[8192]{0:T(1024)}, u32[]{:S(2)}) copy-start(f32[8192]{0:T(1024)} %param.13) | copy-start | bytes 98308
  8.3 7.0 %collective-permute-start.1 = (bf16[560,128]{1,0:T(8,128)(2,1)S(1)}, bf16[560,128]{1,0:T(8,128)(2,1)S(1)}, u32[]{:S(2)}, u32[]{:S(2)}) collective-permute-start(bf16[560,128]{1,0:T(8,128)(2,1)S(1)} %get-tuple-element.40.refs_1_), channel_id=1, source_target_pairs={{0,8},{4,12},{8,0},{12,4},{16,24},{20,28},{24,16},{28,20},{1,9},{5... | collective-permute-start | bytes 430088 | tf_op jit(solution)/shard_map/ppermute | solution.py:504
  15.6 4.4 %collective-permute-start.2 = (bf16[304,128]{1,0:T(8,128)(2,1)S(1)}, bf16[304,128]{1,0:T(8,128)(2,1)S(1)}, u32[]{:S(2)}, u32[]{:S(2)}) collective-permute-start(bf16[304,128]{1,0:T(8,128)(2,1)S(1)} %get-tuple-element.42), channel_id=1, source_target_pairs={{0,16},{4,20},{8,24},{12,28},{16,0},{20,4},{24,8},{28,12},{1,17},{... | collective-permute-start | bytes 233480 | tf_op jit(solution)/shard_map/ppermute | solution.py:504
  20.0 6.2 %copy-start = (bf16[128,2048]{1,0:T(8,128)(2,1)S(1)}, bf16[128,2048]{1,0:T(8,128)(2,1)}, u32[]{:S(2)}) copy-start(bf16[128,2048]{1,0:T(8,128)(2,1)} %refs_5_.1) | copy-start | bytes 1572868
  20.0 6.2 %copy-start.1 = (bf16[128,2048]{1,0:T(8,128)(2,1)S(1)}, bf16[128,2048]{1,0:T(8,128)(2,1)}, u32[]{:S(2)}) copy-start(bf16[128,2048]{1,0:T(8,128)(2,1)} %refs_6_.1) | copy-start | bytes 1572868
  20.0 6.2 %copy-start.2 = (bf16[128,2048]{1,0:T(8,128)(2,1)S(1)}, bf16[128,2048]{1,0:T(8,128)(2,1)}, u32[]{:S(2)}) copy-start(bf16[128,2048]{1,0:T(8,128)(2,1)} %refs_7_.1) | copy-start | bytes 1572868
  20.3 1.3 %collective-permute-start.3 = (bf16[304,128]{1,0:T(8,128)(2,1)S(1)}, bf16[304,128]{1,0:T(8,128)(2,1)S(1)}, u32[]{:S(2)}, u32[]{:S(2)}) collective-permute-start(bf16[304,128]{1,0:T(8,128)(2,1)S(1)} %get-tuple-element.44.refs_7_.refs_1_), channel_id=1, source_target_pairs={{0,4},{4,0},{8,12},{12,8},{16,20},{20,16},{24,28},{28,24},{1,5},{5... | collective-permute-start | bytes 233480 | tf_op jit(solution)/shard_map/ppermute | solution.py:504
  21.6 7.3 %collective-permute-start.6 = (bf16[48,128]{1,0:T(8,128)(2,1)S(1)}, bf16[48,128]{1,0:T(8,128)(2,1)S(1)}, u32[]{:S(2)}, u32[]{:S(2)}) collective-permute-start(bf16[48,128]{1,0:T(8,128)(2,1)S(1)} %merge.1.refs_0_), channel_id=1, source_target_pairs={{0,3},{1,2},{2,1},{3,0},{4,7},{5,6},{6,5},{7,4},{8,11},{9,10},{10,... | collective-permute-start | bytes 36872 | tf_op jit(solution)/shard_map/ppermute | solution.py:613
  25.6 4.6 %collective-permute-start.5 = (bf16[48,128]{1,0:T(8,128)(2,1)S(1)}, bf16[48,128]{1,0:T(8,128)(2,1)S(1)}, u32[]{:S(2)}, u32[]{:S(2)}) collective-permute-start(bf16[48,128]{1,0:T(8,128)(2,1)S(1)} %merge.1.refs_0_), channel_id=1, source_target_pairs={{0,2},{1,3},{2,0},{3,1},{4,6},{5,7},{6,4},{7,5},{8,10},{9,11},{10,... | collective-permute-start | bytes 36872 | tf_op jit(solution)/shard_map/ppermute | solution.py:613
  25.6 4.6 %collective-permute-start.4 = (bf16[48,128]{1,0:T(8,128)(2,1)S(1)}, bf16[48,128]{1,0:T(8,128)(2,1)S(1)}, u32[]{:S(2)}, u32[]{:S(2)}) collective-permute-start(bf16[48,128]{1,0:T(8,128)(2,1)S(1)} %merge.1.refs_0_), channel_id=1, source_target_pairs={{0,1},{1,0},{2,3},{3,2},{4,5},{5,4},{6,7},{7,6},{8,9},{9,8},{10,11... | collective-permute-start | bytes 36872 | tf_op jit(solution)/shard_map/ppermute | solution.py:613

commit v18 on v16

--- a/solution.py
+++ b/solution.py
@@ -13,7 +13,7 @@
 BF16 = jnp.bfloat16
 EXACT = lax.Precision.HIGHEST
 VMEM_LIMIT = 40 * 1024 * 1024
-GATES_LIMIT = 53400 * 1024
+GATES_LIMIT = 53200 * 1024
 PARAMS = pltpu.CompilerParams(vmem_limit_bytes=VMEM_LIMIT)
 
 
@@ -83,30 +83,51 @@
     return pl.multiple_of(lax.axis_index("ch") * groups, LANES)
 
 
-def gates_kernel(q_any, k_any, v_any, c_any, gated_ref, dgate_ref, turned_ref, q_ref, k_ref, v_ref, c_ref, sems, *, steps):
-    tokens, width = q_ref.shape
-    wide = width // steps
-    sources = ((k_any, k_ref), (v_any, v_ref), (c_any, c_ref), (q_any, q_ref))
-    cuts = [slice(step * wide, (step + 1) * wide) for step in range(steps)]
-    copies = [
-        [pltpu.make_async_copy(far.at[:, cut], near.at[:, cut], sems.at[n, step]) for n, (far, near) in enumerate(sources)]
-        for step, cut in enumerate(cuts)
-    ]
+def column_copies(sources, sems, half, half_steps, wide):
+    found = []
+    for step in range(half_steps):
+        near_cut = pl.ds(step * wide, wide)
+        cut = pl.ds(pl.multiple_of((half * half_steps + step) * wide, LANES), wide)
+        found.append(
+            [
+                pltpu.make_async_copy(far.at[:, cut], near.at[:, near_cut], sems.at[n, step])
+                for n, (far, near) in enumerate(sources)
+            ]
+        )
+    return found
+
+
+def gate_step(copies, near, step, start, wide, flip, gated_ref, dgate_ref, turned_ref):
+    for copy in copies[step]:
+        copy.wait()
+    near_cut = slice(step * wide, (step + 1) * wide)
+    q_ref, k_ref, v_ref, c_ref = near
+    cut = pl.ds(pl.multiple_of(start * LANES, LANES), wide)
+    dgate = gate(c_ref[:, near_cut], q_ref[:, near_cut])
+    gated = gate(k_ref[:, near_cut], v_ref[:, near_cut])
+    turned = mxu(flip, dgate).astype(BF16)
+    gated_ref[:, cut], dgate_ref[:, cut], turned_ref[:, cut] = gated, dgate, turned
+    return gated, turned
+
+
+def gates_kernel(q_any, k_any, v_any, c_any, gated_ref, dgate_ref, turned_ref, q_ref, k_ref, v_ref, c_ref, sems, *, inner):
+    tokens, half_width = q_ref.shape
+    wide = inner * LANES
+    half_steps = half_width // wide
+    half = 1 - lax.rem(lax.axis_index("ctx"), 2)
+    near = (q_ref, k_ref, v_ref, c_ref)
+    copies = column_copies(tuple(zip((q_any, k_any, v_any, c_any), near)), sems, half, half_steps, wide)
     for step in copies:
         for copy in step:
             copy.start()
     flip = reversal(tokens)
-    for step, cut in enumerate(cuts):
-        for copy in copies[step]:
-            copy.wait()
-        dgate = gate(c_ref[:, cut], q_ref[:, cut])
-        dgate_ref[:, cut] = dgate
-        gated_ref[:, cut] = gate(k_ref[:, cut], v_ref[:, cut])
-        turned_ref[:, cut] = mxu(flip, dgate).astype(BF16)
-
-
-def states_kernel(logs_ref, res_ref, gated_ref, turned_ref, send_ref, keep_ref, rows_ref, table_ref,
-                  *, group, poles, inner):
+    for step in range(half_steps):
+        start = (half * half_steps + step) * inner
+        gate_step(copies, near, step, start, wide, flip, gated_ref, dgate_ref, turned_ref)
+
+
+def states_kernel(logs_ref, res_ref, q_any, k_any, v_any, c_any, gated_in, _, turned_in, send_ref, keep_ref, gated_ref,
+                  dgate_ref, turned_ref, rows_ref, table_ref, q_ref, k_ref, v_ref, c_ref, sems, *, group, poles, inner):
     tokens, _ = gated_ref.shape
     per_block = LANES // group
     _, blocks, _ = rows_ref.shape
@@ -114,12 +135,19 @@
     groups = blocks * per_block
     wide = inner * LANES
     core = lax.rem(lax.axis_index("ctx"), 2)
+    half_steps = half_blocks // inner
+    near = (q_ref, k_ref, v_ref, c_ref)
+    copies = column_copies(tuple(zip((q_any, k_any, v_any, c_any), near)), sems, core, half_steps, wide)
+    for step in copies:
+        for copy in step:
+            copy.start()
     first = shard_start(groups)
     for n, ref in enumerate((logs_ref, res_ref)):
         table_ref[n] = ref[:, pl.ds(first, groups)]
     rows_ref[0] = jnp.exp(flat_rows(table_ref[0], poles))
     rows_ref[1] = flat_rows(table_ref[1], poles)
 
+    flip = reversal(tokens)
     back_pos = (tokens - 1 - iota((tokens, LANES), 0)).astype(F32)
     back_lane = (tokens - 1 - iota((1, tokens), 1)).astype(F32)
     wide_group = over(within(iota((poles, 2 * LANES), 1), LANES), group)
@@ -128,10 +156,13 @@
     for turn, msg_ref in enumerate((send_ref, keep_ref)):
         base = lax.rem(core + 1 + turn, 2) * half_blocks
 
-        def body(step, carry, base=base, msg_ref=msg_ref):
+        for step in range(half_steps):
             start = base + step * inner
-            cut = pl.ds(pl.multiple_of(start * LANES, LANES), wide)
-            gated, turned = gated_ref[:, cut], turned_ref[:, cut]
+            if turn == 0:
+                cut = pl.ds(pl.multiple_of(start * LANES, LANES), wide)
+                gated, turned = gated_in[:, cut], turned_in[:, cut]
+            else:
+                gated, turned = gate_step(copies, near, step, start, wide, flip, gated_ref, dgate_ref, turned_ref)
             tables = [jnp.exp(-rows_ref[0, pl.ds(start + j, 1), :] * back_pos).T for j in range(inner)]
             found = []
             for j in range(inner):
@@ -147,11 +178,8 @@
                         total = jnp.where(wide_group == g, found[j][row : row + poles], total)
                     folded.append(total)
                 out = [folded[0][:, :LANES], folded[0][:, LANES:], folded[1][:, :LANES], folded[1][:, LANES:]]
-                row = pl.multiple_of((step * inner + j) * 4 * poles, 4 * poles)
-                msg_ref[pl.ds(row, 4 * poles), :] = jnp.concatenate(out, axis=0).astype(BF16)
-            return carry
-
-        lax.fori_loop(0, half_blocks // inner, body, 0)
+                row = (step * inner + j) * 4 * poles
+                msg_ref[row : row + 4 * poles, :] = jnp.concatenate(out, axis=0).astype(BF16)
 
 
 def lags_kernel(lag_rates_ref, gated_ref, dgate_ref, turned_ref, *rest, second, group, poles, inner):
@@ -509,28 +537,35 @@
         return lax.ppermute(value, "ctx", [(i, i ^ (1 << level)) for i in range(parts)])
 
     operand = shape(tokens, width, dtype=BF16)
-    gated, dgate, turned = pl.pallas_call(
-        lambda *refs: gates_kernel(*refs, steps=steps),
+    scratch = [pltpu.VMEM((tokens, width // 2), BF16)] * 4 + [pltpu.SemaphoreType.DMA((4, steps // 2))]
+    inputs = (queries, key_input, value_input, cotangent)
+    gates = pl.pallas_call(
+        lambda *refs: gates_kernel(*refs, inner=inner),
         in_specs=[anywhere] * 4,
         out_specs=[vmem] * 3,
         out_shape=[operand] * 3,
-        scratch_shapes=[pltpu.VMEM((tokens, width), BF16)] * 4 + [pltpu.SemaphoreType.DMA((4, steps))],
+        scratch_shapes=scratch,
         compiler_params=pltpu.CompilerParams(vmem_limit_bytes=GATES_LIMIT),
         name="gates",
-    )(queries, key_input, value_input, cotangent)
-    outgoing, message, rows, params = pl.pallas_call(
+    )(*inputs)
+    outgoing, message, gated, dgate, turned, rows, params = pl.pallas_call(
         lambda *refs: states_kernel(*refs, inner=inner, **sizes),
-        in_specs=[vmem] * 4,
-        out_specs=[vmem] * 4,
+        in_specs=[vmem] * 2 + [anywhere] * 4 + [vmem] * 3,
+        out_specs=[vmem] * 7,
         out_shape=[
             shape(2 * half_rows, LANES, dtype=BF16),
             shape(2 * half_rows, LANES, dtype=BF16),
+            operand,
+            operand,
+            operand,
             shape(2, blocks, LANES),
             shape(2, poles, groups),
         ],
-        compiler_params=PARAMS,
+        input_output_aliases={6: 2, 7: 3, 8: 4},
+        scratch_shapes=scratch,
+        compiler_params=pltpu.CompilerParams(vmem_limit_bytes=GATES_LIMIT),
         name="states",
-    )(log_rates, residues, gated, turned)
+    )(log_rates, residues, *inputs, *gates)
 
     rates, lag_rates = pl.pallas_call(
         lambda *refs: tables_kernel(*refs, inner=inner, **sizes),

time: 30.6 us -> 31 us (1.013)
  Pallas kernels: 14.9 us -> 15.3 us
    pallas_call x1, Pallas kernels: 1.78 us -> 2.7 us  [local(): pl.pallas_call(lambda *refs: states_kernel(*refs, inner=inner, **sizes),...]
    pallas_call x1, Pallas kernels: 2.2 us -> 1.66 us  [local(): pl.pallas_call(lambda *refs: gates_kernel(*refs, inner=inner), in_specs=[...]
  transfers between devices with their start and end apart: 8 -> 8, of which waited for: 4 -> 4; matrix products, arithmetic and copies ran while one was open for 0% -> 0% of each run, Pallas kernels for 31% -> 30%
where the time goes in v18:
time: 31 us; the launch traced here: 30.9 us
  Pallas kernels  15.3 us (49%)
  starting transfers between devices  9.49 us (31%)
  waiting for transfers between devices  5.24 us (17%)
  between operations  0.82 us (3%)
    ppermute x5, starting transfers between devices, swap(): lax.ppermute(value, 'ctx', [(i, i ^ 1 << level) for i in range(parts)])  5.04 us
    ppermute x3, starting transfers between devices, local(): lax.ppermute(merged, 'ch', [(i, i ^ mask) for i in range(shards)])  4.45 us
    ppermute x5, waiting for transfers between devices, swap(): lax.ppermute(value, 'ctx', [(i, i ^ 1 << level) for i in range(parts)])  4.17 us
    pallas_call x2, Pallas kernels, convolve(): pl.pallas_call(lambda *refs: conv_kernel(*refs, first_step=first_step, in...  3.64 us
    pallas_call x1, Pallas kernels, local(): pl.pallas_call(lambda *refs: output_kernel(*refs, **sizes), grid=(steps,)...  2.73 us
    pallas_call x2, Pallas kernels, local_sums(): pl.pallas_call(lambda *refs: lags_kernel(*refs, second=second, inner=inne...  2.7 us
    pallas_call x1, Pallas kernels, local(): pl.pallas_call(lambda *refs: states_kernel(*refs, inner=inner, **sizes),...  2.7 us
    pallas_call x1, Pallas kernels, local(): pl.pallas_call(lambda *refs: gates_kernel(*refs, inner=inner), in_specs=[...  1.66 us
  transfers between devices with their start and end apart: 8, of which 4 were waited for; matrix products, arithmetic and copies ran while one was open for 0% of the time, Pallas kernels for 30%

profile of v18, /device:TPU:0, one launch (start us, length us, event | category | flops | bytes accessed | tf_op | source)
XLA Modules:
  0.0 30.9 jit_solution(3333628276805852508)
XLA Ops:
  0.6 0.0 copy-start.4
  0.6 0.0 copy-start.5
  0.7 1.7 %gates.1 = (bf16[128,2048]{1,0:T(8,128)(2,1)S(1)}, bf16[128,2048]{1,0:T(8,128)(2,1)S(1)}, bf16[128,2048]{1,0:T(8,128)(2,1)S(1)}) custom-call(bf16[128,2048]{1,0:T(8,128)(2,1)} %refs_2_.3, bf16[128,2048]{1,0:T(8,128)(2,1)} %refs_5_.3, bf16[128,2048]{1,0:T(8,128)(2,1)} %refs_6_.1, bf16[128,2048]{1,0:T(8,128)(2,1)} %refs_7_.1), custom_call_target="tpu_custom_call" | custom-call | tf_op jit(solution)/shard_map/gates/pallas_call | solution.py:542
  2.3 0.0 copy-done.4
  2.3 0.0 copy-done.5
  2.3 2.7 %states.1 = (bf16[512,128]{1,0:T(8,128)(2,1)S(1)}, bf16[512,128]{1,0:T(8,128)(2,1)S(1)}, bf16[128,2048]{1,0:T(8,128)(2,1)S(1)}, bf16[128,2048]{1,0:T(8,128)(2,1)...) custom-call(f32[16,512]{1,0:T(8,128)S(1)} %bitcast.8, ...), custom_call_target="tpu_custom_call", output_to_operand_aliasing={{2}: (6, {}), {3}: (7, {}), {4}: (8, {})} | custom-call | tf_op jit(solution)/shard_map/states/pallas_call | solution.py:551
  5.0 0.5 %collective-permute-start = (bf16[512,128]{1,0:T(8,128)(2,1)S(1)}, bf16[512,128]{1,0:T(8,128)(2,1)S(1)}, u32[]{:S(2)}, u32[]{:S(2)}) collective-permute-start(bf16[512,128]{1,0:T(8,128)(2,1)S(1)} %get-tuple-element.43), channel_id=1, source_target_pairs={{0,4},{4,0},{8,12},{12,8},{16,20},{20,16},{24,28},{28,24},{1,5},{5... | collective-permute-start | bytes 393224 | tf_op jit(solution)/shard_map/ppermute | solution.py:537
  5.6 0.4 %tables.1 = (f32[16,16,128]{2,1,0:T(8,128)S(1)}, f32[16,16,256]{2,1,0:T(8,128)S(1)}) custom-call(f32[2,16,128]{2,1,0:T(8,128)S(1)} %get-tuple-element.37.refs_0_), custom_call_target="tpu_custom_call" | custom-call | flops 1000000000 | bytes 1000000 | tf_op jit(solution)/shard_map/tables/pallas_call | solution.py:570
  5.9 0.7 %lags.2.refs_3_ = f32[32,128]{1,0:T(8,128)S(1)} custom-call(f32[16,16,256]{2,1,0:T(8,128)S(1)} %get-tuple-element.39.refs_0_.refs_4_, bf16[128,2048]{1,0:T(8,128)(2,1)S(1)} %get-tuple-element.40.refs_1_.refs_5_, bf16[128,2048]{1,0:T(8,128)(2,1)S(1)} %get-tuple-element.44.refs_2_, bf16[128,2048]{1,0:T(8,128)(2,1)S(1)} %get-tuple-element.41.refs_3_.refs_6_), custom_call_target="tpu_custom_call" | custom-call | flops 536870912 | bytes 3145728 | tf_op jit(solution)/shard_map/lags/pallas_call | solution.py:585
  6.6 0.0 copy-start.3
  6.6 0.0 collective-permute-done.refs_2_
  6.6 0.3 combine.3
  6.9 2.8 %collective-permute-start.1 = (bf16[512,128]{1,0:T(8,128)(2,1)S(1)}, bf16[512,128]{1,0:T(8,128)(2,1)S(1)}, u32[]{:S(2)}, u32[]{:S(2)}) collective-permute-start(bf16[512,128]{1,0:T(8,128)(2,1)S(1)} %get-tuple-element.45.refs_1_), channel_id=1, source_target_pairs={{0,8},{4,12},{8,0},{12,4},{16,24},{20,28},{24,16},{28,20},{1,9},{5... | collective-permute-start | bytes 393224 | tf_op jit(solution)/shard_map/ppermute | solution.py:537
  9.7 2.0 %lags.3.refs_2_ = bf16[48,128]{1,0:T(8,128)(2,1)S(1)} custom-call(f32[16,16,256]{2,1,0:T(8,128)S(1)} %get-tuple-element.39.refs_0_.refs_4_, bf16[128,2048]{1,0:T(8,128)(2,1)S(1)} %get-tuple-element.40.refs_1_.refs_5_, bf16[128,2048]{1,0:T(8,128)(2,1)S(1)} %get-tuple-element.44.refs_2_, bf16[128,2048]{1,0:T(8,128)(2,1)S(1)} %get-tuple-element.41.refs_3_.refs_6_, ...), custom_call_target="tpu_custom_call" | custom-call | flops 536870912 | bytes 3145728 | tf_op jit(solution)/shard_map/lags/pallas_call | solution.py:585
  11.7 0.1 collective-permute-start.2
  11.8 3.7 %collective-permute-done.2.refs_4_ = bf16[48,128]{1,0:T(8,128)(2,1)S(1)} collective-permute-done((bf16[48,128]{1,0:T(8,128)(2,1)S(1)}, bf16[48,128]{1,0:T(8,128)(2,1)S(1)}, u32[]{:S(2)}, u32[]{:S(2)}) %collective-permute-start.2) | collective-permute-done | bytes 12320 | tf_op jit(solution)/shard_map/ppermute | solution.py:537
  15.5 0.0 collective-permute-done.1.refs_3_
  15.5 0.3 combine.4
  15.8 1.6 %collective-permute-start.3 = (bf16[304,128]{1,0:T(8,128)(2,1)S(1)}, bf16[304,128]{1,0:T(8,128)(2,1)S(1)}, u32[]{:S(2)}, u32[]{:S(2)}) collective-permute-start(bf16[304,128]{1,0:T(8,128)(2,1)S(1)} %get-tuple-element.50), channel_id=1, source_target_pairs={{0,16},{4,20},{8,24},{12,28},{16,0},{20,4},{24,8},{28,12},{1,17},{... | collective-permute-start | bytes 233480 | tf_op jit(solution)/shard_map/ppermute | solution.py:537
  17.4 0.0 copy-done.3
  17.4 2.7 %conv.2.refs_5_.refs_1_ = f32[128,3072]{1,0:T(8,128)S(1)} custom-call(f32[2,16,128]{2,1,0:T(8,128)S(1)} %get-tuple-element.37.refs_0_, f32[2,16,128]{2,1,0:T(8,128)S(1)} %get-tuple-element.36.refs_1_.refs_0_, f32[64,128]{1,0:T(8,128)S(1)} %bitcast.6, f32[16,16,128]{2,1,0:T(8,128)S(1)} %get-tuple-element.38.refs_0_.refs_3_, ...), custom_call_target="tpu_custom_call" | custom-call | flops 536870912 | bytes 3145728 | tf_op jit(solution)/shard_map/conv/pallas_call | solution.py:598
  20.1 0.1 collective-permute-done.3.refs_3_
  20.2 0.3 combine.5
  20.5 0.0 copy-start
  20.6 0.0 copy-start.1
  20.6 0.0 copy-start.2
  20.6 0.1 collective-permute-start.4
  20.7 0.9 %conv.3.refs_2_.refs_3_ = f32[128,1024]{1,0:T(8,128)S(1)} custom-call(f32[2,16,128]{2,1,0:T(8,128)S(1)} %get-tuple-element.37.refs_0_, f32[2,16,128]{2,1,0:T(8,128)S(1)} %get-tuple-element.36.refs_1_.refs_0_, f32[64,128]{1,0:T(8,128)S(1)} %bitcast.7, f32[16,16,128]{2,1,0:T(8,128)S(1)} %get-tuple-element.38.refs_0_.refs_3_, ...), custom_call_target="tpu_custom_call" | custom-call | flops 536870912 | bytes 3145728 | tf_op jit(solution)/shard_map/conv/pallas_call | solution.py:598
  21.6 0.3 %collective-permute-done.4.refs_4_.refs_2_ = bf16[304,128]{1,0:T(8,128)(2,1)S(1)} collective-permute-done((bf16[304,128]{1,0:T(8,128)(2,1)S(1)}, bf16[304,128]{1,0:T(8,128)(2,1)S(1)}, u32[]{:S(2)}, u32[]{:S(2)}) %collective-permute-start.4) | collective-permute-done | bytes 77856 | tf_op jit(solution)/shard_map/ppermute | solution.py:537
  21.9 3.7 %collective-permute-start.7 = (bf16[48,128]{1,0:T(8,128)(2,1)S(1)}, bf16[48,128]{1,0:T(8,128)(2,1)S(1)}, u32[]{:S(2)}, u32[]{:S(2)}) collective-permute-start(bf16[48,128]{1,0:T(8,128)(2,1)S(1)} %merge.1.refs_0_), channel_id=1, source_target_pairs={{0,3},{1,2},{2,1},{3,0},{4,7},{5,6},{6,5},{7,4},{8,11},{9,10},{10,... | collective-permute-start | bytes 36872 | tf_op jit(solution)/shard_map/ppermute | solution.py:665
  25.6 0.0 collective-permute-start.6
  25.6 0.8 %collective-permute-start.5 = (bf16[48,128]{1,0:T(8,128)(2,1)S(1)}, bf16[48,128]{1,0:T(8,128)(2,1)S(1)}, u32[]{:S(2)}, u32[]{:S(2)}) collective-permute-start(bf16[48,128]{1,0:T(8,128)(2,1)S(1)} %merge.1.refs_0_), channel_id=1, source_target_pairs={{0,1},{1,0},{2,3},{3,2},{4,5},{5,4},{6,7},{7,6},{8,9},{9,8},{10,11... | collective-permute-start | bytes 36872 | tf_op jit(solution)/shard_map/ppermute | solution.py:665
  26.4 0.0 copy-done
  26.4 0.0 copy-done.1
  26.4 0.0 copy-done.2
  26.4 2.7 %outputs.1 = (bf16[128,2048]{1,0:T(8,128)(2,1)}, bf16[128,2048]{1,0:T(8,128)(2,1)}, bf16[128,2048]{1,0:T(8,128)(2,1)}) custom-call(f32[2,16,128]{2,1,0:T(8,128)S(1)} %get-tuple-element.36.refs_1_.refs_0_, f32[128,3072]{1,0:T(8,128)S(1)} %conv.2.refs_5_.refs_1_, f32[128,1024]{1,0:T(8,128)S(1)} %conv.3.refs_2_.refs_3_, ...), custom_call_target="tpu_custom_call" | custom-call | flops 536870912 | bytes 3145728 | tf_op jit(solution)/shard_map/outputs/pallas_call | solution.py:668
  29.1 0.0 collective-permute-done.7.refs_3_
  29.1 1.1 %collective-permute-done.6.refs_2_ = bf16[48,128]{1,0:T(8,128)(2,1)S(1)} collective-permute-done((bf16[48,128]{1,0:T(8,128)(2,1)S(1)}, bf16[48,128]{1,0:T(8,128)(2,1)S(1)}, u32[]{:S(2)}, u32[]{:S(2)}) %collective-permute-start.6) | collective-permute-done | bytes 12320 | tf_op jit(solution)/shard_map/ppermute | solution.py:665
  30.2 0.0 collective-permute-done.5.refs_1_
  30.2 0.6 %assemble.1 = (f32[16,512]{1,0:T(8,128)}, f32[16,512]{1,0:T(8,128)}, f32[64,128]{1,0:T(8,128)}) custom-call(bf16[48,128]{1,0:T(8,128)(2,1)S(1)} %merge.1.refs_0_, bf16[48,128]{1,0:T(8,128)(2,1)S(1)} %collective-permute-done.5.refs_1_, bf16[48,128]{1,0:T(8,128)(2,1)S(1)} %collective-permute-done.6.refs_2_, bf16[48,128]{1,0:T(8,128)(2,1)S(1)} %collective-permute-done.7.refs_3_), custom_call_target="tpu_custom_call" | custom-call | tf_op jit(solution)/shard_map/assemble/pallas_call | solution.py:679
  (1 shorter events, 0.0 us)
Async XLA Ops:
  0.6 1.7 %copy-start.4 = (f32[512,16]{0,1:T(8,128)S(1)}, f32[512,16]{0,1:T(8,128)}, u32[]{:S(2)}) copy-start(f32[512,16]{0,1:T(8,128)} %param.12) | copy-start | bytes 98308
  0.6 1.7 %copy-start.5 = (f32[512,16]{0,1:T(8,128)S(1)}, f32[512,16]{0,1:T(8,128)}, u32[]{:S(2)}) copy-start(f32[512,16]{0,1:T(8,128)} %param.11) | copy-start | bytes 98308
  5.0 1.6 %collective-permute-start = (bf16[512,128]{1,0:T(8,128)(2,1)S(1)}, bf16[512,128]{1,0:T(8,128)(2,1)S(1)}, u32[]{:S(2)}, u32[]{:S(2)}) collective-permute-start(bf16[512,128]{1,0:T(8,128)(2,1)S(1)} %get-tuple-element.43), channel_id=1, source_target_pairs={{0,4},{4,0},{8,12},{12,8},{16,20},{20,16},{24,28},{28,24},{1,5},{5... | collective-permute-start | bytes 393224 | tf_op jit(solution)/shard_map/ppermute | solution.py:537
  6.6 10.8 %copy-start.3 = (f32[8192]{0:T(1024)S(1)}, f32[8192]{0:T(1024)}, u32[]{:S(2)}) copy-start(f32[8192]{0:T(1024)} %param.13) | copy-start | bytes 98308
  6.9 8.6 %collective-permute-start.1 = (bf16[512,128]{1,0:T(8,128)(2,1)S(1)}, bf16[512,128]{1,0:T(8,128)(2,1)S(1)}, u32[]{:S(2)}, u32[]{:S(2)}) collective-permute-start(bf16[512,128]{1,0:T(8,128)(2,1)S(1)} %get-tuple-element.45.refs_1_), channel_id=1, source_target_pairs={{0,8},{4,12},{8,0},{12,4},{16,24},{20,28},{24,16},{28,20},{1,9},{5... | collective-permute-start | bytes 393224 | tf_op jit(solution)/shard_map/ppermute | solution.py:537
  11.7 3.8 %collective-permute-start.2 = (bf16[48,128]{1,0:T(8,128)(2,1)S(1)}, bf16[48,128]{1,0:T(8,128)(2,1)S(1)}, u32[]{:S(2)}, u32[]{:S(2)}) collective-permute-start(bf16[48,128]{1,0:T(8,128)(2,1)S(1)} %lags.3.refs_2_), channel_id=1, source_target_pairs={{0,8},{4,12},{8,0},{12,4},{16,24},{20,28},{24,16},{28,20},{1,9},{5... | collective-permute-start | bytes 36872 | tf_op jit(solution)/shard_map/ppermute | solution.py:537
  15.8 4.4 %collective-permute-start.3 = (bf16[304,128]{1,0:T(8,128)(2,1)S(1)}, bf16[304,128]{1,0:T(8,128)(2,1)S(1)}, u32[]{:S(2)}, u32[]{:S(2)}) collective-permute-start(bf16[304,128]{1,0:T(8,128)(2,1)S(1)} %get-tuple-element.50), channel_id=1, source_target_pairs={{0,16},{4,20},{8,24},{12,28},{16,0},{20,4},{24,8},{28,12},{1,17},{... | collective-permute-start | bytes 233480 | tf_op jit(solution)/shard_map/ppermute | solution.py:537
  20.5 5.9 %copy-start = (bf16[128,2048]{1,0:T(8,128)(2,1)S(1)}, bf16[128,2048]{1,0:T(8,128)(2,1)}, u32[]{:S(2)}) copy-start(bf16[128,2048]{1,0:T(8,128)(2,1)} %refs_5_.3) | copy-start | bytes 1572868
  20.6 5.8 %copy-start.1 = (bf16[128,2048]{1,0:T(8,128)(2,1)S(1)}, bf16[128,2048]{1,0:T(8,128)(2,1)}, u32[]{:S(2)}) copy-start(bf16[128,2048]{1,0:T(8,128)(2,1)} %refs_6_.1) | copy-start | bytes 1572868
  20.6 5.8 %copy-start.2 = (bf16[128,2048]{1,0:T(8,128)(2,1)S(1)}, bf16[128,2048]{1,0:T(8,128)(2,1)}, u32[]{:S(2)}) copy-start(bf16[128,2048]{1,0:T(8,128)(2,1)} %refs_7_.1) | copy-start | bytes 1572868
  20.6 1.3 %collective-permute-start.4 = (bf16[304,128]{1,0:T(8,128)(2,1)S(1)}, bf16[304,128]{1,0:T(8,128)(2,1)S(1)}, u32[]{:S(2)}, u32[]{:S(2)}) collective-permute-start(bf16[304,128]{1,0:T(8,128)(2,1)S(1)} %get-tuple-element.52.refs_7_.refs_1_), channel_id=1, source_target_pairs={{0,4},{4,0},{8,12},{12,8},{16,20},{20,16},{24,28},{28,24},{1,5},{5... | collective-permute-start | bytes 233480 | tf_op jit(solution)/shard_map/ppermute | solution.py:537
  21.9 7.2 %collective-permute-start.7 = (bf16[48,128]{1,0:T(8,128)(2,1)S(1)}, bf16[48,128]{1,0:T(8,128)(2,1)S(1)}, u32[]{:S(2)}, u32[]{:S(2)}) collective-permute-start(bf16[48,128]{1,0:T(8,128)(2,1)S(1)} %merge.1.refs_0_), channel_id=1, source_target_pairs={{0,3},{1,2},{2,1},{3,0},{4,7},{5,6},{6,5},{7,4},{8,11},{9,10},{10,... | collective-permute-start | bytes 36872 | tf_op jit(solution)/shard_map/ppermute | solution.py:665
  25.6 4.6 %collective-permute-start.6 = (bf16[48,128]{1,0:T(8,128)(2,1)S(1)}, bf16[48,128]{1,0:T(8,128)(2,1)S(1)}, u32[]{:S(2)}, u32[]{:S(2)}) collective-permute-start(bf16[48,128]{1,0:T(8,128)(2,1)S(1)} %merge.1.refs_0_), channel_id=1, source_target_pairs={{0,2},{1,3},{2,0},{3,1},{4,6},{5,7},{6,4},{7,5},{8,10},{9,11},{10,... | collective-permute-start | bytes 36872 | tf_op jit(solution)/shard_map/ppermute | solution.py:665
  25.6 4.6 %collective-permute-start.5 = (bf16[48,128]{1,0:T(8,128)(2,1)S(1)}, bf16[48,128]{1,0:T(8,128)(2,1)S(1)}, u32[]{:S(2)}, u32[]{:S(2)}) collective-permute-start(bf16[48,128]{1,0:T(8,128)(2,1)S(1)} %merge.1.refs_0_), channel_id=1, source_target_pairs={{0,1},{1,0},{2,3},{3,2},{4,5},{5,4},{6,7},{7,6},{8,9},{9,8},{10,11... | collective-permute-start | bytes 36872 | tf_op jit(solution)/shard_map/ppermute | solution.py:665

commit v19 on v14

--- a/solution.py
+++ b/solution.py
@@ -146,11 +146,12 @@
                         total = jnp.where(wide_group == g, found[j][row : row + poles], total)
                     folded.append(total)
                 out = [folded[0][:, :LANES], folded[0][:, LANES:], folded[1][:, :LANES], folded[1][:, LANES:]]
-                row = pl.multiple_of((step * inner + j) * 4 * poles, 4 * poles)
-                msg_ref[pl.ds(row, 4 * poles), :] = jnp.concatenate(out, axis=0).astype(BF16)
+                row = (step * inner + j) * 4 * poles
+                msg_ref[row : row + 4 * poles, :] = jnp.concatenate(out, axis=0).astype(BF16)
             return carry
 
-        lax.fori_loop(0, half_blocks // inner, body, 0)
+        for step in range(half_steps):
+            body(step, 0)
 
 
 def lags_kernel(lag_rates_ref, gated_ref, dgate_ref, turned_ref, *rest, second, group, poles, inner):

time: 30.5 us -> 30.5 us (level)
  no operation moved by 1% of the time
where the time goes in v19:
time: 30.5 us; the launch traced here: 30.3 us
  Pallas kernels  14 us (46%)
  starting transfers between devices  9.51 us (31%)
  waiting for transfers between devices  5.23 us (17%)
  other arithmetic  0.78 us (3%)
  between operations  0.78 us (3%)
    ppermute x5, starting transfers between devices, swap(): lax.ppermute(value, 'ctx', [(i, i ^ 1 << level) for i in range(parts)])  5.06 us
    ppermute x3, starting transfers between devices, local(): lax.ppermute(merged, 'ch', [(i, i ^ mask) for i in range(shards)])  4.45 us
    ppermute x5, waiting for transfers between devices, swap(): lax.ppermute(value, 'ctx', [(i, i ^ 1 << level) for i in range(parts)])  4.16 us
    pallas_call x2, Pallas kernels, convolve(): pl.pallas_call(lambda *refs: conv_kernel(*refs, first_step=first_step, in...  3.64 us
    pallas_call x1, Pallas kernels, local(): pl.pallas_call(lambda *refs: states_kernel(*refs, inner=inner, **sizes),...  3.08 us
    pallas_call x1, Pallas kernels, local(): pl.pallas_call(lambda *refs: output_kernel(*refs, **sizes), grid=(steps,)...  2.74 us
    pallas_call x2, Pallas kernels, local_sums(): pl.pallas_call(lambda *refs: lags_kernel(*refs, second=second, inner=inne...  2.71 us
    ppermute x3, waiting for transfers between devices, local(): lax.ppermute(merged, 'ch', [(i, i ^ mask) for i in range(shards)])  1.08 us
  transfers between devices with their start and end apart: 8, of which 4 were waited for; matrix products, arithmetic and copies ran while one was open for 0% of the time, Pallas kernels for 31%

profile of v19, /device:TPU:0, one launch (start us, length us, event | category | flops | bytes accessed | tf_op | source)
XLA Modules:
  0.0 30.3 jit_solution(2364634650005779289)
XLA Ops:
  0.6 0.8 %pad_maximum_fusion.refs_0_ = f32[2,16,512]{2,1,0:T(8,128)S(1)} fusion(f32[1,16,512]{2,1,0:T(8,128)} %bitcast.12, f32[1,16,512]{2,1,0:T(8,128)} %bitcast.13), kind=kLoop, calls=%fused_computation | loop fusion | flops 16384 | bytes 131072 | tf_op jit(solution)/shard_map/stack | solution.py:529
  1.4 3.1 %states.1 = (bf16[512,128]{1,0:T(8,128)(2,1)S(1)}, bf16[512,128]{1,0:T(8,128)(2,1)S(1)}, bf16[128,2048]{1,0:T(8,128)(2,1)S(1)}, bf16[128,2048]{1,0:T(8,128)(2,1)...) custom-call(f32[2,16,512]{2,1,0:T(8,128)S(1)} %pad_maximum_fusion.refs_0_, ...), custom_call_target="tpu_custom_call" | custom-call | tf_op jit(solution)/shard_map/states/pallas_call | solution.py:512
  4.5 0.5 %collective-permute-start = (bf16[512,128]{1,0:T(8,128)(2,1)S(1)}, bf16[512,128]{1,0:T(8,128)(2,1)S(1)}, u32[]{:S(2)}, u32[]{:S(2)}) collective-permute-start(bf16[512,128]{1,0:T(8,128)(2,1)S(1)} %get-tuple-element.37), channel_id=1, source_target_pairs={{0,4},{4,0},{8,12},{12,8},{16,20},{20,16},{24,28},{28,24},{1,5},{5... | collective-permute-start | bytes 393224 | tf_op jit(solution)/shard_map/ppermute | solution.py:509
  5.0 0.4 %tables.1 = (f32[16,16,128]{2,1,0:T(8,128)S(1)}, f32[16,16,256]{2,1,0:T(8,128)S(1)}) custom-call(f32[2,16,128]{2,1,0:T(8,128)S(1)} %get-tuple-element.31.refs_0_), custom_call_target="tpu_custom_call" | custom-call | flops 1000000000 | bytes 1000000 | tf_op jit(solution)/shard_map/tables/pallas_call | solution.py:531
  5.4 0.7 %lags.2.refs_3_ = f32[32,128]{1,0:T(8,128)S(1)} custom-call(f32[16,16,256]{2,1,0:T(8,128)S(1)} %get-tuple-element.33.refs_0_.refs_4_, bf16[128,2048]{1,0:T(8,128)(2,1)S(1)} %get-tuple-element.34.refs_1_.refs_5_, bf16[128,2048]{1,0:T(8,128)(2,1)S(1)} %get-tuple-element.38.refs_2_, bf16[128,2048]{1,0:T(8,128)(2,1)S(1)} %get-tuple-element.35.refs_3_.refs_6_), custom_call_target="tpu_custom_call" | custom-call | flops 536870912 | bytes 3145728 | tf_op jit(solution)/shard_map/lags/pallas_call | solution.py:546
  6.1 0.0 copy-start.3
  6.1 0.0 collective-permute-done.refs_2_
  6.1 0.3 combine.3
  6.4 2.8 %collective-permute-start.1 = (bf16[512,128]{1,0:T(8,128)(2,1)S(1)}, bf16[512,128]{1,0:T(8,128)(2,1)S(1)}, u32[]{:S(2)}, u32[]{:S(2)}) collective-permute-start(bf16[512,128]{1,0:T(8,128)(2,1)S(1)} %get-tuple-element.39.refs_1_), channel_id=1, source_target_pairs={{0,8},{4,12},{8,0},{12,4},{16,24},{20,28},{24,16},{28,20},{1,9},{5... | collective-permute-start | bytes 393224 | tf_op jit(solution)/shard_map/ppermute | solution.py:509
  9.2 2.0 %lags.3.refs_2_ = bf16[48,128]{1,0:T(8,128)(2,1)S(1)} custom-call(f32[16,16,256]{2,1,0:T(8,128)S(1)} %get-tuple-element.33.refs_0_.refs_4_, bf16[128,2048]{1,0:T(8,128)(2,1)S(1)} %get-tuple-element.34.refs_1_.refs_5_, bf16[128,2048]{1,0:T(8,128)(2,1)S(1)} %get-tuple-element.38.refs_2_, bf16[128,2048]{1,0:T(8,128)(2,1)S(1)} %get-tuple-element.35.refs_3_.refs_6_, ...), custom_call_target="tpu_custom_call" | custom-call | flops 536870912 | bytes 3145728 | tf_op jit(solution)/shard_map/lags/pallas_call | solution.py:546
  11.2 0.1 collective-permute-start.2
  11.3 3.7 %collective-permute-done.2.refs_4_ = bf16[48,128]{1,0:T(8,128)(2,1)S(1)} collective-permute-done((bf16[48,128]{1,0:T(8,128)(2,1)S(1)}, bf16[48,128]{1,0:T(8,128)(2,1)S(1)}, u32[]{:S(2)}, u32[]{:S(2)}) %collective-permute-start.2) | collective-permute-done | bytes 12320 | tf_op jit(solution)/shard_map/ppermute | solution.py:509
  15.0 0.0 collective-permute-done.1.refs_3_
  15.0 0.3 combine.4
  15.3 1.6 %collective-permute-start.3 = (bf16[304,128]{1,0:T(8,128)(2,1)S(1)}, bf16[304,128]{1,0:T(8,128)(2,1)S(1)}, u32[]{:S(2)}, u32[]{:S(2)}) collective-permute-start(bf16[304,128]{1,0:T(8,128)(2,1)S(1)} %get-tuple-element.44), channel_id=1, source_target_pairs={{0,16},{4,20},{8,24},{12,28},{16,0},{20,4},{24,8},{28,12},{1,17},{... | collective-permute-start | bytes 233480 | tf_op jit(solution)/shard_map/ppermute | solution.py:509
  16.9 0.0 copy-done.3
  16.9 2.7 %conv.2.refs_5_.refs_1_ = f32[128,3072]{1,0:T(8,128)S(1)} custom-call(f32[2,16,128]{2,1,0:T(8,128)S(1)} %get-tuple-element.31.refs_0_, f32[2,16,128]{2,1,0:T(8,128)S(1)} %get-tuple-element.30.refs_1_.refs_0_, f32[64,128]{1,0:T(8,128)S(1)} %bitcast.10, f32[16,16,128]{2,1,0:T(8,128)S(1)} %get-tuple-element.32.refs_0_.refs_3_, ...), custom_call_target="tpu_custom_call" | custom-call | flops 536870912 | bytes 3145728 | tf_op jit(solution)/shard_map/conv/pallas_call | solution.py:559
  19.6 0.1 collective-permute-done.3.refs_3_
  19.7 0.3 combine.5
  20.0 0.0 copy-start
  20.0 0.0 copy-start.1
  20.0 0.0 copy-start.2
  20.1 0.1 collective-permute-start.4
  20.1 0.9 %conv.3.refs_2_.refs_3_ = f32[128,1024]{1,0:T(8,128)S(1)} custom-call(f32[2,16,128]{2,1,0:T(8,128)S(1)} %get-tuple-element.31.refs_0_, f32[2,16,128]{2,1,0:T(8,128)S(1)} %get-tuple-element.30.refs_1_.refs_0_, f32[64,128]{1,0:T(8,128)S(1)} %bitcast.11, f32[16,16,128]{2,1,0:T(8,128)S(1)} %get-tuple-element.32.refs_0_.refs_3_, ...), custom_call_target="tpu_custom_call" | custom-call | flops 536870912 | bytes 3145728 | tf_op jit(solution)/shard_map/conv/pallas_call | solution.py:559
  21.1 0.3 %collective-permute-done.4.refs_4_.refs_2_ = bf16[304,128]{1,0:T(8,128)(2,1)S(1)} collective-permute-done((bf16[304,128]{1,0:T(8,128)(2,1)S(1)}, bf16[304,128]{1,0:T(8,128)(2,1)S(1)}, u32[]{:S(2)}, u32[]{:S(2)}) %collective-permute-start.4) | collective-permute-done | bytes 77856 | tf_op jit(solution)/shard_map/ppermute | solution.py:509
  21.4 3.7 %collective-permute-start.7 = (bf16[48,128]{1,0:T(8,128)(2,1)S(1)}, bf16[48,128]{1,0:T(8,128)(2,1)S(1)}, u32[]{:S(2)}, u32[]{:S(2)}) collective-permute-start(bf16[48,128]{1,0:T(8,128)(2,1)S(1)} %merge.1.refs_0_), channel_id=1, source_target_pairs={{0,3},{1,2},{2,1},{3,0},{4,7},{5,6},{6,5},{7,4},{8,11},{9,10},{10,... | collective-permute-start | bytes 36872 | tf_op jit(solution)/shard_map/ppermute | solution.py:626
  25.1 0.0 collective-permute-start.6
  25.1 0.8 %collective-permute-start.5 = (bf16[48,128]{1,0:T(8,128)(2,1)S(1)}, bf16[48,128]{1,0:T(8,128)(2,1)S(1)}, u32[]{:S(2)}, u32[]{:S(2)}) collective-permute-start(bf16[48,128]{1,0:T(8,128)(2,1)S(1)} %merge.1.refs_0_), channel_id=1, source_target_pairs={{0,1},{1,0},{2,3},{3,2},{4,5},{5,4},{6,7},{7,6},{8,9},{9,8},{10,11... | collective-permute-start | bytes 36872 | tf_op jit(solution)/shard_map/ppermute | solution.py:626
  25.9 0.0 copy-done
  25.9 0.0 copy-done.1
  25.9 0.0 copy-done.2
  25.9 2.7 %outputs.1 = (bf16[128,2048]{1,0:T(8,128)(2,1)}, bf16[128,2048]{1,0:T(8,128)(2,1)}, bf16[128,2048]{1,0:T(8,128)(2,1)}) custom-call(f32[2,16,128]{2,1,0:T(8,128)S(1)} %get-tuple-element.30.refs_1_.refs_0_, f32[128,3072]{1,0:T(8,128)S(1)} %conv.2.refs_5_.refs_1_, f32[128,1024]{1,0:T(8,128)S(1)} %conv.3.refs_2_.refs_3_, ...), custom_call_target="tpu_custom_call" | custom-call | flops 536870912 | bytes 3145728 | tf_op jit(solution)/shard_map/outputs/pallas_call | solution.py:629
  28.6 0.0 collective-permute-done.7.refs_3_
  28.6 1.1 %collective-permute-done.6.refs_2_ = bf16[48,128]{1,0:T(8,128)(2,1)S(1)} collective-permute-done((bf16[48,128]{1,0:T(8,128)(2,1)S(1)}, bf16[48,128]{1,0:T(8,128)(2,1)S(1)}, u32[]{:S(2)}, u32[]{:S(2)}) %collective-permute-start.6) | collective-permute-done | bytes 12320 | tf_op jit(solution)/shard_map/ppermute | solution.py:626
  29.7 0.0 collective-permute-done.5.refs_1_
  29.7 0.6 %assemble.1 = (f32[16,512]{1,0:T(8,128)}, f32[16,512]{1,0:T(8,128)}, f32[64,128]{1,0:T(8,128)}) custom-call(bf16[48,128]{1,0:T(8,128)(2,1)S(1)} %merge.1.refs_0_, bf16[48,128]{1,0:T(8,128)(2,1)S(1)} %collective-permute-done.5.refs_1_, bf16[48,128]{1,0:T(8,128)(2,1)S(1)} %collective-permute-done.6.refs_2_, bf16[48,128]{1,0:T(8,128)(2,1)S(1)} %collective-permute-done.7.refs_3_), custom_call_target="tpu_custom_call" | custom-call | tf_op jit(solution)/shard_map/assemble/pallas_call | solution.py:640
  (1 shorter events, 0.0 us)
Async XLA Ops:
  4.5 1.6 %collective-permute-start = (bf16[512,128]{1,0:T(8,128)(2,1)S(1)}, bf16[512,128]{1,0:T(8,128)(2,1)S(1)}, u32[]{:S(2)}, u32[]{:S(2)}) collective-permute-start(bf16[512,128]{1,0:T(8,128)(2,1)S(1)} %get-tuple-element.37), channel_id=1, source_target_pairs={{0,4},{4,0},{8,12},{12,8},{16,20},{20,16},{24,28},{28,24},{1,5},{5... | collective-permute-start | bytes 393224 | tf_op jit(solution)/shard_map/ppermute | solution.py:509
  6.1 10.8 %copy-start.3 = (f32[8192]{0:T(1024)S(1)}, f32[8192]{0:T(1024)}, u32[]{:S(2)}) copy-start(f32[8192]{0:T(1024)} %param.13) | copy-start | bytes 98308
  6.4 8.6 %collective-permute-start.1 = (bf16[512,128]{1,0:T(8,128)(2,1)S(1)}, bf16[512,128]{1,0:T(8,128)(2,1)S(1)}, u32[]{:S(2)}, u32[]{:S(2)}) collective-permute-start(bf16[512,128]{1,0:T(8,128)(2,1)S(1)} %get-tuple-element.39.refs_1_), channel_id=1, source_target_pairs={{0,8},{4,12},{8,0},{12,4},{16,24},{20,28},{24,16},{28,20},{1,9},{5... | collective-permute-start | bytes 393224 | tf_op jit(solution)/shard_map/ppermute | solution.py:509
  11.2 3.8 %collective-permute-start.2 = (bf16[48,128]{1,0:T(8,128)(2,1)S(1)}, bf16[48,128]{1,0:T(8,128)(2,1)S(1)}, u32[]{:S(2)}, u32[]{:S(2)}) collective-permute-start(bf16[48,128]{1,0:T(8,128)(2,1)S(1)} %lags.3.refs_2_), channel_id=1, source_target_pairs={{0,8},{4,12},{8,0},{12,4},{16,24},{20,28},{24,16},{28,20},{1,9},{5... | collective-permute-start | bytes 36872 | tf_op jit(solution)/shard_map/ppermute | solution.py:509
  15.3 4.4 %collective-permute-start.3 = (bf16[304,128]{1,0:T(8,128)(2,1)S(1)}, bf16[304,128]{1,0:T(8,128)(2,1)S(1)}, u32[]{:S(2)}, u32[]{:S(2)}) collective-permute-start(bf16[304,128]{1,0:T(8,128)(2,1)S(1)} %get-tuple-element.44), channel_id=1, source_target_pairs={{0,16},{4,20},{8,24},{12,28},{16,0},{20,4},{24,8},{28,12},{1,17},{... | collective-permute-start | bytes 233480 | tf_op jit(solution)/shard_map/ppermute | solution.py:509
  20.0 5.9 %copy-start = (bf16[128,2048]{1,0:T(8,128)(2,1)S(1)}, bf16[128,2048]{1,0:T(8,128)(2,1)}, u32[]{:S(2)}) copy-start(bf16[128,2048]{1,0:T(8,128)(2,1)} %refs_5_.1) | copy-start | bytes 1572868
  20.0 5.8 %copy-start.1 = (bf16[128,2048]{1,0:T(8,128)(2,1)S(1)}, bf16[128,2048]{1,0:T(8,128)(2,1)}, u32[]{:S(2)}) copy-start(bf16[128,2048]{1,0:T(8,128)(2,1)} %refs_6_.1) | copy-start | bytes 1572868
  20.0 5.8 %copy-start.2 = (bf16[128,2048]{1,0:T(8,128)(2,1)S(1)}, bf16[128,2048]{1,0:T(8,128)(2,1)}, u32[]{:S(2)}) copy-start(bf16[128,2048]{1,0:T(8,128)(2,1)} %refs_7_.1) | copy-start | bytes 1572868
  20.1 1.3 %collective-permute-start.4 = (bf16[304,128]{1,0:T(8,128)(2,1)S(1)}, bf16[304,128]{1,0:T(8,128)(2,1)S(1)}, u32[]{:S(2)}, u32[]{:S(2)}) collective-permute-start(bf16[304,128]{1,0:T(8,128)(2,1)S(1)} %get-tuple-element.46.refs_7_.refs_1_), channel_id=1, source_target_pairs={{0,4},{4,0},{8,12},{12,8},{16,20},{20,16},{24,28},{28,24},{1,5},{5... | collective-permute-start | bytes 233480 | tf_op jit(solution)/shard_map/ppermute | solution.py:509
  21.4 7.2 %collective-permute-start.7 = (bf16[48,128]{1,0:T(8,128)(2,1)S(1)}, bf16[48,128]{1,0:T(8,128)(2,1)S(1)}, u32[]{:S(2)}, u32[]{:S(2)}) collective-permute-start(bf16[48,128]{1,0:T(8,128)(2,1)S(1)} %merge.1.refs_0_), channel_id=1, source_target_pairs={{0,3},{1,2},{2,1},{3,0},{4,7},{5,6},{6,5},{7,4},{8,11},{9,10},{10,... | collective-permute-start | bytes 36872 | tf_op jit(solution)/shard_map/ppermute | solution.py:626
  25.1 4.6 %collective-permute-start.6 = (bf16[48,128]{1,0:T(8,128)(2,1)S(1)}, bf16[48,128]{1,0:T(8,128)(2,1)S(1)}, u32[]{:S(2)}, u32[]{:S(2)}) collective-permute-start(bf16[48,128]{1,0:T(8,128)(2,1)S(1)} %merge.1.refs_0_), channel_id=1, source_target_pairs={{0,2},{1,3},{2,0},{3,1},{4,6},{5,7},{6,4},{7,5},{8,10},{9,11},{10,... | collective-permute-start | bytes 36872 | tf_op jit(solution)/shard_map/ppermute | solution.py:626
  25.1 4.6 %collective-permute-start.5 = (bf16[48,128]{1,0:T(8,128)(2,1)S(1)}, bf16[48,128]{1,0:T(8,128)(2,1)S(1)}, u32[]{:S(2)}, u32[]{:S(2)}) collective-permute-start(bf16[48,128]{1,0:T(8,128)(2,1)S(1)} %merge.1.refs_0_), channel_id=1, source_target_pairs={{0,1},{1,0},{2,3},{3,2},{4,5},{5,4},{6,7},{7,6},{8,9},{9,8},{10,11... | collective-permute-start | bytes 36872 | tf_op jit(solution)/shard_map/ppermute | solution.py:626

commit v20 on v19

--- a/solution.py
+++ b/solution.py
@@ -510,7 +510,7 @@
 
     far = pl.BlockSpec(memory_space=pl.ANY)
     outgoing, message, gated, dgate, turned, rows, params = pl.pallas_call(
-        lambda *refs: states_kernel(*refs, inner=inner, **sizes),
+        lambda *refs: states_kernel(*refs, inner=inner // 2, **sizes),
         in_specs=[vmem] + [far] * 4,
         out_specs=[vmem] * 7,
         out_shape=[
@@ -523,7 +523,7 @@
             shape(2, poles, groups),
         ],
         scratch_shapes=[pltpu.VMEM((tokens, width), BF16)] * 4
-        + [pltpu.SemaphoreType.DMA((4, steps))],
+        + [pltpu.SemaphoreType.DMA((4, 2 * steps))],
         compiler_params=pltpu.CompilerParams(vmem_limit_bytes=53000 * 1024),
         name="states",
     )(jnp.stack([log_rates, residues]), queries, key_input, value_input, cotangent)

time: 30.5 us -> 31.7 us (1.039)
  Pallas kernels: 14 us -> 15.2 us
    pallas_call x1, Pallas kernels: 3.08 us -> 4.25 us  [local(): pl.pallas_call(lambda *refs: states_kernel(*refs, inner=inner // 2, **siz...]
  transfers between devices with their start and end apart: 8 -> 8, of which waited for: 4 -> 4; matrix products, arithmetic and copies ran while one was open for 0% -> 0% of each run, Pallas kernels for 31% -> 30%
where the time goes in v20:
time: 31.7 us; the launch traced here: 31.5 us
  Pallas kernels  15.2 us (48%)
  starting transfers between devices  9.5 us (30%)
  waiting for transfers between devices  5.23 us (16%)
  other arithmetic  0.78 us (2%)
  between operations  0.78 us (2%)
    ppermute x5, starting transfers between devices, swap(): lax.ppermute(value, 'ctx', [(i, i ^ 1 << level) for i in range(parts)])  5.05 us
    ppermute x3, starting transfers between devices, local(): lax.ppermute(merged, 'ch', [(i, i ^ mask) for i in range(shards)])  4.45 us
    pallas_call x1, Pallas kernels, local(): pl.pallas_call(lambda *refs: states_kernel(*refs, inner=inner // 2, **siz...  4.25 us
    ppermute x5, waiting for transfers between devices, swap(): lax.ppermute(value, 'ctx', [(i, i ^ 1 << level) for i in range(parts)])  4.17 us
    pallas_call x2, Pallas kernels, convolve(): pl.pallas_call(lambda *refs: conv_kernel(*refs, first_step=first_step, in...  3.63 us
    pallas_call x1, Pallas kernels, local(): pl.pallas_call(lambda *refs: output_kernel(*refs, **sizes), grid=(steps,)...  2.74 us
    pallas_call x2, Pallas kernels, local_sums(): pl.pallas_call(lambda *refs: lags_kernel(*refs, second=second, inner=inne...  2.71 us
    ppermute x3, waiting for transfers between devices, local(): lax.ppermute(merged, 'ch', [(i, i ^ mask) for i in range(shards)])  1.07 us
  transfers between devices with their start and end apart: 8, of which 4 were waited for; matrix products, arithmetic and copies ran while one was open for 0% of the time, Pallas kernels for 30%

profile of v20, /device:TPU:0, one launch (start us, length us, event | category | flops | bytes accessed | tf_op | source)
XLA Modules:
  0.0 31.5 jit_solution(8500261975280244430)
XLA Ops:
  0.6 0.8 %pad_maximum_fusion.refs_0_ = f32[2,16,512]{2,1,0:T(8,128)S(1)} fusion(f32[1,16,512]{2,1,0:T(8,128)} %bitcast.12, f32[1,16,512]{2,1,0:T(8,128)} %bitcast.13), kind=kLoop, calls=%fused_computation | loop fusion | flops 16384 | bytes 131072 | tf_op jit(solution)/shard_map/stack | solution.py:529
  1.4 4.2 %states.1 = (bf16[512,128]{1,0:T(8,128)(2,1)S(1)}, bf16[512,128]{1,0:T(8,128)(2,1)S(1)}, bf16[128,2048]{1,0:T(8,128)(2,1)S(1)}, bf16[128,2048]{1,0:T(8,128)(2,1)...) custom-call(f32[2,16,512]{2,1,0:T(8,128)S(1)} %pad_maximum_fusion.refs_0_, ...), custom_call_target="tpu_custom_call" | custom-call | tf_op jit(solution)/shard_map/states/pallas_call | solution.py:512
  5.7 0.5 %collective-permute-start = (bf16[512,128]{1,0:T(8,128)(2,1)S(1)}, bf16[512,128]{1,0:T(8,128)(2,1)S(1)}, u32[]{:S(2)}, u32[]{:S(2)}) collective-permute-start(bf16[512,128]{1,0:T(8,128)(2,1)S(1)} %get-tuple-element.37), channel_id=1, source_target_pairs={{0,4},{4,0},{8,12},{12,8},{16,20},{20,16},{24,28},{28,24},{1,5},{5... | collective-permute-start | bytes 393224 | tf_op jit(solution)/shard_map/ppermute | solution.py:509
  6.2 0.4 %tables.1 = (f32[16,16,128]{2,1,0:T(8,128)S(1)}, f32[16,16,256]{2,1,0:T(8,128)S(1)}) custom-call(f32[2,16,128]{2,1,0:T(8,128)S(1)} %get-tuple-element.31.refs_0_), custom_call_target="tpu_custom_call" | custom-call | flops 1000000000 | bytes 1000000 | tf_op jit(solution)/shard_map/tables/pallas_call | solution.py:531
  6.5 0.7 %lags.2.refs_3_ = f32[32,128]{1,0:T(8,128)S(1)} custom-call(f32[16,16,256]{2,1,0:T(8,128)S(1)} %get-tuple-element.33.refs_0_.refs_4_, bf16[128,2048]{1,0:T(8,128)(2,1)S(1)} %get-tuple-element.34.refs_1_.refs_5_, bf16[128,2048]{1,0:T(8,128)(2,1)S(1)} %get-tuple-element.38.refs_2_, bf16[128,2048]{1,0:T(8,128)(2,1)S(1)} %get-tuple-element.35.refs_3_.refs_6_), custom_call_target="tpu_custom_call" | custom-call | flops 536870912 | bytes 3145728 | tf_op jit(solution)/shard_map/lags/pallas_call | solution.py:546
  7.2 0.0 copy-start.3
  7.3 0.0 collective-permute-done.refs_2_
  7.3 0.3 combine.3
  7.5 2.8 %collective-permute-start.1 = (bf16[512,128]{1,0:T(8,128)(2,1)S(1)}, bf16[512,128]{1,0:T(8,128)(2,1)S(1)}, u32[]{:S(2)}, u32[]{:S(2)}) collective-permute-start(bf16[512,128]{1,0:T(8,128)(2,1)S(1)} %get-tuple-element.39.refs_1_), channel_id=1, source_target_pairs={{0,8},{4,12},{8,0},{12,4},{16,24},{20,28},{24,16},{28,20},{1,9},{5... | collective-permute-start | bytes 393224 | tf_op jit(solution)/shard_map/ppermute | solution.py:509
  10.4 2.0 %lags.3.refs_2_ = bf16[48,128]{1,0:T(8,128)(2,1)S(1)} custom-call(f32[16,16,256]{2,1,0:T(8,128)S(1)} %get-tuple-element.33.refs_0_.refs_4_, bf16[128,2048]{1,0:T(8,128)(2,1)S(1)} %get-tuple-element.34.refs_1_.refs_5_, bf16[128,2048]{1,0:T(8,128)(2,1)S(1)} %get-tuple-element.38.refs_2_, bf16[128,2048]{1,0:T(8,128)(2,1)S(1)} %get-tuple-element.35.refs_3_.refs_6_, ...), custom_call_target="tpu_custom_call" | custom-call | flops 536870912 | bytes 3145728 | tf_op jit(solution)/shard_map/lags/pallas_call | solution.py:546
  12.4 0.1 collective-permute-start.2
  12.5 3.7 %collective-permute-done.2.refs_4_ = bf16[48,128]{1,0:T(8,128)(2,1)S(1)} collective-permute-done((bf16[48,128]{1,0:T(8,128)(2,1)S(1)}, bf16[48,128]{1,0:T(8,128)(2,1)S(1)}, u32[]{:S(2)}, u32[]{:S(2)}) %collective-permute-start.2) | collective-permute-done | bytes 12320 | tf_op jit(solution)/shard_map/ppermute | solution.py:509
  16.1 0.0 collective-permute-done.1.refs_3_
  16.1 0.3 combine.4
  16.4 1.6 %collective-permute-start.3 = (bf16[304,128]{1,0:T(8,128)(2,1)S(1)}, bf16[304,128]{1,0:T(8,128)(2,1)S(1)}, u32[]{:S(2)}, u32[]{:S(2)}) collective-permute-start(bf16[304,128]{1,0:T(8,128)(2,1)S(1)} %get-tuple-element.44), channel_id=1, source_target_pairs={{0,16},{4,20},{8,24},{12,28},{16,0},{20,4},{24,8},{28,12},{1,17},{... | collective-permute-start | bytes 233480 | tf_op jit(solution)/shard_map/ppermute | solution.py:509
  18.0 0.0 copy-done.3
  18.0 2.7 %conv.2.refs_5_.refs_1_ = f32[128,3072]{1,0:T(8,128)S(1)} custom-call(f32[2,16,128]{2,1,0:T(8,128)S(1)} %get-tuple-element.31.refs_0_, f32[2,16,128]{2,1,0:T(8,128)S(1)} %get-tuple-element.30.refs_1_.refs_0_, f32[64,128]{1,0:T(8,128)S(1)} %bitcast.10, f32[16,16,128]{2,1,0:T(8,128)S(1)} %get-tuple-element.32.refs_0_.refs_3_, ...), custom_call_target="tpu_custom_call" | custom-call | flops 536870912 | bytes 3145728 | tf_op jit(solution)/shard_map/conv/pallas_call | solution.py:559
  20.7 0.1 collective-permute-done.3.refs_3_
  20.9 0.3 combine.5
  21.1 0.0 copy-start
  21.2 0.0 copy-start.1
  21.2 0.0 copy-start.2
  21.2 0.1 collective-permute-start.4
  21.3 0.9 %conv.3.refs_2_.refs_3_ = f32[128,1024]{1,0:T(8,128)S(1)} custom-call(f32[2,16,128]{2,1,0:T(8,128)S(1)} %get-tuple-element.31.refs_0_, f32[2,16,128]{2,1,0:T(8,128)S(1)} %get-tuple-element.30.refs_1_.refs_0_, f32[64,128]{1,0:T(8,128)S(1)} %bitcast.11, f32[16,16,128]{2,1,0:T(8,128)S(1)} %get-tuple-element.32.refs_0_.refs_3_, ...), custom_call_target="tpu_custom_call" | custom-call | flops 536870912 | bytes 3145728 | tf_op jit(solution)/shard_map/conv/pallas_call | solution.py:559
  22.2 0.3 %collective-permute-done.4.refs_4_.refs_2_ = bf16[304,128]{1,0:T(8,128)(2,1)S(1)} collective-permute-done((bf16[304,128]{1,0:T(8,128)(2,1)S(1)}, bf16[304,128]{1,0:T(8,128)(2,1)S(1)}, u32[]{:S(2)}, u32[]{:S(2)}) %collective-permute-start.4) | collective-permute-done | bytes 77856 | tf_op jit(solution)/shard_map/ppermute | solution.py:509
  22.6 3.7 %collective-permute-start.7 = (bf16[48,128]{1,0:T(8,128)(2,1)S(1)}, bf16[48,128]{1,0:T(8,128)(2,1)S(1)}, u32[]{:S(2)}, u32[]{:S(2)}) collective-permute-start(bf16[48,128]{1,0:T(8,128)(2,1)S(1)} %merge.1.refs_0_), channel_id=1, source_target_pairs={{0,3},{1,2},{2,1},{3,0},{4,7},{5,6},{6,5},{7,4},{8,11},{9,10},{10,... | collective-permute-start | bytes 36872 | tf_op jit(solution)/shard_map/ppermute | solution.py:626
  26.2 0.0 collective-permute-start.6
  26.2 0.8 %collective-permute-start.5 = (bf16[48,128]{1,0:T(8,128)(2,1)S(1)}, bf16[48,128]{1,0:T(8,128)(2,1)S(1)}, u32[]{:S(2)}, u32[]{:S(2)}) collective-permute-start(bf16[48,128]{1,0:T(8,128)(2,1)S(1)} %merge.1.refs_0_), channel_id=1, source_target_pairs={{0,1},{1,0},{2,3},{3,2},{4,5},{5,4},{6,7},{7,6},{8,9},{9,8},{10,11... | collective-permute-start | bytes 36872 | tf_op jit(solution)/shard_map/ppermute | solution.py:626
  27.0 0.0 copy-done
  27.0 0.0 copy-done.1
  27.0 0.0 copy-done.2
  27.0 2.7 %outputs.1 = (bf16[128,2048]{1,0:T(8,128)(2,1)}, bf16[128,2048]{1,0:T(8,128)(2,1)}, bf16[128,2048]{1,0:T(8,128)(2,1)}) custom-call(f32[2,16,128]{2,1,0:T(8,128)S(1)} %get-tuple-element.30.refs_1_.refs_0_, f32[128,3072]{1,0:T(8,128)S(1)} %conv.2.refs_5_.refs_1_, f32[128,1024]{1,0:T(8,128)S(1)} %conv.3.refs_2_.refs_3_, ...), custom_call_target="tpu_custom_call" | custom-call | flops 536870912 | bytes 3145728 | tf_op jit(solution)/shard_map/outputs/pallas_call | solution.py:629
  29.8 0.0 collective-permute-done.7.refs_3_
  29.8 1.1 %collective-permute-done.6.refs_2_ = bf16[48,128]{1,0:T(8,128)(2,1)S(1)} collective-permute-done((bf16[48,128]{1,0:T(8,128)(2,1)S(1)}, bf16[48,128]{1,0:T(8,128)(2,1)S(1)}, u32[]{:S(2)}, u32[]{:S(2)}) %collective-permute-start.6) | collective-permute-done | bytes 12320 | tf_op jit(solution)/shard_map/ppermute | solution.py:626
  30.8 0.0 collective-permute-done.5.refs_1_
  30.8 0.6 %assemble.1 = (f32[16,512]{1,0:T(8,128)}, f32[16,512]{1,0:T(8,128)}, f32[64,128]{1,0:T(8,128)}) custom-call(bf16[48,128]{1,0:T(8,128)(2,1)S(1)} %merge.1.refs_0_, bf16[48,128]{1,0:T(8,128)(2,1)S(1)} %collective-permute-done.5.refs_1_, bf16[48,128]{1,0:T(8,128)(2,1)S(1)} %collective-permute-done.6.refs_2_, bf16[48,128]{1,0:T(8,128)(2,1)S(1)} %collective-permute-done.7.refs_3_), custom_call_target="tpu_custom_call" | custom-call | tf_op jit(solution)/shard_map/assemble/pallas_call | solution.py:640
  (1 shorter events, 0.0 us)
Async XLA Ops:
  5.7 1.6 %collective-permute-start = (bf16[512,128]{1,0:T(8,128)(2,1)S(1)}, bf16[512,128]{1,0:T(8,128)(2,1)S(1)}, u32[]{:S(2)}, u32[]{:S(2)}) collective-permute-start(bf16[512,128]{1,0:T(8,128)(2,1)S(1)} %get-tuple-element.37), channel_id=1, source_target_pairs={{0,4},{4,0},{8,12},{12,8},{16,20},{20,16},{24,28},{28,24},{1,5},{5... | collective-permute-start | bytes 393224 | tf_op jit(solution)/shard_map/ppermute | solution.py:509
  7.2 10.8 %copy-start.3 = (f32[8192]{0:T(1024)S(1)}, f32[8192]{0:T(1024)}, u32[]{:S(2)}) copy-start(f32[8192]{0:T(1024)} %param.13) | copy-start | bytes 98308
  7.5 8.6 %collective-permute-start.1 = (bf16[512,128]{1,0:T(8,128)(2,1)S(1)}, bf16[512,128]{1,0:T(8,128)(2,1)S(1)}, u32[]{:S(2)}, u32[]{:S(2)}) collective-permute-start(bf16[512,128]{1,0:T(8,128)(2,1)S(1)} %get-tuple-element.39.refs_1_), channel_id=1, source_target_pairs={{0,8},{4,12},{8,0},{12,4},{16,24},{20,28},{24,16},{28,20},{1,9},{5... | collective-permute-start | bytes 393224 | tf_op jit(solution)/shard_map/ppermute | solution.py:509
  12.4 3.8 %collective-permute-start.2 = (bf16[48,128]{1,0:T(8,128)(2,1)S(1)}, bf16[48,128]{1,0:T(8,128)(2,1)S(1)}, u32[]{:S(2)}, u32[]{:S(2)}) collective-permute-start(bf16[48,128]{1,0:T(8,128)(2,1)S(1)} %lags.3.refs_2_), channel_id=1, source_target_pairs={{0,8},{4,12},{8,0},{12,4},{16,24},{20,28},{24,16},{28,20},{1,9},{5... | collective-permute-start | bytes 36872 | tf_op jit(solution)/shard_map/ppermute | solution.py:509
  16.4 4.4 %collective-permute-start.3 = (bf16[304,128]{1,0:T(8,128)(2,1)S(1)}, bf16[304,128]{1,0:T(8,128)(2,1)S(1)}, u32[]{:S(2)}, u32[]{:S(2)}) collective-permute-start(bf16[304,128]{1,0:T(8,128)(2,1)S(1)} %get-tuple-element.44), channel_id=1, source_target_pairs={{0,16},{4,20},{8,24},{12,28},{16,0},{20,4},{24,8},{28,12},{1,17},{... | collective-permute-start | bytes 233480 | tf_op jit(solution)/shard_map/ppermute | solution.py:509
  21.1 5.9 %copy-start = (bf16[128,2048]{1,0:T(8,128)(2,1)S(1)}, bf16[128,2048]{1,0:T(8,128)(2,1)}, u32[]{:S(2)}) copy-start(bf16[128,2048]{1,0:T(8,128)(2,1)} %refs_5_.1) | copy-start | bytes 1572868
  21.2 5.8 %copy-start.1 = (bf16[128,2048]{1,0:T(8,128)(2,1)S(1)}, bf16[128,2048]{1,0:T(8,128)(2,1)}, u32[]{:S(2)}) copy-start(bf16[128,2048]{1,0:T(8,128)(2,1)} %refs_6_.1) | copy-start | bytes 1572868
  21.2 5.8 %copy-start.2 = (bf16[128,2048]{1,0:T(8,128)(2,1)S(1)}, bf16[128,2048]{1,0:T(8,128)(2,1)}, u32[]{:S(2)}) copy-start(bf16[128,2048]{1,0:T(8,128)(2,1)} %refs_7_.1) | copy-start | bytes 1572868
  21.2 1.3 %collective-permute-start.4 = (bf16[304,128]{1,0:T(8,128)(2,1)S(1)}, bf16[304,128]{1,0:T(8,128)(2,1)S(1)}, u32[]{:S(2)}, u32[]{:S(2)}) collective-permute-start(bf16[304,128]{1,0:T(8,128)(2,1)S(1)} %get-tuple-element.46.refs_7_.refs_1_), channel_id=1, source_target_pairs={{0,4},{4,0},{8,12},{12,8},{16,20},{20,16},{24,28},{28,24},{1,5},{5... | collective-permute-start | bytes 233480 | tf_op jit(solution)/shard_map/ppermute | solution.py:509
  22.6 7.2 %collective-permute-start.7 = (bf16[48,128]{1,0:T(8,128)(2,1)S(1)}, bf16[48,128]{1,0:T(8,128)(2,1)S(1)}, u32[]{:S(2)}, u32[]{:S(2)}) collective-permute-start(bf16[48,128]{1,0:T(8,128)(2,1)S(1)} %merge.1.refs_0_), channel_id=1, source_target_pairs={{0,3},{1,2},{2,1},{3,0},{4,7},{5,6},{6,5},{7,4},{8,11},{9,10},{10,... | collective-permute-start | bytes 36872 | tf_op jit(solution)/shard_map/ppermute | solution.py:626
  26.2 4.6 %collective-permute-start.6 = (bf16[48,128]{1,0:T(8,128)(2,1)S(1)}, bf16[48,128]{1,0:T(8,128)(2,1)S(1)}, u32[]{:S(2)}, u32[]{:S(2)}) collective-permute-start(bf16[48,128]{1,0:T(8,128)(2,1)S(1)} %merge.1.refs_0_), channel_id=1, source_target_pairs={{0,2},{1,3},{2,0},{3,1},{4,6},{5,7},{6,4},{7,5},{8,10},{9,11},{10,... | collective-permute-start | bytes 36872 | tf_op jit(solution)/shard_map/ppermute | solution.py:626
  26.2 4.6 %collective-permute-start.5 = (bf16[48,128]{1,0:T(8,128)(2,1)S(1)}, bf16[48,128]{1,0:T(8,128)(2,1)S(1)}, u32[]{:S(2)}, u32[]{:S(2)}) collective-permute-start(bf16[48,128]{1,0:T(8,128)(2,1)S(1)} %merge.1.refs_0_), channel_id=1, source_target_pairs={{0,1},{1,0},{2,3},{3,2},{4,5},{5,4},{6,7},{7,6},{8,9},{9,8},{10,11... | collective-permute-start | bytes 36872 | tf_op jit(solution)/shard_map/ppermute | solution.py:626
